TPU v7x, 32 devices: a whole 2x2x4 slice. The times are simulated.
32 devices in a mesh: parts: 2 (over x), store: 8 (over z, y), tensor: 2 (over core).
Axes of the slice: x: 2, y: 2, z: 4, core: 2. Of those that a mesh axis runs over, the one named last changes fastest.
Arguments:
- x_in: bfloat16 [2, 256, 8192], P(None, ('parts', 'store'), 'tensor'), parts along dimension 1, may hold values from -6 to 6
- q_base: bfloat16 [2, 256, 8192], P(None, ('parts', 'store'), 'tensor'), parts along dimension 1, may hold values from -120 to 120
- k_new: bfloat16 [2, 256, 1024], P(None, ('parts', 'store'), 'tensor'), parts along dimension 1, may hold values from -4.2 to 4.2
- v_new: bfloat16 [2, 256, 1024], P(None, ('parts', 'store'), 'tensor'), parts along dimension 1, may hold values from -6 to 6
- cache_k: bfloat16 [256, 512, 1024], P(('parts', 'store'), None, 'tensor'), parts along dimension 0, may hold values from -4 to 4
- cache_v: bfloat16 [256, 512, 1024], P(('parts', 'store'), None, 'tensor'), parts along dimension 0, may hold values from -6 to 6
- lengths: int32 [256], P(('parts', 'store')), parts along dimension 0, may hold values from 1 to 512, 16384 in all
- adapter_ids: int32 [256], P(('parts', 'store')), parts along dimension 0, may hold values from 0 to 63, as said below
- slot_of: int32 [128], P('parts'), parts along dimension 0, may hold values from 0 to 63, as said below
- a_query: bfloat16 [8192, 64, 16], P(None, 'store'), may hold values from -0.0625 to 0.0625
- b_query: bfloat16 [64, 16, 8192], P('store', None, 'tensor'), may hold values from -0.75 to 0.75
- a_output: bfloat16 [8192, 64, 16], P(None, 'store'), may hold values from -0.0625 to 0.0625
- b_output: bfloat16 [64, 16, 8192], P('store', None, 'tensor'), may hold values from -0.75 to 0.75
Outputs:
- attn_out: bfloat16 [2, 256, 8192], P(None, ('parts', 'store'), 'tensor'), parts along dimension 1
- adapter_out: bfloat16 [2, 256, 8192], P(None, ('parts', 'store'), 'tensor'), parts along dimension 1
There are 2 independent parts, one for each index of `parts`. A program takes and returns all parts, laid end to end along the dimension named above; an argument that names none is the same for every part. Nothing has to cross between parts.
Inputs may be any that keep to these rules, and one draw needn't show every extreme that they name: `adapter_ids`: each row names an adapter of the store. In every aligned block of 16 rows (the rows of one device), at most 2 rows name adapters whose slot lies in one aligned block of 8 slots, and in every draw one such slot block is named by exactly 2 rows of every row block. `slot_of`: A permutation: each slot holds one adapter. The lengths of the 128 rows of one part sum to 16384; each part is drawn for itself, so the whole array over all parts sums to that times the number of parts. One row of each part has length exactly 512.
All inputs are finite; a program needn't handle non-finite values. No bound on the sum of `lengths` on one device may be relied on, other than what follows from the above.
Results may differ from a plain program's by a relative error of at most 0.008.
Values may be sent and summed in bfloat16 or wider, within the bound.
No kernel may reach another device: no remote copies, remote signals or barrier semaphores. Data moves between devices by JAX's collectives and lax.ppermute only.
A program may use at most 128 MiB of HBM per device.

v0:
```python
import math

import jax
import jax.numpy as jnp
from jax import lax
from jax.sharding import PartitionSpec as P

HD = 128
CAP = 2


def remote(activations, a_store, b_store, dispatch, slot_buffer):
    widened = lax.all_gather(activations, "tensor", axis=2, tiled=True)
    width = widened.shape[2]
    owner_count = slot_buffer.shape[0]
    capacity = slot_buffer.shape[1]
    adapt_local = a_store.shape[1]
    rank_size = a_store.shape[2]
    outgoing = jnp.einsum("rp,srw->psw", dispatch, widened, preferred_element_type=jnp.float32)
    outgoing = outgoing.astype(jnp.bfloat16).reshape(owner_count, capacity, 2, width)
    a_flat = a_store.reshape(width, adapt_local * rank_size)
    b_flat = b_store.reshape(adapt_local * rank_size, b_store.shape[2])
    buffer = lax.all_to_all(outgoing, "store", split_axis=0, concat_axis=0, tiled=True)
    slots_in = lax.all_to_all(slot_buffer, "store", split_axis=0, concat_axis=0, tiled=True)
    sources = buffer.shape[0]
    items = buffer.shape[1]
    flat_rows = buffer.reshape(sources * items * 2, width)
    projected = jnp.dot(flat_rows, a_flat, preferred_element_type=jnp.float32)
    projected = projected.reshape(sources, items, 2, adapt_local, rank_size)
    select = slots_in[:, :, None] == jnp.arange(adapt_local, dtype=jnp.int32)[None, None, :]
    low_rank = jnp.sum(jnp.where(select[:, :, None, :, None], projected, 0.0), axis=3)
    rounded = low_rank.astype(jnp.bfloat16)
    spread = jnp.where(
        select[:, :, None, :, None], rounded[:, :, :, None, :], jnp.zeros((), jnp.bfloat16)
    )
    spread = spread.reshape(sources * items * 2, adapt_local * rank_size)
    delta = (2.0 * jnp.dot(spread, b_flat, preferred_element_type=jnp.float32)).astype(jnp.bfloat16)
    delta = delta.reshape(sources, items, 2, b_flat.shape[1])
    returned = lax.all_to_all(delta, "store", split_axis=0, concat_axis=0, tiled=True)
    returned = returned.reshape(owner_count * capacity, 2, returned.shape[3])
    return jnp.einsum("rp,psq->srq", dispatch, returned, preferred_element_type=jnp.float32)


def attend(queries, cache_k, cache_v, k_new, v_new, lengths):
    row_count = cache_k.shape[0]
    length_max = cache_k.shape[1]
    kv_heads = cache_k.shape[2] // HD
    groups = queries.shape[2] // HD // kv_heads
    scale = 1.0 / math.sqrt(HD)
    grouped = queries.reshape(2, row_count, kv_heads, groups, HD)
    keys_all = cache_k.reshape(row_count, length_max, kv_heads, HD)
    values_all = cache_v.reshape(row_count, length_max, kv_heads, HD)
    new_keys = k_new.reshape(2, row_count, kv_heads, HD)
    new_values = v_new.reshape(2, row_count, kv_heads, HD)
    cached = (
        jnp.einsum("srgjd,rlgd->srgjl", grouped, keys_all, preferred_element_type=jnp.float32)
        * scale
    )
    valid = jnp.arange(length_max, dtype=jnp.int32)[None, :] < lengths[:, None]
    cached = jnp.where(valid[None, :, None, None, :], cached, -jnp.inf)
    fresh = (
        jnp.einsum("srgjd,trgd->srgjt", grouped, new_keys, preferred_element_type=jnp.float32)
        * scale
    )
    steps_ok = jnp.arange(2, dtype=jnp.int32)[None, :] <= jnp.arange(2, dtype=jnp.int32)[:, None]
    fresh = jnp.where(steps_ok[:, None, None, None, :], fresh, -jnp.inf)
    top = jnp.maximum(jnp.max(cached, axis=-1), jnp.max(fresh, axis=-1))[..., None]
    cached_exp = jnp.exp(cached - top)
    fresh_exp = jnp.exp(fresh - top)
    total = jnp.sum(cached_exp, axis=-1, keepdims=True) + jnp.sum(fresh_exp, axis=-1, keepdims=True)
    weight_cached = (cached_exp / total).astype(jnp.bfloat16)
    weight_fresh = (fresh_exp / total).astype(jnp.bfloat16)
    mixed = jnp.einsum(
        "srgjl,rlgd->srgjd", weight_cached, values_all, preferred_element_type=jnp.float32
    )
    mixed = mixed + jnp.einsum(
        "srgjt,trgd->srgjd", weight_fresh, new_values, preferred_element_type=jnp.float32
    )
    return mixed.astype(jnp.bfloat16).reshape(2, row_count, kv_heads * groups * HD)


def shards(
    x_in,
    q_base,
    k_new,
    v_new,
    cache_k,
    cache_v,
    lengths,
    adapter_ids,
    slot_of,
    a_query,
    b_query,
    a_output,
    b_output,
):
    row_count = x_in.shape[1]
    owner_count = lax.axis_size("store")
    adapt_local = a_query.shape[1]
    table = jnp.arange(slot_of.shape[0], dtype=jnp.int32)
    global_slot = jnp.sum(
        jnp.where(adapter_ids[:, None] == table[None, :], slot_of[None, :], 0), axis=1
    )
    owner_of = global_slot // adapt_local
    local_slot = global_slot % adapt_local
    positions = jnp.arange(row_count, dtype=jnp.int32)
    earlier = positions[None, :] < positions[:, None]
    same_owner = owner_of[None, :] == owner_of[:, None]
    rank_in = jnp.sum(jnp.where(earlier & same_owner, 1, 0), axis=1)
    target = owner_of * CAP + rank_in
    places = jnp.arange(owner_count * CAP, dtype=jnp.int32)
    hits = target[:, None] == places[None, :]
    dispatch = hits.astype(jnp.bfloat16)
    slot_buffer = jnp.sum(jnp.where(hits, local_slot[:, None], 0), axis=0)
    slot_buffer = slot_buffer.reshape(owner_count, CAP)
    query_delta = remote(x_in, a_query, b_query, dispatch, slot_buffer)
    queries = (q_base.astype(jnp.float32) + query_delta).astype(jnp.bfloat16)
    attn_out = attend(queries, cache_k, cache_v, k_new, v_new, lengths)
    adapter_out = remote(attn_out, a_output, b_output, dispatch, slot_buffer).astype(jnp.bfloat16)
    return (attn_out, adapter_out)


def solution(mesh):
    in_specs = (
        P(None, ("parts", "store"), "tensor"),
        P(None, ("parts", "store"), "tensor"),
        P(None, ("parts", "store"), "tensor"),
        P(None, ("parts", "store"), "tensor"),
        P(("parts", "store"), None, "tensor"),
        P(("parts", "store"), None, "tensor"),
        P(("parts", "store")),
        P(("parts", "store")),
        P("parts"),
        P(None, "store", None),
        P("store", None, "tensor"),
        P(None, "store", None),
        P("store", None, "tensor"),
    )
    out_specs = (P(None, ("parts", "store"), "tensor"), P(None, ("parts", "store"), "tensor"))
    return jax.shard_map(shards, mesh=mesh, in_specs=in_specs, out_specs=out_specs, check_vma=False)
```

profile of v0, /device:TPU:0, one launch (start us, length us, event | category | flops | bytes accessed | tf_op | source)
XLA Modules:
  0.0 121.7 jit_solution(17292490447106288918)
XLA Ops:
  0.6 0.0 copy-start
  0.6 1.0 select_reduce_fusion.2
  1.7 0.2 select_reduce_fusion.1
  1.9 0.1 select_reduce_fusion
  1.9 0.7 all_to_all.19
  2.6 7.3 %all-to-all-start = ((s32[8,1,2]{2,1,0:T(1,128)}), s32[8,1,2]{2,1,0:T(1,128)S(1)}, u32[]{:S(2)}, u32[]{:S(2)}) async-start(s32[8,1,2]{2,1,0:T(1,128)} %bitcast), calls=%async_computation | async-start | bytes 8192 | tf_op jit(solution)/shard_map/all_to_all | solution.py:24
  9.9 2.4 %all_gather.6 = bf16[2,16,8192]{2,1,0:T(8,128)(2,1)S(1)} all-gather(bf16[2,16,4096]{2,1,0:T(8,128)(2,1)} %param.13), channel_id=1, replica_groups=mesh['parts'=2,'store'=8,'tensor'=2] {'tensor'}, dimensions={2}, use_global_device_ids=true | all-gather | bytes 786432 | tf_op jit(solution)/shard_map/all_gather | solution.py:13
  12.3 0.4 convolution_convert_fusion.1
  12.7 1.3 %copy.93 = bf16[16,2,8192]{2,1,0:T(2,128)(2,1)} copy(bf16[16,2,8192]{2,0,1:T(8,128)(2,1)S(1)} %convolution_convert_fusion.1) | data formatting | bytes 1048576 | tf_op jit(solution)/shard_map/reshape | solution.py:20
  14.0 2.3 %all-to-all-done = s32[8,1,2]{2,1,0:T(1,128)S(1)} async-done(((s32[8,1,2]{2,1,0:T(1,128)}), s32[8,1,2]{2,1,0:T(1,128)S(1)}, u32[]{:S(2)}, u32[]{:S(2)}) %all-to-all-start) | async-done | bytes 96 | tf_op jit(solution)/shard_map/all_to_all | solution.py:24
  16.3 3.7 %all-to-all-start.1 = ((bf16[8,2,2,8192]{3,2,1,0:T(2,128)(2,1)}), bf16[8,2,2,8192]{3,2,1,0:T(2,128)(2,1)S(1)}, u32[]{:S(2)}, u32[]{:S(2)}) async-start(bf16[8,2,2,8192]{3,2,1,0:T(2,128)(2,1)} %bitcast.3), calls=%async_computation.1 | async-start | bytes 1048576 | tf_op jit(solution)/shard_map/all_to_all | solution.py:23
  20.0 0.1 copy.64
  20.1 14.7 %all-to-all-done.1 = bf16[8,2,2,8192]{3,2,1,0:T(2,128)(2,1)S(1)} async-done(((bf16[8,2,2,8192]{3,2,1,0:T(2,128)(2,1)}), bf16[8,2,2,8192]{3,2,1,0:T(2,128)(2,1)S(1)}, u32[]{:S(2)}, u32[]{:S(2)}) %all-to-all-start.1) | async-done | bytes 524320 | tf_op jit(solution)/shard_map/all_to_all | solution.py:23
  34.8 0.8 copy-done.4
  35.6 4.1 %fusion.28 = bf16[8,2,2,16]{3,0,2,1:T(8,128)(2,1)S(1)} fusion(bf16[8192,8,16]{0,2,1:T(8,128)(2,1)S(1)} %copy-done, bf16[8,2,2,8192,1]{3,2,1,0,4:T(2,128)(2,1)} %bitcast.102, pred[8,2,8]{0,2,1:T(8,128)(4,1)S(1)} %iota_compare_fusion.1), kind=kOutput, calls=%fused_computation.34 | convolution fusion | flops 67116544 | bytes 2622592 | tf_op jit(solution)/shard_map/dot_general | solution.py:28
  39.7 0.1 broadcast_select_fusion.1
  39.9 0.1 select_n.94
  40.0 0.3 fusion.6
  40.2 0.9 reshape.201
  41.1 3.6 %all-to-all-start.2 = ((bf16[8,2,2,4096]{3,2,1,0:T(2,128)(2,1)}), bf16[8,2,2,4096]{3,2,1,0:T(2,128)(2,1)S(1)}, u32[]{:S(2)}, u32[]{:S(2)}) async-start(bf16[8,2,2,4096]{3,2,1,0:T(2,128)(2,1)} %reshape.201), calls=%async_computation.2 | async-start | bytes 524288 | tf_op jit(solution)/shard_map/all_to_all | solution.py:39
  44.8 12.5 %reshape.204 = bf16[16,512,4,128]{3,2,1,0:T(4,128)(2,1)} reshape(bf16[16,512,512]{2,1,0:T(8,128)(2,1)} %param.17) | data formatting | bytes 16777216 | tf_op jit(solution)/shard_map/reshape | solution.py:51
  57.3 0.0 copy-start.7
  57.4 0.0 copy-start.8
  57.4 0.0 copy-start.5
  57.4 12.6 %reshape.206 = bf16[16,512,4,128]{3,2,1,0:T(4,128)(2,1)} reshape(bf16[16,512,512]{2,1,0:T(8,128)(2,1)} %param.18) | data formatting | bytes 16777216 | tf_op jit(solution)/shard_map/reshape | solution.py:52
  70.0 0.1 iota_compare_fusion
  70.1 0.0 all-to-all-done.2
  70.1 0.3 fusion.5
  70.5 5.9 %bitcast_reduce_fusion = (f32[2,16,4,8]{3,0,2,1:T(2,128)S(1)}, f32[16,4,2,8,512]{4,3,2,1,0:T(8,128)S(1)}) fusion(pred[16,512]{1,0:T(8,128)(4,1)S(1)} %iota_compare_fusion, bf16[16,512,4,128,1]{3,2,1,0,4:T(4,128)(2,1)} %bitcast.90, bf16[2,16,4,8,128]{4,3,2,1,0:T(8,128)(2,1)S(1)} %bitcast.97), kind=kOutput, calls=%fused_computation.20 | convolution fusion | flops 135789568 | bytes 10760192 | tf_op jit(solution)/shard_map/srgjd,rlgd->srgjl/dot_general | solution.py:56
  76.4 1.3 %fusion.59 = (f32[2,16,4,8]{3,0,2,1:T(2,128)S(1)}, f32[2,16,4,8,2]{3,4,0,2,1:T(2,128)S(1)}) fusion(bf16[2,16,4,128,1]{3,2,1,0,4:T(4,128)(2,1)S(1)} %bitcast.105, bf16[2,16,4,8,128]{4,3,2,1,0:T(8,128)(2,1)S(1)} %bitcast.98, pred[2,2]{1,0:T(4,128)(4,1)S(1)} %iota_compare_fusion.5), kind=kOutput, calls=%fused_computation.78 | convolution fusion | flops 529408 | bytes 307204 | tf_op jit(solution)/shard_map/srgjd,trgd->srgjt/dot_general | solution.py:62
  77.7 0.8 fusion.14
  78.5 0.3 fusion.42
  78.9 1.7 %fusion = f32[16,4,2,8,128]{4,3,2,1,0:T(8,128)S(1)} fusion(bf16[16,512,4,128,1]{3,2,1,0,4:T(4,128)(2,1)S(1)} %bitcast.93, f32[16,4,2,8,512]{4,3,2,1,0:T(8,128)S(1)} %get-tuple-element.5, f32[2,16,4,8]{3,0,2,1:T(2,128)S(1)} %add.47, f32[2,16,4,8]{3,0,2,1:T(2,128)S(1)} %max.7, pred[16,512]{1,0:T(8,128)(4,1)S(1)} %iota_compare_fusion), kind=kOutput, calls=%fused_computation.2 | convolution fusion | flops 136839168 | bytes 11026432 | tf_op jit(solution)/shard_map/srgjl,rlgd->srgjd/dot_general | solution.py:73
  80.6 0.3 fusion.16
  81.0 0.1 reshape.208
  81.2 0.0 copy-start.3
  81.2 0.0 copy-start.9
  81.2 2.3 %all_gather.7 = bf16[2,16,8192]{2,1,0:T(8,128)(2,1)S(1)} all-gather(bf16[2,16,4096]{2,1,0:T(8,128)(2,1)S(1)} %reshape.208), channel_id=1, replica_groups=mesh['parts'=2,'store'=8,'tensor'=2] {'tensor'}, dimensions={2}, use_global_device_ids=true | all-gather | bytes 786432 | tf_op jit(solution)/shard_map/all_gather | solution.py:13
  83.5 0.4 convolution_convert_fusion
  83.9 0.5 copy.106
  84.5 20.6 %all_to_all.30 = bf16[8,2,2,8192]{3,2,1,0:T(2,128)(2,1)S(1)} all-to-all(bf16[8,2,2,8192]{3,2,1,0:T(2,128)(2,1)S(1)} %bitcast.94), channel_id=1, replica_groups=mesh['parts'=2,'store'=8,'tensor'=2] {'store'}, dimensions={0} | all-to-all | bytes 1048576 | tf_op jit(solution)/shard_map/all_to_all | solution.py:23
  105.0 3.0 %fusion.25 = bf16[8,2,2,16]{3,0,2,1:T(8,128)(2,1)S(1)} fusion(bf16[8192,8,16]{0,2,1:T(8,128)(2,1)S(1)} %copy-done.9, bf16[8,2,2,8192,1]{3,2,1,0,4:T(2,128)(2,1)S(1)} %bitcast.103, pred[8,2,8]{0,2,1:T(8,128)(4,1)S(1)} %iota_compare_fusion.1), kind=kOutput, calls=%fused_computation.33 | convolution fusion | flops 67116544 | bytes 2622592 | tf_op jit(solution)/shard_map/dot_general | solution.py:28
  108.1 0.1 broadcast_select_fusion
  108.2 0.1 select_n.101
  108.3 0.3 fusion.7
  108.6 0.2 reshape.212
  108.8 12.0 %all_to_all.31 = bf16[8,2,2,4096]{3,2,1,0:T(2,128)(2,1)S(1)} all-to-all(bf16[8,2,2,4096]{3,2,1,0:T(2,128)(2,1)S(1)} %reshape.212), channel_id=1, replica_groups=mesh['parts'=2,'store'=8,'tensor'=2] {'store'}, dimensions={0} | all-to-all | bytes 524288 | tf_op jit(solution)/shard_map/all_to_all | solution.py:39
  120.8 1.0 fusion.8
  (30 shorter events, 0.3 us)
Async XLA Ops:
  0.6 35.0 %copy-start = (bf16[8192,8,16]{0,2,1:T(8,128)(2,1)S(1)}, bf16[8192,8,16]{0,2,1:T(8,128)(2,1)}, u32[]{:S(2)}) copy-start(bf16[8192,8,16]{0,2,1:T(8,128)(2,1)} %param.22) | copy-start | bytes 6291460
  2.6 13.7 %all-to-all-start = ((s32[8,1,2]{2,1,0:T(1,128)}), s32[8,1,2]{2,1,0:T(1,128)S(1)}, u32[]{:S(2)}, u32[]{:S(2)}) async-start(s32[8,1,2]{2,1,0:T(1,128)} %bitcast), calls=%async_computation | async-start | bytes 8192 | tf_op jit(solution)/shard_map/all_to_all | solution.py:24
  16.3 18.5 %all-to-all-start.1 = ((bf16[8,2,2,8192]{3,2,1,0:T(2,128)(2,1)}), bf16[8,2,2,8192]{3,2,1,0:T(2,128)(2,1)S(1)}, u32[]{:S(2)}, u32[]{:S(2)}) async-start(bf16[8,2,2,8192]{3,2,1,0:T(2,128)(2,1)} %bitcast.3), calls=%async_computation.1 | async-start | bytes 1048576 | tf_op jit(solution)/shard_map/all_to_all | solution.py:23
  34.8 0.8 copy-start.4
  35.6 4.3 %copy-start.1 = (bf16[8,16,4096]{2,1,0:T(8,128)(2,1)S(1)}, bf16[8,16,4096]{2,1,0:T(8,128)(2,1)}, u32[]{:S(2)}) copy-start(bf16[8,16,4096]{2,1,0:T(8,128)(2,1)} %param.23) | copy-start | bytes 3145732
  41.1 28.9 %all-to-all-start.2 = ((bf16[8,2,2,4096]{3,2,1,0:T(2,128)(2,1)}), bf16[8,2,2,4096]{3,2,1,0:T(2,128)(2,1)S(1)}, u32[]{:S(2)}, u32[]{:S(2)}) async-start(bf16[8,2,2,4096]{3,2,1,0:T(2,128)(2,1)} %reshape.201), calls=%async_computation.2 | async-start | bytes 524288 | tf_op jit(solution)/shard_map/all_to_all | solution.py:39
  44.8 12.5 %copy-start.6 = (bf16[2,16,512]{2,1,0:T(8,128)(2,1)S(1)}, bf16[2,16,512]{2,1,0:T(8,128)(2,1)}, u32[]{:S(2)}) copy-start(bf16[2,16,512]{2,1,0:T(8,128)(2,1)} %param.15) | copy-start | bytes 98308
  57.3 12.6 %copy-start.7 = (bf16[2,16,512]{2,1,0:T(8,128)(2,1)S(1)}, bf16[2,16,512]{2,1,0:T(8,128)(2,1)}, u32[]{:S(2)}) copy-start(bf16[2,16,512]{2,1,0:T(8,128)(2,1)} %param.16) | copy-start | bytes 98308
  57.4 12.6 %copy-start.8 = (s32[16]{0:T(128)S(1)}, s32[16]{0:T(128)}, u32[]{:S(2)}) copy-start(s32[16]{0:T(128)} %param.19) | copy-start | bytes 196
  57.4 12.7 %copy-start.5 = (bf16[2,16,4096]{2,1,0:T(8,128)(2,1)S(1)}, bf16[2,16,4096]{2,1,0:T(8,128)(2,1)}, u32[]{:S(2)}) copy-start(bf16[2,16,4096]{2,1,0:T(8,128)(2,1)} %param.14) | copy-start | bytes 786436
  70.4 8.4 %slice-start = ((s8[8388608]{0:T(1024)(128)(4,1)}), s8[4194304]{0:T(1024)(128)(4,1)S(1)}, s32[]{:S(2)}) async-start(s8[8388608]{0:T(1024)(128)(4,1)} %bitcast.91), calls=%async_computation.5 | async-start | bytes 8388608
  70.5 8.4 %slice-start.1 = ((s8[8388608]{0:T(1024)(128)(4,1)}), s8[4194304]{0:T(1024)(128)(4,1)S(1)}, s32[]{:S(2)}) async-start(s8[8388608]{0:T(1024)(128)(4,1)} %bitcast.91), calls=%async_computation.6 | async-start | bytes 8388608
  81.2 26.9 %copy-start.3 = (bf16[2,16,4096]{2,1,0:T(8,128)(2,1)}, bf16[2,16,4096]{2,1,0:T(8,128)(2,1)S(1)}, u32[]{:S(2)}) copy-start(bf16[2,16,4096]{2,1,0:T(8,128)(2,1)S(1)} %reshape.208) | copy-start | bytes 786436
  81.2 23.9 %copy-start.9 = (bf16[8192,8,16]{0,2,1:T(8,128)(2,1)S(1)}, bf16[8192,8,16]{0,2,1:T(8,128)(2,1)}, u32[]{:S(2)}) copy-start(bf16[8192,8,16]{0,2,1:T(8,128)(2,1)} %param.24) | copy-start | bytes 6291460
  105.0 3.2 %copy-start.2 = (bf16[8,16,4096]{2,1,0:T(8,128)(2,1)S(1)}, bf16[8,16,4096]{2,1,0:T(8,128)(2,1)}, u32[]{:S(2)}) copy-start(bf16[8,16,4096]{2,1,0:T(8,128)(2,1)} %param.25) | copy-start | bytes 3145732
where the time goes:
time: 123 us; the launch traced here: 122 us
  blocking collectives  37.3 us (30%)
  local copies, waits for them, and re-layouts  30.2 us (25%)
  matrix products  19.1 us (16%)
  waiting for transfers between devices  17 us (14%)
  starting transfers between devices  14.7 us (12%)
  other arithmetic  2.68 us (2%)
    all_to_all x1, blocking collectives, remote(): lax.all_to_all(outgoing, 'store', split_axis=0, concat_axis=0, tiled=True)  20.6 us
    all_to_all x1, waiting for transfers between devices, remote(): lax.all_to_all(outgoing, 'store', split_axis=0, concat_axis=0, tiled=True)  14.7 us
    reshape x1, local copies, waits for them, and re-layouts, attend(): values_all = cache_v.reshape(row_count, length_max, kv_heads, HD)  12.6 us
    reshape x1, local copies, waits for them, and re-layouts, attend(): keys_all = cache_k.reshape(row_count, length_max, kv_heads, HD)  12.5 us
    all_to_all x1, blocking collectives, remote(): lax.all_to_all(delta, 'store', split_axis=0, concat_axis=0, tiled=True)  12 us
    all_to_all x1, starting transfers between devices, remote(): lax.all_to_all(slot_buffer, 'store', split_axis=0, concat_axis=0, tiled=T...  7.28 us
    dot_general x2, matrix products, remote(): projected = jnp.dot(flat_rows, a_flat, preferred_element_type=jnp.float32)  7.11 us
    dot_general x1, matrix products, attend(): jnp.einsum('srgjd,rlgd->srgjl', grouped, keys_all, preferred_element_type...  5.93 us
  transfers between devices with their start and end apart: 3, of which 2 were waited for; matrix products, arithmetic and copies ran while one was open for 22% of the time, Pallas kernels for 0%

commit v1 on v0

v1 whole, which is shorter than its diff:
```python
import functools
import math

import jax
import jax.numpy as jnp
from jax import lax
from jax.experimental import pallas as pl
from jax.experimental.pallas import tpu as pltpu
from jax.sharding import PartitionSpec as P

HD = 128
CAP = 2
STEPS = 2
CHUNK = 128
QUAD = 4
BF16 = jnp.bfloat16
F32 = jnp.float32
I32 = jnp.int32
VMEM = pl.BlockSpec(memory_space=pltpu.VMEM)
SMEM = pl.BlockSpec(memory_space=pltpu.SMEM)
ANY = pl.BlockSpec(memory_space=pl.ANY)


def iota(shape, dim):
    return lax.broadcasted_iota(I32, shape, dim)


def one_hot(hits):
    return jnp.where(hits, 1.0, 0.0).astype(BF16)


def stacked(ref, heads, wide):
    return jnp.concatenate(
        [ref[s, :, c * wide : (c + 1) * wide] for c in range(heads) for s in range(STEPS)], axis=0
    )


def pack_matrix(row_at, owners, heads, rows):
    items = CAP * STEPS
    block = heads * items
    shape = (block, heads * STEPS * rows)
    at = iota(shape, 0)
    col = iota(shape, 1)
    base = (at // items) * (STEPS * rows) + (at % STEPS) * rows
    first = (at // STEPS) % CAP == 0
    parts = []
    for i in range(owners):
        row = jnp.where(first, row_at[i * CAP], row_at[i * CAP + 1])
        parts.append(one_hot((col == base + row) & (row >= 0)))
    return jnp.concatenate(parts, axis=0)


def unpack_matrix(place_of, owners, heads, rows):
    items = CAP * STEPS
    block = heads * items
    shape = (rows, owners * block)
    at = iota(shape, 0)
    col = iota(shape, 1)
    spot = jnp.zeros(shape, I32)
    for r in range(rows):
        place = place_of[r]
        spot = jnp.where(at == r, (place // CAP) * block + (place % CAP) * STEPS, spot)
    return jnp.concatenate(
        [one_hot(col == spot + (c * items + s)) for c in range(heads) for s in range(STEPS)], axis=0
    )


def regroup_matrix(owners, heads):
    items = CAP * STEPS
    total = owners * heads * items
    at = iota((total, total), 0)
    col = iota((total, total), 1)
    head = at // (owners * items)
    owner = (at // items) % owners
    return one_hot(col == owner * (heads * items) + head * items + at % items)


def ungroup_matrix(owners, heads):
    items = CAP * STEPS
    total = owners * heads * items
    at = iota((total, total), 0)
    col = iota((total, total), 1)
    owner = at // (heads * items)
    head = (at // items) % heads
    return one_hot(col == head * (owners * items) + owner * items + at % items)


def exact(matrix, values):
    return jnp.dot(matrix, values, preferred_element_type=F32).astype(BF16)


def dispatch_kernel(owners, heads, adapt, rank, me, ids, slot_of, lengths, x_ref, *refs):
    place_of, row_at, slot_at, order, *blocks = refs
    rows = x_ref.shape[1]
    wide = x_ref.shape[2] // heads
    for p in range(owners * CAP):
        row_at[p] = -1
        slot_at[p] = -1
    for r in range(rows):
        slot = slot_of[ids[r]]
        relative = (slot // adapt) ^ me[0]
        taken = jnp.where(row_at[relative * CAP] >= 0, 1, 0)
        place = relative * CAP + taken
        row_at[place] = r
        slot_at[place] = slot % adapt
        place_of[r] = place
    sizes = [lengths[r] for r in range(rows)]
    for r in range(rows):
        ahead = jnp.int32(0)
        for q in range(rows):
            if q != r:
                longer = sizes[q] >= sizes[r] if q < r else sizes[q] > sizes[r]
                ahead = ahead + jnp.where(longer, 1, 0)
        order[ahead] = r
    items = CAP * STEPS
    block = heads * items
    packed = exact(pack_matrix(row_at, owners, heads, rows), stacked(x_ref, heads, wide))
    at = iota((block, adapt * rank), 0)
    lane_slot = iota((block, adapt * rank), 1) // rank
    first = (at // STEPS) % CAP == 0
    for i in range(owners):
        blocks[i][:, :wide] = packed[i * block : (i + 1) * block]
        slot = jnp.where(first, slot_at[i * CAP], slot_at[i * CAP + 1])
        blocks[i][:, wide:] = one_hot(lane_slot == slot)


def project_kernel(owners, heads, wide, first, a_ref, *refs):
    if first:
        blocks, (part_ref, mask_ref) = refs[:owners], refs[owners:]
    else:
        blocks, (mask_in, part_ref) = refs[:owners], refs[owners:]
    grouped = regroup_matrix(owners, heads)
    items = owners * CAP * STEPS
    arrived = jnp.concatenate([b[:, :wide] for b in blocks], axis=0)
    arrived = exact(grouped, arrived)
    if first:
        masks = jnp.concatenate([b[:, wide:] for b in blocks], axis=0)
        mask = jnp.dot(grouped[:items], masks, preferred_element_type=F32)
        mask_ref[...] = mask
    else:
        mask = mask_in[...]
    total = jnp.zeros(mask.shape, F32)
    for c in range(heads):
        total = total + lax.dot_general(
            arrived[c * items : (c + 1) * items],
            a_ref[:, c * wide : (c + 1) * wide],
            (((1,), (1,)), ((), ())),
            preferred_element_type=F32,
        )
    part_ref[...] = total * mask


def expand_kernel(owners, heads, wide, mine, other, b_ref, *blocks):
    low_rank = (mine[...] + other[...]).astype(BF16)
    pieces = []
    for c in range(heads):
        product = jnp.dot(
            low_rank, b_ref[:, c * wide : (c + 1) * wide], preferred_element_type=F32
        )
        pieces.append((2.0 * product).astype(BF16))
    back = exact(ungroup_matrix(owners, heads), jnp.concatenate(pieces, axis=0))
    block = heads * CAP * STEPS
    for i in range(owners):
        blocks[i][...] = back[i * block : (i + 1) * block]


def attend_kernel(
    owners, heads, place_of, row_at, order, lengths, q_ref, kn_ref, vn_ref, k_any, v_any, *refs
):
    blocks = refs[:owners]
    out_ref = refs[owners]
    outgoing = refs[owners + 1 : 2 * owners + 1]
    k_buf, v_buf, q_buf, o_buf, k_sem, v_sem = refs[2 * owners + 1 :]
    rows = q_ref.shape[1]
    wide = q_ref.shape[2] // heads
    groups = wide // HD
    span = STEPS * groups
    width = heads * HD
    sizes = k_any.shape[1] // CHUNK

    def copies(row, amount):
        part = pl.ds(0, amount * CHUNK)
        return (
            pltpu.make_async_copy(k_any.at[row, part], k_buf.at[row, part], k_sem.at[row]),
            pltpu.make_async_copy(v_any.at[row, part], v_buf.at[row, part], v_sem.at[row]),
        )

    def per_quad(action):
        def body(quad, carry):
            longest = lengths[order[quad * QUAD]]
            amount = (longest + CHUNK - 1) // CHUNK
            for size in range(1, sizes + 1):

                @pl.when(amount == size)
                def _():
                    action([order[quad * QUAD + j] for j in range(QUAD)], size)

            return carry

        lax.fori_loop(0, rows // QUAD, body, 0)

    def begin(rows_in, size):
        for row in rows_in:
            for copy in copies(row, size):
                copy.start()

    per_quad(begin)

    delta = jnp.dot(
        unpack_matrix(place_of, owners, heads, rows),
        jnp.concatenate([b[...] for b in blocks], axis=0),
        preferred_element_type=F32,
    )
    query = (stacked(q_ref, heads, wide).astype(F32) + delta).astype(BF16).astype(F32)
    for c in range(heads):
        for s in range(STEPS):
            top = (c * STEPS + s) * rows
            for j in range(groups):
                q_buf[pl.ds(c * span + s * groups + j, rows, stride=heads * span), :] = query[
                    top : top + rows, j * HD : (j + 1) * HD
                ]

    scale = 1.0 / math.sqrt(HD)
    new_keys = jnp.concatenate([kn_ref[t] for t in range(STEPS)], axis=0)
    new_values = jnp.concatenate([vn_ref[t] for t in range(STEPS)], axis=0)
    total = heads * span
    diagonal = iota((total, width), 0) // span == iota((total, width), 1) // HD
    fresh_shape = (total, STEPS * rows)
    step_of = (iota(fresh_shape, 0) // groups) % STEPS
    fresh_at = iota(fresh_shape, 1)
    in_time = fresh_at // rows <= step_of
    contract = (((1,), (1,)), ((), ()))

    def attend(rows_in, size):
        for row in rows_in:
            for copy in copies(row, size):
                copy.wait()
        length_now = size * CHUNK
        position = iota((total, length_now), 1)
        for row in rows_in:
            start = pl.multiple_of(row * total, total)
            one = q_buf[pl.ds(start, total), :].astype(BF16)
            spread = jnp.where(diagonal, jnp.concatenate([one] * heads, axis=1), jnp.zeros((), BF16))
            keys = k_buf[row, :length_now, :]
            values = v_buf[row, :length_now, :]
            cached = lax.dot_general(spread, keys, contract, preferred_element_type=F32) * scale
            cached = jnp.where(position < lengths[row], cached, -jnp.inf)
            fresh = lax.dot_general(spread, new_keys, contract, preferred_element_type=F32) * scale
            fresh = jnp.where(in_time & (fresh_at % rows == row), fresh, -jnp.inf)
            top = jnp.maximum(
                jnp.max(cached, axis=1, keepdims=True), jnp.max(fresh, axis=1, keepdims=True)
            )
            cached = jnp.exp(cached - top)
            fresh = jnp.exp(fresh - top)
            norm = jnp.sum(cached, axis=1, keepdims=True) + jnp.sum(fresh, axis=1, keepdims=True)
            share = 1.0 / norm
            mixed = jnp.dot((cached * share).astype(BF16), values, preferred_element_type=F32)
            mixed = mixed + jnp.dot(
                (fresh * share).astype(BF16), new_values, preferred_element_type=F32
            )
            o_buf[pl.ds(start, total), :] = jnp.concatenate(
                [
                    mixed[c * span : (c + 1) * span, c * HD : (c + 1) * HD]
                    for c in range(heads)
                ],
                axis=0,
            )

    per_quad(attend)

    results = []
    for c in range(heads):
        for s in range(STEPS):
            tiles = [
                o_buf[pl.ds(c * span + s * groups + j, rows, stride=heads * span), :].astype(BF16)
                for j in range(groups)
            ]
            piece = jnp.concatenate(tiles, axis=1)
            out_ref[s, :, c * wide : (c + 1) * wide] = piece
            results.append(piece)
    packed = exact(pack_matrix(row_at, owners, heads, rows), jnp.concatenate(results, axis=0))
    block = heads * CAP * STEPS
    for i in range(owners):
        outgoing[i][...] = packed[i * block : (i + 1) * block]


def collect_kernel(owners, heads, place_of, *refs):
    blocks, out_ref = refs[:owners], refs[owners]
    rows = out_ref.shape[1]
    wide = out_ref.shape[2] // heads
    arrived = jnp.concatenate([b[...] for b in blocks], axis=0)
    values = exact(unpack_matrix(place_of, owners, heads, rows), arrived)
    for c in range(heads):
        for s in range(STEPS):
            top = (c * STEPS + s) * rows
            out_ref[s, :, c * wide : (c + 1) * wide] = values[top : top + rows]


def exchange(blocks):
    owners = len(blocks)
    arrived = [blocks[0]] + [None] * (owners - 1)
    for i in range(owners - 1, 0, -1):
        arrived[i] = lax.ppermute(blocks[i], "store", [(s, s ^ i) for s in range(owners)])
    return arrived


def swap_cores(part):
    return lax.ppermute(part, "tensor", [(0, 1), (1, 0)])


def shards(
    x_in,
    q_base,
    k_new,
    v_new,
    cache_k,
    cache_v,
    lengths,
    adapter_ids,
    slot_of,
    a_query,
    b_query,
    a_output,
    b_output,
):
    owners = lax.axis_size("store")
    rows = x_in.shape[1]
    width = x_in.shape[2]
    heads = cache_k.shape[2] // HD
    wide = width // heads
    adapt, rank = a_query.shape[1:]
    lanes = adapt * rank
    block = heads * CAP * STEPS
    items = owners * CAP * STEPS
    me = lax.axis_index("store").astype(I32).reshape(1)
    core = lax.axis_index("tensor")

    def half(a_store):
        flat = jnp.transpose(a_store, (1, 2, 0)).reshape(lanes, a_store.shape[0])
        return lax.dynamic_slice(flat, (0, core * width), (lanes, width))

    shape = jax.ShapeDtypeStruct
    small = pltpu.CompilerParams(vmem_limit_bytes=16 * 1024 * 1024)

    place_of, row_at, _, order, *blocks = pl.pallas_call(
        functools.partial(dispatch_kernel, owners, heads, adapt, rank),
        out_shape=[
            shape((rows,), I32),
            shape((owners * CAP,), I32),
            shape((owners * CAP,), I32),
            shape((rows,), I32),
        ]
        + [shape((block, wide + lanes), BF16)] * owners,
        in_specs=[SMEM] * 4 + [VMEM],
        out_specs=[SMEM] * 4 + [VMEM] * owners,
        compiler_params=small,
        name="dispatch",
    )(me, adapter_ids, slot_of, lengths, x_in)

    arrived = exchange(blocks)
    part, mask = pl.pallas_call(
        functools.partial(project_kernel, owners, heads, wide, True),
        out_shape=[shape((items, lanes), F32)] * 2,
        in_specs=[VMEM] * (owners + 1),
        out_specs=[VMEM] * 2,
        compiler_params=small,
        name="project_query",
    )(half(a_query), *arrived)

    def expand(part, b_store, name):
        return pl.pallas_call(
            functools.partial(expand_kernel, owners, heads, wide),
            out_shape=[shape((block, wide), BF16)] * owners,
            in_specs=[VMEM] * 3,
            out_specs=[VMEM] * owners,
            compiler_params=small,
            name=name,
        )(part, swap_cores(part), b_store.reshape(lanes, width))

    returned = exchange(expand(part, b_query, "expand_query"))

    attn_out, *outgoing = pl.pallas_call(
        functools.partial(attend_kernel, owners, heads),
        out_shape=[shape((STEPS, rows, width), BF16)] + [shape((block, wide), BF16)] * owners,
        in_specs=[SMEM] * 4 + [VMEM] * 3 + [ANY] * 2 + [VMEM] * owners,
        out_specs=[VMEM] * (owners + 1),
        scratch_shapes=[
            pltpu.VMEM(cache_k.shape, BF16),
            pltpu.VMEM(cache_v.shape, BF16),
            pltpu.VMEM((rows * STEPS * width // HD, HD), F32),
            pltpu.VMEM((rows * STEPS * width // HD, HD), F32),
            pltpu.SemaphoreType.DMA((rows,)),
            pltpu.SemaphoreType.DMA((rows,)),
        ],
        compiler_params=pltpu.CompilerParams(vmem_limit_bytes=32 * 1024 * 1024),
        name="attend",
    )(place_of, row_at, order, lengths, q_base, k_new, v_new, cache_k, cache_v, *returned)

    arrived = exchange(outgoing)
    part = pl.pallas_call(
        functools.partial(project_kernel, owners, heads, wide, False),
        out_shape=shape((items, lanes), F32),
        in_specs=[VMEM] * (owners + 2),
        out_specs=VMEM,
        compiler_params=small,
        name="project_output",
    )(half(a_output), *arrived, mask)
    returned = exchange(expand(part, b_output, "expand_output"))
    adapter_out = pl.pallas_call(
        functools.partial(collect_kernel, owners, heads),
        out_shape=shape((STEPS, rows, width), BF16),
        in_specs=[SMEM] + [VMEM] * owners,
        out_specs=VMEM,
        compiler_params=small,
        name="collect",
    )(place_of, *returned)
    return (attn_out, adapter_out)


def solution(mesh):
    in_specs = (
        P(None, ("parts", "store"), "tensor"),
        P(None, ("parts", "store"), "tensor"),
        P(None, ("parts", "store"), "tensor"),
        P(None, ("parts", "store"), "tensor"),
        P(("parts", "store"), None, "tensor"),
        P(("parts", "store"), None, "tensor"),
        P(("parts", "store")),
        P(("parts", "store")),
        P("parts"),
        P(None, "store", None),
        P("store", None, "tensor"),
        P(None, "store", None),
        P("store", None, "tensor"),
    )
    out_specs = (P(None, ("parts", "store"), "tensor"), P(None, ("parts", "store"), "tensor"))
    return jax.shard_map(shards, mesh=mesh, in_specs=in_specs, out_specs=out_specs, check_vma=False)
```

time: 123 us -> 96.8 us (0.79)
  blocking collectives: 37.3 us -> 0 us
  starting transfers between devices: 14.7 us -> 46.6 us
  local copies, waits for them, and re-layouts: 30.2 us -> 10 us
  Pallas kernels: 0 us -> 19.4 us
  matrix products: 19.1 us -> 0 us
  other arithmetic: 2.68 us -> 0 us
  waiting for transfers between devices: 17 us -> 19.6 us
    ppermute x0 -> x30, starting transfers between devices: none -> 46.6 us  [the longest x28 46.6 us: exchange(): lax.ppermute(blocks[i], 'store', [(s, s ^ i) for s in range(owners)])]
    all_to_all x2 -> x0, blocking collectives: 32.6 us -> none  [the longest x1 20.6 us: remote(): lax.all_to_all(outgoing, 'store', split_axis=0, concat_axis=0, tiled=True)]
    reshape x9 -> x0, local copies, waits for them, and re-layouts: 28.2 us -> none  [the longest x1 12.6 us: attend(): values_all = cache_v.reshape(row_count, length_max, kv_heads, HD)]
    ppermute x0 -> x30, waiting for transfers between devices: none -> 19.6 us  [the longest x28 17.2 us: exchange(): lax.ppermute(blocks[i], 'store', [(s, s ^ i) for s in range(owners)])]
    pallas_call x0 -> x7, Pallas kernels: none -> 19.4 us  [the longest x1 14 us: shards(): pl.pallas_call(functools.partial(attend_kernel, owners, heads), out_shape...]
    dot_general x12 -> x0, matrix products: 19.1 us -> none  [the longest x2 7.11 us: remote(): projected = jnp.dot(flat_rows, a_flat, preferred_element_type=jnp.float32)]
    all_to_all x3 -> x0, waiting for transfers between devices: 17 us -> none  [the longest x1 14.7 us: remote(): lax.all_to_all(outgoing, 'store', split_axis=0, concat_axis=0, tiled=True)]
    all_to_all x3 -> x0, starting transfers between devices: 14.7 us -> none  [the longest x1 7.28 us: remote(): lax.all_to_all(slot_buffer, 'store', split_axis=0, concat_axis=0, tiled=T...]
  transfers between devices with their start and end apart: 3 -> 30, of which waited for: 2 -> 12; matrix products, arithmetic and copies ran while one was open for 22% -> 0% of each run, Pallas kernels for 0% -> 0%
where the time goes in v1:
time: 96.8 us; the launch traced here: 96.4 us
  starting transfers between devices  46.6 us (48%)
  waiting for transfers between devices  19.6 us (20%)
  Pallas kernels  19.4 us (20%)
  local copies, waits for them, and re-layouts  10 us (10%)
    ppermute x28, starting transfers between devices, exchange(): lax.ppermute(blocks[i], 'store', [(s, s ^ i) for s in range(owners)])  46.6 us
    ppermute x28, waiting for transfers between devices, exchange(): lax.ppermute(blocks[i], 'store', [(s, s ^ i) for s in range(owners)])  17.2 us
    pallas_call x1, Pallas kernels, shards(): pl.pallas_call(functools.partial(attend_kernel, owners, heads), out_shape...  14 us
    unnamed x28, local copies, waits for them, and re-layouts  9.86 us
    ppermute x2, waiting for transfers between devices, swap_cores(): return lax.ppermute(part, 'tensor', [(0, 1), (1, 0)])  2.4 us
  transfers between devices with their start and end apart: 30, of which 12 were waited for; matrix products, arithmetic and copies ran while one was open for 0% of the time, Pallas kernels for 0%

profile of v1, /device:TPU:0, one launch (start us, length us, event | category | flops | bytes accessed | tf_op | source)
XLA Modules:
  0.0 96.4 jit_solution(6128080738333992863)
XLA Ops:
  0.7 1.1 %copy-done.6 = bf16[2,16,4096]{2,1,0:T(8,128)(2,1)S(1)} copy-done((bf16[2,16,4096]{2,1,0:T(8,128)(2,1)S(1)}, bf16[2,16,4096]{2,1,0:T(8,128)(2,1)}, u32[]{:S(2)}) %copy-start.6) | copy-done | bytes 262168
  1.8 0.7 copy-done.9
  2.4 0.7 copy-done.11
  3.1 0.7 copy-done.12
  3.7 1.7 %dispatch.1 = (s32[16]{0:T(128)S(1)}, s32[16]{0:T(128)S(1)}, s32[16]{0:T(128)}, s32[16]{0:T(128)S(1)}, bf16[16,1152]{1,0:T(8,128)(2,1)S(1)}, /*index=5*/bf16[16,...) custom-call(s32[1]{0:T(128)} %bitcast.me, ...), custom_call_target="tpu_custom_call" | custom-call | tf_op jit(solution)/shard_map/dispatch/pallas_call | solution.py:345
  5.5 3.0 %collective-permute-start = (bf16[16,1152]{1,0:T(8,128)(2,1)}, bf16[16,1152]{1,0:T(8,128)(2,1)S(1)}, u32[]{:S(2)}, u32[]{:S(2)}) collective-permute-start(bf16[16,1152]{1,0:T(8,128)(2,1)} %get-tuple-element.44), channel_id=1, source_target_pairs={{0,2},{2,0},{4,6},{6,4},{8,10},{10,8},{12,14},{14,12},{1,3},{3,1},... | collective-permute-start | bytes 110600 | tf_op jit(solution)/shard_map/ppermute | solution.py:303
  8.5 1.6 %collective-permute-start.1 = (bf16[16,1152]{1,0:T(8,128)(2,1)}, bf16[16,1152]{1,0:T(8,128)(2,1)S(1)}, u32[]{:S(2)}, u32[]{:S(2)}) collective-permute-start(bf16[16,1152]{1,0:T(8,128)(2,1)} %get-tuple-element.45), channel_id=1, source_target_pairs={{0,4},{2,6},{4,0},{6,2},{8,12},{10,14},{12,8},{14,10},{1,5},{3,7},... | collective-permute-start | bytes 110600 | tf_op jit(solution)/shard_map/ppermute | solution.py:303
  10.1 3.0 %collective-permute-start.3 = (bf16[16,1152]{1,0:T(8,128)(2,1)S(1)}, bf16[16,1152]{1,0:T(8,128)(2,1)S(1)}, u32[]{:S(2)}, u32[]{:S(2)}) collective-permute-start(bf16[16,1152]{1,0:T(8,128)(2,1)S(1)} %get-tuple-element.47), channel_id=1, source_target_pairs={{0,8},{2,10},{4,12},{6,14},{8,0},{10,2},{12,4},{14,6},{1,9},{3,11}... | collective-permute-start | bytes 110600 | tf_op jit(solution)/shard_map/ppermute | solution.py:303
  13.1 1.3 %collective-permute-start.4 = (bf16[16,1152]{1,0:T(8,128)(2,1)S(1)}, bf16[16,1152]{1,0:T(8,128)(2,1)S(1)}, u32[]{:S(2)}, u32[]{:S(2)}) collective-permute-start(bf16[16,1152]{1,0:T(8,128)(2,1)S(1)} %get-tuple-element.48), channel_id=1, source_target_pairs={{0,10},{2,8},{4,14},{6,12},{8,2},{10,0},{12,6},{14,4},{1,11},{3,9}... | collective-permute-start | bytes 110600 | tf_op jit(solution)/shard_map/ppermute | solution.py:303
  14.3 3.6 %collective-permute-start.5 = (bf16[16,1152]{1,0:T(8,128)(2,1)S(1)}, bf16[16,1152]{1,0:T(8,128)(2,1)S(1)}, u32[]{:S(2)}, u32[]{:S(2)}) collective-permute-start(bf16[16,1152]{1,0:T(8,128)(2,1)S(1)} %get-tuple-element.49), channel_id=1, source_target_pairs={{0,12},{2,14},{4,8},{6,10},{8,4},{10,6},{12,0},{14,2},{1,13},{3,15... | collective-permute-start | bytes 110600 | tf_op jit(solution)/shard_map/ppermute | solution.py:303
  18.0 0.1 constant_dynamic-slice_fusion.1.a_ref
  18.1 0.9 collective-permute-done.4.refs_5_
  19.0 1.2 %collective-permute-done.5.refs_6_ = bf16[16,1152]{1,0:T(8,128)(2,1)S(1)} collective-permute-done((bf16[16,1152]{1,0:T(8,128)(2,1)S(1)}, bf16[16,1152]{1,0:T(8,128)(2,1)S(1)}, u32[]{:S(2)}, u32[]{:S(2)}) %collective-permute-start.5) | collective-permute-done | bytes 36896 | tf_op jit(solution)/shard_map/ppermute | solution.py:303
  20.3 4.3 %collective-permute-done.6.refs_7_ = bf16[16,1152]{1,0:T(8,128)(2,1)S(1)} collective-permute-done((bf16[16,1152]{1,0:T(8,128)(2,1)S(1)}, bf16[16,1152]{1,0:T(8,128)(2,1)S(1)}, u32[]{:S(2)}, u32[]{:S(2)}) %collective-permute-start.6) | collective-permute-done | bytes 36896 | tf_op jit(solution)/shard_map/ppermute | solution.py:303
  24.6 0.6 project_query.1
  25.2 1.2 %collective-permute-done.7.other = f32[32,128]{1,0:T(8,128)S(1)} collective-permute-done((f32[32,128]{1,0:T(8,128)S(1)}, f32[32,128]{1,0:T(8,128)S(1)}, u32[]{:S(2)}, u32[]{:S(2)}) %collective-permute-start.7) | collective-permute-done | bytes 16416 | tf_op jit(solution)/shard_map/ppermute | solution.py:308
  26.4 0.5 expand_query.1
  26.9 0.6 collective-permute-start.8
  27.5 3.0 %collective-permute-start.10 = (bf16[16,1024]{1,0:T(8,128)(2,1)S(1)}, bf16[16,1024]{1,0:T(8,128)(2,1)S(1)}, u32[]{:S(2)}, u32[]{:S(2)}) collective-permute-start(bf16[16,1024]{1,0:T(8,128)(2,1)S(1)} %get-tuple-element.55), channel_id=1, source_target_pairs={{0,6},{2,4},{4,2},{6,0},{8,14},{10,12},{12,10},{14,8},{1,7},{3,5},... | collective-permute-start | bytes 98312 | tf_op jit(solution)/shard_map/ppermute | solution.py:303
  30.5 2.9 %collective-permute-start.12 = (bf16[16,1024]{1,0:T(8,128)(2,1)S(1)}, bf16[16,1024]{1,0:T(8,128)(2,1)S(1)}, u32[]{:S(2)}, u32[]{:S(2)}) collective-permute-start(bf16[16,1024]{1,0:T(8,128)(2,1)S(1)} %get-tuple-element.57), channel_id=1, source_target_pairs={{0,10},{2,8},{4,14},{6,12},{8,2},{10,0},{12,6},{14,4},{1,11},{3,9}... | collective-permute-start | bytes 98312 | tf_op jit(solution)/shard_map/ppermute | solution.py:303
  33.3 0.5 collective-permute-start.13
  33.8 4.3 %collective-permute-start.14 = (bf16[16,1024]{1,0:T(8,128)(2,1)S(1)}, bf16[16,1024]{1,0:T(8,128)(2,1)S(1)}, u32[]{:S(2)}, u32[]{:S(2)}) collective-permute-start(bf16[16,1024]{1,0:T(8,128)(2,1)S(1)} %get-tuple-element.59), channel_id=1, source_target_pairs={{0,14},{2,12},{4,10},{6,8},{8,6},{10,4},{12,2},{14,0},{1,15},{3,13... | collective-permute-start | bytes 98312 | tf_op jit(solution)/shard_map/ppermute | solution.py:303
  38.1 0.9 collective-permute-done.13.refs_6_
  39.0 1.4 %collective-permute-done.14.refs_7_ = bf16[16,1024]{1,0:T(8,128)(2,1)S(1)} collective-permute-done((bf16[16,1024]{1,0:T(8,128)(2,1)S(1)}, bf16[16,1024]{1,0:T(8,128)(2,1)S(1)}, u32[]{:S(2)}, u32[]{:S(2)}) %collective-permute-start.14) | collective-permute-done | bytes 32800 | tf_op jit(solution)/shard_map/ppermute | solution.py:303
  40.4 3.4 %copy-done.1 = bf16[16,512,512]{2,1,0:T(8,128)(2,1)S(1)} copy-done((bf16[16,512,512]{2,1,0:T(8,128)(2,1)S(1)}, bf16[16,512,512]{2,1,0:T(8,128)(2,1)}, u32[]{:S(2)}) %copy-start.1) | copy-done | bytes 8388632
  43.8 3.4 %copy-done.2 = bf16[16,512,512]{2,1,0:T(8,128)(2,1)S(1)} copy-done((bf16[16,512,512]{2,1,0:T(8,128)(2,1)S(1)}, bf16[16,512,512]{2,1,0:T(8,128)(2,1)}, u32[]{:S(2)}) %copy-start.2) | copy-done | bytes 8388632
  47.2 14.0 %attend.1 = (bf16[2,16,4096]{2,1,0:T(8,128)(2,1)}, bf16[16,1024]{1,0:T(8,128)(2,1)S(1)}, bf16[16,1024]{1,0:T(8,128)(2,1)S(1)}, bf16[16,1024]{1,0:T(8,128)(2,1)S(...) custom-call(s32[16]{0:T(128)S(1)} %get-tuple-element.40.place_of, ...), custom_call_target="tpu_custom_call" | custom-call | tf_op jit(solution)/shard_map/attend/pallas_call | solution.py:382
  61.2 1.4 %collective-permute-start.15 = (bf16[16,1024]{1,0:T(8,128)(2,1)S(1)}, bf16[16,1024]{1,0:T(8,128)(2,1)S(1)}, u32[]{:S(2)}, u32[]{:S(2)}) collective-permute-start(bf16[16,1024]{1,0:T(8,128)(2,1)S(1)} %get-tuple-element.62), channel_id=1, source_target_pairs={{0,2},{2,0},{4,6},{6,4},{8,10},{10,8},{12,14},{14,12},{1,3},{3,1},... | collective-permute-start | bytes 98312 | tf_op jit(solution)/shard_map/ppermute | solution.py:303
  62.6 2.1 %collective-permute-start.17 = (bf16[16,1024]{1,0:T(8,128)(2,1)S(1)}, bf16[16,1024]{1,0:T(8,128)(2,1)S(1)}, u32[]{:S(2)}, u32[]{:S(2)}) collective-permute-start(bf16[16,1024]{1,0:T(8,128)(2,1)S(1)} %get-tuple-element.64), channel_id=1, source_target_pairs={{0,6},{2,4},{4,2},{6,0},{8,14},{10,12},{12,10},{14,8},{1,7},{3,5},... | collective-permute-start | bytes 98312 | tf_op jit(solution)/shard_map/ppermute | solution.py:303
  64.8 2.8 %collective-permute-start.18 = (bf16[16,1024]{1,0:T(8,128)(2,1)S(1)}, bf16[16,1024]{1,0:T(8,128)(2,1)S(1)}, u32[]{:S(2)}, u32[]{:S(2)}) collective-permute-start(bf16[16,1024]{1,0:T(8,128)(2,1)S(1)} %get-tuple-element.65), channel_id=1, source_target_pairs={{0,8},{2,10},{4,12},{6,14},{8,0},{10,2},{12,4},{14,6},{1,9},{3,11}... | collective-permute-start | bytes 98312 | tf_op jit(solution)/shard_map/ppermute | solution.py:303
  67.5 1.0 collective-permute-start.19
  68.5 3.5 %collective-permute-start.20 = (bf16[16,1024]{1,0:T(8,128)(2,1)S(1)}, bf16[16,1024]{1,0:T(8,128)(2,1)S(1)}, u32[]{:S(2)}, u32[]{:S(2)}) collective-permute-start(bf16[16,1024]{1,0:T(8,128)(2,1)S(1)} %get-tuple-element.67), channel_id=1, source_target_pairs={{0,12},{2,14},{4,8},{6,10},{8,4},{10,6},{12,0},{14,2},{1,13},{3,15... | collective-permute-start | bytes 98312 | tf_op jit(solution)/shard_map/ppermute | solution.py:303
  72.0 0.9 collective-permute-start.21
  72.9 0.1 constant_dynamic-slice_fusion.a_ref
  73.0 0.6 collective-permute-done.19.refs_5_
  73.6 0.7 collective-permute-done.20.refs_6_
  74.3 4.4 %collective-permute-done.21.refs_7_ = bf16[16,1024]{1,0:T(8,128)(2,1)S(1)} collective-permute-done((bf16[16,1024]{1,0:T(8,128)(2,1)S(1)}, bf16[16,1024]{1,0:T(8,128)(2,1)S(1)}, u32[]{:S(2)}, u32[]{:S(2)}) %collective-permute-start.21) | collective-permute-done | bytes 32800 | tf_op jit(solution)/shard_map/ppermute | solution.py:303
  78.6 0.6 project_output.1.mine
  79.3 1.2 %collective-permute-done.22.other = f32[32,128]{1,0:T(8,128)S(1)} collective-permute-done((f32[32,128]{1,0:T(8,128)S(1)}, f32[32,128]{1,0:T(8,128)S(1)}, u32[]{:S(2)}, u32[]{:S(2)}) %collective-permute-start.22) | collective-permute-done | bytes 16416 | tf_op jit(solution)/shard_map/ppermute | solution.py:308
  80.4 0.5 expand_output.1
  80.9 1.4 %collective-permute-start.23 = (bf16[16,1024]{1,0:T(8,128)(2,1)S(1)}, bf16[16,1024]{1,0:T(8,128)(2,1)S(1)}, u32[]{:S(2)}, u32[]{:S(2)}) collective-permute-start(bf16[16,1024]{1,0:T(8,128)(2,1)S(1)} %get-tuple-element.71), channel_id=1, source_target_pairs={{0,2},{2,0},{4,6},{6,4},{8,10},{10,8},{12,14},{14,12},{1,3},{3,1},... | collective-permute-start | bytes 98312 | tf_op jit(solution)/shard_map/ppermute | solution.py:303
  82.3 2.1 %collective-permute-start.25 = (bf16[16,1024]{1,0:T(8,128)(2,1)S(1)}, bf16[16,1024]{1,0:T(8,128)(2,1)S(1)}, u32[]{:S(2)}, u32[]{:S(2)}) collective-permute-start(bf16[16,1024]{1,0:T(8,128)(2,1)S(1)} %get-tuple-element.73), channel_id=1, source_target_pairs={{0,6},{2,4},{4,2},{6,0},{8,14},{10,12},{12,10},{14,8},{1,7},{3,5},... | collective-permute-start | bytes 98312 | tf_op jit(solution)/shard_map/ppermute | solution.py:303
  84.5 3.7 %collective-permute-start.27 = (bf16[16,1024]{1,0:T(8,128)(2,1)S(1)}, bf16[16,1024]{1,0:T(8,128)(2,1)S(1)}, u32[]{:S(2)}, u32[]{:S(2)}) collective-permute-start(bf16[16,1024]{1,0:T(8,128)(2,1)S(1)} %get-tuple-element.75), channel_id=1, source_target_pairs={{0,10},{2,8},{4,14},{6,12},{8,2},{10,0},{12,6},{14,4},{1,11},{3,9}... | collective-permute-start | bytes 98312 | tf_op jit(solution)/shard_map/ppermute | solution.py:303
  88.2 0.1 collective-permute-start.28
  88.2 3.9 %collective-permute-start.29 = (bf16[16,1024]{1,0:T(8,128)(2,1)S(1)}, bf16[16,1024]{1,0:T(8,128)(2,1)S(1)}, u32[]{:S(2)}, u32[]{:S(2)}) collective-permute-start(bf16[16,1024]{1,0:T(8,128)(2,1)S(1)} %get-tuple-element.77), channel_id=1, source_target_pairs={{0,14},{2,12},{4,10},{6,8},{8,6},{10,4},{12,2},{14,0},{1,15},{3,13... | collective-permute-start | bytes 98312 | tf_op jit(solution)/shard_map/ppermute | solution.py:303
  92.1 1.8 %collective-permute-done.28.refs_6_ = bf16[16,1024]{1,0:T(8,128)(2,1)S(1)} collective-permute-done((bf16[16,1024]{1,0:T(8,128)(2,1)S(1)}, bf16[16,1024]{1,0:T(8,128)(2,1)S(1)}, u32[]{:S(2)}, u32[]{:S(2)}) %collective-permute-start.28) | collective-permute-done | bytes 32800 | tf_op jit(solution)/shard_map/ppermute | solution.py:303
  93.9 1.0 %collective-permute-done.29.refs_7_ = bf16[16,1024]{1,0:T(8,128)(2,1)S(1)} collective-permute-done((bf16[16,1024]{1,0:T(8,128)(2,1)S(1)}, bf16[16,1024]{1,0:T(8,128)(2,1)S(1)}, u32[]{:S(2)}, u32[]{:S(2)}) %collective-permute-start.29) | collective-permute-done | bytes 32800 | tf_op jit(solution)/shard_map/ppermute | solution.py:303
  94.9 1.5 %collect.1 = bf16[2,16,4096]{2,1,0:T(8,128)(2,1)} custom-call(s32[16]{0:T(128)S(1)} %get-tuple-element.40.place_of, bf16[16,1024]{1,0:T(8,128)(2,1)S(1)} %get-tuple-element.70.refs_0_, bf16[16,1024]{1,0:T(8,128)(2,1)S(1)} %collective-permute-done.23.refs_1_, bf16[16,1024]{1,0:T(8,128)(2,1)S(1)} %collective-permute-done.24.refs_2_, ...), custom_call_target="tpu_custom_call" | custom-call | tf_op jit(solution)/shard_map/collect/pallas_call | solution.py:409
  (49 shorter events, 0.1 us)
Async XLA Ops:
  0.6 17.3 %copy-start = (bf16[8192,8,16]{0,2,1:T(8,128)(2,1)S(1)}, bf16[8192,8,16]{0,2,1:T(8,128)(2,1)}, u32[]{:S(2)}) copy-start(bf16[8192,8,16]{0,2,1:T(8,128)(2,1)} %param.22) | copy-start | bytes 6291460
  0.6 25.8 %copy-start.3 = (bf16[8,16,4096]{2,1,0:T(8,128)(2,1)S(1)}, bf16[8,16,4096]{2,1,0:T(8,128)(2,1)}, u32[]{:S(2)}) copy-start(bf16[8,16,4096]{2,1,0:T(8,128)(2,1)} %param.23) | copy-start | bytes 3145732
  0.7 1.1 %copy-start.6 = (bf16[2,16,4096]{2,1,0:T(8,128)(2,1)S(1)}, bf16[2,16,4096]{2,1,0:T(8,128)(2,1)}, u32[]{:S(2)}) copy-start(bf16[2,16,4096]{2,1,0:T(8,128)(2,1)} %x_ref.1) | copy-start | bytes 786436
  1.8 0.7 copy-start.9
  2.4 0.7 copy-start.11
  3.1 0.7 copy-start.12
  5.5 8.9 %collective-permute-start = (bf16[16,1152]{1,0:T(8,128)(2,1)}, bf16[16,1152]{1,0:T(8,128)(2,1)S(1)}, u32[]{:S(2)}, u32[]{:S(2)}) collective-permute-start(bf16[16,1152]{1,0:T(8,128)(2,1)} %get-tuple-element.44), channel_id=1, source_target_pairs={{0,2},{2,0},{4,6},{6,4},{8,10},{10,8},{12,14},{14,12},{1,3},{3,1},... | collective-permute-start | bytes 110600 | tf_op jit(solution)/shard_map/ppermute | solution.py:303
  8.5 9.5 %collective-permute-start.1 = (bf16[16,1152]{1,0:T(8,128)(2,1)}, bf16[16,1152]{1,0:T(8,128)(2,1)S(1)}, u32[]{:S(2)}, u32[]{:S(2)}) collective-permute-start(bf16[16,1152]{1,0:T(8,128)(2,1)} %get-tuple-element.45), channel_id=1, source_target_pairs={{0,4},{2,6},{4,0},{6,2},{8,12},{10,14},{12,8},{14,10},{1,5},{3,7},... | collective-permute-start | bytes 110600 | tf_op jit(solution)/shard_map/ppermute | solution.py:303
  10.1 8.0 %collective-permute-start.2 = (bf16[16,1152]{1,0:T(8,128)(2,1)}, bf16[16,1152]{1,0:T(8,128)(2,1)S(1)}, u32[]{:S(2)}, u32[]{:S(2)}) collective-permute-start(bf16[16,1152]{1,0:T(8,128)(2,1)} %get-tuple-element.46), channel_id=1, source_target_pairs={{0,6},{2,4},{4,2},{6,0},{8,14},{10,12},{12,10},{14,8},{1,7},{3,5},... | collective-permute-start | bytes 110600 | tf_op jit(solution)/shard_map/ppermute | solution.py:303
  10.1 8.0 %collective-permute-start.3 = (bf16[16,1152]{1,0:T(8,128)(2,1)S(1)}, bf16[16,1152]{1,0:T(8,128)(2,1)S(1)}, u32[]{:S(2)}, u32[]{:S(2)}) collective-permute-start(bf16[16,1152]{1,0:T(8,128)(2,1)S(1)} %get-tuple-element.47), channel_id=1, source_target_pairs={{0,8},{2,10},{4,12},{6,14},{8,0},{10,2},{12,4},{14,6},{1,9},{3,11}... | collective-permute-start | bytes 110600 | tf_op jit(solution)/shard_map/ppermute | solution.py:303
  13.1 6.0 %collective-permute-start.4 = (bf16[16,1152]{1,0:T(8,128)(2,1)S(1)}, bf16[16,1152]{1,0:T(8,128)(2,1)S(1)}, u32[]{:S(2)}, u32[]{:S(2)}) collective-permute-start(bf16[16,1152]{1,0:T(8,128)(2,1)S(1)} %get-tuple-element.48), channel_id=1, source_target_pairs={{0,10},{2,8},{4,14},{6,12},{8,2},{10,0},{12,6},{14,4},{1,11},{3,9}... | collective-permute-start | bytes 110600 | tf_op jit(solution)/shard_map/ppermute | solution.py:303
  14.3 5.9 %collective-permute-start.5 = (bf16[16,1152]{1,0:T(8,128)(2,1)S(1)}, bf16[16,1152]{1,0:T(8,128)(2,1)S(1)}, u32[]{:S(2)}, u32[]{:S(2)}) collective-permute-start(bf16[16,1152]{1,0:T(8,128)(2,1)S(1)} %get-tuple-element.49), channel_id=1, source_target_pairs={{0,12},{2,14},{4,8},{6,10},{8,4},{10,6},{12,0},{14,2},{1,13},{3,15... | collective-permute-start | bytes 110600 | tf_op jit(solution)/shard_map/ppermute | solution.py:303
  18.0 6.7 %collective-permute-start.6 = (bf16[16,1152]{1,0:T(8,128)(2,1)S(1)}, bf16[16,1152]{1,0:T(8,128)(2,1)S(1)}, u32[]{:S(2)}, u32[]{:S(2)}) collective-permute-start(bf16[16,1152]{1,0:T(8,128)(2,1)S(1)} %get-tuple-element.50), channel_id=1, source_target_pairs={{0,14},{2,12},{4,10},{6,8},{8,6},{10,4},{12,2},{14,0},{1,15},{3,13... | collective-permute-start | bytes 110600 | tf_op jit(solution)/shard_map/ppermute | solution.py:303
  18.0 22.4 %copy-start.5 = (bf16[2,16,4096]{2,1,0:T(8,128)(2,1)S(1)}, bf16[2,16,4096]{2,1,0:T(8,128)(2,1)}, u32[]{:S(2)}) copy-start(bf16[2,16,4096]{2,1,0:T(8,128)(2,1)} %q_ref.1) | copy-start | bytes 786436
  18.0 22.4 %copy-start.7 = (bf16[2,16,512]{2,1,0:T(8,128)(2,1)S(1)}, bf16[2,16,512]{2,1,0:T(8,128)(2,1)}, u32[]{:S(2)}) copy-start(bf16[2,16,512]{2,1,0:T(8,128)(2,1)} %kn_ref.1) | copy-start | bytes 98308
  18.0 22.4 %copy-start.8 = (bf16[2,16,512]{2,1,0:T(8,128)(2,1)S(1)}, bf16[2,16,512]{2,1,0:T(8,128)(2,1)}, u32[]{:S(2)}) copy-start(bf16[2,16,512]{2,1,0:T(8,128)(2,1)} %vn_ref.1) | copy-start | bytes 98308
  18.0 22.4 %copy-start.10 = (s32[16]{0:T(128)S(1)}, s32[16]{0:T(128)}, u32[]{:S(2)}) copy-start(s32[16]{0:T(128)} %lengths.3) | copy-start | bytes 196
  25.2 1.2 %collective-permute-start.7 = (f32[32,128]{1,0:T(8,128)S(1)}, f32[32,128]{1,0:T(8,128)S(1)}, u32[]{:S(2)}, u32[]{:S(2)}) collective-permute-start(f32[32,128]{1,0:T(8,128)S(1)} %get-tuple-element.51.mine), channel_id=1, source_target_pairs={{0,1},{1,0},{2,3},{3,2},{4,5},{5,4},{6,7},{7,6},{8,9},{9,8},{10,11... | collective-permute-start | bytes 49160 | tf_op jit(solution)/shard_map/ppermute | solution.py:308
  26.9 6.4 %collective-permute-start.8 = (bf16[16,1024]{1,0:T(8,128)(2,1)S(1)}, bf16[16,1024]{1,0:T(8,128)(2,1)S(1)}, u32[]{:S(2)}, u32[]{:S(2)}) collective-permute-start(bf16[16,1024]{1,0:T(8,128)(2,1)S(1)} %get-tuple-element.53), channel_id=1, source_target_pairs={{0,2},{2,0},{4,6},{6,4},{8,10},{10,8},{12,14},{14,12},{1,3},{3,1},... | collective-permute-start | bytes 98312 | tf_op jit(solution)/shard_map/ppermute | solution.py:303
  27.5 6.3 %collective-permute-start.9 = (bf16[16,1024]{1,0:T(8,128)(2,1)S(1)}, bf16[16,1024]{1,0:T(8,128)(2,1)S(1)}, u32[]{:S(2)}, u32[]{:S(2)}) collective-permute-start(bf16[16,1024]{1,0:T(8,128)(2,1)S(1)} %get-tuple-element.54), channel_id=1, source_target_pairs={{0,4},{2,6},{4,0},{6,2},{8,12},{10,14},{12,8},{14,10},{1,5},{3,7},... | collective-permute-start | bytes 98312 | tf_op jit(solution)/shard_map/ppermute | solution.py:303
  27.5 10.6 %collective-permute-start.10 = (bf16[16,1024]{1,0:T(8,128)(2,1)S(1)}, bf16[16,1024]{1,0:T(8,128)(2,1)S(1)}, u32[]{:S(2)}, u32[]{:S(2)}) collective-permute-start(bf16[16,1024]{1,0:T(8,128)(2,1)S(1)} %get-tuple-element.55), channel_id=1, source_target_pairs={{0,6},{2,4},{4,2},{6,0},{8,14},{10,12},{12,10},{14,8},{1,7},{3,5},... | collective-permute-start | bytes 98312 | tf_op jit(solution)/shard_map/ppermute | solution.py:303
  30.4 7.7 %collective-permute-start.11 = (bf16[16,1024]{1,0:T(8,128)(2,1)S(1)}, bf16[16,1024]{1,0:T(8,128)(2,1)S(1)}, u32[]{:S(2)}, u32[]{:S(2)}) collective-permute-start(bf16[16,1024]{1,0:T(8,128)(2,1)S(1)} %get-tuple-element.56), channel_id=1, source_target_pairs={{0,8},{2,10},{4,12},{6,14},{8,0},{10,2},{12,4},{14,6},{1,9},{3,11}... | collective-permute-start | bytes 98312 | tf_op jit(solution)/shard_map/ppermute | solution.py:303
  30.5 7.7 %collective-permute-start.12 = (bf16[16,1024]{1,0:T(8,128)(2,1)S(1)}, bf16[16,1024]{1,0:T(8,128)(2,1)S(1)}, u32[]{:S(2)}, u32[]{:S(2)}) collective-permute-start(bf16[16,1024]{1,0:T(8,128)(2,1)S(1)} %get-tuple-element.57), channel_id=1, source_target_pairs={{0,10},{2,8},{4,14},{6,12},{8,2},{10,0},{12,6},{14,4},{1,11},{3,9}... | collective-permute-start | bytes 98312 | tf_op jit(solution)/shard_map/ppermute | solution.py:303
  33.3 5.7 %collective-permute-start.13 = (bf16[16,1024]{1,0:T(8,128)(2,1)S(1)}, bf16[16,1024]{1,0:T(8,128)(2,1)S(1)}, u32[]{:S(2)}, u32[]{:S(2)}) collective-permute-start(bf16[16,1024]{1,0:T(8,128)(2,1)S(1)} %get-tuple-element.58), channel_id=1, source_target_pairs={{0,12},{2,14},{4,8},{6,10},{8,4},{10,6},{12,0},{14,2},{1,13},{3,15... | collective-permute-start | bytes 98312 | tf_op jit(solution)/shard_map/ppermute | solution.py:303
  33.8 6.6 %collective-permute-start.14 = (bf16[16,1024]{1,0:T(8,128)(2,1)S(1)}, bf16[16,1024]{1,0:T(8,128)(2,1)S(1)}, u32[]{:S(2)}, u32[]{:S(2)}) collective-permute-start(bf16[16,1024]{1,0:T(8,128)(2,1)S(1)} %get-tuple-element.59), channel_id=1, source_target_pairs={{0,14},{2,12},{4,10},{6,8},{8,6},{10,4},{12,2},{14,0},{1,15},{3,13... | collective-permute-start | bytes 98312 | tf_op jit(solution)/shard_map/ppermute | solution.py:303
  40.4 3.4 %copy-start.1 = (bf16[16,512,512]{2,1,0:T(8,128)(2,1)S(1)}, bf16[16,512,512]{2,1,0:T(8,128)(2,1)}, u32[]{:S(2)}) copy-start(bf16[16,512,512]{2,1,0:T(8,128)(2,1)} %k_any.1) | copy-start | bytes 25165828
  43.8 3.4 %copy-start.2 = (bf16[16,512,512]{2,1,0:T(8,128)(2,1)S(1)}, bf16[16,512,512]{2,1,0:T(8,128)(2,1)}, u32[]{:S(2)}) copy-start(bf16[16,512,512]{2,1,0:T(8,128)(2,1)} %v_any.1) | copy-start | bytes 25165828
  47.2 25.7 %copy-start.13 = (bf16[8192,8,16]{0,2,1:T(8,128)(2,1)S(1)}, bf16[8192,8,16]{0,2,1:T(8,128)(2,1)}, u32[]{:S(2)}) copy-start(bf16[8192,8,16]{0,2,1:T(8,128)(2,1)} %param.24) | copy-start | bytes 6291460
  61.2 19.2 %copy-start.4 = (bf16[8,16,4096]{2,1,0:T(8,128)(2,1)S(1)}, bf16[8,16,4096]{2,1,0:T(8,128)(2,1)}, u32[]{:S(2)}) copy-start(bf16[8,16,4096]{2,1,0:T(8,128)(2,1)} %param.25) | copy-start | bytes 3145732
  61.2 7.3 %collective-permute-start.15 = (bf16[16,1024]{1,0:T(8,128)(2,1)S(1)}, bf16[16,1024]{1,0:T(8,128)(2,1)S(1)}, u32[]{:S(2)}, u32[]{:S(2)}) collective-permute-start(bf16[16,1024]{1,0:T(8,128)(2,1)S(1)} %get-tuple-element.62), channel_id=1, source_target_pairs={{0,2},{2,0},{4,6},{6,4},{8,10},{10,8},{12,14},{14,12},{1,3},{3,1},... | collective-permute-start | bytes 98312 | tf_op jit(solution)/shard_map/ppermute | solution.py:303
  62.6 9.4 %collective-permute-start.16 = (bf16[16,1024]{1,0:T(8,128)(2,1)S(1)}, bf16[16,1024]{1,0:T(8,128)(2,1)S(1)}, u32[]{:S(2)}, u32[]{:S(2)}) collective-permute-start(bf16[16,1024]{1,0:T(8,128)(2,1)S(1)} %get-tuple-element.63), channel_id=1, source_target_pairs={{0,4},{2,6},{4,0},{6,2},{8,12},{10,14},{12,8},{14,10},{1,5},{3,7},... | collective-permute-start | bytes 98312 | tf_op jit(solution)/shard_map/ppermute | solution.py:303
  62.6 10.4 %collective-permute-start.17 = (bf16[16,1024]{1,0:T(8,128)(2,1)S(1)}, bf16[16,1024]{1,0:T(8,128)(2,1)S(1)}, u32[]{:S(2)}, u32[]{:S(2)}) collective-permute-start(bf16[16,1024]{1,0:T(8,128)(2,1)S(1)} %get-tuple-element.64), channel_id=1, source_target_pairs={{0,6},{2,4},{4,2},{6,0},{8,14},{10,12},{12,10},{14,8},{1,7},{3,5},... | collective-permute-start | bytes 98312 | tf_op jit(solution)/shard_map/ppermute | solution.py:303
  64.8 8.2 %collective-permute-start.18 = (bf16[16,1024]{1,0:T(8,128)(2,1)S(1)}, bf16[16,1024]{1,0:T(8,128)(2,1)S(1)}, u32[]{:S(2)}, u32[]{:S(2)}) collective-permute-start(bf16[16,1024]{1,0:T(8,128)(2,1)S(1)} %get-tuple-element.65), channel_id=1, source_target_pairs={{0,8},{2,10},{4,12},{6,14},{8,0},{10,2},{12,4},{14,6},{1,9},{3,11}... | collective-permute-start | bytes 98312 | tf_op jit(solution)/shard_map/ppermute | solution.py:303
  67.5 6.1 %collective-permute-start.19 = (bf16[16,1024]{1,0:T(8,128)(2,1)S(1)}, bf16[16,1024]{1,0:T(8,128)(2,1)S(1)}, u32[]{:S(2)}, u32[]{:S(2)}) collective-permute-start(bf16[16,1024]{1,0:T(8,128)(2,1)S(1)} %get-tuple-element.66), channel_id=1, source_target_pairs={{0,10},{2,8},{4,14},{6,12},{8,2},{10,0},{12,6},{14,4},{1,11},{3,9}... | collective-permute-start | bytes 98312 | tf_op jit(solution)/shard_map/ppermute | solution.py:303
  68.5 5.8 %collective-permute-start.20 = (bf16[16,1024]{1,0:T(8,128)(2,1)S(1)}, bf16[16,1024]{1,0:T(8,128)(2,1)S(1)}, u32[]{:S(2)}, u32[]{:S(2)}) collective-permute-start(bf16[16,1024]{1,0:T(8,128)(2,1)S(1)} %get-tuple-element.67), channel_id=1, source_target_pairs={{0,12},{2,14},{4,8},{6,10},{8,4},{10,6},{12,0},{14,2},{1,13},{3,15... | collective-permute-start | bytes 98312 | tf_op jit(solution)/shard_map/ppermute | solution.py:303
  72.0 6.6 %collective-permute-start.21 = (bf16[16,1024]{1,0:T(8,128)(2,1)S(1)}, bf16[16,1024]{1,0:T(8,128)(2,1)S(1)}, u32[]{:S(2)}, u32[]{:S(2)}) collective-permute-start(bf16[16,1024]{1,0:T(8,128)(2,1)S(1)} %get-tuple-element.68), channel_id=1, source_target_pairs={{0,14},{2,12},{4,10},{6,8},{8,6},{10,4},{12,2},{14,0},{1,15},{3,13... | collective-permute-start | bytes 98312 | tf_op jit(solution)/shard_map/ppermute | solution.py:303
  79.2 1.2 %collective-permute-start.22 = (f32[32,128]{1,0:T(8,128)S(1)}, f32[32,128]{1,0:T(8,128)S(1)}, u32[]{:S(2)}, u32[]{:S(2)}) collective-permute-start(f32[32,128]{1,0:T(8,128)S(1)} %project_output.1.mine), channel_id=1, source_target_pairs={{0,1},{1,0},{2,3},{3,2},{4,5},{5,4},{6,7},{7,6},{8,9},{9,8},{10,11... | collective-permute-start | bytes 49160 | tf_op jit(solution)/shard_map/ppermute | solution.py:308
  80.9 7.3 %collective-permute-start.23 = (bf16[16,1024]{1,0:T(8,128)(2,1)S(1)}, bf16[16,1024]{1,0:T(8,128)(2,1)S(1)}, u32[]{:S(2)}, u32[]{:S(2)}) collective-permute-start(bf16[16,1024]{1,0:T(8,128)(2,1)S(1)} %get-tuple-element.71), channel_id=1, source_target_pairs={{0,2},{2,0},{4,6},{6,4},{8,10},{10,8},{12,14},{14,12},{1,3},{3,1},... | collective-permute-start | bytes 98312 | tf_op jit(solution)/shard_map/ppermute | solution.py:303
  82.3 5.9 %collective-permute-start.24 = (bf16[16,1024]{1,0:T(8,128)(2,1)S(1)}, bf16[16,1024]{1,0:T(8,128)(2,1)S(1)}, u32[]{:S(2)}, u32[]{:S(2)}) collective-permute-start(bf16[16,1024]{1,0:T(8,128)(2,1)S(1)} %get-tuple-element.72), channel_id=1, source_target_pairs={{0,4},{2,6},{4,0},{6,2},{8,12},{10,14},{12,8},{14,10},{1,5},{3,7},... | collective-permute-start | bytes 98312 | tf_op jit(solution)/shard_map/ppermute | solution.py:303
  82.3 9.8 %collective-permute-start.25 = (bf16[16,1024]{1,0:T(8,128)(2,1)S(1)}, bf16[16,1024]{1,0:T(8,128)(2,1)S(1)}, u32[]{:S(2)}, u32[]{:S(2)}) collective-permute-start(bf16[16,1024]{1,0:T(8,128)(2,1)S(1)} %get-tuple-element.73), channel_id=1, source_target_pairs={{0,6},{2,4},{4,2},{6,0},{8,14},{10,12},{12,10},{14,8},{1,7},{3,5},... | collective-permute-start | bytes 98312 | tf_op jit(solution)/shard_map/ppermute | solution.py:303
  84.5 7.7 %collective-permute-start.26 = (bf16[16,1024]{1,0:T(8,128)(2,1)S(1)}, bf16[16,1024]{1,0:T(8,128)(2,1)S(1)}, u32[]{:S(2)}, u32[]{:S(2)}) collective-permute-start(bf16[16,1024]{1,0:T(8,128)(2,1)S(1)} %get-tuple-element.74), channel_id=1, source_target_pairs={{0,8},{2,10},{4,12},{6,14},{8,0},{10,2},{12,4},{14,6},{1,9},{3,11}... | collective-permute-start | bytes 98312 | tf_op jit(solution)/shard_map/ppermute | solution.py:303
  84.5 7.7 %collective-permute-start.27 = (bf16[16,1024]{1,0:T(8,128)(2,1)S(1)}, bf16[16,1024]{1,0:T(8,128)(2,1)S(1)}, u32[]{:S(2)}, u32[]{:S(2)}) collective-permute-start(bf16[16,1024]{1,0:T(8,128)(2,1)S(1)} %get-tuple-element.75), channel_id=1, source_target_pairs={{0,10},{2,8},{4,14},{6,12},{8,2},{10,0},{12,6},{14,4},{1,11},{3,9}... | collective-permute-start | bytes 98312 | tf_op jit(solution)/shard_map/ppermute | solution.py:303
  88.2 5.7 %collective-permute-start.28 = (bf16[16,1024]{1,0:T(8,128)(2,1)S(1)}, bf16[16,1024]{1,0:T(8,128)(2,1)S(1)}, u32[]{:S(2)}, u32[]{:S(2)}) collective-permute-start(bf16[16,1024]{1,0:T(8,128)(2,1)S(1)} %get-tuple-element.76), channel_id=1, source_target_pairs={{0,12},{2,14},{4,8},{6,10},{8,4},{10,6},{12,0},{14,2},{1,13},{3,15... | collective-permute-start | bytes 98312 | tf_op jit(solution)/shard_map/ppermute | solution.py:303
  88.2 6.6 %collective-permute-start.29 = (bf16[16,1024]{1,0:T(8,128)(2,1)S(1)}, bf16[16,1024]{1,0:T(8,128)(2,1)S(1)}, u32[]{:S(2)}, u32[]{:S(2)}) collective-permute-start(bf16[16,1024]{1,0:T(8,128)(2,1)S(1)} %get-tuple-element.77), channel_id=1, source_target_pairs={{0,14},{2,12},{4,10},{6,8},{8,6},{10,4},{12,2},{14,0},{1,15},{3,13... | collective-permute-start | bytes 98312 | tf_op jit(solution)/shard_map/ppermute | solution.py:303

commit v2 on v1

--- a/solution.py
+++ b/solution.py
@@ -18,7 +18,7 @@
 I32 = jnp.int32
 VMEM = pl.BlockSpec(memory_space=pltpu.VMEM)
 SMEM = pl.BlockSpec(memory_space=pltpu.SMEM)
-ANY = pl.BlockSpec(memory_space=pl.ANY)
+HBM = pl.BlockSpec(memory_space=pltpu.HBM)
 
 
 def iota(shape, dim):
@@ -89,16 +89,41 @@
     return jnp.dot(matrix, values, preferred_element_type=F32).astype(BF16)
 
 
-def dispatch_kernel(owners, heads, adapt, rank, me, ids, slot_of, lengths, x_ref, *refs):
-    place_of, row_at, slot_at, order, *blocks = refs
+def dispatch_kernel(
+    owners,
+    heads,
+    adapt,
+    rank,
+    ids_hbm,
+    slot_of_hbm,
+    lengths_hbm,
+    x_hbm,
+    place_of,
+    row_at,
+    order,
+    blocks,
+    slot_at,
+    ids,
+    slot_of,
+    lengths,
+    x_ref,
+    sems,
+):
+    sources = (ids_hbm, slot_of_hbm, lengths_hbm, x_hbm)
+    targets = (ids, slot_of, lengths, x_ref)
+    copies = [pltpu.make_async_copy(a, b, sems.at[k]) for k, (a, b) in enumerate(zip(sources, targets))]
+    for copy in copies:
+        copy.start()
     rows = x_ref.shape[1]
     wide = x_ref.shape[2] // heads
+    for copy in copies[:3]:
+        copy.wait()
     for p in range(owners * CAP):
         row_at[p] = -1
         slot_at[p] = -1
     for r in range(rows):
         slot = slot_of[ids[r]]
-        relative = (slot // adapt) ^ me[0]
+        relative = slot // adapt
         taken = jnp.where(row_at[relative * CAP] >= 0, 1, 0)
         place = relative * CAP + taken
         row_at[place] = r
@@ -114,27 +139,28 @@
         order[ahead] = r
     items = CAP * STEPS
     block = heads * items
+    copies[3].wait()
     packed = exact(pack_matrix(row_at, owners, heads, rows), stacked(x_ref, heads, wide))
     at = iota((block, adapt * rank), 0)
     lane_slot = iota((block, adapt * rank), 1) // rank
     first = (at // STEPS) % CAP == 0
     for i in range(owners):
-        blocks[i][:, :wide] = packed[i * block : (i + 1) * block]
+        blocks[i, :, :wide] = packed[i * block : (i + 1) * block]
         slot = jnp.where(first, slot_at[i * CAP], slot_at[i * CAP + 1])
-        blocks[i][:, wide:] = one_hot(lane_slot == slot)
-
-
-def project_kernel(owners, heads, wide, first, a_ref, *refs):
+        blocks[i, :, wide:] = one_hot(lane_slot == slot)
+
+
+def project_kernel(owners, heads, wide, first, a_ref, blocks, *refs):
     if first:
-        blocks, (part_ref, mask_ref) = refs[:owners], refs[owners:]
+        part_ref, mask_ref = refs
     else:
-        blocks, (mask_in, part_ref) = refs[:owners], refs[owners:]
+        mask_in, part_ref = refs
     grouped = regroup_matrix(owners, heads)
     items = owners * CAP * STEPS
-    arrived = jnp.concatenate([b[:, :wide] for b in blocks], axis=0)
+    arrived = jnp.concatenate([blocks[i, :, :wide] for i in range(owners)], axis=0)
     arrived = exact(grouped, arrived)
     if first:
-        masks = jnp.concatenate([b[:, wide:] for b in blocks], axis=0)
+        masks = jnp.concatenate([blocks[i, :, wide:] for i in range(owners)], axis=0)
         mask = jnp.dot(grouped[:items], masks, preferred_element_type=F32)
         mask_ref[...] = mask
     else:
@@ -150,7 +176,7 @@
     part_ref[...] = total * mask
 
 
-def expand_kernel(owners, heads, wide, mine, other, b_ref, *blocks):
+def expand_kernel(owners, heads, wide, mine, other, b_ref, blocks):
     low_rank = (mine[...] + other[...]).astype(BF16)
     pieces = []
     for c in range(heads):
@@ -161,16 +187,31 @@
     back = exact(ungroup_matrix(owners, heads), jnp.concatenate(pieces, axis=0))
     block = heads * CAP * STEPS
     for i in range(owners):
-        blocks[i][...] = back[i * block : (i + 1) * block]
+        blocks[i] = back[i * block : (i + 1) * block]
 
 
 def attend_kernel(
-    owners, heads, place_of, row_at, order, lengths, q_ref, kn_ref, vn_ref, k_any, v_any, *refs
+    owners,
+    heads,
+    place_of,
+    row_at,
+    order,
+    lengths,
+    q_ref,
+    kn_ref,
+    vn_ref,
+    k_any,
+    v_any,
+    blocks,
+    out_ref,
+    outgoing,
+    k_buf,
+    v_buf,
+    q_buf,
+    o_buf,
+    k_sem,
+    v_sem,
 ):
-    blocks = refs[:owners]
-    out_ref = refs[owners]
-    outgoing = refs[owners + 1 : 2 * owners + 1]
-    k_buf, v_buf, q_buf, o_buf, k_sem, v_sem = refs[2 * owners + 1 :]
     rows = q_ref.shape[1]
     wide = q_ref.shape[2] // heads
     groups = wide // HD
@@ -208,7 +249,7 @@
 
     delta = jnp.dot(
         unpack_matrix(place_of, owners, heads, rows),
-        jnp.concatenate([b[...] for b in blocks], axis=0),
+        jnp.concatenate([blocks[i] for i in range(owners)], axis=0),
         preferred_element_type=F32,
     )
     query = (stacked(q_ref, heads, wide).astype(F32) + delta).astype(BF16).astype(F32)
@@ -281,14 +322,13 @@
     packed = exact(pack_matrix(row_at, owners, heads, rows), jnp.concatenate(results, axis=0))
     block = heads * CAP * STEPS
     for i in range(owners):
-        outgoing[i][...] = packed[i * block : (i + 1) * block]
-
-
-def collect_kernel(owners, heads, place_of, *refs):
-    blocks, out_ref = refs[:owners], refs[owners]
+        outgoing[i] = packed[i * block : (i + 1) * block]
+
+
+def collect_kernel(owners, heads, place_of, blocks, out_ref):
     rows = out_ref.shape[1]
     wide = out_ref.shape[2] // heads
-    arrived = jnp.concatenate([b[...] for b in blocks], axis=0)
+    arrived = jnp.concatenate([blocks[i] for i in range(owners)], axis=0)
     values = exact(unpack_matrix(place_of, owners, heads, rows), arrived)
     for c in range(heads):
         for s in range(STEPS):
@@ -297,11 +337,7 @@
 
 
 def exchange(blocks):
-    owners = len(blocks)
-    arrived = [blocks[0]] + [None] * (owners - 1)
-    for i in range(owners - 1, 0, -1):
-        arrived[i] = lax.ppermute(blocks[i], "store", [(s, s ^ i) for s in range(owners)])
-    return arrived
+    return lax.all_to_all(blocks, "store", split_axis=0, concat_axis=0, tiled=True)
 
 
 def swap_cores(part):
@@ -332,7 +368,6 @@
     lanes = adapt * rank
     block = heads * CAP * STEPS
     items = owners * CAP * STEPS
-    me = lax.axis_index("store").astype(I32).reshape(1)
     core = lax.axis_index("tensor")
 
     def half(a_store):
@@ -342,48 +377,56 @@
     shape = jax.ShapeDtypeStruct
     small = pltpu.CompilerParams(vmem_limit_bytes=16 * 1024 * 1024)
 
-    place_of, row_at, _, order, *blocks = pl.pallas_call(
+    sent = shape((owners, block, wide), BF16)
+    place_of, row_at, order, blocks = pl.pallas_call(
         functools.partial(dispatch_kernel, owners, heads, adapt, rank),
         out_shape=[
             shape((rows,), I32),
             shape((owners * CAP,), I32),
-            shape((owners * CAP,), I32),
             shape((rows,), I32),
-        ]
-        + [shape((block, wide + lanes), BF16)] * owners,
-        in_specs=[SMEM] * 4 + [VMEM],
-        out_specs=[SMEM] * 4 + [VMEM] * owners,
+            shape((owners, block, wide + lanes), BF16),
+        ],
+        in_specs=[HBM] * 4,
+        out_specs=[SMEM] * 3 + [VMEM],
+        scratch_shapes=[
+            pltpu.SMEM((owners * CAP,), I32),
+            pltpu.SMEM(adapter_ids.shape, I32),
+            pltpu.SMEM(slot_of.shape, I32),
+            pltpu.SMEM(lengths.shape, I32),
+            pltpu.VMEM(x_in.shape, BF16),
+            pltpu.SemaphoreType.DMA((4,)),
+        ],
         compiler_params=small,
         name="dispatch",
-    )(me, adapter_ids, slot_of, lengths, x_in)
+    )(adapter_ids, slot_of, lengths, x_in)
 
     arrived = exchange(blocks)
     part, mask = pl.pallas_call(
         functools.partial(project_kernel, owners, heads, wide, True),
         out_shape=[shape((items, lanes), F32)] * 2,
-        in_specs=[VMEM] * (owners + 1),
+        in_specs=[VMEM] * 2,
         out_specs=[VMEM] * 2,
         compiler_params=small,
         name="project_query",
-    )(half(a_query), *arrived)
+    )(half(a_query), arrived)
 
     def expand(part, b_store, name):
         return pl.pallas_call(
             functools.partial(expand_kernel, owners, heads, wide),
-            out_shape=[shape((block, wide), BF16)] * owners,
+            out_shape=sent,
             in_specs=[VMEM] * 3,
-            out_specs=[VMEM] * owners,
+            out_specs=VMEM,
             compiler_params=small,
             name=name,
         )(part, swap_cores(part), b_store.reshape(lanes, width))
 
     returned = exchange(expand(part, b_query, "expand_query"))
 
-    attn_out, *outgoing = pl.pallas_call(
+    attn_out, outgoing = pl.pallas_call(
         functools.partial(attend_kernel, owners, heads),
-        out_shape=[shape((STEPS, rows, width), BF16)] + [shape((block, wide), BF16)] * owners,
-        in_specs=[SMEM] * 4 + [VMEM] * 3 + [ANY] * 2 + [VMEM] * owners,
-        out_specs=[VMEM] * (owners + 1),
+        out_shape=[shape((STEPS, rows, width), BF16), sent],
+        in_specs=[SMEM] * 4 + [VMEM] * 3 + [HBM] * 2 + [VMEM],
+        out_specs=[VMEM] * 2,
         scratch_shapes=[
             pltpu.VMEM(cache_k.shape, BF16),
             pltpu.VMEM(cache_v.shape, BF16),
@@ -394,26 +437,26 @@
         ],
         compiler_params=pltpu.CompilerParams(vmem_limit_bytes=32 * 1024 * 1024),
         name="attend",
-    )(place_of, row_at, order, lengths, q_base, k_new, v_new, cache_k, cache_v, *returned)
+    )(place_of, row_at, order, lengths, q_base, k_new, v_new, cache_k, cache_v, returned)
 
     arrived = exchange(outgoing)
     part = pl.pallas_call(
         functools.partial(project_kernel, owners, heads, wide, False),
         out_shape=shape((items, lanes), F32),
-        in_specs=[VMEM] * (owners + 2),
+        in_specs=[VMEM] * 3,
         out_specs=VMEM,
         compiler_params=small,
         name="project_output",
-    )(half(a_output), *arrived, mask)
+    )(half(a_output), arrived, mask)
     returned = exchange(expand(part, b_output, "expand_output"))
     adapter_out = pl.pallas_call(
         functools.partial(collect_kernel, owners, heads),
         out_shape=shape((STEPS, rows, width), BF16),
-        in_specs=[SMEM] + [VMEM] * owners,
+        in_specs=[SMEM, VMEM],
         out_specs=VMEM,
         compiler_params=small,
         name="collect",
-    )(place_of, *returned)
+    )(place_of, returned)
     return (attn_out, adapter_out)
 
 

time: 96.8 us -> 91 us (0.940)
  starting transfers between devices: 46.6 us -> 11 us
  blocking collectives: 0 us -> 25.3 us
  local copies, waits for them, and re-layouts: 10 us -> 13.7 us
  Pallas kernels: 19.4 us -> 20.5 us
    ppermute x28 -> x0, starting transfers between devices: 46.6 us -> none  [exchange(): lax.ppermute(blocks[i], 'store', [(s, s ^ i) for s in range(owners)])]
    all_to_all x0 -> x2, blocking collectives: none -> 25.3 us  [exchange(): lax.all_to_all(blocks, 'store', split_axis=0, concat_axis=0, tiled=True)]
    ppermute x28 -> x0, waiting for transfers between devices: 17.2 us -> none  [exchange(): lax.ppermute(blocks[i], 'store', [(s, s ^ i) for s in range(owners)])]
    all_to_all x0 -> x2, waiting for transfers between devices: none -> 16.8 us  [exchange(): lax.all_to_all(blocks, 'store', split_axis=0, concat_axis=0, tiled=True)]
    all_to_all x0 -> x2, starting transfers between devices: none -> 11 us  [exchange(): lax.all_to_all(blocks, 'store', split_axis=0, concat_axis=0, tiled=True)]
    unnamed x28 -> x26, local copies, waits for them, and re-layouts: 9.86 us -> 12.3 us
    dynamic_slice x2, local copies, waits for them, and re-layouts: 0.17 us -> 1.37 us  [half(): return lax.dynamic_slice(flat, (0, core * width), (lanes, width))]
  transfers between devices with their start and end apart: 30 -> 4, of which waited for: 12 -> 4; matrix products, arithmetic and copies ran while one was open for 0% -> 2% of each run, Pallas kernels for 0% -> 0%
where the time goes in v2:
time: 91 us; the launch traced here: 90.4 us
  blocking collectives  25.3 us (28%)
  Pallas kernels  20.5 us (23%)
  waiting for transfers between devices  19.2 us (21%)
  local copies, waits for them, and re-layouts  13.7 us (15%)
  starting transfers between devices  11 us (12%)
    all_to_all x2, blocking collectives, exchange(): lax.all_to_all(blocks, 'store', split_axis=0, concat_axis=0, tiled=True)  25.3 us
    all_to_all x2, waiting for transfers between devices, exchange(): lax.all_to_all(blocks, 'store', split_axis=0, concat_axis=0, tiled=True)  16.8 us
    pallas_call x1, Pallas kernels, shards(): pl.pallas_call(functools.partial(attend_kernel, owners, heads), out_shape...  14.9 us
    unnamed x26, local copies, waits for them, and re-layouts  12.3 us
    all_to_all x2, starting transfers between devices, exchange(): lax.all_to_all(blocks, 'store', split_axis=0, concat_axis=0, tiled=True)  11 us
    ppermute x2, waiting for transfers between devices, swap_cores(): return lax.ppermute(part, 'tensor', [(0, 1), (1, 0)])  2.4 us
    pallas_call x1, Pallas kernels, shards(): pl.pallas_call(functools.partial(dispatch_kernel, owners, heads, adapt, r...  1.98 us
  transfers between devices with their start and end apart: 4, of which 4 were waited for; matrix products, arithmetic and copies ran while one was open for 2% of the time, Pallas kernels for 0%

profile of v2, /device:TPU:0, one launch (start us, length us, event | category | flops | bytes accessed | tf_op | source)
XLA Modules:
  0.0 90.4 jit_solution(11273947810566055647)
XLA Ops:
  0.6 0.0 copy-start
  0.6 0.0 copy-start.6
  0.7 1.1 %copy-done.6 = bf16[2,16,4096]{2,1,0:T(8,128)(2,1)S(1)} copy-done((bf16[2,16,4096]{2,1,0:T(8,128)(2,1)S(1)}, bf16[2,16,4096]{2,1,0:T(8,128)(2,1)}, u32[]{:S(2)}) %copy-start.6) | copy-done | bytes 262168
  1.7 0.0 copy-start.9
  1.7 0.7 copy-done.9
  2.4 0.0 copy-start.11
  2.4 0.7 copy-done.11
  3.1 0.0 copy-start.12
  3.1 0.7 copy-done.12
  3.7 2.0 %dispatch.1 = (s32[16]{0:T(128)S(1)}, s32[16]{0:T(128)S(1)}, s32[16]{0:T(128)S(1)}, bf16[8,16,1152]{2,1,0:T(8,128)(2,1)}) custom-call(s32[16]{0:T(128)S(1)} %copy-done.11, s32[64]{0:T(128)S(1)} %copy-done.12, s32[16]{0:T(128)S(1)} %copy-done.9, bf16[2,16,4096]{2,1,0:T(8,128)(2,1)S(1)} %copy-done.6), custom_call_target="tpu_custom_call" | custom-call | tf_op jit(solution)/shard_map/dispatch/pallas_call | solution.py:381
  5.7 7.3 %all-to-all-start = ((bf16[8,16,1152]{2,1,0:T(8,128)(2,1)}), bf16[8,16,1152]{2,1,0:T(8,128)(2,1)S(1)}, u32[]{:S(2)}, u32[]{:S(2)}) async-start(bf16[8,16,1152]{2,1,0:T(8,128)(2,1)} %get-tuple-element.13), calls=%async_computation | async-start | bytes 589824 | tf_op jit(solution)/shard_map/all_to_all | solution.py:340
  13.0 0.0 copy-done
  13.0 0.1 constant_dynamic-slice_fusion.1.a_ref
  13.1 0.0 copy-start.7
  13.1 0.0 copy-start.8
  13.1 0.0 copy-start.10
  13.1 9.5 %all-to-all-done.blocks = bf16[8,16,1152]{2,1,0:T(8,128)(2,1)S(1)} async-done(((bf16[8,16,1152]{2,1,0:T(8,128)(2,1)}), bf16[8,16,1152]{2,1,0:T(8,128)(2,1)S(1)}, u32[]{:S(2)}, u32[]{:S(2)}) %all-to-all-start) | async-done | bytes 294944 | tf_op jit(solution)/shard_map/all_to_all | solution.py:340
  22.6 0.0 copy-start.5
  22.6 0.6 project_query.1
  23.2 0.0 collective-permute-start
  23.2 1.2 %collective-permute-done.other = f32[32,128]{1,0:T(8,128)S(1)} collective-permute-done((f32[32,128]{1,0:T(8,128)S(1)}, f32[32,128]{1,0:T(8,128)S(1)}, u32[]{:S(2)}, u32[]{:S(2)}) %collective-permute-start) | collective-permute-done | bytes 16416 | tf_op jit(solution)/shard_map/ppermute | solution.py:344
  24.4 0.0 copy-start.3
  24.4 1.2 %copy-done.3 = bf16[8,16,4096]{2,1,0:T(8,128)(2,1)S(1)} copy-done((bf16[8,16,4096]{2,1,0:T(8,128)(2,1)S(1)}, bf16[8,16,4096]{2,1,0:T(8,128)(2,1)}, u32[]{:S(2)}) %copy-start.3) | copy-done | bytes 1048600
  25.7 0.5 expand_query.1
  26.1 12.6 %all_to_all.20.blocks = bf16[8,16,1024]{2,1,0:T(8,128)(2,1)S(1)} all-to-all(bf16[8,16,1024]{2,1,0:T(8,128)(2,1)S(1)} %expand_query.1), channel_id=1, replica_groups=mesh['parts'=2,'store'=8,'tensor'=2] {'store'}, dimensions={0} | all-to-all | bytes 524288 | tf_op jit(solution)/shard_map/all_to_all | solution.py:340
  38.8 0.0 copy-done.7
  38.8 0.0 copy-done.8
  38.8 0.0 copy-done.10
  38.8 0.0 copy-done.5
  38.8 0.0 copy-start.1
  38.8 3.4 %copy-done.1 = bf16[16,512,512]{2,1,0:T(8,128)(2,1)S(1)} copy-done((bf16[16,512,512]{2,1,0:T(8,128)(2,1)S(1)}, bf16[16,512,512]{2,1,0:T(8,128)(2,1)}, u32[]{:S(2)}) %copy-start.1) | copy-done | bytes 8388632
  42.2 0.0 copy-start.2
  42.2 3.4 %copy-done.2 = bf16[16,512,512]{2,1,0:T(8,128)(2,1)S(1)} copy-done((bf16[16,512,512]{2,1,0:T(8,128)(2,1)S(1)}, bf16[16,512,512]{2,1,0:T(8,128)(2,1)}, u32[]{:S(2)}) %copy-start.2) | copy-done | bytes 8388632
  45.6 14.9 %attend.1 = (bf16[2,16,4096]{2,1,0:T(8,128)(2,1)}, bf16[8,16,1024]{2,1,0:T(8,128)(2,1)}) custom-call(s32[16]{0:T(128)S(1)} %get-tuple-element.10.place_of, s32[16]{0:T(128)S(1)} %get-tuple-element.11.row_at, s32[16]{0:T(128)S(1)} %get-tuple-element.12.order, s32[16]{0:T(128)S(1)} %copy-done.10, bf16[2,16,4096]{2,1,0:T(8,128)(2,1)S(1)} %copy-done.5, ...), custom_call_target="tpu_custom_call" | custom-call | tf_op jit(solution)/shard_map/attend/pallas_call | solution.py:425
  60.4 3.7 %all-to-all-start.2 = ((bf16[8,16,1024]{2,1,0:T(8,128)(2,1)}), bf16[8,16,1024]{2,1,0:T(8,128)(2,1)S(1)}, u32[]{:S(2)}, u32[]{:S(2)}) async-start(bf16[8,16,1024]{2,1,0:T(8,128)(2,1)} %get-tuple-element.16), calls=%async_computation.2 | async-start | bytes 524288 | tf_op jit(solution)/shard_map/all_to_all | solution.py:340
  64.1 1.3 %constant_dynamic-slice_fusion.a_ref = bf16[128,4096]{1,0:T(8,128)(2,1)S(1)} fusion(bf16[128,8192]{1,0:T(8,128)(2,1)} %bitcast.11, s32[]{:T(128)S(6)} %select_n.4), kind=kLoop, calls=%fused_computation | loop fusion | bytes 2097156 | tf_op jit(solution)/shard_map/dynamic_slice | solution.py:375
  65.4 7.3 %all-to-all-done.2.blocks = bf16[8,16,1024]{2,1,0:T(8,128)(2,1)S(1)} async-done(((bf16[8,16,1024]{2,1,0:T(8,128)(2,1)}), bf16[8,16,1024]{2,1,0:T(8,128)(2,1)S(1)}, u32[]{:S(2)}, u32[]{:S(2)}) %all-to-all-start.2) | async-done | bytes 262176 | tf_op jit(solution)/shard_map/all_to_all | solution.py:340
  72.7 0.6 project_output.1.mine
  73.3 0.0 collective-permute-start.1
  73.3 1.2 %collective-permute-done.1.other = f32[32,128]{1,0:T(8,128)S(1)} collective-permute-done((f32[32,128]{1,0:T(8,128)S(1)}, f32[32,128]{1,0:T(8,128)S(1)}, u32[]{:S(2)}, u32[]{:S(2)}) %collective-permute-start.1) | collective-permute-done | bytes 16416 | tf_op jit(solution)/shard_map/ppermute | solution.py:344
  74.5 0.0 copy-start.4
  74.5 1.2 %copy-done.4 = bf16[8,16,4096]{2,1,0:T(8,128)(2,1)S(1)} copy-done((bf16[8,16,4096]{2,1,0:T(8,128)(2,1)S(1)}, bf16[8,16,4096]{2,1,0:T(8,128)(2,1)}, u32[]{:S(2)}) %copy-start.4) | copy-done | bytes 1048600
  75.7 0.5 expand_output.1
  76.2 12.6 %all_to_all.21.blocks = bf16[8,16,1024]{2,1,0:T(8,128)(2,1)S(1)} all-to-all(bf16[8,16,1024]{2,1,0:T(8,128)(2,1)S(1)} %expand_output.1), channel_id=1, replica_groups=mesh['parts'=2,'store'=8,'tensor'=2] {'store'}, dimensions={0} | all-to-all | bytes 524288 | tf_op jit(solution)/shard_map/all_to_all | solution.py:340
  88.8 1.5 %collect.1 = bf16[2,16,4096]{2,1,0:T(8,128)(2,1)} custom-call(s32[16]{0:T(128)S(1)} %get-tuple-element.10.place_of, bf16[8,16,1024]{2,1,0:T(8,128)(2,1)S(1)} %all_to_all.21.blocks), custom_call_target="tpu_custom_call" | custom-call | tf_op jit(solution)/shard_map/collect/pallas_call | solution.py:452
Async XLA Ops:
  0.6 12.4 %copy-start = (bf16[8192,8,16]{0,2,1:T(8,128)(2,1)S(1)}, bf16[8192,8,16]{0,2,1:T(8,128)(2,1)}, u32[]{:S(2)}) copy-start(bf16[8192,8,16]{0,2,1:T(8,128)(2,1)} %param.22) | copy-start | bytes 6291460
  0.6 1.1 %copy-start.6 = (bf16[2,16,4096]{2,1,0:T(8,128)(2,1)S(1)}, bf16[2,16,4096]{2,1,0:T(8,128)(2,1)}, u32[]{:S(2)}) copy-start(bf16[2,16,4096]{2,1,0:T(8,128)(2,1)} %x_hbm.1) | copy-start | bytes 786436
  1.7 0.7 copy-start.9
  2.4 0.7 copy-start.11
  3.1 0.7 copy-start.12
  5.7 16.9 %all-to-all-start = ((bf16[8,16,1152]{2,1,0:T(8,128)(2,1)}), bf16[8,16,1152]{2,1,0:T(8,128)(2,1)S(1)}, u32[]{:S(2)}, u32[]{:S(2)}) async-start(bf16[8,16,1152]{2,1,0:T(8,128)(2,1)} %get-tuple-element.13), calls=%async_computation | async-start | bytes 589824 | tf_op jit(solution)/shard_map/all_to_all | solution.py:340
  13.1 25.7 %copy-start.7 = (bf16[2,16,512]{2,1,0:T(8,128)(2,1)S(1)}, bf16[2,16,512]{2,1,0:T(8,128)(2,1)}, u32[]{:S(2)}) copy-start(bf16[2,16,512]{2,1,0:T(8,128)(2,1)} %kn_ref.1) | copy-start | bytes 98308
  13.1 25.7 %copy-start.8 = (bf16[2,16,512]{2,1,0:T(8,128)(2,1)S(1)}, bf16[2,16,512]{2,1,0:T(8,128)(2,1)}, u32[]{:S(2)}) copy-start(bf16[2,16,512]{2,1,0:T(8,128)(2,1)} %vn_ref.1) | copy-start | bytes 98308
  13.1 25.7 %copy-start.10 = (s32[16]{0:T(128)S(1)}, s32[16]{0:T(128)}, u32[]{:S(2)}) copy-start(s32[16]{0:T(128)} %lengths.1) | copy-start | bytes 196
  22.6 16.2 %copy-start.5 = (bf16[2,16,4096]{2,1,0:T(8,128)(2,1)S(1)}, bf16[2,16,4096]{2,1,0:T(8,128)(2,1)}, u32[]{:S(2)}) copy-start(bf16[2,16,4096]{2,1,0:T(8,128)(2,1)} %q_ref.1) | copy-start | bytes 786436
  23.2 1.2 %collective-permute-start = (f32[32,128]{1,0:T(8,128)S(1)}, f32[32,128]{1,0:T(8,128)S(1)}, u32[]{:S(2)}, u32[]{:S(2)}) collective-permute-start(f32[32,128]{1,0:T(8,128)S(1)} %get-tuple-element.14.mine), channel_id=1, source_target_pairs={{0,1},{1,0},{2,3},{3,2},{4,5},{5,4},{6,7},{7,6},{8,9},{9,8},{10,11... | collective-permute-start | bytes 49160 | tf_op jit(solution)/shard_map/ppermute | solution.py:344
  24.4 1.2 %copy-start.3 = (bf16[8,16,4096]{2,1,0:T(8,128)(2,1)S(1)}, bf16[8,16,4096]{2,1,0:T(8,128)(2,1)}, u32[]{:S(2)}) copy-start(bf16[8,16,4096]{2,1,0:T(8,128)(2,1)} %param.23) | copy-start | bytes 3145732
  38.8 3.4 %copy-start.1 = (bf16[16,512,512]{2,1,0:T(8,128)(2,1)S(1)}, bf16[16,512,512]{2,1,0:T(8,128)(2,1)}, u32[]{:S(2)}) copy-start(bf16[16,512,512]{2,1,0:T(8,128)(2,1)} %k_any.1) | copy-start | bytes 25165828
  42.2 3.4 %copy-start.2 = (bf16[16,512,512]{2,1,0:T(8,128)(2,1)S(1)}, bf16[16,512,512]{2,1,0:T(8,128)(2,1)}, u32[]{:S(2)}) copy-start(bf16[16,512,512]{2,1,0:T(8,128)(2,1)} %v_any.1) | copy-start | bytes 25165828
  60.4 12.3 %all-to-all-start.2 = ((bf16[8,16,1024]{2,1,0:T(8,128)(2,1)}), bf16[8,16,1024]{2,1,0:T(8,128)(2,1)S(1)}, u32[]{:S(2)}, u32[]{:S(2)}) async-start(bf16[8,16,1024]{2,1,0:T(8,128)(2,1)} %get-tuple-element.16), calls=%async_computation.2 | async-start | bytes 524288 | tf_op jit(solution)/shard_map/all_to_all | solution.py:340
  73.3 1.2 %collective-permute-start.1 = (f32[32,128]{1,0:T(8,128)S(1)}, f32[32,128]{1,0:T(8,128)S(1)}, u32[]{:S(2)}, u32[]{:S(2)}) collective-permute-start(f32[32,128]{1,0:T(8,128)S(1)} %project_output.1.mine), channel_id=1, source_target_pairs={{0,1},{1,0},{2,3},{3,2},{4,5},{5,4},{6,7},{7,6},{8,9},{9,8},{10,11... | collective-permute-start | bytes 49160 | tf_op jit(solution)/shard_map/ppermute | solution.py:344
  74.5 1.2 %copy-start.4 = (bf16[8,16,4096]{2,1,0:T(8,128)(2,1)S(1)}, bf16[8,16,4096]{2,1,0:T(8,128)(2,1)}, u32[]{:S(2)}) copy-start(bf16[8,16,4096]{2,1,0:T(8,128)(2,1)} %param.25) | copy-start | bytes 3145732

commit v3 on v2

--- a/solution.py
+++ b/solution.py
@@ -35,24 +35,36 @@
     )
 
 
-def pack_matrix(row_at, owners, heads, rows):
+def pack_matrix(row_at, owners, heads, rows, by_row):
     items = CAP * STEPS
     block = heads * items
     shape = (block, heads * STEPS * rows)
     at = iota(shape, 0)
     col = iota(shape, 1)
-    base = (at // items) * (STEPS * rows) + (at % STEPS) * rows
+    head_step = (at // items) * STEPS + at % STEPS
+    base = head_step if by_row else head_step * rows
+    factor = heads * STEPS if by_row else 1
     first = (at // STEPS) % CAP == 0
     parts = []
     for i in range(owners):
         row = jnp.where(first, row_at[i * CAP], row_at[i * CAP + 1])
-        parts.append(one_hot((col == base + row) & (row >= 0)))
+        parts.append(one_hot((col == base + row * factor) & (row >= 0)))
     return jnp.concatenate(parts, axis=0)
 
 
-def unpack_matrix(place_of, owners, heads, rows):
+def unpack_matrix(place_of, owners, heads, rows, by_row):
     items = CAP * STEPS
     block = heads * items
+    pairs = heads * STEPS
+    if by_row:
+        shape = (pairs, owners * block)
+        at = iota(shape, 0)
+        col = iota(shape, 1) - ((at // STEPS) * items + at % STEPS)
+        parts = []
+        for r in range(rows):
+            place = place_of[r]
+            parts.append(one_hot(col == (place // CAP) * block + (place % CAP) * STEPS))
+        return jnp.concatenate(parts, axis=0)
     shape = (rows, owners * block)
     at = iota(shape, 0)
     col = iota(shape, 1)
@@ -65,6 +77,20 @@
     )
 
 
+def by_row_matrix(heads, rows):
+    pairs = heads * STEPS
+    at = iota((pairs * rows, pairs * rows), 0)
+    col = iota((pairs * rows, pairs * rows), 1)
+    return one_hot(col == (at % pairs) * rows + at // pairs)
+
+
+def by_pair_matrix(heads, rows):
+    pairs = heads * STEPS
+    at = iota((pairs * rows, pairs * rows), 0)
+    col = iota((pairs * rows, pairs * rows), 1)
+    return one_hot(col == (at % rows) * pairs + at // rows)
+
+
 def regroup_matrix(owners, heads):
     items = CAP * STEPS
     total = owners * heads * items
@@ -96,27 +122,23 @@
     rank,
     ids_hbm,
     slot_of_hbm,
-    lengths_hbm,
     x_hbm,
     place_of,
     row_at,
-    order,
     blocks,
     slot_at,
     ids,
     slot_of,
-    lengths,
     x_ref,
     sems,
 ):
-    sources = (ids_hbm, slot_of_hbm, lengths_hbm, x_hbm)
-    targets = (ids, slot_of, lengths, x_ref)
-    copies = [pltpu.make_async_copy(a, b, sems.at[k]) for k, (a, b) in enumerate(zip(sources, targets))]
+    pairs = ((ids_hbm, ids), (slot_of_hbm, slot_of), (x_hbm, x_ref))
+    copies = [pltpu.make_async_copy(a, b, sems.at[k]) for k, (a, b) in enumerate(pairs)]
     for copy in copies:
         copy.start()
     rows = x_ref.shape[1]
     wide = x_ref.shape[2] // heads
-    for copy in copies[:3]:
+    for copy in copies[:2]:
         copy.wait()
     for p in range(owners * CAP):
         row_at[p] = -1
@@ -129,18 +151,10 @@
         row_at[place] = r
         slot_at[place] = slot % adapt
         place_of[r] = place
-    sizes = [lengths[r] for r in range(rows)]
-    for r in range(rows):
-        ahead = jnp.int32(0)
-        for q in range(rows):
-            if q != r:
-                longer = sizes[q] >= sizes[r] if q < r else sizes[q] > sizes[r]
-                ahead = ahead + jnp.where(longer, 1, 0)
-        order[ahead] = r
     items = CAP * STEPS
     block = heads * items
-    copies[3].wait()
-    packed = exact(pack_matrix(row_at, owners, heads, rows), stacked(x_ref, heads, wide))
+    copies[2].wait()
+    packed = exact(pack_matrix(row_at, owners, heads, rows, False), stacked(x_ref, heads, wide))
     at = iota((block, adapt * rank), 0)
     lane_slot = iota((block, adapt * rank), 1) // rank
     first = (at // STEPS) % CAP == 0
@@ -152,7 +166,7 @@
 
 def project_kernel(owners, heads, wide, first, a_ref, blocks, *refs):
     if first:
-        part_ref, mask_ref = refs
+        after, part_ref, mask_ref = refs
     else:
         mask_in, part_ref = refs
     grouped = regroup_matrix(owners, heads)
@@ -190,6 +204,55 @@
         blocks[i] = back[i * block : (i + 1) * block]
 
 
+def quads(order, lengths, rows, sizes, action):
+    def body(quad, carry):
+        longest = lengths[order[quad * QUAD]]
+        amount = (longest + CHUNK - 1) // CHUNK
+        for size in range(1, sizes + 1):
+
+            @pl.when(amount == size)
+            def _():
+                action([order[quad * QUAD + j] for j in range(QUAD)], size)
+
+        return carry
+
+    lax.fori_loop(0, rows // QUAD, body, 0)
+
+
+def prefetch_kernel(after, lengths_hbm, k_hbm, v_hbm, order, k_out, v_out, lengths, k_sem, v_sem):
+    pltpu.sync_copy(lengths_hbm, lengths)
+    rows = k_hbm.shape[0]
+    sizes = [lengths[r] for r in range(rows)]
+    for r in range(rows):
+        ahead = jnp.int32(0)
+        for q in range(rows):
+            if q != r:
+                longer = sizes[q] >= sizes[r] if q < r else sizes[q] > sizes[r]
+                ahead = ahead + jnp.where(longer, 1, 0)
+        order[ahead] = r
+
+    def copies(row, size):
+        part = pl.ds(0, size * CHUNK)
+        return (
+            pltpu.make_async_copy(k_hbm.at[row, part], k_out.at[row, part], k_sem.at[row]),
+            pltpu.make_async_copy(v_hbm.at[row, part], v_out.at[row, part], v_sem.at[row]),
+        )
+
+    def begin(rows_in, size):
+        for row in rows_in:
+            for copy in copies(row, size):
+                copy.start()
+
+    def finish(rows_in, size):
+        for row in rows_in:
+            for copy in copies(row, size):
+                copy.wait()
+
+    chunks = k_hbm.shape[1] // CHUNK
+    quads(order, lengths, rows, chunks, begin)
+    quads(order, lengths, rows, chunks, finish)
+
+
 def attend_kernel(
     owners,
     heads,
@@ -200,136 +263,95 @@
     q_ref,
     kn_ref,
     vn_ref,
-    k_any,
-    v_any,
+    k_ref,
+    v_ref,
     blocks,
     out_ref,
     outgoing,
-    k_buf,
-    v_buf,
     q_buf,
     o_buf,
-    k_sem,
-    v_sem,
 ):
     rows = q_ref.shape[1]
     wide = q_ref.shape[2] // heads
     groups = wide // HD
-    span = STEPS * groups
+    pairs = heads * STEPS
+    total = groups * pairs
     width = heads * HD
-    sizes = k_any.shape[1] // CHUNK
-
-    def copies(row, amount):
-        part = pl.ds(0, amount * CHUNK)
-        return (
-            pltpu.make_async_copy(k_any.at[row, part], k_buf.at[row, part], k_sem.at[row]),
-            pltpu.make_async_copy(v_any.at[row, part], v_buf.at[row, part], v_sem.at[row]),
-        )
-
-    def per_quad(action):
-        def body(quad, carry):
-            longest = lengths[order[quad * QUAD]]
-            amount = (longest + CHUNK - 1) // CHUNK
-            for size in range(1, sizes + 1):
-
-                @pl.when(amount == size)
-                def _():
-                    action([order[quad * QUAD + j] for j in range(QUAD)], size)
-
-            return carry
-
-        lax.fori_loop(0, rows // QUAD, body, 0)
-
-    def begin(rows_in, size):
-        for row in rows_in:
-            for copy in copies(row, size):
-                copy.start()
-
-    per_quad(begin)
 
     delta = jnp.dot(
-        unpack_matrix(place_of, owners, heads, rows),
+        unpack_matrix(place_of, owners, heads, rows, True),
         jnp.concatenate([blocks[i] for i in range(owners)], axis=0),
         preferred_element_type=F32,
     )
-    query = (stacked(q_ref, heads, wide).astype(F32) + delta).astype(BF16).astype(F32)
-    for c in range(heads):
-        for s in range(STEPS):
-            top = (c * STEPS + s) * rows
-            for j in range(groups):
-                q_buf[pl.ds(c * span + s * groups + j, rows, stride=heads * span), :] = query[
-                    top : top + rows, j * HD : (j + 1) * HD
-                ]
-
-    scale = 1.0 / math.sqrt(HD)
+    base = jnp.dot(
+        by_row_matrix(heads, rows), stacked(q_ref, heads, wide), preferred_element_type=F32
+    )
+    q_buf[...] = base + delta
+
+    factor = math.log2(math.e) / math.sqrt(HD)
     new_keys = jnp.concatenate([kn_ref[t] for t in range(STEPS)], axis=0)
     new_values = jnp.concatenate([vn_ref[t] for t in range(STEPS)], axis=0)
-    total = heads * span
-    diagonal = iota((total, width), 0) // span == iota((total, width), 1) // HD
+    diagonal = (iota((total, width), 0) // STEPS) % heads == iota((total, width), 1) // HD
+    own_head = [(iota((total, HD), 0) // STEPS) % heads == c for c in range(heads)]
     fresh_shape = (total, STEPS * rows)
-    step_of = (iota(fresh_shape, 0) // groups) % STEPS
     fresh_at = iota(fresh_shape, 1)
-    in_time = fresh_at // rows <= step_of
+    in_time = fresh_at // rows <= iota(fresh_shape, 0) % STEPS
     contract = (((1,), (1,)), ((), ()))
 
     def attend(rows_in, size):
+        extent = size * CHUNK
+        position = iota((total, extent), 1)
+        results = []
         for row in rows_in:
-            for copy in copies(row, size):
-                copy.wait()
-        length_now = size * CHUNK
-        position = iota((total, length_now), 1)
-        for row in rows_in:
-            start = pl.multiple_of(row * total, total)
-            one = q_buf[pl.ds(start, total), :].astype(BF16)
+            start = pl.multiple_of(row * pairs, pairs)
+            flat = q_buf[pl.ds(start, pairs), :]
+            one = jnp.concatenate(
+                [flat[:, j * HD : (j + 1) * HD] for j in range(groups)], axis=0
+            ).astype(BF16)
             spread = jnp.where(diagonal, jnp.concatenate([one] * heads, axis=1), jnp.zeros((), BF16))
-            keys = k_buf[row, :length_now, :]
-            values = v_buf[row, :length_now, :]
-            cached = lax.dot_general(spread, keys, contract, preferred_element_type=F32) * scale
+            cached = lax.dot_general(
+                spread, k_ref[row, :extent, :], contract, preferred_element_type=F32
+            )
             cached = jnp.where(position < lengths[row], cached, -jnp.inf)
-            fresh = lax.dot_general(spread, new_keys, contract, preferred_element_type=F32) * scale
+            fresh = lax.dot_general(spread, new_keys, contract, preferred_element_type=F32)
             fresh = jnp.where(in_time & (fresh_at % rows == row), fresh, -jnp.inf)
             top = jnp.maximum(
                 jnp.max(cached, axis=1, keepdims=True), jnp.max(fresh, axis=1, keepdims=True)
             )
-            cached = jnp.exp(cached - top)
-            fresh = jnp.exp(fresh - top)
+            cached = jnp.exp2((cached - top) * factor)
+            fresh = jnp.exp2((fresh - top) * factor)
             norm = jnp.sum(cached, axis=1, keepdims=True) + jnp.sum(fresh, axis=1, keepdims=True)
-            share = 1.0 / norm
-            mixed = jnp.dot((cached * share).astype(BF16), values, preferred_element_type=F32)
-            mixed = mixed + jnp.dot(
-                (fresh * share).astype(BF16), new_values, preferred_element_type=F32
+            mixed = jnp.dot(
+                cached.astype(BF16), v_ref[row, :extent, :], preferred_element_type=F32
+            ) + jnp.dot(fresh.astype(BF16), new_values, preferred_element_type=F32)
+            own = jnp.zeros((total, HD), F32)
+            for c in range(heads):
+                own = jnp.where(own_head[c], mixed[:, c * HD : (c + 1) * HD], own)
+            results.append((start, own / norm))
+        for start, own in results:
+            o_buf[pl.ds(start, pairs), :] = jnp.concatenate(
+                [own[j * pairs : (j + 1) * pairs] for j in range(groups)], axis=1
             )
-            o_buf[pl.ds(start, total), :] = jnp.concatenate(
-                [
-                    mixed[c * span : (c + 1) * span, c * HD : (c + 1) * HD]
-                    for c in range(heads)
-                ],
-                axis=0,
-            )
-
-    per_quad(attend)
-
-    results = []
-    for c in range(heads):
-        for s in range(STEPS):
-            tiles = [
-                o_buf[pl.ds(c * span + s * groups + j, rows, stride=heads * span), :].astype(BF16)
-                for j in range(groups)
-            ]
-            piece = jnp.concatenate(tiles, axis=1)
-            out_ref[s, :, c * wide : (c + 1) * wide] = piece
-            results.append(piece)
-    packed = exact(pack_matrix(row_at, owners, heads, rows), jnp.concatenate(results, axis=0))
+
+    quads(order, lengths, rows, k_ref.shape[1] // CHUNK, attend)
+
+    mixed = o_buf[...].astype(BF16)
+    packed = exact(pack_matrix(row_at, owners, heads, rows, True), mixed)
     block = heads * CAP * STEPS
     for i in range(owners):
         outgoing[i] = packed[i * block : (i + 1) * block]
+    final = exact(by_pair_matrix(heads, rows), mixed)
+    for c in range(heads):
+        for s in range(STEPS):
+            at = (c * STEPS + s) * rows
+            out_ref[s, :, c * wide : (c + 1) * wide] = final[at : at + rows]
 
 
 def collect_kernel(owners, heads, place_of, blocks, out_ref):
     rows = out_ref.shape[1]
     wide = out_ref.shape[2] // heads
     arrived = jnp.concatenate([blocks[i] for i in range(owners)], axis=0)
-    values = exact(unpack_matrix(place_of, owners, heads, rows), arrived)
+    values = exact(unpack_matrix(place_of, owners, heads, rows, False), arrived)
     for c in range(heads):
         for s in range(STEPS):
             top = (c * STEPS + s) * rows
@@ -338,6 +360,14 @@
 
 def exchange(blocks):
     return lax.all_to_all(blocks, "store", split_axis=0, concat_axis=0, tiled=True)
+
+
+def in_hbm(array):
+    return pltpu.with_memory_space_constraint(array, pltpu.HBM)
+
+
+def in_vmem(array):
+    return pltpu.with_memory_space_constraint(array, pltpu.VMEM)
 
 
 def swap_cores(part):
@@ -378,37 +408,54 @@
     small = pltpu.CompilerParams(vmem_limit_bytes=16 * 1024 * 1024)
 
     sent = shape((owners, block, wide), BF16)
-    place_of, row_at, order, blocks = pl.pallas_call(
+    place_of, row_at, blocks = pl.pallas_call(
         functools.partial(dispatch_kernel, owners, heads, adapt, rank),
         out_shape=[
             shape((rows,), I32),
             shape((owners * CAP,), I32),
-            shape((rows,), I32),
             shape((owners, block, wide + lanes), BF16),
         ],
-        in_specs=[HBM] * 4,
-        out_specs=[SMEM] * 3 + [VMEM],
+        in_specs=[HBM] * 3,
+        out_specs=[SMEM] * 2 + [VMEM],
         scratch_shapes=[
             pltpu.SMEM((owners * CAP,), I32),
             pltpu.SMEM(adapter_ids.shape, I32),
             pltpu.SMEM(slot_of.shape, I32),
-            pltpu.SMEM(lengths.shape, I32),
             pltpu.VMEM(x_in.shape, BF16),
-            pltpu.SemaphoreType.DMA((4,)),
+            pltpu.SemaphoreType.DMA((3,)),
         ],
         compiler_params=small,
         name="dispatch",
-    )(adapter_ids, slot_of, lengths, x_in)
+    )(in_hbm(adapter_ids), in_hbm(slot_of), in_hbm(x_in))
+
+    order, keys, values = pl.pallas_call(
+        prefetch_kernel,
+        out_shape=[
+            shape((rows,), I32),
+            pltpu.VMEM(cache_k.shape, BF16),
+            pltpu.VMEM(cache_v.shape, BF16),
+        ],
+        in_specs=[SMEM] + [HBM] * 3,
+        out_specs=[SMEM, VMEM, VMEM],
+        scratch_shapes=[
+            pltpu.SMEM(lengths.shape, I32),
+            pltpu.SemaphoreType.DMA((rows,)),
+            pltpu.SemaphoreType.DMA((rows,)),
+        ],
+        compiler_params=small,
+        cost_estimate=pl.CostEstimate(flops=0, bytes_accessed=8 * 1024 * 1024, transcendentals=0),
+        name="prefetch",
+    )(place_of, in_hbm(lengths), in_hbm(cache_k), in_hbm(cache_v))
 
     arrived = exchange(blocks)
     part, mask = pl.pallas_call(
         functools.partial(project_kernel, owners, heads, wide, True),
         out_shape=[shape((items, lanes), F32)] * 2,
-        in_specs=[VMEM] * 2,
+        in_specs=[VMEM] * 2 + [SMEM],
         out_specs=[VMEM] * 2,
         compiler_params=small,
         name="project_query",
-    )(half(a_query), arrived)
+    )(half(a_query), arrived, order)
 
     def expand(part, b_store, name):
         return pl.pallas_call(
@@ -425,19 +472,15 @@
     attn_out, outgoing = pl.pallas_call(
         functools.partial(attend_kernel, owners, heads),
         out_shape=[shape((STEPS, rows, width), BF16), sent],
-        in_specs=[SMEM] * 4 + [VMEM] * 3 + [HBM] * 2 + [VMEM],
+        in_specs=[SMEM] * 4 + [VMEM] * 6,
         out_specs=[VMEM] * 2,
         scratch_shapes=[
-            pltpu.VMEM(cache_k.shape, BF16),
-            pltpu.VMEM(cache_v.shape, BF16),
-            pltpu.VMEM((rows * STEPS * width // HD, HD), F32),
-            pltpu.VMEM((rows * STEPS * width // HD, HD), F32),
-            pltpu.SemaphoreType.DMA((rows,)),
-            pltpu.SemaphoreType.DMA((rows,)),
+            pltpu.VMEM((rows * STEPS * heads, wide), F32),
+            pltpu.VMEM((rows * STEPS * heads, wide), F32),
         ],
-        compiler_params=pltpu.CompilerParams(vmem_limit_bytes=32 * 1024 * 1024),
+        compiler_params=pltpu.CompilerParams(vmem_limit_bytes=24 * 1024 * 1024),
         name="attend",
-    )(place_of, row_at, order, lengths, q_base, k_new, v_new, cache_k, cache_v, returned)
+    )(place_of, row_at, order, lengths, q_base, k_new, v_new, in_vmem(keys), in_vmem(values), returned)
 
     arrived = exchange(outgoing)
     part = pl.pallas_call(

time: 91 us -> 88.3 us (0.970)
  waiting for transfers between devices: 19.2 us -> 9.67 us
  local copies, waits for them, and re-layouts: 13.7 us -> 18 us
  blocking collectives: 25.3 us -> 28 us
    all_to_all x2, waiting for transfers between devices: 16.8 us -> 7.27 us  [exchange(): lax.all_to_all(blocks, 'store', split_axis=0, concat_axis=0, tiled=True)]
    pallas_call x1, Pallas kernels: 14.9 us -> 8.23 us  [shards(): pl.pallas_call(functools.partial(attend_kernel, owners, heads), out_shape...]
    pallas_call x0 -> x1, Pallas kernels: none -> 5.58 us  [shards(): pl.pallas_call(prefetch_kernel, out_shape=[shape((rows,), I32), pltpu.VME...]
    unnamed x26 -> x22, local copies, waits for them, and re-layouts: 12.3 us -> 16.6 us
    all_to_all x2, blocking collectives: 25.3 us -> 28 us  [exchange(): lax.all_to_all(blocks, 'store', split_axis=0, concat_axis=0, tiled=True)]
  transfers between devices with their start and end apart: 4 -> 4, of which waited for: 4 -> 3; matrix products, arithmetic and copies ran while one was open for 2% -> 2% of each run, Pallas kernels for 0% -> 6%
where the time goes in v3:
time: 88.3 us; the launch traced here: 87.6 us
  blocking collectives  28 us (32%)
  Pallas kernels  20 us (23%)
  local copies, waits for them, and re-layouts  18 us (20%)
  starting transfers between devices  11.2 us (13%)
  waiting for transfers between devices  9.67 us (11%)
    all_to_all x2, blocking collectives, exchange(): lax.all_to_all(blocks, 'store', split_axis=0, concat_axis=0, tiled=True)  28 us
    unnamed x22, local copies, waits for them, and re-layouts  16.6 us
    all_to_all x2, starting transfers between devices, exchange(): lax.all_to_all(blocks, 'store', split_axis=0, concat_axis=0, tiled=True)  11.2 us
    pallas_call x1, Pallas kernels, shards(): pl.pallas_call(functools.partial(attend_kernel, owners, heads), out_shape...  8.23 us
    all_to_all x2, waiting for transfers between devices, exchange(): lax.all_to_all(blocks, 'store', split_axis=0, concat_axis=0, tiled=True)  7.27 us
    pallas_call x1, Pallas kernels, shards(): pl.pallas_call(prefetch_kernel, out_shape=[shape((rows,), I32), pltpu.VME...  5.58 us
    ppermute x2, waiting for transfers between devices, swap_cores(): return lax.ppermute(part, 'tensor', [(0, 1), (1, 0)])  2.4 us
    pallas_call x1, Pallas kernels, shards(): pl.pallas_call(functools.partial(dispatch_kernel, owners, heads, adapt, r...  2.05 us
  transfers between devices with their start and end apart: 4, of which 3 were waited for; matrix products, arithmetic and copies ran while one was open for 2% of the time, Pallas kernels for 6%

profile of v3, /device:TPU:0, one launch (start us, length us, event | category | flops | bytes accessed | tf_op | source)
XLA Modules:
  0.0 87.6 jit_solution(12473756803910103443)
XLA Ops:
  0.6 0.0 copy-start
  0.6 2.1 %dispatch.1 = (s32[16]{0:T(128)S(1)}, s32[16]{0:T(128)S(1)}, bf16[8,16,1152]{2,1,0:T(8,128)(2,1)}) custom-call(s32[16]{0:T(128)} %ids_hbm.1, s32[64]{0:T(128)} %slot_of_hbm.1, bf16[2,16,4096]{2,1,0:T(8,128)(2,1)} %x_hbm.1), custom_call_target="tpu_custom_call" | custom-call | tf_op jit(solution)/shard_map/dispatch/pallas_call | solution.py:411
  2.7 7.3 %all-to-all-start = ((bf16[8,16,1152]{2,1,0:T(8,128)(2,1)}), bf16[8,16,1152]{2,1,0:T(8,128)(2,1)S(1)}, u32[]{:S(2)}, u32[]{:S(2)}) async-start(bf16[8,16,1152]{2,1,0:T(8,128)(2,1)} %get-tuple-element.17), calls=%async_computation | async-start | bytes 589824 | tf_op jit(solution)/shard_map/all_to_all | solution.py:362
  10.0 0.0 copy-start.8
  10.0 0.0 copy-start.9
  10.0 0.0 copy-start.10
  10.0 5.6 %prefetch.1 = (s32[16]{0:T(128)S(1)}, bf16[16,512,512]{2,1,0:T(8,128)(2,1)S(1)}, bf16[16,512,512]{2,1,0:T(8,128)(2,1)S(1)}) custom-call(s32[16]{0:T(128)S(1)} %get-tuple-element.12.after.place_of, s32[16]{0:T(128)} %lengths.1, bf16[16,512,512]{2,1,0:T(8,128)(2,1)} %k_hbm.1, bf16[16,512,512]{2,1,0:T(8,128)(2,1)} %v_hbm.1), custom_call_target="tpu_custom_call" | custom-call | bytes 8388608 | tf_op jit(solution)/shard_map/prefetch/pallas_call | solution.py:431
  15.6 0.0 copy-start.1
  15.6 3.2 %copy-done.1 = bf16[16,512,512]{2,1,0:T(8,128)(2,1)} copy-done((bf16[16,512,512]{2,1,0:T(8,128)(2,1)}, bf16[16,512,512]{2,1,0:T(8,128)(2,1)S(1)}, u32[]{:S(2)}) %copy-start.1) | copy-done | bytes 8388632
  18.9 0.0 copy-start.3
  18.9 3.2 %copy-done.3 = bf16[16,512,512]{2,1,0:T(8,128)(2,1)} copy-done((bf16[16,512,512]{2,1,0:T(8,128)(2,1)}, bf16[16,512,512]{2,1,0:T(8,128)(2,1)S(1)}, u32[]{:S(2)}) %copy-start.3) | copy-done | bytes 8388632
  22.1 0.0 copy-done
  22.1 0.1 constant_dynamic-slice_fusion.1.a_ref
  22.2 0.0 all-to-all-done.blocks
  22.2 1.1 %project_query.1 = (f32[32,128]{1,0:T(8,128)S(1)}, f32[32,128]{1,0:T(8,128)S(1)}) custom-call(bf16[128,4096]{1,0:T(8,128)(2,1)S(1)} %constant_dynamic-slice_fusion.1.a_ref, bf16[8,16,1152]{2,1,0:T(8,128)(2,1)S(1)} %all-to-all-done.blocks, s32[16]{0:T(128)S(1)} %get-tuple-element.14.refs_0_.order), custom_call_target="tpu_custom_call" | custom-call | tf_op jit(solution)/shard_map/project_query/pallas_call | solution.py:451
  23.3 0.0 collective-permute-start
  23.3 1.2 %collective-permute-done.other = f32[32,128]{1,0:T(8,128)S(1)} collective-permute-done((f32[32,128]{1,0:T(8,128)S(1)}, f32[32,128]{1,0:T(8,128)S(1)}, u32[]{:S(2)}, u32[]{:S(2)}) %collective-permute-start) | collective-permute-done | bytes 16416 | tf_op jit(solution)/shard_map/ppermute | solution.py:374
  24.5 0.0 copy-start.5
  24.5 1.2 %copy-done.5 = bf16[8,16,4096]{2,1,0:T(8,128)(2,1)S(1)} copy-done((bf16[8,16,4096]{2,1,0:T(8,128)(2,1)S(1)}, bf16[8,16,4096]{2,1,0:T(8,128)(2,1)}, u32[]{:S(2)}) %copy-start.5) | copy-done | bytes 1048600
  25.8 0.4 expand_query.1
  26.2 15.3 %all_to_all.20.blocks = bf16[8,16,1024]{2,1,0:T(8,128)(2,1)S(1)} all-to-all(bf16[8,16,1024]{2,1,0:T(8,128)(2,1)S(1)} %expand_query.1), channel_id=1, replica_groups=mesh['parts'=2,'store'=8,'tensor'=2] {'store'}, dimensions={0} | all-to-all | bytes 524288 | tf_op jit(solution)/shard_map/all_to_all | solution.py:362
  41.5 0.0 copy-done.8
  41.5 0.0 copy-done.9
  41.5 0.0 copy-done.10
  41.5 0.0 copy-start.2
  41.6 3.4 %copy-done.2 = bf16[16,512,512]{2,1,0:T(8,128)(2,1)S(1)} copy-done((bf16[16,512,512]{2,1,0:T(8,128)(2,1)S(1)}, bf16[16,512,512]{2,1,0:T(8,128)(2,1)}, u32[]{:S(2)}) %copy-start.2) | copy-done | bytes 8388632
  44.9 0.0 copy-start.4
  44.9 3.4 %copy-done.4 = bf16[16,512,512]{2,1,0:T(8,128)(2,1)S(1)} copy-done((bf16[16,512,512]{2,1,0:T(8,128)(2,1)S(1)}, bf16[16,512,512]{2,1,0:T(8,128)(2,1)}, u32[]{:S(2)}) %copy-start.4) | copy-done | bytes 8388632
  48.3 0.0 copy-start.7
  48.3 0.9 %copy-done.7 = bf16[2,16,4096]{2,1,0:T(8,128)(2,1)S(1)} copy-done((bf16[2,16,4096]{2,1,0:T(8,128)(2,1)S(1)}, bf16[2,16,4096]{2,1,0:T(8,128)(2,1)}, u32[]{:S(2)}) %copy-start.7) | copy-done | bytes 262168
  49.3 8.2 %attend.1 = (bf16[2,16,4096]{2,1,0:T(8,128)(2,1)}, bf16[8,16,1024]{2,1,0:T(8,128)(2,1)}) custom-call(s32[16]{0:T(128)S(1)} %get-tuple-element.12.after.place_of, s32[16]{0:T(128)S(1)} %get-tuple-element.13.row_at, s32[16]{0:T(128)S(1)} %get-tuple-element.14.refs_0_.order, s32[16]{0:T(128)S(1)} %copy-done.10, bf16[2,16,4096]{2,1,0:T(8,128)(2,1)S(1)} %copy-done.7, ...), custom_call_target="tpu_custom_call" | custom-call | tf_op jit(solution)/shard_map/attend/pallas_call | solution.py:472
  57.5 3.9 %all-to-all-start.2 = ((bf16[8,16,1024]{2,1,0:T(8,128)(2,1)}), bf16[8,16,1024]{2,1,0:T(8,128)(2,1)S(1)}, u32[]{:S(2)}, u32[]{:S(2)}) async-start(bf16[8,16,1024]{2,1,0:T(8,128)(2,1)} %get-tuple-element.20), calls=%async_computation.2 | async-start | bytes 524288 | tf_op jit(solution)/shard_map/all_to_all | solution.py:362
  61.4 1.3 %constant_dynamic-slice_fusion.a_ref = bf16[128,4096]{1,0:T(8,128)(2,1)S(1)} fusion(bf16[128,8192]{1,0:T(8,128)(2,1)} %bitcast.11, s32[]{:T(128)S(6)} %select_n.4), kind=kLoop, calls=%fused_computation | loop fusion | bytes 2097156 | tf_op jit(solution)/shard_map/dynamic_slice | solution.py:405
  62.7 7.3 %all-to-all-done.2.blocks = bf16[8,16,1024]{2,1,0:T(8,128)(2,1)S(1)} async-done(((bf16[8,16,1024]{2,1,0:T(8,128)(2,1)}), bf16[8,16,1024]{2,1,0:T(8,128)(2,1)S(1)}, u32[]{:S(2)}, u32[]{:S(2)}) %all-to-all-start.2) | async-done | bytes 262176 | tf_op jit(solution)/shard_map/all_to_all | solution.py:362
  70.0 0.6 project_output.1.mine
  70.6 0.0 collective-permute-start.1
  70.6 1.2 %collective-permute-done.1.other = f32[32,128]{1,0:T(8,128)S(1)} collective-permute-done((f32[32,128]{1,0:T(8,128)S(1)}, f32[32,128]{1,0:T(8,128)S(1)}, u32[]{:S(2)}, u32[]{:S(2)}) %collective-permute-start.1) | collective-permute-done | bytes 16416 | tf_op jit(solution)/shard_map/ppermute | solution.py:374
  71.8 0.0 copy-start.6
  71.8 1.2 %copy-done.6 = bf16[8,16,4096]{2,1,0:T(8,128)(2,1)S(1)} copy-done((bf16[8,16,4096]{2,1,0:T(8,128)(2,1)S(1)}, bf16[8,16,4096]{2,1,0:T(8,128)(2,1)}, u32[]{:S(2)}) %copy-start.6) | copy-done | bytes 1048600
  73.0 0.5 expand_output.1
  73.5 12.6 %all_to_all.21.blocks = bf16[8,16,1024]{2,1,0:T(8,128)(2,1)S(1)} all-to-all(bf16[8,16,1024]{2,1,0:T(8,128)(2,1)S(1)} %expand_output.1), channel_id=1, replica_groups=mesh['parts'=2,'store'=8,'tensor'=2] {'store'}, dimensions={0} | all-to-all | bytes 524288 | tf_op jit(solution)/shard_map/all_to_all | solution.py:362
  86.1 1.5 %collect.1 = bf16[2,16,4096]{2,1,0:T(8,128)(2,1)} custom-call(s32[16]{0:T(128)S(1)} %get-tuple-element.12.after.place_of, bf16[8,16,1024]{2,1,0:T(8,128)(2,1)S(1)} %all_to_all.21.blocks), custom_call_target="tpu_custom_call" | custom-call | tf_op jit(solution)/shard_map/collect/pallas_call | solution.py:495
Async XLA Ops:
  0.6 21.5 %copy-start = (bf16[8192,8,16]{0,2,1:T(8,128)(2,1)S(1)}, bf16[8192,8,16]{0,2,1:T(8,128)(2,1)}, u32[]{:S(2)}) copy-start(bf16[8192,8,16]{0,2,1:T(8,128)(2,1)} %param.22) | copy-start | bytes 6291460
  2.7 19.5 %all-to-all-start = ((bf16[8,16,1152]{2,1,0:T(8,128)(2,1)}), bf16[8,16,1152]{2,1,0:T(8,128)(2,1)S(1)}, u32[]{:S(2)}, u32[]{:S(2)}) async-start(bf16[8,16,1152]{2,1,0:T(8,128)(2,1)} %get-tuple-element.17), calls=%async_computation | async-start | bytes 589824 | tf_op jit(solution)/shard_map/all_to_all | solution.py:362
  10.0 31.5 %copy-start.8 = (bf16[2,16,512]{2,1,0:T(8,128)(2,1)S(1)}, bf16[2,16,512]{2,1,0:T(8,128)(2,1)}, u32[]{:S(2)}) copy-start(bf16[2,16,512]{2,1,0:T(8,128)(2,1)} %kn_ref.1) | copy-start | bytes 98308
  10.0 31.5 %copy-start.9 = (bf16[2,16,512]{2,1,0:T(8,128)(2,1)S(1)}, bf16[2,16,512]{2,1,0:T(8,128)(2,1)}, u32[]{:S(2)}) copy-start(bf16[2,16,512]{2,1,0:T(8,128)(2,1)} %vn_ref.1) | copy-start | bytes 98308
  10.0 31.5 %copy-start.10 = (s32[16]{0:T(128)S(1)}, s32[16]{0:T(128)}, u32[]{:S(2)}) copy-start(s32[16]{0:T(128)} %lengths.1) | copy-start | bytes 196
  15.6 3.2 %copy-start.1 = (bf16[16,512,512]{2,1,0:T(8,128)(2,1)}, bf16[16,512,512]{2,1,0:T(8,128)(2,1)S(1)}, u32[]{:S(2)}) copy-start(bf16[16,512,512]{2,1,0:T(8,128)(2,1)S(1)} %get-tuple-element.15.k_ref) | copy-start | bytes 25165828
  18.9 3.2 %copy-start.3 = (bf16[16,512,512]{2,1,0:T(8,128)(2,1)}, bf16[16,512,512]{2,1,0:T(8,128)(2,1)S(1)}, u32[]{:S(2)}) copy-start(bf16[16,512,512]{2,1,0:T(8,128)(2,1)S(1)} %get-tuple-element.16.v_ref) | copy-start | bytes 25165828
  23.3 1.2 %collective-permute-start = (f32[32,128]{1,0:T(8,128)S(1)}, f32[32,128]{1,0:T(8,128)S(1)}, u32[]{:S(2)}, u32[]{:S(2)}) collective-permute-start(f32[32,128]{1,0:T(8,128)S(1)} %get-tuple-element.18.mine), channel_id=1, source_target_pairs={{0,1},{1,0},{2,3},{3,2},{4,5},{5,4},{6,7},{7,6},{8,9},{9,8},{10,11... | collective-permute-start | bytes 49160 | tf_op jit(solution)/shard_map/ppermute | solution.py:374
  24.5 1.2 %copy-start.5 = (bf16[8,16,4096]{2,1,0:T(8,128)(2,1)S(1)}, bf16[8,16,4096]{2,1,0:T(8,128)(2,1)}, u32[]{:S(2)}) copy-start(bf16[8,16,4096]{2,1,0:T(8,128)(2,1)} %param.23) | copy-start | bytes 3145732
  41.5 3.4 %copy-start.2 = (bf16[16,512,512]{2,1,0:T(8,128)(2,1)S(1)}, bf16[16,512,512]{2,1,0:T(8,128)(2,1)}, u32[]{:S(2)}) copy-start(bf16[16,512,512]{2,1,0:T(8,128)(2,1)} %copy-done.1) | copy-start | bytes 25165828
  44.9 3.4 %copy-start.4 = (bf16[16,512,512]{2,1,0:T(8,128)(2,1)S(1)}, bf16[16,512,512]{2,1,0:T(8,128)(2,1)}, u32[]{:S(2)}) copy-start(bf16[16,512,512]{2,1,0:T(8,128)(2,1)} %copy-done.3) | copy-start | bytes 25165828
  48.3 0.9 %copy-start.7 = (bf16[2,16,4096]{2,1,0:T(8,128)(2,1)S(1)}, bf16[2,16,4096]{2,1,0:T(8,128)(2,1)}, u32[]{:S(2)}) copy-start(bf16[2,16,4096]{2,1,0:T(8,128)(2,1)} %q_ref.1) | copy-start | bytes 786436
  57.5 12.5 %all-to-all-start.2 = ((bf16[8,16,1024]{2,1,0:T(8,128)(2,1)}), bf16[8,16,1024]{2,1,0:T(8,128)(2,1)S(1)}, u32[]{:S(2)}, u32[]{:S(2)}) async-start(bf16[8,16,1024]{2,1,0:T(8,128)(2,1)} %get-tuple-element.20), calls=%async_computation.2 | async-start | bytes 524288 | tf_op jit(solution)/shard_map/all_to_all | solution.py:362
  70.6 1.2 %collective-permute-start.1 = (f32[32,128]{1,0:T(8,128)S(1)}, f32[32,128]{1,0:T(8,128)S(1)}, u32[]{:S(2)}, u32[]{:S(2)}) collective-permute-start(f32[32,128]{1,0:T(8,128)S(1)} %project_output.1.mine), channel_id=1, source_target_pairs={{0,1},{1,0},{2,3},{3,2},{4,5},{5,4},{6,7},{7,6},{8,9},{9,8},{10,11... | collective-permute-start | bytes 49160 | tf_op jit(solution)/shard_map/ppermute | solution.py:374
  71.8 1.2 %copy-start.6 = (bf16[8,16,4096]{2,1,0:T(8,128)(2,1)S(1)}, bf16[8,16,4096]{2,1,0:T(8,128)(2,1)}, u32[]{:S(2)}) copy-start(bf16[8,16,4096]{2,1,0:T(8,128)(2,1)} %param.25) | copy-start | bytes 3145732

commit v4 on v3

--- a/solution.py
+++ b/solution.py
@@ -122,23 +122,26 @@
     rank,
     ids_hbm,
     slot_of_hbm,
+    lengths_hbm,
     x_hbm,
     place_of,
     row_at,
+    order,
     blocks,
     slot_at,
     ids,
     slot_of,
+    lengths,
     x_ref,
     sems,
 ):
-    pairs = ((ids_hbm, ids), (slot_of_hbm, slot_of), (x_hbm, x_ref))
+    pairs = ((ids_hbm, ids), (slot_of_hbm, slot_of), (lengths_hbm, lengths), (x_hbm, x_ref))
     copies = [pltpu.make_async_copy(a, b, sems.at[k]) for k, (a, b) in enumerate(pairs)]
     for copy in copies:
         copy.start()
     rows = x_ref.shape[1]
     wide = x_ref.shape[2] // heads
-    for copy in copies[:2]:
+    for copy in copies[:3]:
         copy.wait()
     for p in range(owners * CAP):
         row_at[p] = -1
@@ -151,9 +154,17 @@
         row_at[place] = r
         slot_at[place] = slot % adapt
         place_of[r] = place
+    sizes = [lengths[r] for r in range(rows)]
+    for r in range(rows):
+        ahead = jnp.int32(0)
+        for q in range(rows):
+            if q != r:
+                shorter = sizes[q] <= sizes[r] if q < r else sizes[q] < sizes[r]
+                ahead = ahead + jnp.where(shorter, 1, 0)
+        order[ahead] = r
     items = CAP * STEPS
     block = heads * items
-    copies[2].wait()
+    copies[3].wait()
     packed = exact(pack_matrix(row_at, owners, heads, rows, False), stacked(x_ref, heads, wide))
     at = iota((block, adapt * rank), 0)
     lane_slot = iota((block, adapt * rank), 1) // rank
@@ -164,9 +175,9 @@
         blocks[i, :, wide:] = one_hot(lane_slot == slot)
 
 
-def project_kernel(owners, heads, wide, first, a_ref, blocks, *refs):
+def project_kernel(owners, heads, wide, first, core, a_ref, blocks, *refs):
     if first:
-        after, part_ref, mask_ref = refs
+        part_ref, mask_ref = refs
     else:
         mask_in, part_ref = refs
     grouped = regroup_matrix(owners, heads)
@@ -183,7 +194,7 @@
     for c in range(heads):
         total = total + lax.dot_general(
             arrived[c * items : (c + 1) * items],
-            a_ref[:, c * wide : (c + 1) * wide],
+            a_ref[:, pl.ds(pl.multiple_of(core[0] * heads * wide + c * wide, wide), wide)],
             (((1,), (1,)), ((), ())),
             preferred_element_type=F32,
         )
@@ -206,7 +217,7 @@
 
 def quads(order, lengths, rows, sizes, action):
     def body(quad, carry):
-        longest = lengths[order[quad * QUAD]]
+        longest = lengths[order[quad * QUAD + QUAD - 1]]
         amount = (longest + CHUNK - 1) // CHUNK
         for size in range(1, sizes + 1):
 
@@ -217,40 +228,6 @@
         return carry
 
     lax.fori_loop(0, rows // QUAD, body, 0)
-
-
-def prefetch_kernel(after, lengths_hbm, k_hbm, v_hbm, order, k_out, v_out, lengths, k_sem, v_sem):
-    pltpu.sync_copy(lengths_hbm, lengths)
-    rows = k_hbm.shape[0]
-    sizes = [lengths[r] for r in range(rows)]
-    for r in range(rows):
-        ahead = jnp.int32(0)
-        for q in range(rows):
-            if q != r:
-                longer = sizes[q] >= sizes[r] if q < r else sizes[q] > sizes[r]
-                ahead = ahead + jnp.where(longer, 1, 0)
-        order[ahead] = r
-
-    def copies(row, size):
-        part = pl.ds(0, size * CHUNK)
-        return (
-            pltpu.make_async_copy(k_hbm.at[row, part], k_out.at[row, part], k_sem.at[row]),
-            pltpu.make_async_copy(v_hbm.at[row, part], v_out.at[row, part], v_sem.at[row]),
-        )
-
-    def begin(rows_in, size):
-        for row in rows_in:
-            for copy in copies(row, size):
-                copy.start()
-
-    def finish(rows_in, size):
-        for row in rows_in:
-            for copy in copies(row, size):
-                copy.wait()
-
-    chunks = k_hbm.shape[1] // CHUNK
-    quads(order, lengths, rows, chunks, begin)
-    quads(order, lengths, rows, chunks, finish)
 
 
 def attend_kernel(
@@ -263,15 +240,35 @@
     q_ref,
     kn_ref,
     vn_ref,
-    k_ref,
-    v_ref,
+    k_hbm,
+    v_hbm,
     blocks,
     out_ref,
     outgoing,
+    k_ref,
+    v_ref,
     q_buf,
     o_buf,
+    k_sem,
+    v_sem,
 ):
     rows = q_ref.shape[1]
+
+    def copies(row, size):
+        part = pl.ds(0, size * CHUNK)
+        return (
+            pltpu.make_async_copy(k_hbm.at[row, part], k_ref.at[row, part], k_sem.at[row]),
+            pltpu.make_async_copy(v_hbm.at[row, part], v_ref.at[row, part], v_sem.at[row]),
+        )
+
+    def begin(rows_in, size):
+        for row in rows_in:
+            for copy in copies(row, size):
+                copy.start()
+
+    chunks = k_hbm.shape[1] // CHUNK
+    quads(order, lengths, rows, chunks, begin)
+
     wide = q_ref.shape[2] // heads
     groups = wide // HD
     pairs = heads * STEPS
@@ -299,6 +296,9 @@
     contract = (((1,), (1,)), ((), ()))
 
     def attend(rows_in, size):
+        for row in rows_in:
+            for copy in copies(row, size):
+                copy.wait()
         extent = size * CHUNK
         position = iota((total, extent), 1)
         results = []
@@ -333,7 +333,7 @@
                 [own[j * pairs : (j + 1) * pairs] for j in range(groups)], axis=1
             )
 
-    quads(order, lengths, rows, k_ref.shape[1] // CHUNK, attend)
+    quads(order, lengths, rows, chunks, attend)
 
     mixed = o_buf[...].astype(BF16)
     packed = exact(pack_matrix(row_at, owners, heads, rows, True), mixed)
@@ -364,10 +364,6 @@
 
 def in_hbm(array):
     return pltpu.with_memory_space_constraint(array, pltpu.HBM)
-
-
-def in_vmem(array):
-    return pltpu.with_memory_space_constraint(array, pltpu.VMEM)
 
 
 def swap_cores(part):
@@ -398,64 +394,46 @@
     lanes = adapt * rank
     block = heads * CAP * STEPS
     items = owners * CAP * STEPS
-    core = lax.axis_index("tensor")
-
-    def half(a_store):
-        flat = jnp.transpose(a_store, (1, 2, 0)).reshape(lanes, a_store.shape[0])
-        return lax.dynamic_slice(flat, (0, core * width), (lanes, width))
+    core = lax.axis_index("tensor").astype(I32).reshape(1)
+
+    def flat(a_store):
+        return jnp.transpose(a_store, (1, 2, 0)).reshape(lanes, a_store.shape[0])
 
     shape = jax.ShapeDtypeStruct
     small = pltpu.CompilerParams(vmem_limit_bytes=16 * 1024 * 1024)
 
     sent = shape((owners, block, wide), BF16)
-    place_of, row_at, blocks = pl.pallas_call(
+    place_of, row_at, order, blocks = pl.pallas_call(
         functools.partial(dispatch_kernel, owners, heads, adapt, rank),
         out_shape=[
             shape((rows,), I32),
             shape((owners * CAP,), I32),
+            shape((rows,), I32),
             shape((owners, block, wide + lanes), BF16),
         ],
-        in_specs=[HBM] * 3,
-        out_specs=[SMEM] * 2 + [VMEM],
+        in_specs=[HBM] * 4,
+        out_specs=[SMEM] * 3 + [VMEM],
         scratch_shapes=[
             pltpu.SMEM((owners * CAP,), I32),
             pltpu.SMEM(adapter_ids.shape, I32),
             pltpu.SMEM(slot_of.shape, I32),
+            pltpu.SMEM(lengths.shape, I32),
             pltpu.VMEM(x_in.shape, BF16),
-            pltpu.SemaphoreType.DMA((3,)),
+            pltpu.SemaphoreType.DMA((4,)),
         ],
         compiler_params=small,
         name="dispatch",
-    )(in_hbm(adapter_ids), in_hbm(slot_of), in_hbm(x_in))
-
-    order, keys, values = pl.pallas_call(
-        prefetch_kernel,
-        out_shape=[
-            shape((rows,), I32),
-            pltpu.VMEM(cache_k.shape, BF16),
-            pltpu.VMEM(cache_v.shape, BF16),
-        ],
-        in_specs=[SMEM] + [HBM] * 3,
-        out_specs=[SMEM, VMEM, VMEM],
-        scratch_shapes=[
-            pltpu.SMEM(lengths.shape, I32),
-            pltpu.SemaphoreType.DMA((rows,)),
-            pltpu.SemaphoreType.DMA((rows,)),
-        ],
-        compiler_params=small,
-        cost_estimate=pl.CostEstimate(flops=0, bytes_accessed=8 * 1024 * 1024, transcendentals=0),
-        name="prefetch",
-    )(place_of, in_hbm(lengths), in_hbm(cache_k), in_hbm(cache_v))
+    )(in_hbm(adapter_ids), in_hbm(slot_of), in_hbm(lengths), in_hbm(x_in))
 
     arrived = exchange(blocks)
     part, mask = pl.pallas_call(
         functools.partial(project_kernel, owners, heads, wide, True),
         out_shape=[shape((items, lanes), F32)] * 2,
-        in_specs=[VMEM] * 2 + [SMEM],
+        in_specs=[SMEM] + [VMEM] * 2,
         out_specs=[VMEM] * 2,
         compiler_params=small,
         name="project_query",
-    )(half(a_query), arrived, order)
+    )(core, flat(a_query), arrived)
 
     def expand(part, b_store, name):
         return pl.pallas_call(
@@ -472,25 +450,29 @@
     attn_out, outgoing = pl.pallas_call(
         functools.partial(attend_kernel, owners, heads),
         out_shape=[shape((STEPS, rows, width), BF16), sent],
-        in_specs=[SMEM] * 4 + [VMEM] * 6,
+        in_specs=[SMEM] * 4 + [VMEM] * 3 + [HBM] * 2 + [VMEM],
         out_specs=[VMEM] * 2,
         scratch_shapes=[
+            pltpu.VMEM(cache_k.shape, BF16),
+            pltpu.VMEM(cache_v.shape, BF16),
             pltpu.VMEM((rows * STEPS * heads, wide), F32),
             pltpu.VMEM((rows * STEPS * heads, wide), F32),
+            pltpu.SemaphoreType.DMA((rows,)),
+            pltpu.SemaphoreType.DMA((rows,)),
         ],
-        compiler_params=pltpu.CompilerParams(vmem_limit_bytes=24 * 1024 * 1024),
+        compiler_params=pltpu.CompilerParams(vmem_limit_bytes=32 * 1024 * 1024),
         name="attend",
-    )(place_of, row_at, order, lengths, q_base, k_new, v_new, in_vmem(keys), in_vmem(values), returned)
+    )(place_of, row_at, order, lengths, q_base, k_new, v_new, in_hbm(cache_k), in_hbm(cache_v), returned)
 
     arrived = exchange(outgoing)
     part = pl.pallas_call(
         functools.partial(project_kernel, owners, heads, wide, False),
         out_shape=shape((items, lanes), F32),
-        in_specs=[VMEM] * 3,
+        in_specs=[SMEM] + [VMEM] * 3,
         out_specs=VMEM,
         compiler_params=small,
         name="project_output",
-    )(half(a_output), arrived, mask)
+    )(core, flat(a_output), arrived, mask)
     returned = exchange(expand(part, b_output, "expand_output"))
     adapter_out = pl.pallas_call(
         functools.partial(collect_kernel, owners, heads),

time: 88.3 us -> 79.5 us (0.900)
  local copies, waits for them, and re-layouts: 18 us -> 5.94 us
  blocking collectives: 28 us -> 36.9 us
  Pallas kernels: 20 us -> 15.9 us
  starting transfers between devices: 11.2 us -> 7.3 us
  waiting for transfers between devices: 9.67 us -> 12 us
    unnamed x22 -> x16, local copies, waits for them, and re-layouts: 16.6 us -> 5.94 us
    all_to_all x2 -> x3, blocking collectives: 28 us -> 36.9 us  [exchange(): lax.all_to_all(blocks, 'store', split_axis=0, concat_axis=0, tiled=True)]
    pallas_call x1 -> x0, Pallas kernels: 5.58 us -> none  [shards(): pl.pallas_call(prefetch_kernel, out_shape=[shape((rows,), I32), pltpu.VME...]
    all_to_all x2 -> x1, starting transfers between devices: 11.2 us -> 7.3 us  [exchange(): lax.all_to_all(blocks, 'store', split_axis=0, concat_axis=0, tiled=True)]
    all_to_all x2 -> x1, waiting for transfers between devices: 7.27 us -> 9.61 us  [exchange(): lax.all_to_all(blocks, 'store', split_axis=0, concat_axis=0, tiled=True)]
    pallas_call x1, Pallas kernels: 8.23 us -> 10.2 us  [shards(): pl.pallas_call(functools.partial(attend_kernel, owners, heads), out_shape...]
    dynamic_slice x2 -> x0, local copies, waits for them, and re-layouts: 1.36 us -> none  [half(): return lax.dynamic_slice(flat, (0, core * width), (lanes, width))]
  transfers between devices with their start and end apart: 4 -> 3, of which waited for: 3 -> 3; matrix products, arithmetic and copies ran while one was open for 2% -> 0% of each run, Pallas kernels for 6% -> 0%
where the time goes in v4:
time: 79.5 us; the launch traced here: 78.8 us
  blocking collectives  36.9 us (46%)
  Pallas kernels  15.9 us (20%)
  waiting for transfers between devices  12 us (15%)
  starting transfers between devices  7.3 us (9%)
  local copies, waits for them, and re-layouts  5.94 us (7%)
    all_to_all x3, blocking collectives, exchange(): lax.all_to_all(blocks, 'store', split_axis=0, concat_axis=0, tiled=True)  36.9 us
    pallas_call x1, Pallas kernels, shards(): pl.pallas_call(functools.partial(attend_kernel, owners, heads), out_shape...  10.2 us
    all_to_all x1, waiting for transfers between devices, exchange(): lax.all_to_all(blocks, 'store', split_axis=0, concat_axis=0, tiled=True)  9.61 us
    all_to_all x1, starting transfers between devices, exchange(): lax.all_to_all(blocks, 'store', split_axis=0, concat_axis=0, tiled=True)  7.3 us
    unnamed x16, local copies, waits for them, and re-layouts  5.94 us
    ppermute x2, waiting for transfers between devices, swap_cores(): return lax.ppermute(part, 'tensor', [(0, 1), (1, 0)])  2.4 us
    pallas_call x1, Pallas kernels, shards(): pl.pallas_call(functools.partial(dispatch_kernel, owners, heads, adapt, r...  2.1 us
  transfers between devices with their start and end apart: 3, of which 3 were waited for; matrix products, arithmetic and copies ran while one was open for 0% of the time, Pallas kernels for 0%

profile of v4, /device:TPU:0, one launch (start us, length us, event | category | flops | bytes accessed | tf_op | source)
XLA Modules:
  0.0 78.8 jit_solution(1060820427327789227)
XLA Ops:
  0.6 2.1 %dispatch.1 = (s32[16]{0:T(128)S(1)}, s32[16]{0:T(128)S(1)}, s32[16]{0:T(128)S(1)}, bf16[8,16,1152]{2,1,0:T(8,128)(2,1)}) custom-call(s32[16]{0:T(128)} %ids_hbm.1, s32[64]{0:T(128)} %slot_of_hbm.1, s32[16]{0:T(128)} %lengths.1, bf16[2,16,4096]{2,1,0:T(8,128)(2,1)} %x_hbm.1), custom_call_target="tpu_custom_call" | custom-call | tf_op jit(solution)/shard_map/dispatch/pallas_call | solution.py:406
  2.7 7.3 %all-to-all-start = ((bf16[8,16,1152]{2,1,0:T(8,128)(2,1)}), bf16[8,16,1152]{2,1,0:T(8,128)(2,1)S(1)}, u32[]{:S(2)}, u32[]{:S(2)}) async-start(bf16[8,16,1152]{2,1,0:T(8,128)(2,1)} %get-tuple-element.13), calls=%async_computation | async-start | bytes 589824 | tf_op jit(solution)/shard_map/all_to_all | solution.py:362
  10.0 9.6 %all-to-all-done.blocks = bf16[8,16,1152]{2,1,0:T(8,128)(2,1)S(1)} async-done(((bf16[8,16,1152]{2,1,0:T(8,128)(2,1)}), bf16[8,16,1152]{2,1,0:T(8,128)(2,1)S(1)}, u32[]{:S(2)}, u32[]{:S(2)}) %all-to-all-start) | async-done | bytes 294944 | tf_op jit(solution)/shard_map/all_to_all | solution.py:362
  19.6 0.0 copy-start
  19.6 1.6 %copy-done = bf16[8192,8,16]{0,2,1:T(8,128)(2,1)S(1)} copy-done((bf16[8192,8,16]{0,2,1:T(8,128)(2,1)S(1)}, bf16[8192,8,16]{0,2,1:T(8,128)(2,1)}, u32[]{:S(2)}) %copy-start) | copy-done | bytes 2097176
  21.2 0.6 project_query.1
  21.8 0.0 collective-permute-start
  21.8 1.2 %collective-permute-done.other = f32[32,128]{1,0:T(8,128)S(1)} collective-permute-done((f32[32,128]{1,0:T(8,128)S(1)}, f32[32,128]{1,0:T(8,128)S(1)}, u32[]{:S(2)}, u32[]{:S(2)}) %collective-permute-start) | collective-permute-done | bytes 16416 | tf_op jit(solution)/shard_map/ppermute | solution.py:370
  23.1 0.0 copy-start.2
  23.1 1.2 %copy-done.2 = bf16[8,16,4096]{2,1,0:T(8,128)(2,1)S(1)} copy-done((bf16[8,16,4096]{2,1,0:T(8,128)(2,1)S(1)}, bf16[8,16,4096]{2,1,0:T(8,128)(2,1)}, u32[]{:S(2)}) %copy-start.2) | copy-done | bytes 1048600
  24.3 0.4 expand_query.1
  24.7 12.6 %all_to_all.20.blocks = bf16[8,16,1024]{2,1,0:T(8,128)(2,1)S(1)} all-to-all(bf16[8,16,1024]{2,1,0:T(8,128)(2,1)S(1)} %expand_query.1), channel_id=1, replica_groups=mesh['parts'=2,'store'=8,'tensor'=2] {'store'}, dimensions={0} | all-to-all | bytes 524288 | tf_op jit(solution)/shard_map/all_to_all | solution.py:362
  37.4 0.0 copy-start.4
  37.4 0.9 %copy-done.4 = bf16[2,16,4096]{2,1,0:T(8,128)(2,1)S(1)} copy-done((bf16[2,16,4096]{2,1,0:T(8,128)(2,1)S(1)}, bf16[2,16,4096]{2,1,0:T(8,128)(2,1)}, u32[]{:S(2)}) %copy-start.4) | copy-done | bytes 262168
  38.3 0.0 copy-start.5
  38.3 0.8 copy-done.5
  39.1 0.0 copy-start.6
  39.1 0.8 copy-done.6
  39.8 0.0 copy-start.7
  39.8 0.7 copy-done.7
  40.5 0.0 copy-start.1
  40.5 0.0 copy-start.3
  40.5 10.2 %attend.1 = (bf16[2,16,4096]{2,1,0:T(8,128)(2,1)}, bf16[8,16,1024]{2,1,0:T(8,128)(2,1)S(1)}) custom-call(s32[16]{0:T(128)S(1)} %get-tuple-element.10.place_of, s32[16]{0:T(128)S(1)} %get-tuple-element.11.row_at, s32[16]{0:T(128)S(1)} %get-tuple-element.12.order, s32[16]{0:T(128)S(1)} %copy-done.7, bf16[2,16,4096]{2,1,0:T(8,128)(2,1)S(1)} %copy-done.4, ...), custom_call_target="tpu_custom_call" | custom-call | tf_op jit(solution)/shard_map/attend/pallas_call | solution.py:450
  50.7 11.6 %all_to_all.21.blocks = bf16[8,16,1024]{2,1,0:T(8,128)(2,1)S(1)} all-to-all(bf16[8,16,1024]{2,1,0:T(8,128)(2,1)S(1)} %get-tuple-element.16), channel_id=1, replica_groups=mesh['parts'=2,'store'=8,'tensor'=2] {'store'}, dimensions={0} | all-to-all | bytes 524288 | tf_op jit(solution)/shard_map/all_to_all | solution.py:362
  62.3 0.0 copy-done.1
  62.3 0.6 project_output.1.mine
  62.9 0.0 collective-permute-start.1
  62.9 1.2 %collective-permute-done.1.other = f32[32,128]{1,0:T(8,128)S(1)} collective-permute-done((f32[32,128]{1,0:T(8,128)S(1)}, f32[32,128]{1,0:T(8,128)S(1)}, u32[]{:S(2)}, u32[]{:S(2)}) %collective-permute-start.1) | collective-permute-done | bytes 16416 | tf_op jit(solution)/shard_map/ppermute | solution.py:370
  64.1 0.0 copy-done.3
  64.1 0.5 expand_output.1
  64.6 12.6 %all_to_all.22.blocks = bf16[8,16,1024]{2,1,0:T(8,128)(2,1)S(1)} all-to-all(bf16[8,16,1024]{2,1,0:T(8,128)(2,1)S(1)} %expand_output.1), channel_id=1, replica_groups=mesh['parts'=2,'store'=8,'tensor'=2] {'store'}, dimensions={0} | all-to-all | bytes 524288 | tf_op jit(solution)/shard_map/all_to_all | solution.py:362
  77.2 1.5 %collect.1 = bf16[2,16,4096]{2,1,0:T(8,128)(2,1)} custom-call(s32[16]{0:T(128)S(1)} %get-tuple-element.10.place_of, bf16[8,16,1024]{2,1,0:T(8,128)(2,1)S(1)} %all_to_all.22.blocks), custom_call_target="tpu_custom_call" | custom-call | tf_op jit(solution)/shard_map/collect/pallas_call | solution.py:477
Async XLA Ops:
  2.7 16.9 %all-to-all-start = ((bf16[8,16,1152]{2,1,0:T(8,128)(2,1)}), bf16[8,16,1152]{2,1,0:T(8,128)(2,1)S(1)}, u32[]{:S(2)}, u32[]{:S(2)}) async-start(bf16[8,16,1152]{2,1,0:T(8,128)(2,1)} %get-tuple-element.13), calls=%async_computation | async-start | bytes 589824 | tf_op jit(solution)/shard_map/all_to_all | solution.py:362
  19.6 1.6 %copy-start = (bf16[8192,8,16]{0,2,1:T(8,128)(2,1)S(1)}, bf16[8192,8,16]{0,2,1:T(8,128)(2,1)}, u32[]{:S(2)}) copy-start(bf16[8192,8,16]{0,2,1:T(8,128)(2,1)} %param.22) | copy-start | bytes 6291460
  21.8 1.2 %collective-permute-start = (f32[32,128]{1,0:T(8,128)S(1)}, f32[32,128]{1,0:T(8,128)S(1)}, u32[]{:S(2)}, u32[]{:S(2)}) collective-permute-start(f32[32,128]{1,0:T(8,128)S(1)} %get-tuple-element.14.mine), channel_id=1, source_target_pairs={{0,1},{1,0},{2,3},{3,2},{4,5},{5,4},{6,7},{7,6},{8,9},{9,8},{10,11... | collective-permute-start | bytes 49160 | tf_op jit(solution)/shard_map/ppermute | solution.py:370
  23.1 1.2 %copy-start.2 = (bf16[8,16,4096]{2,1,0:T(8,128)(2,1)S(1)}, bf16[8,16,4096]{2,1,0:T(8,128)(2,1)}, u32[]{:S(2)}) copy-start(bf16[8,16,4096]{2,1,0:T(8,128)(2,1)} %param.23) | copy-start | bytes 3145732
  37.4 1.0 %copy-start.4 = (bf16[2,16,4096]{2,1,0:T(8,128)(2,1)S(1)}, bf16[2,16,4096]{2,1,0:T(8,128)(2,1)}, u32[]{:S(2)}) copy-start(bf16[2,16,4096]{2,1,0:T(8,128)(2,1)} %q_ref.1) | copy-start | bytes 786436
  38.3 0.8 copy-start.5
  39.1 0.8 copy-start.6
  39.8 0.7 copy-start.7
  40.5 21.8 %copy-start.1 = (bf16[8192,8,16]{0,2,1:T(8,128)(2,1)S(1)}, bf16[8192,8,16]{0,2,1:T(8,128)(2,1)}, u32[]{:S(2)}) copy-start(bf16[8192,8,16]{0,2,1:T(8,128)(2,1)} %param.24) | copy-start | bytes 6291460
  40.5 23.6 %copy-start.3 = (bf16[8,16,4096]{2,1,0:T(8,128)(2,1)S(1)}, bf16[8,16,4096]{2,1,0:T(8,128)(2,1)}, u32[]{:S(2)}) copy-start(bf16[8,16,4096]{2,1,0:T(8,128)(2,1)} %param.25) | copy-start | bytes 3145732
  62.9 1.2 %collective-permute-start.1 = (f32[32,128]{1,0:T(8,128)S(1)}, f32[32,128]{1,0:T(8,128)S(1)}, u32[]{:S(2)}, u32[]{:S(2)}) collective-permute-start(f32[32,128]{1,0:T(8,128)S(1)} %project_output.1.mine), channel_id=1, source_target_pairs={{0,1},{1,0},{2,3},{3,2},{4,5},{5,4},{6,7},{7,6},{8,9},{9,8},{10,11... | collective-permute-start | bytes 49160 | tf_op jit(solution)/shard_map/ppermute | solution.py:370

commit v5 on v4

v5 whole, which is shorter than its diff:
```python
import functools
import math

import jax
import jax.numpy as jnp
from jax import lax
from jax.experimental import pallas as pl
from jax.experimental.pallas import tpu as pltpu
from jax.sharding import PartitionSpec as P

HD = 128
CAP = 2
STEPS = 2
CHUNK = 128
QUAD = 4
BF16 = jnp.bfloat16
F32 = jnp.float32
I32 = jnp.int32
VMEM = pl.BlockSpec(memory_space=pltpu.VMEM)
SMEM = pl.BlockSpec(memory_space=pltpu.SMEM)
HBM = pl.BlockSpec(memory_space=pltpu.HBM)


def iota(shape, dim):
    return lax.broadcasted_iota(I32, shape, dim)


def over(x, n):
    return lax.shift_right_logical(x, jnp.full_like(x, n.bit_length() - 1)) if n & (n - 1) == 0 else x // n


def rest(x, n):
    return x & (n - 1) if n & (n - 1) == 0 else x % n


def one_hot(hits):
    return jnp.where(hits, 1.0, 0.0).astype(BF16)


def stacked(ref, heads, wide):
    return jnp.concatenate(
        [ref[s, :, c * wide : (c + 1) * wide] for c in range(heads) for s in range(STEPS)], axis=0
    )


def pack_matrix(meta, owners, heads, rows, by_row):
    items = CAP * STEPS
    block = heads * items
    shape = (block, heads * STEPS * rows)
    at = iota(shape, 0)
    col = iota(shape, 1)
    head_step = over(at, items) * STEPS + rest(at, STEPS)
    offset = col - (head_step if by_row else head_step * rows)
    factor = heads * STEPS if by_row else 1
    first = rest(over(at, STEPS), CAP) == 0
    if not by_row:
        offset = jnp.where((offset >= 0) & (offset < rows), offset, -1)
    parts = []
    for i in range(owners):
        here = [meta[rows + i * CAP + k] for k in range(CAP)]
        spots = [jnp.where(h >= 0, h * factor, -rows * factor * heads * STEPS * 2) for h in here]
        parts.append(one_hot(offset == jnp.where(first, spots[0], spots[1])))
    return jnp.concatenate(parts, axis=0)


def unpack_matrix(meta, owners, heads, rows, by_row):
    items = CAP * STEPS
    block = heads * items
    pairs = heads * STEPS
    spots = [over(meta[r], CAP) * block + rest(meta[r], CAP) * STEPS for r in range(rows)]
    if by_row:
        shape = (pairs, owners * block)
        at = iota(shape, 0)
        col = iota(shape, 1) - (over(at, STEPS) * items + rest(at, STEPS))
        return jnp.concatenate([one_hot(col == spots[r]) for r in range(rows)], axis=0)
    shape = (rows, owners * block)
    at = iota(shape, 0)
    col = iota(shape, 1)
    spot = jnp.zeros(shape, I32)
    for r in range(rows):
        spot = jnp.where(at == r, spots[r], spot)
    offset = col - spot
    return jnp.concatenate(
        [one_hot(offset == c * items + s) for c in range(heads) for s in range(STEPS)], axis=0
    )


def by_row_matrix(heads, rows):
    pairs = heads * STEPS
    shape = (pairs * rows, pairs * rows)
    at = iota(shape, 0)
    return one_hot(iota(shape, 1) == rest(at, pairs) * rows + over(at, pairs))


def by_pair_matrix(heads, rows):
    pairs = heads * STEPS
    shape = (pairs * rows, pairs * rows)
    at = iota(shape, 0)
    return one_hot(iota(shape, 1) == rest(at, rows) * pairs + over(at, rows))


def regroup_matrix(owners, heads):
    items = CAP * STEPS
    total = owners * heads * items
    at = iota((total, total), 0)
    head = over(at, owners * items)
    owner = rest(over(at, items), owners)
    return one_hot(
        iota((total, total), 1) == owner * (heads * items) + head * items + rest(at, items)
    )


def ungroup_matrix(owners, heads):
    items = CAP * STEPS
    total = owners * heads * items
    at = iota((total, total), 0)
    owner = over(at, heads * items)
    head = rest(over(at, items), heads)
    return one_hot(
        iota((total, total), 1) == head * (owners * items) + owner * items + rest(at, items)
    )


def exact(matrix, values):
    return jnp.dot(matrix, values, preferred_element_type=F32).astype(BF16)


def dispatch_kernel(
    owners,
    heads,
    adapt,
    rank,
    ids_hbm,
    slot_of_hbm,
    lengths_hbm,
    x_hbm,
    meta,
    blocks,
    slot_at,
    ids,
    slot_of,
    lengths,
    x_ref,
    sems,
):
    pairs = ((ids_hbm, ids), (slot_of_hbm, slot_of), (lengths_hbm, lengths), (x_hbm, x_ref))
    copies = [pltpu.make_async_copy(a, b, sems.at[k]) for k, (a, b) in enumerate(pairs)]
    for copy in copies:
        copy.start()
    rows = x_ref.shape[1]
    wide = x_ref.shape[2] // heads
    for copy in copies[:3]:
        copy.wait()
    row_at = rows
    order = rows + owners * CAP
    spans = order + rows
    for p in range(owners * CAP):
        meta[row_at + p] = -1
        slot_at[p] = -1
    for r in range(rows):
        slot = slot_of[ids[r]]
        first = over(slot, adapt) * CAP
        place = first + jnp.where(meta[row_at + first] >= 0, 1, 0)
        meta[row_at + place] = r
        slot_at[place] = rest(slot, adapt)
        meta[r] = place
    sizes = [lengths[r] for r in range(rows)]
    for r in range(rows):
        ahead = jnp.int32(0)
        for q in range(rows):
            if q != r:
                shorter = sizes[q] <= sizes[r] if q < r else sizes[q] < sizes[r]
                ahead = ahead + jnp.where(shorter, 1, 0)
        meta[order + ahead] = r
        meta[spans + r] = sizes[r]
    items = CAP * STEPS
    block = heads * items
    copies[3].wait()
    packed = exact(pack_matrix(meta, owners, heads, rows, False), stacked(x_ref, heads, wide))
    at = iota((block, adapt * rank), 0)
    lane_slot = over(iota((block, adapt * rank), 1), rank)
    first = rest(over(at, STEPS), CAP) == 0
    for i in range(owners):
        blocks[i, :, :wide] = packed[i * block : (i + 1) * block]
        slot = jnp.where(first, slot_at[i * CAP], slot_at[i * CAP + 1])
        blocks[i, :, wide:] = one_hot(lane_slot == slot)


def project_kernel(owners, heads, wide, first, a_ref, blocks, *refs):
    core = lax.axis_index("tensor")
    if first:
        part_ref, mask_ref = refs
    else:
        mask_in, part_ref = refs
    grouped = regroup_matrix(owners, heads)
    items = owners * CAP * STEPS
    arrived = jnp.concatenate([blocks[i, :, :wide] for i in range(owners)], axis=0)
    arrived = exact(grouped, arrived)
    if first:
        masks = jnp.concatenate([blocks[i, :, wide:] for i in range(owners)], axis=0)
        mask = jnp.dot(grouped[:items], masks, preferred_element_type=F32)
        mask_ref[...] = mask
    else:
        mask = mask_in[...]
    total = jnp.zeros(mask.shape, F32)
    for c in range(heads):
        total = total + lax.dot_general(
            arrived[c * items : (c + 1) * items],
            a_ref[:, pl.ds(pl.multiple_of(core * (heads * wide) + c * wide, wide), wide)],
            (((1,), (1,)), ((), ())),
            preferred_element_type=F32,
        )
    part_ref[...] = total * mask


def expand_kernel(owners, heads, wide, mine, other, b_ref, blocks):
    low_rank = (mine[...] + other[...]).astype(BF16)
    pieces = []
    for c in range(heads):
        product = jnp.dot(
            low_rank, b_ref[:, c * wide : (c + 1) * wide], preferred_element_type=F32
        )
        pieces.append((2.0 * product).astype(BF16))
    back = exact(ungroup_matrix(owners, heads), jnp.concatenate(pieces, axis=0))
    block = heads * CAP * STEPS
    for i in range(owners):
        blocks[i] = back[i * block : (i + 1) * block]


def quads(row_of, span_of, rows, sizes, action):
    def body(quad, carry):
        amount = over(span_of(row_of(quad * QUAD + QUAD - 1)) + (CHUNK - 1), CHUNK)
        for size in range(1, sizes + 1):

            @pl.when(amount == size)
            def _():
                action([row_of(quad * QUAD + j) for j in range(QUAD)], size)

        return carry

    lax.fori_loop(0, rows // QUAD, body, 0)


def attend_kernel(
    owners,
    heads,
    meta,
    q_hbm,
    kn_hbm,
    vn_hbm,
    k_hbm,
    v_hbm,
    blocks,
    out_ref,
    outgoing,
    q_ref,
    kn_ref,
    vn_ref,
    k_ref,
    v_ref,
    mask_ref,
    q_buf,
    o_buf,
    k_sem,
    v_sem,
    sems,
):
    rows = q_hbm.shape[1]
    wide = q_hbm.shape[2] // heads
    groups = wide // HD
    pairs = heads * STEPS
    total = groups * pairs
    width = heads * HD
    fresh_rows = STEPS * rows

    singles = [pltpu.make_async_copy(q_hbm, q_ref, sems.at[0])]
    for k, (source, target) in enumerate(((kn_hbm, kn_ref), (vn_hbm, vn_ref))):
        for t in range(STEPS):
            part = target.at[pl.ds(t * rows, rows)]
            singles.append(pltpu.make_async_copy(source.at[t], part, sems.at[1 + k * STEPS + t]))
    for copy in singles:
        copy.start()

    def row_of(place):
        return meta[rows + owners * CAP + place]

    def span_of(row):
        return meta[2 * rows + owners * CAP + row]

    def copies(row, size):
        part = pl.ds(0, size * CHUNK)
        return (
            pltpu.make_async_copy(k_hbm.at[row, part], k_ref.at[row, part], k_sem.at[row]),
            pltpu.make_async_copy(v_hbm.at[row, part], v_ref.at[row, part], v_sem.at[row]),
        )

    def begin(rows_in, size):
        for row in rows_in:
            for copy in copies(row, size):
                copy.start()

    chunks = k_hbm.shape[1] // CHUNK
    quads(row_of, span_of, rows, chunks, begin)

    head_at = rest(over(iota((total, width), 0), STEPS), heads)
    mask_ref[...] = one_hot(head_at == over(iota((total, width), 1), HD))
    head_own = rest(over(iota((total, HD), 0), STEPS), heads)
    blank = jnp.zeros((CHUNK - fresh_rows, width), BF16)
    kn_ref[fresh_rows:, :] = blank
    vn_ref[fresh_rows:, :] = blank

    delta = jnp.dot(
        unpack_matrix(meta, owners, heads, rows, True),
        jnp.concatenate([blocks[i] for i in range(owners)], axis=0),
        preferred_element_type=F32,
    )
    by_row = by_row_matrix(heads, rows)
    for copy in singles:
        copy.wait()
    base = jnp.dot(by_row, stacked(q_ref, heads, wide), preferred_element_type=F32)
    q_buf[...] = base + delta

    factor = math.log2(math.e) / math.sqrt(HD)
    fresh_shape = (total, CHUNK)
    fresh_at = iota(fresh_shape, 1)
    fresh_step = over(fresh_at, rows)
    fresh_row = jnp.where(fresh_step <= rest(iota(fresh_shape, 0), STEPS), rest(fresh_at, rows), rows)
    contract = (((1,), (1,)), ((), ()))

    def attend(rows_in, size):
        for row in rows_in:
            for copy in copies(row, size):
                copy.wait()
        extent = size * CHUNK
        position = iota((total, extent), 1)
        results = []
        for row in rows_in:
            start = pl.multiple_of(row * pairs, pairs)
            flat = q_buf[pl.ds(start, pairs), :]
            one = jnp.concatenate(
                [flat[:, j * HD : (j + 1) * HD] for j in range(groups)], axis=0
            ).astype(BF16)
            spread = jnp.concatenate([one] * heads, axis=1) * mask_ref[...]
            cached = lax.dot_general(
                spread, k_ref[row, :extent, :], contract, preferred_element_type=F32
            )
            cached = jnp.where(position < span_of(row), cached, -jnp.inf)
            fresh = lax.dot_general(spread, kn_ref[...], contract, preferred_element_type=F32)
            fresh = jnp.where(fresh_row == row, fresh, -jnp.inf)
            scores = jnp.concatenate([cached, fresh], axis=1)
            top = jnp.max(scores, axis=1, keepdims=True)
            weights = jnp.exp2((scores - top) * factor)
            norm = jnp.sum(weights, axis=1, keepdims=True)
            weights = weights.astype(BF16)
            mixed = jnp.dot(
                weights[:, :extent], v_ref[row, :extent, :], preferred_element_type=F32
            ) + jnp.dot(weights[:, extent:], vn_ref[...], preferred_element_type=F32)
            own = mixed[:, :HD]
            for c in range(1, heads):
                own = jnp.where(head_own == c, mixed[:, c * HD : (c + 1) * HD], own)
            results.append((start, own * (1.0 / norm)))
        for start, own in results:
            o_buf[pl.ds(start, pairs), :] = jnp.concatenate(
                [own[j * pairs : (j + 1) * pairs] for j in range(groups)], axis=1
            )

    quads(row_of, span_of, rows, chunks, attend)

    mixed = o_buf[...].astype(BF16)
    packed = exact(pack_matrix(meta, owners, heads, rows, True), mixed)
    block = heads * CAP * STEPS
    for i in range(owners):
        outgoing[i] = packed[i * block : (i + 1) * block]
    final = exact(by_pair_matrix(heads, rows), mixed)
    for c in range(heads):
        for s in range(STEPS):
            at = (c * STEPS + s) * rows
            out_ref[s, :, c * wide : (c + 1) * wide] = final[at : at + rows]


def collect_kernel(owners, heads, meta, blocks, out_ref):
    rows = out_ref.shape[1]
    wide = out_ref.shape[2] // heads
    arrived = jnp.concatenate([blocks[i] for i in range(owners)], axis=0)
    values = exact(unpack_matrix(meta, owners, heads, rows, False), arrived)
    for c in range(heads):
        for s in range(STEPS):
            top = (c * STEPS + s) * rows
            out_ref[s, :, c * wide : (c + 1) * wide] = values[top : top + rows]


def exchange(blocks):
    return lax.all_to_all(blocks, "store", split_axis=0, concat_axis=0, tiled=True)


def in_hbm(array):
    return pltpu.with_memory_space_constraint(array, pltpu.HBM)


def swap_cores(part):
    return lax.ppermute(part, "tensor", [(0, 1), (1, 0)])


def shards(
    x_in,
    q_base,
    k_new,
    v_new,
    cache_k,
    cache_v,
    lengths,
    adapter_ids,
    slot_of,
    a_query,
    b_query,
    a_output,
    b_output,
):
    owners = lax.axis_size("store")
    rows = x_in.shape[1]
    width = x_in.shape[2]
    heads = cache_k.shape[2] // HD
    wide = width // heads
    adapt, rank = a_query.shape[1:]
    lanes = adapt * rank
    block = heads * CAP * STEPS
    items = owners * CAP * STEPS
    def flat(a_store):
        return jnp.transpose(a_store, (1, 2, 0)).reshape(lanes, a_store.shape[0])

    shape = jax.ShapeDtypeStruct
    small = pltpu.CompilerParams(vmem_limit_bytes=16 * 1024 * 1024)

    sent = shape((owners, block, wide), BF16)
    meta, blocks = pl.pallas_call(
        functools.partial(dispatch_kernel, owners, heads, adapt, rank),
        out_shape=[
            shape((3 * rows + owners * CAP,), I32),
            shape((owners, block, wide + lanes), BF16),
        ],
        in_specs=[HBM] * 4,
        out_specs=[SMEM, VMEM],
        scratch_shapes=[
            pltpu.SMEM((owners * CAP,), I32),
            pltpu.SMEM(adapter_ids.shape, I32),
            pltpu.SMEM(slot_of.shape, I32),
            pltpu.SMEM(lengths.shape, I32),
            pltpu.VMEM(x_in.shape, BF16),
            pltpu.SemaphoreType.DMA((4,)),
        ],
        compiler_params=small,
        name="dispatch",
    )(in_hbm(adapter_ids), in_hbm(slot_of), in_hbm(lengths), in_hbm(x_in))

    arrived = exchange(blocks)
    part, mask = pl.pallas_call(
        functools.partial(project_kernel, owners, heads, wide, True),
        out_shape=[shape((items, lanes), F32)] * 2,
        in_specs=[VMEM] * 2,
        out_specs=[VMEM] * 2,
        compiler_params=small,
        name="project_query",
    )(flat(a_query), arrived)

    def expand(part, b_store, name):
        return pl.pallas_call(
            functools.partial(expand_kernel, owners, heads, wide),
            out_shape=sent,
            in_specs=[VMEM] * 3,
            out_specs=VMEM,
            compiler_params=small,
            name=name,
        )(part, swap_cores(part), b_store.reshape(lanes, width))

    returned = exchange(expand(part, b_query, "expand_query"))

    attn_out, outgoing = pl.pallas_call(
        functools.partial(attend_kernel, owners, heads),
        out_shape=[pltpu.VMEM((STEPS, rows, width), BF16), sent],
        in_specs=[SMEM] + [HBM] * 5 + [VMEM],
        out_specs=[VMEM] * 2,
        scratch_shapes=[
            pltpu.VMEM(q_base.shape, BF16),
            pltpu.VMEM((CHUNK, heads * HD), BF16),
            pltpu.VMEM((CHUNK, heads * HD), BF16),
            pltpu.VMEM(cache_k.shape, BF16),
            pltpu.VMEM(cache_v.shape, BF16),
            pltpu.VMEM((STEPS * wide // HD * heads, heads * HD), BF16),
            pltpu.VMEM((rows * STEPS * heads, wide), F32),
            pltpu.VMEM((rows * STEPS * heads, wide), F32),
            pltpu.SemaphoreType.DMA((rows,)),
            pltpu.SemaphoreType.DMA((rows,)),
            pltpu.SemaphoreType.DMA((1 + 2 * STEPS,)),
        ],
        compiler_params=pltpu.CompilerParams(vmem_limit_bytes=32 * 1024 * 1024),
        name="attend",
    )(meta, *map(in_hbm, (q_base, k_new, v_new, cache_k, cache_v)), returned)

    arrived = exchange(outgoing)
    part = pl.pallas_call(
        functools.partial(project_kernel, owners, heads, wide, False),
        out_shape=shape((items, lanes), F32),
        in_specs=[VMEM] * 3,
        out_specs=VMEM,
        compiler_params=small,
        name="project_output",
    )(flat(a_output), arrived, mask)
    returned = exchange(expand(part, b_output, "expand_output"))
    adapter_out = pl.pallas_call(
        functools.partial(collect_kernel, owners, heads),
        out_shape=shape((STEPS, rows, width), BF16),
        in_specs=[SMEM, VMEM],
        out_specs=VMEM,
        compiler_params=small,
        name="collect",
    )(meta, returned)
    return (attn_out, adapter_out)


def solution(mesh):
    in_specs = (
        P(None, ("parts", "store"), "tensor"),
        P(None, ("parts", "store"), "tensor"),
        P(None, ("parts", "store"), "tensor"),
        P(None, ("parts", "store"), "tensor"),
        P(("parts", "store"), None, "tensor"),
        P(("parts", "store"), None, "tensor"),
        P(("parts", "store")),
        P(("parts", "store")),
        P("parts"),
        P(None, "store", None),
        P("store", None, "tensor"),
        P(None, "store", None),
        P("store", None, "tensor"),
    )
    out_specs = (P(None, ("parts", "store"), "tensor"), P(None, ("parts", "store"), "tensor"))
    return jax.shard_map(shards, mesh=mesh, in_specs=in_specs, out_specs=out_specs, check_vma=False)
```

time: 79.5 us -> 76.2 us (0.958)
  blocking collectives: 36.9 us -> 40.9 us
  starting transfers between devices: 7.3 us -> 3.59 us
  local copies, waits for them, and re-layouts: 5.94 us -> 3.53 us
  waiting for transfers between devices: 12 us -> 11 us
    all_to_all x3, blocking collectives: 36.9 us -> 40.9 us  [exchange(): lax.all_to_all(blocks, 'store', split_axis=0, concat_axis=0, tiled=True)]
    all_to_all x1, starting transfers between devices: 7.3 us -> 3.59 us  [exchange(): lax.all_to_all(blocks, 'store', split_axis=0, concat_axis=0, tiled=True)]
    unnamed x16 -> x9, local copies, waits for them, and re-layouts: 5.94 us -> 3.53 us
    all_to_all x1, waiting for transfers between devices: 9.61 us -> 8.59 us  [exchange(): lax.all_to_all(blocks, 'store', split_axis=0, concat_axis=0, tiled=True)]
  transfers between devices with their start and end apart: 3 -> 3, of which waited for: 3 -> 3; matrix products, arithmetic and copies ran while one was open for 0% -> 1% of each run, Pallas kernels for 0% -> 0%
where the time goes in v5:
time: 76.2 us; the launch traced here: 75.4 us
  blocking collectives  40.9 us (54%)
  Pallas kernels  15.7 us (21%)
  waiting for transfers between devices  11 us (14%)
  starting transfers between devices  3.59 us (5%)
  local copies, waits for them, and re-layouts  3.53 us (5%)
    all_to_all x3, blocking collectives, exchange(): lax.all_to_all(blocks, 'store', split_axis=0, concat_axis=0, tiled=True)  40.9 us
    pallas_call x1, Pallas kernels, shards(): pl.pallas_call(functools.partial(attend_kernel, owners, heads), out_shape...  9.58 us
    all_to_all x1, waiting for transfers between devices, exchange(): lax.all_to_all(blocks, 'store', split_axis=0, concat_axis=0, tiled=True)  8.59 us
    all_to_all x1, starting transfers between devices, exchange(): lax.all_to_all(blocks, 'store', split_axis=0, concat_axis=0, tiled=True)  3.59 us
    unnamed x9, local copies, waits for them, and re-layouts  3.53 us
    ppermute x2, waiting for transfers between devices, swap_cores(): return lax.ppermute(part, 'tensor', [(0, 1), (1, 0)])  2.4 us
    pallas_call x1, Pallas kernels, shards(): pl.pallas_call(functools.partial(dispatch_kernel, owners, heads, adapt, r...  1.86 us
    pallas_call x2, Pallas kernels, expand(): pl.pallas_call(functools.partial(expand_kernel, owners, heads, wide), out...  1.62 us
  transfers between devices with their start and end apart: 3, of which 3 were waited for; matrix products, arithmetic and copies ran while one was open for 1% of the time, Pallas kernels for 0%

profile of v5, /device:TPU:0, one launch (start us, length us, event | category | flops | bytes accessed | tf_op | source)
XLA Modules:
  0.0 75.4 jit_solution(12997119091536029064)
XLA Ops:
  0.6 1.9 %dispatch.1 = (s32[64]{0:T(128)S(1)}, bf16[8,16,1152]{2,1,0:T(8,128)(2,1)S(1)}) custom-call(s32[16]{0:T(128)} %ids_hbm.1, s32[64]{0:T(128)} %slot_of_hbm.1, s32[16]{0:T(128)} %lengths_hbm.1, bf16[2,16,4096]{2,1,0:T(8,128)(2,1)} %x_hbm.1), custom_call_target="tpu_custom_call" | custom-call | tf_op jit(solution)/shard_map/dispatch/pallas_call | solution.py:435
  2.5 17.4 %all_to_all.20.blocks = bf16[8,16,1152]{2,1,0:T(8,128)(2,1)S(1)} all-to-all(bf16[8,16,1152]{2,1,0:T(8,128)(2,1)S(1)} %get-tuple-element.9), channel_id=1, replica_groups=mesh['parts'=2,'store'=8,'tensor'=2] {'store'}, dimensions={0} | all-to-all | bytes 589824 | tf_op jit(solution)/shard_map/all_to_all | solution.py:393
  19.9 0.0 copy-start
  19.9 1.6 %copy-done = bf16[8192,8,16]{0,2,1:T(8,128)(2,1)S(1)} copy-done((bf16[8192,8,16]{0,2,1:T(8,128)(2,1)S(1)}, bf16[8192,8,16]{0,2,1:T(8,128)(2,1)}, u32[]{:S(2)}) %copy-start) | copy-done | bytes 2097176
  21.5 0.6 project_query.1
  22.1 0.0 collective-permute-start
  22.1 1.2 %collective-permute-done.other = f32[32,128]{1,0:T(8,128)S(1)} collective-permute-done((f32[32,128]{1,0:T(8,128)S(1)}, f32[32,128]{1,0:T(8,128)S(1)}, u32[]{:S(2)}, u32[]{:S(2)}) %collective-permute-start) | collective-permute-done | bytes 16416 | tf_op jit(solution)/shard_map/ppermute | solution.py:401
  23.3 0.0 copy-start.2
  23.3 1.2 %copy-done.2 = bf16[8,16,4096]{2,1,0:T(8,128)(2,1)S(1)} copy-done((bf16[8,16,4096]{2,1,0:T(8,128)(2,1)S(1)}, bf16[8,16,4096]{2,1,0:T(8,128)(2,1)}, u32[]{:S(2)}) %copy-start.2) | copy-done | bytes 1048600
  24.6 0.4 expand_query.1
  25.0 11.9 %all_to_all.21.blocks = bf16[8,16,1024]{2,1,0:T(8,128)(2,1)S(1)} all-to-all(bf16[8,16,1024]{2,1,0:T(8,128)(2,1)S(1)} %expand_query.1), channel_id=1, replica_groups=mesh['parts'=2,'store'=8,'tensor'=2] {'store'}, dimensions={0} | all-to-all | bytes 524288 | tf_op jit(solution)/shard_map/all_to_all | solution.py:393
  37.0 0.0 copy-start.1
  37.0 0.0 copy-start.3
  37.0 9.6 %attend.1 = (bf16[2,16,4096]{2,1,0:T(8,128)(2,1)S(1)}, bf16[8,16,1024]{2,1,0:T(8,128)(2,1)S(1)}) custom-call(s32[64]{0:T(128)S(1)} %get-tuple-element.8.meta, bf16[2,16,4096]{2,1,0:T(8,128)(2,1)} %q_hbm.1, bf16[2,16,512]{2,1,0:T(8,128)(2,1)} %kn_hbm.1, bf16[2,16,512]{2,1,0:T(8,128)(2,1)} %vn_hbm.1, bf16[16,512,512]{2,1,0:T(8,128)(2,1)} %k_hbm.1, ...), custom_call_target="tpu_custom_call" | custom-call | tf_op jit(solution)/shard_map/attend/pallas_call | solution.py:477
  46.5 11.5 %all_to_all.22.blocks = bf16[8,16,1024]{2,1,0:T(8,128)(2,1)S(1)} all-to-all(bf16[8,16,1024]{2,1,0:T(8,128)(2,1)S(1)} %get-tuple-element.12), channel_id=1, replica_groups=mesh['parts'=2,'store'=8,'tensor'=2] {'store'}, dimensions={0} | all-to-all | bytes 524288 | tf_op jit(solution)/shard_map/all_to_all | solution.py:393
  58.1 0.0 copy-done.1
  58.1 0.6 project_output.1.mine
  58.7 0.0 collective-permute-start.1
  58.7 1.2 %collective-permute-done.1.other = f32[32,128]{1,0:T(8,128)S(1)} collective-permute-done((f32[32,128]{1,0:T(8,128)S(1)}, f32[32,128]{1,0:T(8,128)S(1)}, u32[]{:S(2)}, u32[]{:S(2)}) %collective-permute-start.1) | collective-permute-done | bytes 16416 | tf_op jit(solution)/shard_map/ppermute | solution.py:401
  59.9 0.0 copy-done.3
  59.9 1.2 %expand_output.1 = bf16[8,16,1024]{2,1,0:T(8,128)(2,1)} custom-call(f32[32,128]{1,0:T(8,128)S(1)} %project_output.1.mine, f32[32,128]{1,0:T(8,128)S(1)} %collective-permute-done.1.other, bf16[128,4096]{1,0:T(8,128)(2,1)S(1)} %bitcast.11), custom_call_target="tpu_custom_call" | custom-call | tf_op jit(solution)/shard_map/expand_output/pallas_call | solution.py:466
  61.0 3.6 %all-to-all-start.3 = ((bf16[8,16,1024]{2,1,0:T(8,128)(2,1)}), bf16[8,16,1024]{2,1,0:T(8,128)(2,1)S(1)}, u32[]{:S(2)}, u32[]{:S(2)}) async-start(bf16[8,16,1024]{2,1,0:T(8,128)(2,1)} %expand_output.1), calls=%async_computation.3 | async-start | bytes 524288 | tf_op jit(solution)/shard_map/all_to_all | solution.py:393
  64.6 0.7 copy.15
  65.3 8.6 %all-to-all-done.3.blocks = bf16[8,16,1024]{2,1,0:T(8,128)(2,1)S(1)} async-done(((bf16[8,16,1024]{2,1,0:T(8,128)(2,1)}), bf16[8,16,1024]{2,1,0:T(8,128)(2,1)S(1)}, u32[]{:S(2)}, u32[]{:S(2)}) %all-to-all-start.3) | async-done | bytes 262176 | tf_op jit(solution)/shard_map/all_to_all | solution.py:393
  73.9 1.5 %collect.1 = bf16[2,16,4096]{2,1,0:T(8,128)(2,1)} custom-call(s32[64]{0:T(128)S(1)} %get-tuple-element.8.meta, bf16[8,16,1024]{2,1,0:T(8,128)(2,1)S(1)} %all-to-all-done.3.blocks), custom_call_target="tpu_custom_call" | custom-call | tf_op jit(solution)/shard_map/collect/pallas_call | solution.py:509
Async XLA Ops:
  19.9 1.6 %copy-start = (bf16[8192,8,16]{0,2,1:T(8,128)(2,1)S(1)}, bf16[8192,8,16]{0,2,1:T(8,128)(2,1)}, u32[]{:S(2)}) copy-start(bf16[8192,8,16]{0,2,1:T(8,128)(2,1)} %param.22) | copy-start | bytes 6291460
  22.1 1.2 %collective-permute-start = (f32[32,128]{1,0:T(8,128)S(1)}, f32[32,128]{1,0:T(8,128)S(1)}, u32[]{:S(2)}, u32[]{:S(2)}) collective-permute-start(f32[32,128]{1,0:T(8,128)S(1)} %get-tuple-element.10.mine), channel_id=1, source_target_pairs={{0,1},{1,0},{2,3},{3,2},{4,5},{5,4},{6,7},{7,6},{8,9},{9,8},{10,11... | collective-permute-start | bytes 49160 | tf_op jit(solution)/shard_map/ppermute | solution.py:401
  23.3 1.2 %copy-start.2 = (bf16[8,16,4096]{2,1,0:T(8,128)(2,1)S(1)}, bf16[8,16,4096]{2,1,0:T(8,128)(2,1)}, u32[]{:S(2)}) copy-start(bf16[8,16,4096]{2,1,0:T(8,128)(2,1)} %param.23) | copy-start | bytes 3145732
  37.0 21.1 %copy-start.1 = (bf16[8192,8,16]{0,2,1:T(8,128)(2,1)S(1)}, bf16[8192,8,16]{0,2,1:T(8,128)(2,1)}, u32[]{:S(2)}) copy-start(bf16[8192,8,16]{0,2,1:T(8,128)(2,1)} %param.24) | copy-start | bytes 6291460
  37.0 22.9 %copy-start.3 = (bf16[8,16,4096]{2,1,0:T(8,128)(2,1)S(1)}, bf16[8,16,4096]{2,1,0:T(8,128)(2,1)}, u32[]{:S(2)}) copy-start(bf16[8,16,4096]{2,1,0:T(8,128)(2,1)} %param.25) | copy-start | bytes 3145732
  58.7 1.2 %collective-permute-start.1 = (f32[32,128]{1,0:T(8,128)S(1)}, f32[32,128]{1,0:T(8,128)S(1)}, u32[]{:S(2)}, u32[]{:S(2)}) collective-permute-start(f32[32,128]{1,0:T(8,128)S(1)} %project_output.1.mine), channel_id=1, source_target_pairs={{0,1},{1,0},{2,3},{3,2},{4,5},{5,4},{6,7},{7,6},{8,9},{9,8},{10,11... | collective-permute-start | bytes 49160 | tf_op jit(solution)/shard_map/ppermute | solution.py:401
  61.0 12.9 %all-to-all-start.3 = ((bf16[8,16,1024]{2,1,0:T(8,128)(2,1)}), bf16[8,16,1024]{2,1,0:T(8,128)(2,1)S(1)}, u32[]{:S(2)}, u32[]{:S(2)}) async-start(bf16[8,16,1024]{2,1,0:T(8,128)(2,1)} %expand_output.1), calls=%async_computation.3 | async-start | bytes 524288 | tf_op jit(solution)/shard_map/all_to_all | solution.py:393

commit v6 on v5

--- a/solution.py
+++ b/solution.py
@@ -121,6 +121,10 @@
     )
 
 
+def in_order(arrived, crossed):
+    return [b for a, c in zip(arrived, crossed) for b in (a[0], c[...])]
+
+
 def exact(matrix, values):
     return jnp.dot(matrix, values, preferred_element_type=F32).astype(BF16)
 
@@ -135,14 +139,10 @@
     lengths_hbm,
     x_hbm,
     meta,
-    blocks,
-    slot_at,
-    ids,
-    slot_of,
-    lengths,
-    x_ref,
-    sems,
+    *refs,
 ):
+    outgoing = refs[: owners // 2]
+    slot_at, ids, slot_of, lengths, x_ref, sems = refs[owners // 2 :]
     pairs = ((ids_hbm, ids), (slot_of_hbm, slot_of), (lengths_hbm, lengths), (x_hbm, x_ref))
     copies = [pltpu.make_async_copy(a, b, sems.at[k]) for k, (a, b) in enumerate(pairs)]
     for copy in copies:
@@ -151,6 +151,7 @@
     wide = x_ref.shape[2] // heads
     for copy in copies[:3]:
         copy.wait()
+    me = lax.axis_index("store")
     row_at = rows
     order = rows + owners * CAP
     spans = order + rows
@@ -159,7 +160,7 @@
         slot_at[p] = -1
     for r in range(rows):
         slot = slot_of[ids[r]]
-        first = over(slot, adapt) * CAP
+        first = (over(slot, adapt) ^ me) * CAP
         place = first + jnp.where(meta[row_at + first] >= 0, 1, 0)
         meta[row_at + place] = r
         slot_at[place] = rest(slot, adapt)
@@ -181,12 +182,14 @@
     lane_slot = over(iota((block, adapt * rank), 1), rank)
     first = rest(over(at, STEPS), CAP) == 0
     for i in range(owners):
-        blocks[i, :, :wide] = packed[i * block : (i + 1) * block]
+        outgoing[i // 2][i % 2, :, :wide] = packed[i * block : (i + 1) * block]
         slot = jnp.where(first, slot_at[i * CAP], slot_at[i * CAP + 1])
-        blocks[i, :, wide:] = one_hot(lane_slot == slot)
-
-
-def project_kernel(owners, heads, wide, first, a_ref, blocks, *refs):
+        outgoing[i // 2][i % 2, :, wide:] = one_hot(lane_slot == slot)
+
+
+def project_kernel(owners, heads, wide, first, a_ref, *refs):
+    blocks = in_order(refs[: owners // 2], refs[owners // 2 : owners])
+    refs = refs[owners:]
     core = lax.axis_index("tensor")
     if first:
         part_ref, mask_ref = refs
@@ -194,10 +197,10 @@
         mask_in, part_ref = refs
     grouped = regroup_matrix(owners, heads)
     items = owners * CAP * STEPS
-    arrived = jnp.concatenate([blocks[i, :, :wide] for i in range(owners)], axis=0)
+    arrived = jnp.concatenate([b[:, :wide] for b in blocks], axis=0)
     arrived = exact(grouped, arrived)
     if first:
-        masks = jnp.concatenate([blocks[i, :, wide:] for i in range(owners)], axis=0)
+        masks = jnp.concatenate([b[:, wide:] for b in blocks], axis=0)
         mask = jnp.dot(grouped[:items], masks, preferred_element_type=F32)
         mask_ref[...] = mask
     else:
@@ -213,7 +216,7 @@
     part_ref[...] = total * mask
 
 
-def expand_kernel(owners, heads, wide, mine, other, b_ref, blocks):
+def expand_kernel(owners, heads, wide, mine, other, b_ref, *outgoing):
     low_rank = (mine[...] + other[...]).astype(BF16)
     pieces = []
     for c in range(heads):
@@ -224,7 +227,7 @@
     back = exact(ungroup_matrix(owners, heads), jnp.concatenate(pieces, axis=0))
     block = heads * CAP * STEPS
     for i in range(owners):
-        blocks[i] = back[i * block : (i + 1) * block]
+        outgoing[i // 2][i % 2] = back[i * block : (i + 1) * block]
 
 
 def quads(row_of, span_of, rows, sizes, action):
@@ -250,21 +253,14 @@
     vn_hbm,
     k_hbm,
     v_hbm,
-    blocks,
-    out_ref,
-    outgoing,
-    q_ref,
-    kn_ref,
-    vn_ref,
-    k_ref,
-    v_ref,
-    mask_ref,
-    q_buf,
-    o_buf,
-    k_sem,
-    v_sem,
-    sems,
+    *refs,
 ):
+    blocks = in_order(refs[: owners // 2], refs[owners // 2 : owners])
+    out_ref = refs[owners]
+    outgoing = refs[owners + 1 : owners + 1 + owners // 2]
+    q_ref, kn_ref, vn_ref, k_ref, v_ref, mask_ref, q_buf, o_buf, k_sem, v_sem, sems = refs[
+        owners + 1 + owners // 2 :
+    ]
     rows = q_hbm.shape[1]
     wide = q_hbm.shape[2] // heads
     groups = wide // HD
@@ -311,7 +307,7 @@
 
     delta = jnp.dot(
         unpack_matrix(meta, owners, heads, rows, True),
-        jnp.concatenate([blocks[i] for i in range(owners)], axis=0),
+        jnp.concatenate(blocks, axis=0),
         preferred_element_type=F32,
     )
     by_row = by_row_matrix(heads, rows)
@@ -370,7 +366,7 @@
     packed = exact(pack_matrix(meta, owners, heads, rows, True), mixed)
     block = heads * CAP * STEPS
     for i in range(owners):
-        outgoing[i] = packed[i * block : (i + 1) * block]
+        outgoing[i // 2][i % 2] = packed[i * block : (i + 1) * block]
     final = exact(by_pair_matrix(heads, rows), mixed)
     for c in range(heads):
         for s in range(STEPS):
@@ -378,10 +374,12 @@
             out_ref[s, :, c * wide : (c + 1) * wide] = final[at : at + rows]
 
 
-def collect_kernel(owners, heads, meta, blocks, out_ref):
+def collect_kernel(owners, heads, meta, *refs):
+    blocks = in_order(refs[: owners // 2], refs[owners // 2 : owners])
+    out_ref = refs[owners]
     rows = out_ref.shape[1]
     wide = out_ref.shape[2] // heads
-    arrived = jnp.concatenate([blocks[i] for i in range(owners)], axis=0)
+    arrived = jnp.concatenate(blocks, axis=0)
     values = exact(unpack_matrix(meta, owners, heads, rows, False), arrived)
     for c in range(heads):
         for s in range(STEPS):
@@ -389,8 +387,15 @@
             out_ref[s, :, c * wide : (c + 1) * wide] = values[top : top + rows]
 
 
-def exchange(blocks):
-    return lax.all_to_all(blocks, "store", split_axis=0, concat_axis=0, tiled=True)
+def exchange(pairs):
+    owners = 2 * len(pairs)
+    arrived = [pairs[0]] + [
+        lax.ppermute(pair, "store", [(s, s ^ (2 * k)) for s in range(owners)])
+        for k, pair in enumerate(pairs)
+        if k > 0
+    ]
+    crossed = [lax.ppermute(pair[1], "store", [(s, s ^ 1) for s in range(owners)]) for pair in arrived]
+    return arrived + crossed
 
 
 def in_hbm(array):
@@ -431,15 +436,15 @@
     shape = jax.ShapeDtypeStruct
     small = pltpu.CompilerParams(vmem_limit_bytes=16 * 1024 * 1024)
 
-    sent = shape((owners, block, wide), BF16)
-    meta, blocks = pl.pallas_call(
+    sent = [shape((2, block, wide), BF16)] * (owners // 2)
+    meta, *blocks = pl.pallas_call(
         functools.partial(dispatch_kernel, owners, heads, adapt, rank),
         out_shape=[
             shape((3 * rows + owners * CAP,), I32),
-            shape((owners, block, wide + lanes), BF16),
-        ],
+        ]
+        + [shape((2, block, wide + lanes), BF16)] * (owners // 2),
         in_specs=[HBM] * 4,
-        out_specs=[SMEM, VMEM],
+        out_specs=[SMEM] + [VMEM] * (owners // 2),
         scratch_shapes=[
             pltpu.SMEM((owners * CAP,), I32),
             pltpu.SMEM(adapter_ids.shape, I32),
@@ -456,29 +461,29 @@
     part, mask = pl.pallas_call(
         functools.partial(project_kernel, owners, heads, wide, True),
         out_shape=[shape((items, lanes), F32)] * 2,
-        in_specs=[VMEM] * 2,
+        in_specs=[VMEM] * (owners + 1),
         out_specs=[VMEM] * 2,
         compiler_params=small,
         name="project_query",
-    )(flat(a_query), arrived)
+    )(flat(a_query), *arrived)
 
     def expand(part, b_store, name):
         return pl.pallas_call(
             functools.partial(expand_kernel, owners, heads, wide),
             out_shape=sent,
             in_specs=[VMEM] * 3,
-            out_specs=VMEM,
+            out_specs=[VMEM] * (owners // 2),
             compiler_params=small,
             name=name,
         )(part, swap_cores(part), b_store.reshape(lanes, width))
 
     returned = exchange(expand(part, b_query, "expand_query"))
 
-    attn_out, outgoing = pl.pallas_call(
+    attn_out, *outgoing = pl.pallas_call(
         functools.partial(attend_kernel, owners, heads),
-        out_shape=[pltpu.VMEM((STEPS, rows, width), BF16), sent],
-        in_specs=[SMEM] + [HBM] * 5 + [VMEM],
-        out_specs=[VMEM] * 2,
+        out_shape=[shape((STEPS, rows, width), BF16)] + sent,
+        in_specs=[SMEM] + [HBM] * 5 + [VMEM] * owners,
+        out_specs=[VMEM] * (1 + owners // 2),
         scratch_shapes=[
             pltpu.VMEM(q_base.shape, BF16),
             pltpu.VMEM((CHUNK, heads * HD), BF16),
@@ -494,26 +499,26 @@
         ],
         compiler_params=pltpu.CompilerParams(vmem_limit_bytes=32 * 1024 * 1024),
         name="attend",
-    )(meta, *map(in_hbm, (q_base, k_new, v_new, cache_k, cache_v)), returned)
+    )(meta, *map(in_hbm, (q_base, k_new, v_new, cache_k, cache_v)), *returned)
 
     arrived = exchange(outgoing)
     part = pl.pallas_call(
         functools.partial(project_kernel, owners, heads, wide, False),
         out_shape=shape((items, lanes), F32),
-        in_specs=[VMEM] * 3,
+        in_specs=[VMEM] * (owners + 2),
         out_specs=VMEM,
         compiler_params=small,
         name="project_output",
-    )(flat(a_output), arrived, mask)
+    )(flat(a_output), *arrived, mask)
     returned = exchange(expand(part, b_output, "expand_output"))
     adapter_out = pl.pallas_call(
         functools.partial(collect_kernel, owners, heads),
         out_shape=shape((STEPS, rows, width), BF16),
-        in_specs=[SMEM, VMEM],
+        in_specs=[SMEM] + [VMEM] * owners,
         out_specs=VMEM,
         compiler_params=small,
         name="collect",
-    )(meta, returned)
+    )(meta, *returned)
     return (attn_out, adapter_out)
 
 

time: 76.2 us -> 82.6 us (1.084)
  blocking collectives: 40.9 us -> 0 us
  starting transfers between devices: 3.59 us -> 34.7 us
  waiting for transfers between devices: 11 us -> 27.5 us
  Pallas kernels: 15.7 us -> 16.6 us
    all_to_all x3 -> x0, blocking collectives: 40.9 us -> none  [exchange(): lax.all_to_all(blocks, 'store', split_axis=0, concat_axis=0, tiled=True)]
    ppermute x0 -> x28, starting transfers between devices: none -> 34.7 us  [the longest x12 18.7 us: exchange(): lax.ppermute(pair, 'store', [(s, s ^ 2 * k) for s in range(owners)])]
    ppermute x0 -> x28, waiting for transfers between devices: none -> 25.1 us  [the longest x12 13.2 us: exchange(): lax.ppermute(pair, 'store', [(s, s ^ 2 * k) for s in range(owners)])]
    all_to_all x1 -> x0, waiting for transfers between devices: 8.59 us -> none  [exchange(): lax.all_to_all(blocks, 'store', split_axis=0, concat_axis=0, tiled=True)]
    all_to_all x1 -> x0, starting transfers between devices: 3.59 us -> none  [exchange(): lax.all_to_all(blocks, 'store', split_axis=0, concat_axis=0, tiled=True)]
    pallas_call x1, Pallas kernels: 9.58 us -> 11.2 us  [shards(): pl.pallas_call(functools.partial(attend_kernel, owners, heads), out_shape...]
    unnamed x9 -> x8, local copies, waits for them, and re-layouts: 3.53 us -> 2.82 us
  transfers between devices with their start and end apart: 3 -> 30, of which waited for: 3 -> 16; matrix products, arithmetic and copies ran while one was open for 1% -> 0% of each run, Pallas kernels for 0% -> 0%
where the time goes in v6:
time: 82.6 us; the launch traced here: 82.4 us
  starting transfers between devices  34.7 us (42%)
  waiting for transfers between devices  27.5 us (33%)
  Pallas kernels  16.6 us (20%)
  local copies, waits for them, and re-layouts  2.88 us (3%)
    ppermute x12, starting transfers between devices, exchange(): lax.ppermute(pair, 'store', [(s, s ^ 2 * k) for s in range(owners)])  18.7 us
    ppermute x16, starting transfers between devices, exchange(): lax.ppermute(pair[1], 'store', [(s, s ^ 1) for s in range(owners)])  16 us
    ppermute x12, waiting for transfers between devices, exchange(): lax.ppermute(pair, 'store', [(s, s ^ 2 * k) for s in range(owners)])  13.2 us
    ppermute x16, waiting for transfers between devices, exchange(): lax.ppermute(pair[1], 'store', [(s, s ^ 1) for s in range(owners)])  11.8 us
    pallas_call x1, Pallas kernels, shards(): pl.pallas_call(functools.partial(attend_kernel, owners, heads), out_shape...  11.2 us
    unnamed x8, local copies, waits for them, and re-layouts  2.82 us
    ppermute x2, waiting for transfers between devices, swap_cores(): return lax.ppermute(part, 'tensor', [(0, 1), (1, 0)])  2.4 us
    pallas_call x1, Pallas kernels, shards(): pl.pallas_call(functools.partial(dispatch_kernel, owners, heads, adapt, r...  1.87 us
  transfers between devices with their start and end apart: 30, of which 16 were waited for; matrix products, arithmetic and copies ran while one was open for 0% of the time, Pallas kernels for 0%

profile of v6, /device:TPU:0, one launch (start us, length us, event | category | flops | bytes accessed | tf_op | source)
XLA Modules:
  0.0 82.4 jit_solution(7173739683462248054)
XLA Ops:
  0.6 1.9 %dispatch.1 = (s32[64]{0:T(128)S(1)}, bf16[2,16,1152]{2,1,0:T(8,128)(2,1)S(1)}, bf16[2,16,1152]{2,1,0:T(8,128)(2,1)S(1)}, bf16[2,16,1152]{2,1,0:T(8,128)(2,1)S(1)}, bf16[2,16,1152]{2,1,0:T(8,128)(2,1)S(1)}) custom-call(s32[16]{0:T(128)} %ids_hbm.1, s32[64]{0:T(128)} %slot_of_hbm.1, s32[16]{0:T(128)} %lengths_hbm.1, bf16[2,16,4096]{2,1,0:T(8,128)(2,1)} %x_hbm.1), custom_call_target="tpu_custom_call" | custom-call | tf_op jit(solution)/shard_map/dispatch/pallas_call | solution.py:440
  2.5 3.1 %collective-permute-start = (bf16[2,16,1152]{2,1,0:T(8,128)(2,1)S(1)}, bf16[2,16,1152]{2,1,0:T(8,128)(2,1)S(1)}, u32[]{:S(2)}, u32[]{:S(2)}) collective-permute-start(bf16[2,16,1152]{2,1,0:T(8,128)(2,1)S(1)} %get-tuple-element.24), channel_id=1, source_target_pairs={{0,4},{2,6},{4,0},{6,2},{8,12},{10,14},{12,8},{14,10},{1,5},{3,7},... | collective-permute-start | bytes 221192 | tf_op jit(solution)/shard_map/ppermute | solution.py:393
  5.6 1.5 %collective-permute-start.3 = (bf16[16,1152]{1,0:T(8,128)(2,1)S(1)}, bf16[16,1152]{1,0:T(8,128)(2,1)S(1)}, u32[]{:S(2)}, u32[]{:S(2)}) collective-permute-start(bf16[16,1152]{1,0:T(8,128)(2,1)S(1)} %slice_bitcast_fusion.3), channel_id=1, source_target_pairs={{0,2},{2,0},{4,6},{6,4},{8,10},{10,8},{12,14},{14,12},{1,3},{3,1},... | collective-permute-start | bytes 110600 | tf_op jit(solution)/shard_map/ppermute | solution.py:397
  7.1 2.6 %collective-permute-start.1 = (bf16[2,16,1152]{2,1,0:T(8,128)(2,1)S(1)}, bf16[2,16,1152]{2,1,0:T(8,128)(2,1)S(1)}, u32[]{:S(2)}, u32[]{:S(2)}) collective-permute-start(bf16[2,16,1152]{2,1,0:T(8,128)(2,1)S(1)} %get-tuple-element.25), channel_id=1, source_target_pairs={{0,8},{2,10},{4,12},{6,14},{8,0},{10,2},{12,4},{14,6},{1,9},{3,11}... | collective-permute-start | bytes 221192 | tf_op jit(solution)/shard_map/ppermute | solution.py:393
  10.3 4.3 %collective-permute-done.1.refs_2_ = bf16[2,16,1152]{2,1,0:T(8,128)(2,1)S(1)} collective-permute-done((bf16[2,16,1152]{2,1,0:T(8,128)(2,1)S(1)}, bf16[2,16,1152]{2,1,0:T(8,128)(2,1)S(1)}, u32[]{:S(2)}, u32[]{:S(2)}) %collective-permute-start.1) | collective-permute-done | bytes 73760 | tf_op jit(solution)/shard_map/ppermute | solution.py:393
  14.6 0.6 collective-permute-start.5
  15.1 0.8 %collective-permute-done.2.refs_3_ = bf16[2,16,1152]{2,1,0:T(8,128)(2,1)S(1)} collective-permute-done((bf16[2,16,1152]{2,1,0:T(8,128)(2,1)S(1)}, bf16[2,16,1152]{2,1,0:T(8,128)(2,1)S(1)}, u32[]{:S(2)}, u32[]{:S(2)}) %collective-permute-start.2) | collective-permute-done | bytes 73760 | tf_op jit(solution)/shard_map/ppermute | solution.py:393
  16.0 0.6 collective-permute-start.6
  16.6 1.9 %collective-permute-done.5.refs_6_ = bf16[16,1152]{1,0:T(8,128)(2,1)S(1)} collective-permute-done((bf16[16,1152]{1,0:T(8,128)(2,1)S(1)}, bf16[16,1152]{1,0:T(8,128)(2,1)S(1)}, u32[]{:S(2)}, u32[]{:S(2)}) %collective-permute-start.5) | collective-permute-done | bytes 36896 | tf_op jit(solution)/shard_map/ppermute | solution.py:397
  18.5 1.4 %collective-permute-done.6.refs_7_ = bf16[16,1152]{1,0:T(8,128)(2,1)S(1)} collective-permute-done((bf16[16,1152]{1,0:T(8,128)(2,1)S(1)}, bf16[16,1152]{1,0:T(8,128)(2,1)S(1)}, u32[]{:S(2)}, u32[]{:S(2)}) %collective-permute-start.6) | collective-permute-done | bytes 36896 | tf_op jit(solution)/shard_map/ppermute | solution.py:397
  19.9 1.6 %copy-done = bf16[8192,8,16]{0,2,1:T(8,128)(2,1)S(1)} copy-done((bf16[8192,8,16]{0,2,1:T(8,128)(2,1)S(1)}, bf16[8192,8,16]{0,2,1:T(8,128)(2,1)}, u32[]{:S(2)}) %copy-start) | copy-done | bytes 2097176
  21.5 0.6 project_query.1
  22.1 1.2 %collective-permute-done.7.other = f32[32,128]{1,0:T(8,128)S(1)} collective-permute-done((f32[32,128]{1,0:T(8,128)S(1)}, f32[32,128]{1,0:T(8,128)S(1)}, u32[]{:S(2)}, u32[]{:S(2)}) %collective-permute-start.7) | collective-permute-done | bytes 16416 | tf_op jit(solution)/shard_map/ppermute | solution.py:406
  23.3 1.2 %copy-done.2 = bf16[8,16,4096]{2,1,0:T(8,128)(2,1)S(1)} copy-done((bf16[8,16,4096]{2,1,0:T(8,128)(2,1)S(1)}, bf16[8,16,4096]{2,1,0:T(8,128)(2,1)}, u32[]{:S(2)}) %copy-start.2) | copy-done | bytes 1048600
  24.6 0.5 expand_query.1
  25.0 0.8 collective-permute-start.8
  25.8 0.6 collective-permute-start.11
  26.4 3.2 %collective-permute-start.9 = (bf16[2,16,1024]{2,1,0:T(8,128)(2,1)S(1)}, bf16[2,16,1024]{2,1,0:T(8,128)(2,1)S(1)}, u32[]{:S(2)}, u32[]{:S(2)}) collective-permute-start(bf16[2,16,1024]{2,1,0:T(8,128)(2,1)S(1)} %get-tuple-element.30), channel_id=1, source_target_pairs={{0,8},{2,10},{4,12},{6,14},{8,0},{10,2},{12,4},{14,6},{1,9},{3,11}... | collective-permute-start | bytes 196616 | tf_op jit(solution)/shard_map/ppermute | solution.py:393
  29.6 0.5 collective-permute-start.10
  30.1 1.4 %collective-permute-start.12 = (bf16[16,1024]{1,0:T(8,128)(2,1)S(1)}, bf16[16,1024]{1,0:T(8,128)(2,1)S(1)}, u32[]{:S(2)}, u32[]{:S(2)}) collective-permute-start(bf16[16,1024]{1,0:T(8,128)(2,1)S(1)} %slice_bitcast_fusion.12), channel_id=1, source_target_pairs={{0,2},{2,0},{4,6},{6,4},{8,10},{10,8},{12,14},{14,12},{1,3},{3,1},... | collective-permute-start | bytes 98312 | tf_op jit(solution)/shard_map/ppermute | solution.py:397
  31.5 1.9 %collective-permute-done.9.refs_2_ = bf16[2,16,1024]{2,1,0:T(8,128)(2,1)S(1)} collective-permute-done((bf16[2,16,1024]{2,1,0:T(8,128)(2,1)S(1)}, bf16[2,16,1024]{2,1,0:T(8,128)(2,1)S(1)}, u32[]{:S(2)}, u32[]{:S(2)}) %collective-permute-start.9) | collective-permute-done | bytes 65568 | tf_op jit(solution)/shard_map/ppermute | solution.py:393
  33.4 1.8 %collective-permute-start.13 = (bf16[16,1024]{1,0:T(8,128)(2,1)S(1)}, bf16[16,1024]{1,0:T(8,128)(2,1)S(1)}, u32[]{:S(2)}, u32[]{:S(2)}) collective-permute-start(bf16[16,1024]{1,0:T(8,128)(2,1)S(1)} %slice_bitcast_fusion.11), channel_id=1, source_target_pairs={{0,2},{2,0},{4,6},{6,4},{8,10},{10,8},{12,14},{14,12},{1,3},{3,1},... | collective-permute-start | bytes 98312 | tf_op jit(solution)/shard_map/ppermute | solution.py:397
  35.2 0.5 collective-permute-done.10.refs_3_
  35.7 0.6 collective-permute-start.14
  36.3 1.1 %collective-permute-done.13.refs_6_ = bf16[16,1024]{1,0:T(8,128)(2,1)S(1)} collective-permute-done((bf16[16,1024]{1,0:T(8,128)(2,1)S(1)}, bf16[16,1024]{1,0:T(8,128)(2,1)S(1)}, u32[]{:S(2)}, u32[]{:S(2)}) %collective-permute-start.13) | collective-permute-done | bytes 32800 | tf_op jit(solution)/shard_map/ppermute | solution.py:397
  37.4 2.2 %collective-permute-done.14.refs_7_ = bf16[16,1024]{1,0:T(8,128)(2,1)S(1)} collective-permute-done((bf16[16,1024]{1,0:T(8,128)(2,1)S(1)}, bf16[16,1024]{1,0:T(8,128)(2,1)S(1)}, u32[]{:S(2)}, u32[]{:S(2)}) %collective-permute-start.14) | collective-permute-done | bytes 32800 | tf_op jit(solution)/shard_map/ppermute | solution.py:397
  39.6 11.2 %attend.1 = (bf16[2,16,4096]{2,1,0:T(8,128)(2,1)}, bf16[2,16,1024]{2,1,0:T(8,128)(2,1)S(1)}, bf16[2,16,1024]{2,1,0:T(8,128)(2,1)S(1)}, bf16[2,16,1024]{2,1,0:T(8,128)(2,1)S(1)}, bf16[2,16,1024]{2,1,0:T(8,128)(2,1)S(1)}) custom-call(s32[64]{0:T(128)S(1)} %get-tuple-element.22.meta, bf16[2,16,4096]{2,1,0:T(8,128)(2,1)} %q_hbm.1, bf16[2,16,512]{2,1,0:T(8,128)(2,1)} %kn_hbm.1, ...), custom_call_target="tpu_custom_call" | custom-call | tf_op jit(solution)/shard_map/attend/pallas_call | solution.py:482
  50.9 0.5 collective-permute-start.18
  51.5 2.9 %collective-permute-start.16 = (bf16[2,16,1024]{2,1,0:T(8,128)(2,1)S(1)}, bf16[2,16,1024]{2,1,0:T(8,128)(2,1)S(1)}, u32[]{:S(2)}, u32[]{:S(2)}) collective-permute-start(bf16[2,16,1024]{2,1,0:T(8,128)(2,1)S(1)} %get-tuple-element.35), channel_id=1, source_target_pairs={{0,8},{2,10},{4,12},{6,14},{8,0},{10,2},{12,4},{14,6},{1,9},{3,11}... | collective-permute-start | bytes 196616 | tf_op jit(solution)/shard_map/ppermute | solution.py:393
  54.3 1.0 %collective-permute-start.17 = (bf16[2,16,1024]{2,1,0:T(8,128)(2,1)S(1)}, bf16[2,16,1024]{2,1,0:T(8,128)(2,1)S(1)}, u32[]{:S(2)}, u32[]{:S(2)}) collective-permute-start(bf16[2,16,1024]{2,1,0:T(8,128)(2,1)S(1)} %get-tuple-element.36), channel_id=1, source_target_pairs={{0,12},{2,14},{4,8},{6,10},{8,4},{10,6},{12,0},{14,2},{1,13},{3,15... | collective-permute-start | bytes 196616 | tf_op jit(solution)/shard_map/ppermute | solution.py:393
  55.5 1.8 %collective-permute-start.19 = (bf16[16,1024]{1,0:T(8,128)(2,1)S(1)}, bf16[16,1024]{1,0:T(8,128)(2,1)S(1)}, u32[]{:S(2)}, u32[]{:S(2)}) collective-permute-start(bf16[16,1024]{1,0:T(8,128)(2,1)S(1)} %slice_bitcast_fusion.9), channel_id=1, source_target_pairs={{0,2},{2,0},{4,6},{6,4},{8,10},{10,8},{12,14},{14,12},{1,3},{3,1},... | collective-permute-start | bytes 98312 | tf_op jit(solution)/shard_map/ppermute | solution.py:397
  57.3 0.9 %collective-permute-start.20 = (bf16[16,1024]{1,0:T(8,128)(2,1)S(1)}, bf16[16,1024]{1,0:T(8,128)(2,1)S(1)}, u32[]{:S(2)}, u32[]{:S(2)}) collective-permute-start(bf16[16,1024]{1,0:T(8,128)(2,1)S(1)} %slice_bitcast_fusion.8), channel_id=1, source_target_pairs={{0,2},{2,0},{4,6},{6,4},{8,10},{10,8},{12,14},{14,12},{1,3},{3,1},... | collective-permute-start | bytes 98312 | tf_op jit(solution)/shard_map/ppermute | solution.py:397
  58.2 2.2 %collective-permute-done.17.refs_3_ = bf16[2,16,1024]{2,1,0:T(8,128)(2,1)S(1)} collective-permute-done((bf16[2,16,1024]{2,1,0:T(8,128)(2,1)S(1)}, bf16[2,16,1024]{2,1,0:T(8,128)(2,1)S(1)}, u32[]{:S(2)}, u32[]{:S(2)}) %collective-permute-start.17) | collective-permute-done | bytes 65568 | tf_op jit(solution)/shard_map/ppermute | solution.py:393
  60.4 1.3 %collective-permute-start.21 = (bf16[16,1024]{1,0:T(8,128)(2,1)S(1)}, bf16[16,1024]{1,0:T(8,128)(2,1)S(1)}, u32[]{:S(2)}, u32[]{:S(2)}) collective-permute-start(bf16[16,1024]{1,0:T(8,128)(2,1)S(1)} %slice_bitcast_fusion.7), channel_id=1, source_target_pairs={{0,2},{2,0},{4,6},{6,4},{8,10},{10,8},{12,14},{14,12},{1,3},{3,1},... | collective-permute-start | bytes 98312 | tf_op jit(solution)/shard_map/ppermute | solution.py:397
  61.7 2.6 %collective-permute-done.21.refs_7_ = bf16[16,1024]{1,0:T(8,128)(2,1)S(1)} collective-permute-done((bf16[16,1024]{1,0:T(8,128)(2,1)S(1)}, bf16[16,1024]{1,0:T(8,128)(2,1)S(1)}, u32[]{:S(2)}, u32[]{:S(2)}) %collective-permute-start.21) | collective-permute-done | bytes 32800 | tf_op jit(solution)/shard_map/ppermute | solution.py:397
  64.3 0.6 project_output.1.mine
  64.9 1.2 %collective-permute-done.22.other = f32[32,128]{1,0:T(8,128)S(1)} collective-permute-done((f32[32,128]{1,0:T(8,128)S(1)}, f32[32,128]{1,0:T(8,128)S(1)}, u32[]{:S(2)}, u32[]{:S(2)}) %collective-permute-start.22) | collective-permute-done | bytes 16416 | tf_op jit(solution)/shard_map/ppermute | solution.py:406
  66.1 0.5 expand_output.1
  66.7 1.4 %collective-permute-start.26 = (bf16[16,1024]{1,0:T(8,128)(2,1)S(1)}, bf16[16,1024]{1,0:T(8,128)(2,1)S(1)}, u32[]{:S(2)}, u32[]{:S(2)}) collective-permute-start(bf16[16,1024]{1,0:T(8,128)(2,1)S(1)} %slice_bitcast_fusion.13), channel_id=1, source_target_pairs={{0,2},{2,0},{4,6},{6,4},{8,10},{10,8},{12,14},{14,12},{1,3},{3,1},... | collective-permute-start | bytes 98312 | tf_op jit(solution)/shard_map/ppermute | solution.py:397
  68.0 2.2 %collective-permute-start.24 = (bf16[2,16,1024]{2,1,0:T(8,128)(2,1)S(1)}, bf16[2,16,1024]{2,1,0:T(8,128)(2,1)S(1)}, u32[]{:S(2)}, u32[]{:S(2)}) collective-permute-start(bf16[2,16,1024]{2,1,0:T(8,128)(2,1)S(1)} %get-tuple-element.40), channel_id=1, source_target_pairs={{0,8},{2,10},{4,12},{6,14},{8,0},{10,2},{12,4},{14,6},{1,9},{3,11}... | collective-permute-start | bytes 196616 | tf_op jit(solution)/shard_map/ppermute | solution.py:393
  70.2 2.1 %collective-permute-start.25 = (bf16[2,16,1024]{2,1,0:T(8,128)(2,1)S(1)}, bf16[2,16,1024]{2,1,0:T(8,128)(2,1)S(1)}, u32[]{:S(2)}, u32[]{:S(2)}) collective-permute-start(bf16[2,16,1024]{2,1,0:T(8,128)(2,1)S(1)} %get-tuple-element.41), channel_id=1, source_target_pairs={{0,12},{2,14},{4,8},{6,10},{8,4},{10,6},{12,0},{14,2},{1,13},{3,15... | collective-permute-start | bytes 196616 | tf_op jit(solution)/shard_map/ppermute | solution.py:393
  72.3 0.7 collective-permute-start.27
  73.1 3.3 %collective-permute-done.24.refs_2_ = bf16[2,16,1024]{2,1,0:T(8,128)(2,1)S(1)} collective-permute-done((bf16[2,16,1024]{2,1,0:T(8,128)(2,1)S(1)}, bf16[2,16,1024]{2,1,0:T(8,128)(2,1)S(1)}, u32[]{:S(2)}, u32[]{:S(2)}) %collective-permute-start.24) | collective-permute-done | bytes 65568 | tf_op jit(solution)/shard_map/ppermute | solution.py:393
  76.3 0.7 collective-permute-start.28
  77.1 1.3 %collective-permute-start.29 = (bf16[16,1024]{1,0:T(8,128)(2,1)S(1)}, bf16[16,1024]{1,0:T(8,128)(2,1)S(1)}, u32[]{:S(2)}, u32[]{:S(2)}) collective-permute-start(bf16[16,1024]{1,0:T(8,128)(2,1)S(1)} %slice_bitcast_fusion.4), channel_id=1, source_target_pairs={{0,2},{2,0},{4,6},{6,4},{8,10},{10,8},{12,14},{14,12},{1,3},{3,1},... | collective-permute-start | bytes 98312 | tf_op jit(solution)/shard_map/ppermute | solution.py:397
  78.4 1.9 %collective-permute-done.28.refs_6_ = bf16[16,1024]{1,0:T(8,128)(2,1)S(1)} collective-permute-done((bf16[16,1024]{1,0:T(8,128)(2,1)S(1)}, bf16[16,1024]{1,0:T(8,128)(2,1)S(1)}, u32[]{:S(2)}, u32[]{:S(2)}) %collective-permute-start.28) | collective-permute-done | bytes 32800 | tf_op jit(solution)/shard_map/ppermute | solution.py:397
  80.2 0.7 collective-permute-done.29.refs_7_
  81.0 1.5 %collect.1 = bf16[2,16,4096]{2,1,0:T(8,128)(2,1)} custom-call(s32[64]{0:T(128)S(1)} %get-tuple-element.22.meta, bf16[2,16,1024]{2,1,0:T(8,128)(2,1)S(1)} %get-tuple-element.38.refs_0_, bf16[2,16,1024]{2,1,0:T(8,128)(2,1)S(1)} %collective-permute-done.23.refs_1_, bf16[2,16,1024]{2,1,0:T(8,128)(2,1)S(1)} %collective-permute-done.24.refs_2_, ...), custom_call_target="tpu_custom_call" | custom-call | tf_op jit(solution)/shard_map/collect/pallas_call | solution.py:514
  (43 shorter events, 1.0 us)
Async XLA Ops:
  2.5 7.4 %collective-permute-start = (bf16[2,16,1152]{2,1,0:T(8,128)(2,1)S(1)}, bf16[2,16,1152]{2,1,0:T(8,128)(2,1)S(1)}, u32[]{:S(2)}, u32[]{:S(2)}) collective-permute-start(bf16[2,16,1152]{2,1,0:T(8,128)(2,1)S(1)} %get-tuple-element.24), channel_id=1, source_target_pairs={{0,4},{2,6},{4,0},{6,2},{8,12},{10,14},{12,8},{14,10},{1,5},{3,7},... | collective-permute-start | bytes 221192 | tf_op jit(solution)/shard_map/ppermute | solution.py:393
  5.6 11.0 %collective-permute-start.3 = (bf16[16,1152]{1,0:T(8,128)(2,1)S(1)}, bf16[16,1152]{1,0:T(8,128)(2,1)S(1)}, u32[]{:S(2)}, u32[]{:S(2)}) collective-permute-start(bf16[16,1152]{1,0:T(8,128)(2,1)S(1)} %slice_bitcast_fusion.3), channel_id=1, source_target_pairs={{0,2},{2,0},{4,6},{6,4},{8,10},{10,8},{12,14},{14,12},{1,3},{3,1},... | collective-permute-start | bytes 110600 | tf_op jit(solution)/shard_map/ppermute | solution.py:397
  7.1 7.5 %collective-permute-start.1 = (bf16[2,16,1152]{2,1,0:T(8,128)(2,1)S(1)}, bf16[2,16,1152]{2,1,0:T(8,128)(2,1)S(1)}, u32[]{:S(2)}, u32[]{:S(2)}) collective-permute-start(bf16[2,16,1152]{2,1,0:T(8,128)(2,1)S(1)} %get-tuple-element.25), channel_id=1, source_target_pairs={{0,8},{2,10},{4,12},{6,14},{8,0},{10,2},{12,4},{14,6},{1,9},{3,11}... | collective-permute-start | bytes 221192 | tf_op jit(solution)/shard_map/ppermute | solution.py:393
  9.7 6.3 %collective-permute-start.2 = (bf16[2,16,1152]{2,1,0:T(8,128)(2,1)S(1)}, bf16[2,16,1152]{2,1,0:T(8,128)(2,1)S(1)}, u32[]{:S(2)}, u32[]{:S(2)}) collective-permute-start(bf16[2,16,1152]{2,1,0:T(8,128)(2,1)S(1)} %get-tuple-element.26), channel_id=1, source_target_pairs={{0,12},{2,14},{4,8},{6,10},{8,4},{10,6},{12,0},{14,2},{1,13},{3,15... | collective-permute-start | bytes 221192 | tf_op jit(solution)/shard_map/ppermute | solution.py:393
  9.9 6.7 %collective-permute-start.4 = (bf16[16,1152]{1,0:T(8,128)(2,1)S(1)}, bf16[16,1152]{1,0:T(8,128)(2,1)S(1)}, u32[]{:S(2)}, u32[]{:S(2)}) collective-permute-start(bf16[16,1152]{1,0:T(8,128)(2,1)S(1)} %slice_bitcast_fusion.2), channel_id=1, source_target_pairs={{0,2},{2,0},{4,6},{6,4},{8,10},{10,8},{12,14},{14,12},{1,3},{3,1},... | collective-permute-start | bytes 110600 | tf_op jit(solution)/shard_map/ppermute | solution.py:397
  14.6 4.0 %collective-permute-start.5 = (bf16[16,1152]{1,0:T(8,128)(2,1)S(1)}, bf16[16,1152]{1,0:T(8,128)(2,1)S(1)}, u32[]{:S(2)}, u32[]{:S(2)}) collective-permute-start(bf16[16,1152]{1,0:T(8,128)(2,1)S(1)} %slice_bitcast_fusion.1), channel_id=1, source_target_pairs={{0,2},{2,0},{4,6},{6,4},{8,10},{10,8},{12,14},{14,12},{1,3},{3,1},... | collective-permute-start | bytes 110600 | tf_op jit(solution)/shard_map/ppermute | solution.py:397
  16.0 4.0 %collective-permute-start.6 = (bf16[16,1152]{1,0:T(8,128)(2,1)S(1)}, bf16[16,1152]{1,0:T(8,128)(2,1)S(1)}, u32[]{:S(2)}, u32[]{:S(2)}) collective-permute-start(bf16[16,1152]{1,0:T(8,128)(2,1)S(1)} %slice_bitcast_fusion), channel_id=1, source_target_pairs={{0,2},{2,0},{4,6},{6,4},{8,10},{10,8},{12,14},{14,12},{1,3},{3,1},... | collective-permute-start | bytes 110600 | tf_op jit(solution)/shard_map/ppermute | solution.py:397
  19.9 1.6 %copy-start = (bf16[8192,8,16]{0,2,1:T(8,128)(2,1)S(1)}, bf16[8192,8,16]{0,2,1:T(8,128)(2,1)}, u32[]{:S(2)}) copy-start(bf16[8192,8,16]{0,2,1:T(8,128)(2,1)} %param.22) | copy-start | bytes 6291460
  22.1 1.2 %collective-permute-start.7 = (f32[32,128]{1,0:T(8,128)S(1)}, f32[32,128]{1,0:T(8,128)S(1)}, u32[]{:S(2)}, u32[]{:S(2)}) collective-permute-start(f32[32,128]{1,0:T(8,128)S(1)} %get-tuple-element.27.mine), channel_id=1, source_target_pairs={{0,1},{1,0},{2,3},{3,2},{4,5},{5,4},{6,7},{7,6},{8,9},{9,8},{10,11... | collective-permute-start | bytes 49160 | tf_op jit(solution)/shard_map/ppermute | solution.py:406
  23.3 1.2 %copy-start.2 = (bf16[8,16,4096]{2,1,0:T(8,128)(2,1)S(1)}, bf16[8,16,4096]{2,1,0:T(8,128)(2,1)}, u32[]{:S(2)}) copy-start(bf16[8,16,4096]{2,1,0:T(8,128)(2,1)} %param.23) | copy-start | bytes 3145732
  25.0 5.1 %collective-permute-start.8 = (bf16[2,16,1024]{2,1,0:T(8,128)(2,1)S(1)}, bf16[2,16,1024]{2,1,0:T(8,128)(2,1)S(1)}, u32[]{:S(2)}, u32[]{:S(2)}) collective-permute-start(bf16[2,16,1024]{2,1,0:T(8,128)(2,1)S(1)} %get-tuple-element.29), channel_id=1, source_target_pairs={{0,4},{2,6},{4,0},{6,2},{8,12},{10,14},{12,8},{14,10},{1,5},{3,7},... | collective-permute-start | bytes 196616 | tf_op jit(solution)/shard_map/ppermute | solution.py:393
  25.8 10.5 %collective-permute-start.11 = (bf16[16,1024]{1,0:T(8,128)(2,1)S(1)}, bf16[16,1024]{1,0:T(8,128)(2,1)S(1)}, u32[]{:S(2)}, u32[]{:S(2)}) collective-permute-start(bf16[16,1024]{1,0:T(8,128)(2,1)S(1)} %slice_bitcast_fusion.15), channel_id=1, source_target_pairs={{0,2},{2,0},{4,6},{6,4},{8,10},{10,8},{12,14},{14,12},{1,3},{3,1},... | collective-permute-start | bytes 98312 | tf_op jit(solution)/shard_map/ppermute | solution.py:397
  26.4 7.0 %collective-permute-start.9 = (bf16[2,16,1024]{2,1,0:T(8,128)(2,1)S(1)}, bf16[2,16,1024]{2,1,0:T(8,128)(2,1)S(1)}, u32[]{:S(2)}, u32[]{:S(2)}) collective-permute-start(bf16[2,16,1024]{2,1,0:T(8,128)(2,1)S(1)} %get-tuple-element.30), channel_id=1, source_target_pairs={{0,8},{2,10},{4,12},{6,14},{8,0},{10,2},{12,4},{14,6},{1,9},{3,11}... | collective-permute-start | bytes 196616 | tf_op jit(solution)/shard_map/ppermute | solution.py:393
  29.6 6.1 %collective-permute-start.10 = (bf16[2,16,1024]{2,1,0:T(8,128)(2,1)S(1)}, bf16[2,16,1024]{2,1,0:T(8,128)(2,1)S(1)}, u32[]{:S(2)}, u32[]{:S(2)}) collective-permute-start(bf16[2,16,1024]{2,1,0:T(8,128)(2,1)S(1)} %get-tuple-element.31), channel_id=1, source_target_pairs={{0,12},{2,14},{4,8},{6,10},{8,4},{10,6},{12,0},{14,2},{1,13},{3,15... | collective-permute-start | bytes 196616 | tf_op jit(solution)/shard_map/ppermute | solution.py:393
  30.1 6.2 %collective-permute-start.12 = (bf16[16,1024]{1,0:T(8,128)(2,1)S(1)}, bf16[16,1024]{1,0:T(8,128)(2,1)S(1)}, u32[]{:S(2)}, u32[]{:S(2)}) collective-permute-start(bf16[16,1024]{1,0:T(8,128)(2,1)S(1)} %slice_bitcast_fusion.12), channel_id=1, source_target_pairs={{0,2},{2,0},{4,6},{6,4},{8,10},{10,8},{12,14},{14,12},{1,3},{3,1},... | collective-permute-start | bytes 98312 | tf_op jit(solution)/shard_map/ppermute | solution.py:397
  33.4 3.9 %collective-permute-start.13 = (bf16[16,1024]{1,0:T(8,128)(2,1)S(1)}, bf16[16,1024]{1,0:T(8,128)(2,1)S(1)}, u32[]{:S(2)}, u32[]{:S(2)}) collective-permute-start(bf16[16,1024]{1,0:T(8,128)(2,1)S(1)} %slice_bitcast_fusion.11), channel_id=1, source_target_pairs={{0,2},{2,0},{4,6},{6,4},{8,10},{10,8},{12,14},{14,12},{1,3},{3,1},... | collective-permute-start | bytes 98312 | tf_op jit(solution)/shard_map/ppermute | solution.py:397
  35.7 3.9 %collective-permute-start.14 = (bf16[16,1024]{1,0:T(8,128)(2,1)S(1)}, bf16[16,1024]{1,0:T(8,128)(2,1)S(1)}, u32[]{:S(2)}, u32[]{:S(2)}) collective-permute-start(bf16[16,1024]{1,0:T(8,128)(2,1)S(1)} %slice_bitcast_fusion.10), channel_id=1, source_target_pairs={{0,2},{2,0},{4,6},{6,4},{8,10},{10,8},{12,14},{14,12},{1,3},{3,1},... | collective-permute-start | bytes 98312 | tf_op jit(solution)/shard_map/ppermute | solution.py:397
  39.6 24.7 %copy-start.1 = (bf16[8192,8,16]{0,2,1:T(8,128)(2,1)S(1)}, bf16[8192,8,16]{0,2,1:T(8,128)(2,1)}, u32[]{:S(2)}) copy-start(bf16[8192,8,16]{0,2,1:T(8,128)(2,1)} %param.24) | copy-start | bytes 6291460
  39.6 26.5 %copy-start.3 = (bf16[8,16,4096]{2,1,0:T(8,128)(2,1)S(1)}, bf16[8,16,4096]{2,1,0:T(8,128)(2,1)}, u32[]{:S(2)}) copy-start(bf16[8,16,4096]{2,1,0:T(8,128)(2,1)} %param.25) | copy-start | bytes 3145732
  50.8 4.7 %collective-permute-start.15 = (bf16[2,16,1024]{2,1,0:T(8,128)(2,1)S(1)}, bf16[2,16,1024]{2,1,0:T(8,128)(2,1)S(1)}, u32[]{:S(2)}, u32[]{:S(2)}) collective-permute-start(bf16[2,16,1024]{2,1,0:T(8,128)(2,1)S(1)} %get-tuple-element.34), channel_id=1, source_target_pairs={{0,4},{2,6},{4,0},{6,2},{8,12},{10,14},{12,8},{14,10},{1,5},{3,7},... | collective-permute-start | bytes 196616 | tf_op jit(solution)/shard_map/ppermute | solution.py:393
  50.9 10.8 %collective-permute-start.18 = (bf16[16,1024]{1,0:T(8,128)(2,1)S(1)}, bf16[16,1024]{1,0:T(8,128)(2,1)S(1)}, u32[]{:S(2)}, u32[]{:S(2)}) collective-permute-start(bf16[16,1024]{1,0:T(8,128)(2,1)S(1)} %slice_bitcast_fusion.14), channel_id=1, source_target_pairs={{0,2},{2,0},{4,6},{6,4},{8,10},{10,8},{12,14},{14,12},{1,3},{3,1},... | collective-permute-start | bytes 98312 | tf_op jit(solution)/shard_map/ppermute | solution.py:397
  51.5 5.9 %collective-permute-start.16 = (bf16[2,16,1024]{2,1,0:T(8,128)(2,1)S(1)}, bf16[2,16,1024]{2,1,0:T(8,128)(2,1)S(1)}, u32[]{:S(2)}, u32[]{:S(2)}) collective-permute-start(bf16[2,16,1024]{2,1,0:T(8,128)(2,1)S(1)} %get-tuple-element.35), channel_id=1, source_target_pairs={{0,8},{2,10},{4,12},{6,14},{8,0},{10,2},{12,4},{14,6},{1,9},{3,11}... | collective-permute-start | bytes 196616 | tf_op jit(solution)/shard_map/ppermute | solution.py:393
  54.3 6.1 %collective-permute-start.17 = (bf16[2,16,1024]{2,1,0:T(8,128)(2,1)S(1)}, bf16[2,16,1024]{2,1,0:T(8,128)(2,1)S(1)}, u32[]{:S(2)}, u32[]{:S(2)}) collective-permute-start(bf16[2,16,1024]{2,1,0:T(8,128)(2,1)S(1)} %get-tuple-element.36), channel_id=1, source_target_pairs={{0,12},{2,14},{4,8},{6,10},{8,4},{10,6},{12,0},{14,2},{1,13},{3,15... | collective-permute-start | bytes 196616 | tf_op jit(solution)/shard_map/ppermute | solution.py:393
  55.5 6.2 %collective-permute-start.19 = (bf16[16,1024]{1,0:T(8,128)(2,1)S(1)}, bf16[16,1024]{1,0:T(8,128)(2,1)S(1)}, u32[]{:S(2)}, u32[]{:S(2)}) collective-permute-start(bf16[16,1024]{1,0:T(8,128)(2,1)S(1)} %slice_bitcast_fusion.9), channel_id=1, source_target_pairs={{0,2},{2,0},{4,6},{6,4},{8,10},{10,8},{12,14},{14,12},{1,3},{3,1},... | collective-permute-start | bytes 98312 | tf_op jit(solution)/shard_map/ppermute | solution.py:397
  57.3 4.4 %collective-permute-start.20 = (bf16[16,1024]{1,0:T(8,128)(2,1)S(1)}, bf16[16,1024]{1,0:T(8,128)(2,1)S(1)}, u32[]{:S(2)}, u32[]{:S(2)}) collective-permute-start(bf16[16,1024]{1,0:T(8,128)(2,1)S(1)} %slice_bitcast_fusion.8), channel_id=1, source_target_pairs={{0,2},{2,0},{4,6},{6,4},{8,10},{10,8},{12,14},{14,12},{1,3},{3,1},... | collective-permute-start | bytes 98312 | tf_op jit(solution)/shard_map/ppermute | solution.py:397
  60.4 3.9 %collective-permute-start.21 = (bf16[16,1024]{1,0:T(8,128)(2,1)S(1)}, bf16[16,1024]{1,0:T(8,128)(2,1)S(1)}, u32[]{:S(2)}, u32[]{:S(2)}) collective-permute-start(bf16[16,1024]{1,0:T(8,128)(2,1)S(1)} %slice_bitcast_fusion.7), channel_id=1, source_target_pairs={{0,2},{2,0},{4,6},{6,4},{8,10},{10,8},{12,14},{14,12},{1,3},{3,1},... | collective-permute-start | bytes 98312 | tf_op jit(solution)/shard_map/ppermute | solution.py:397
  64.9 1.2 %collective-permute-start.22 = (f32[32,128]{1,0:T(8,128)S(1)}, f32[32,128]{1,0:T(8,128)S(1)}, u32[]{:S(2)}, u32[]{:S(2)}) collective-permute-start(f32[32,128]{1,0:T(8,128)S(1)} %project_output.1.mine), channel_id=1, source_target_pairs={{0,1},{1,0},{2,3},{3,2},{4,5},{5,4},{6,7},{7,6},{8,9},{9,8},{10,11... | collective-permute-start | bytes 49160 | tf_op jit(solution)/shard_map/ppermute | solution.py:406
  66.6 5.8 %collective-permute-start.23 = (bf16[2,16,1024]{2,1,0:T(8,128)(2,1)S(1)}, bf16[2,16,1024]{2,1,0:T(8,128)(2,1)S(1)}, u32[]{:S(2)}, u32[]{:S(2)}) collective-permute-start(bf16[2,16,1024]{2,1,0:T(8,128)(2,1)S(1)} %get-tuple-element.39), channel_id=1, source_target_pairs={{0,4},{2,6},{4,0},{6,2},{8,12},{10,14},{12,8},{14,10},{1,5},{3,7},... | collective-permute-start | bytes 196616 | tf_op jit(solution)/shard_map/ppermute | solution.py:393
  66.7 11.7 %collective-permute-start.26 = (bf16[16,1024]{1,0:T(8,128)(2,1)S(1)}, bf16[16,1024]{1,0:T(8,128)(2,1)S(1)}, u32[]{:S(2)}, u32[]{:S(2)}) collective-permute-start(bf16[16,1024]{1,0:T(8,128)(2,1)S(1)} %slice_bitcast_fusion.13), channel_id=1, source_target_pairs={{0,2},{2,0},{4,6},{6,4},{8,10},{10,8},{12,14},{14,12},{1,3},{3,1},... | collective-permute-start | bytes 98312 | tf_op jit(solution)/shard_map/ppermute | solution.py:397
  68.0 8.3 %collective-permute-start.24 = (bf16[2,16,1024]{2,1,0:T(8,128)(2,1)S(1)}, bf16[2,16,1024]{2,1,0:T(8,128)(2,1)S(1)}, u32[]{:S(2)}, u32[]{:S(2)}) collective-permute-start(bf16[2,16,1024]{2,1,0:T(8,128)(2,1)S(1)} %get-tuple-element.40), channel_id=1, source_target_pairs={{0,8},{2,10},{4,12},{6,14},{8,0},{10,2},{12,4},{14,6},{1,9},{3,11}... | collective-permute-start | bytes 196616 | tf_op jit(solution)/shard_map/ppermute | solution.py:393
  70.2 6.9 %collective-permute-start.25 = (bf16[2,16,1024]{2,1,0:T(8,128)(2,1)S(1)}, bf16[2,16,1024]{2,1,0:T(8,128)(2,1)S(1)}, u32[]{:S(2)}, u32[]{:S(2)}) collective-permute-start(bf16[2,16,1024]{2,1,0:T(8,128)(2,1)S(1)} %get-tuple-element.41), channel_id=1, source_target_pairs={{0,12},{2,14},{4,8},{6,10},{8,4},{10,6},{12,0},{14,2},{1,13},{3,15... | collective-permute-start | bytes 196616 | tf_op jit(solution)/shard_map/ppermute | solution.py:393
  72.3 6.0 %collective-permute-start.27 = (bf16[16,1024]{1,0:T(8,128)(2,1)S(1)}, bf16[16,1024]{1,0:T(8,128)(2,1)S(1)}, u32[]{:S(2)}, u32[]{:S(2)}) collective-permute-start(bf16[16,1024]{1,0:T(8,128)(2,1)S(1)} %slice_bitcast_fusion.6), channel_id=1, source_target_pairs={{0,2},{2,0},{4,6},{6,4},{8,10},{10,8},{12,14},{14,12},{1,3},{3,1},... | collective-permute-start | bytes 98312 | tf_op jit(solution)/shard_map/ppermute | solution.py:397
  76.3 3.9 %collective-permute-start.28 = (bf16[16,1024]{1,0:T(8,128)(2,1)S(1)}, bf16[16,1024]{1,0:T(8,128)(2,1)S(1)}, u32[]{:S(2)}, u32[]{:S(2)}) collective-permute-start(bf16[16,1024]{1,0:T(8,128)(2,1)S(1)} %slice_bitcast_fusion.5), channel_id=1, source_target_pairs={{0,2},{2,0},{4,6},{6,4},{8,10},{10,8},{12,14},{14,12},{1,3},{3,1},... | collective-permute-start | bytes 98312 | tf_op jit(solution)/shard_map/ppermute | solution.py:397
  77.1 3.9 %collective-permute-start.29 = (bf16[16,1024]{1,0:T(8,128)(2,1)S(1)}, bf16[16,1024]{1,0:T(8,128)(2,1)S(1)}, u32[]{:S(2)}, u32[]{:S(2)}) collective-permute-start(bf16[16,1024]{1,0:T(8,128)(2,1)S(1)} %slice_bitcast_fusion.4), channel_id=1, source_target_pairs={{0,2},{2,0},{4,6},{6,4},{8,10},{10,8},{12,14},{14,12},{1,3},{3,1},... | collective-permute-start | bytes 98312 | tf_op jit(solution)/shard_map/ppermute | solution.py:397

commit v7 on v5

--- a/solution.py
+++ b/solution.py
@@ -134,8 +134,12 @@
     slot_of_hbm,
     lengths_hbm,
     x_hbm,
+    a_hbm,
+    b_hbm,
     meta,
     blocks,
+    a_out,
+    b_out,
     slot_at,
     ids,
     slot_of,
@@ -143,7 +147,16 @@
     x_ref,
     sems,
 ):
-    pairs = ((ids_hbm, ids), (slot_of_hbm, slot_of), (lengths_hbm, lengths), (x_hbm, x_ref))
+    width = x_hbm.shape[2]
+    start = pl.multiple_of(lax.axis_index("tensor") * width, width)
+    pairs = (
+        (ids_hbm, ids),
+        (slot_of_hbm, slot_of),
+        (lengths_hbm, lengths),
+        (x_hbm, x_ref),
+        (a_hbm.at[:, pl.ds(start, width)], a_out),
+        (b_hbm, b_out),
+    )
     copies = [pltpu.make_async_copy(a, b, sems.at[k]) for k, (a, b) in enumerate(pairs)]
     for copy in copies:
         copy.start()
@@ -184,10 +197,12 @@
         blocks[i, :, :wide] = packed[i * block : (i + 1) * block]
         slot = jnp.where(first, slot_at[i * CAP], slot_at[i * CAP + 1])
         blocks[i, :, wide:] = one_hot(lane_slot == slot)
+    for copy in copies[4:]:
+        copy.wait()
 
 
 def project_kernel(owners, heads, wide, first, a_ref, blocks, *refs):
-    core = lax.axis_index("tensor")
+    core = lax.axis_index("tensor") if a_ref.shape[1] > heads * wide else 0
     if first:
         part_ref, mask_ref = refs
     else:
@@ -251,7 +266,7 @@
     k_hbm,
     v_hbm,
     blocks,
-    out_ref,
+    out_hbm,
     outgoing,
     q_ref,
     kn_ref,
@@ -304,7 +319,7 @@
 
     head_at = rest(over(iota((total, width), 0), STEPS), heads)
     mask_ref[...] = one_hot(head_at == over(iota((total, width), 1), HD))
-    head_own = rest(over(iota((total, HD), 0), STEPS), heads)
+    head_own = rest(over(iota((QUAD * total, HD), 0), STEPS), heads)
     blank = jnp.zeros((CHUNK - fresh_rows, width), BF16)
     kn_ref[fresh_rows:, :] = blank
     vn_ref[fresh_rows:, :] = blank
@@ -333,60 +348,93 @@
                 copy.wait()
         extent = size * CHUNK
         position = iota((total, extent), 1)
-        results = []
-        for row in rows_in:
-            start = pl.multiple_of(row * pairs, pairs)
+        starts = [pl.multiple_of(row * pairs, pairs) for row in rows_in]
+        spreads = []
+        for start in starts:
             flat = q_buf[pl.ds(start, pairs), :]
             one = jnp.concatenate(
                 [flat[:, j * HD : (j + 1) * HD] for j in range(groups)], axis=0
             ).astype(BF16)
-            spread = jnp.concatenate([one] * heads, axis=1) * mask_ref[...]
-            cached = lax.dot_general(
-                spread, k_ref[row, :extent, :], contract, preferred_element_type=F32
+            spreads.append(jnp.concatenate([one] * heads, axis=1) * mask_ref[...])
+        cached = [
+            lax.dot_general(spread, k_ref[row, :extent, :], contract, preferred_element_type=F32)
+            for row, spread in zip(rows_in, spreads)
+        ]
+        fresh = lax.dot_general(
+            jnp.concatenate(spreads, axis=0), kn_ref[...], contract, preferred_element_type=F32
+        )
+        scores = jnp.concatenate(
+            [
+                jnp.concatenate(
+                    [
+                        jnp.where(position < span_of(row), cached[k], -jnp.inf),
+                        jnp.where(fresh_row == row, fresh[k * total : (k + 1) * total], -jnp.inf),
+                    ],
+                    axis=1,
+                )
+                for k, row in enumerate(rows_in)
+            ],
+            axis=0,
+        )
+        top = jnp.max(scores, axis=1, keepdims=True)
+        weights = jnp.exp2((scores - top) * factor)
+        share = 1.0 / jnp.sum(weights, axis=1, keepdims=True)
+        weights = weights.astype(BF16)
+        mixed = jnp.dot(weights[:, extent:], vn_ref[...], preferred_element_type=F32)
+        mixed = mixed + jnp.concatenate(
+            [
+                jnp.dot(
+                    weights[k * total : (k + 1) * total, :extent],
+                    v_ref[row, :extent, :],
+                    preferred_element_type=F32,
+                )
+                for k, row in enumerate(rows_in)
+            ],
+            axis=0,
+        )
+        own = mixed[:, :HD]
+        for c in range(1, heads):
+            own = jnp.where(head_own == c, mixed[:, c * HD : (c + 1) * HD], own)
+        own = own * share
+        for k, start in enumerate(starts):
+            one = own[k * total : (k + 1) * total]
+            o_buf[pl.ds(start, pairs), :] = jnp.concatenate(
+                [one[j * pairs : (j + 1) * pairs] for j in range(groups)], axis=1
             )
-            cached = jnp.where(position < span_of(row), cached, -jnp.inf)
-            fresh = lax.dot_general(spread, kn_ref[...], contract, preferred_element_type=F32)
-            fresh = jnp.where(fresh_row == row, fresh, -jnp.inf)
-            scores = jnp.concatenate([cached, fresh], axis=1)
-            top = jnp.max(scores, axis=1, keepdims=True)
-            weights = jnp.exp2((scores - top) * factor)
-            norm = jnp.sum(weights, axis=1, keepdims=True)
-            weights = weights.astype(BF16)
-            mixed = jnp.dot(
-                weights[:, :extent], v_ref[row, :extent, :], preferred_element_type=F32
-            ) + jnp.dot(weights[:, extent:], vn_ref[...], preferred_element_type=F32)
-            own = mixed[:, :HD]
-            for c in range(1, heads):
-                own = jnp.where(head_own == c, mixed[:, c * HD : (c + 1) * HD], own)
-            results.append((start, own * (1.0 / norm)))
-        for start, own in results:
-            o_buf[pl.ds(start, pairs), :] = jnp.concatenate(
-                [own[j * pairs : (j + 1) * pairs] for j in range(groups)], axis=1
-            )
 
     quads(row_of, span_of, rows, chunks, attend)
 
     mixed = o_buf[...].astype(BF16)
+    final = exact(by_pair_matrix(heads, rows), mixed)
+    for c in range(heads):
+        for s in range(STEPS):
+            at = (c * STEPS + s) * rows
+            q_ref[s, :, c * wide : (c + 1) * wide] = final[at : at + rows]
+    result = pltpu.make_async_copy(q_ref, out_hbm, sems.at[0])
+    result.start()
     packed = exact(pack_matrix(meta, owners, heads, rows, True), mixed)
     block = heads * CAP * STEPS
     for i in range(owners):
         outgoing[i] = packed[i * block : (i + 1) * block]
-    final = exact(by_pair_matrix(heads, rows), mixed)
-    for c in range(heads):
-        for s in range(STEPS):
-            at = (c * STEPS + s) * rows
-            out_ref[s, :, c * wide : (c + 1) * wide] = final[at : at + rows]
-
-
-def collect_kernel(owners, heads, meta, blocks, out_ref):
+    result.wait()
+
+
+def collect_kernel(owners, heads, meta, blocks, out_hbm, out_ref, sems):
     rows = out_ref.shape[1]
     wide = out_ref.shape[2] // heads
+    span = STEPS * rows
     arrived = jnp.concatenate([blocks[i] for i in range(owners)], axis=0)
-    values = exact(unpack_matrix(meta, owners, heads, rows, False), arrived)
+    spread = unpack_matrix(meta, owners, heads, rows, False)
+    copies = []
     for c in range(heads):
+        values = exact(spread[c * span : (c + 1) * span], arrived)
         for s in range(STEPS):
-            top = (c * STEPS + s) * rows
-            out_ref[s, :, c * wide : (c + 1) * wide] = values[top : top + rows]
+            out_ref[s, :, c * wide : (c + 1) * wide] = values[s * rows : (s + 1) * rows]
+        part = (slice(None), slice(None), pl.ds(c * wide, wide))
+        copies.append(pltpu.make_async_copy(out_ref.at[part], out_hbm.at[part], sems.at[c]))
+        copies[-1].start()
+    for copy in copies:
+        copy.wait()
 
 
 def exchange(blocks):
@@ -432,25 +480,30 @@
     small = pltpu.CompilerParams(vmem_limit_bytes=16 * 1024 * 1024)
 
     sent = shape((owners, block, wide), BF16)
-    meta, blocks = pl.pallas_call(
+    meta, blocks, a_near, b_near = pl.pallas_call(
         functools.partial(dispatch_kernel, owners, heads, adapt, rank),
         out_shape=[
             shape((3 * rows + owners * CAP,), I32),
             shape((owners, block, wide + lanes), BF16),
+            pltpu.VMEM((lanes, width), BF16),
+            pltpu.VMEM((lanes, width), BF16),
         ],
-        in_specs=[HBM] * 4,
-        out_specs=[SMEM, VMEM],
+        in_specs=[HBM] * 6,
+        out_specs=[SMEM] + [VMEM] * 3,
         scratch_shapes=[
             pltpu.SMEM((owners * CAP,), I32),
             pltpu.SMEM(adapter_ids.shape, I32),
             pltpu.SMEM(slot_of.shape, I32),
             pltpu.SMEM(lengths.shape, I32),
             pltpu.VMEM(x_in.shape, BF16),
-            pltpu.SemaphoreType.DMA((4,)),
+            pltpu.SemaphoreType.DMA((6,)),
         ],
         compiler_params=small,
         name="dispatch",
-    )(in_hbm(adapter_ids), in_hbm(slot_of), in_hbm(lengths), in_hbm(x_in))
+    )(
+        *map(in_hbm, (adapter_ids, slot_of, lengths, x_in, flat(a_query))),
+        in_hbm(b_query.reshape(lanes, width)),
+    )
 
     arrived = exchange(blocks)
     part, mask = pl.pallas_call(
@@ -460,7 +513,7 @@
         out_specs=[VMEM] * 2,
         compiler_params=small,
         name="project_query",
-    )(flat(a_query), arrived)
+    )(a_near, arrived)
 
     def expand(part, b_store, name):
         return pl.pallas_call(
@@ -470,15 +523,15 @@
             out_specs=VMEM,
             compiler_params=small,
             name=name,
-        )(part, swap_cores(part), b_store.reshape(lanes, width))
-
-    returned = exchange(expand(part, b_query, "expand_query"))
+        )(part, swap_cores(part), b_store)
+
+    returned = exchange(expand(part, b_near, "expand_query"))
 
     attn_out, outgoing = pl.pallas_call(
         functools.partial(attend_kernel, owners, heads),
-        out_shape=[pltpu.VMEM((STEPS, rows, width), BF16), sent],
+        out_shape=[shape((STEPS, rows, width), BF16), sent],
         in_specs=[SMEM] + [HBM] * 5 + [VMEM],
-        out_specs=[VMEM] * 2,
+        out_specs=[HBM, VMEM],
         scratch_shapes=[
             pltpu.VMEM(q_base.shape, BF16),
             pltpu.VMEM((CHUNK, heads * HD), BF16),
@@ -505,12 +558,16 @@
         compiler_params=small,
         name="project_output",
     )(flat(a_output), arrived, mask)
-    returned = exchange(expand(part, b_output, "expand_output"))
+    returned = exchange(expand(part, b_output.reshape(lanes, width), "expand_output"))
     adapter_out = pl.pallas_call(
         functools.partial(collect_kernel, owners, heads),
         out_shape=shape((STEPS, rows, width), BF16),
         in_specs=[SMEM, VMEM],
-        out_specs=VMEM,
+        out_specs=HBM,
+        scratch_shapes=[
+            pltpu.VMEM((STEPS, rows, width), BF16),
+            pltpu.SemaphoreType.DMA((heads,)),
+        ],
         compiler_params=small,
         name="collect",
     )(meta, returned)

time: 76.2 us -> 71 us (0.932)
  blocking collectives: 40.9 us -> 53.5 us
  waiting for transfers between devices: 11 us -> 2.4 us
  starting transfers between devices: 3.59 us -> 0.01 us
  local copies, waits for them, and re-layouts: 3.53 us -> 0.01 us
  Pallas kernels: 15.7 us -> 13.8 us
    all_to_all x3 -> x4, blocking collectives: 40.9 us -> 53.5 us  [exchange(): lax.all_to_all(blocks, 'store', split_axis=0, concat_axis=0, tiled=True)]
    all_to_all x1 -> x0, waiting for transfers between devices: 8.59 us -> none  [exchange(): lax.all_to_all(blocks, 'store', split_axis=0, concat_axis=0, tiled=True)]
    all_to_all x1 -> x0, starting transfers between devices: 3.59 us -> none  [exchange(): lax.all_to_all(blocks, 'store', split_axis=0, concat_axis=0, tiled=True)]
    unnamed x9 -> x4, local copies, waits for them, and re-layouts: 3.53 us -> 0.01 us
    pallas_call x1, Pallas kernels: 9.58 us -> 7.97 us  [shards(): pl.pallas_call(functools.partial(attend_kernel, owners, heads), out_shape...]
  transfers between devices with their start and end apart: 3 -> 2, of which waited for: 3 -> 2; matrix products, arithmetic and copies ran while one was open for 1% -> 0% of each run, Pallas kernels for 0% -> 0%
where the time goes in v7:
time: 71 us; the launch traced here: 70.5 us
  blocking collectives  53.5 us (75%)
  Pallas kernels  13.8 us (19%)
  waiting for transfers between devices  2.4 us (3%)
    all_to_all x4, blocking collectives, exchange(): lax.all_to_all(blocks, 'store', split_axis=0, concat_axis=0, tiled=True)  53.5 us
    pallas_call x1, Pallas kernels, shards(): pl.pallas_call(functools.partial(attend_kernel, owners, heads), out_shape...  7.97 us
    ppermute x2, waiting for transfers between devices, swap_cores(): return lax.ppermute(part, 'tensor', [(0, 1), (1, 0)])  2.4 us
    pallas_call x1, Pallas kernels, shards(): pl.pallas_call(functools.partial(dispatch_kernel, owners, heads, adapt, r...  2.28 us
    pallas_call x1, Pallas kernels, shards(): pl.pallas_call(functools.partial(collect_kernel, owners, heads), out_shap...  1.49 us
  transfers between devices with their start and end apart: 2, of which 2 were waited for; matrix products, arithmetic and copies ran while one was open for 0% of the time, Pallas kernels for 0%

profile of v7, /device:TPU:0, one launch (start us, length us, event | category | flops | bytes accessed | tf_op | source)
XLA Modules:
  0.0 70.5 jit_solution(2458093353073909940)
XLA Ops:
  0.6 2.3 %dispatch.1 = (s32[64]{0:T(128)S(1)}, bf16[8,16,1152]{2,1,0:T(8,128)(2,1)S(1)}, bf16[128,4096]{1,0:T(8,128)(2,1)S(1)}, bf16[128,4096]{1,0:T(8,128)(2,1)S(1)}) custom-call(s32[16]{0:T(128)} %ids_hbm.1, s32[64]{0:T(128)} %slot_of_hbm.1, s32[16]{0:T(128)} %lengths_hbm.1, bf16[2,16,4096]{2,1,0:T(8,128)(2,1)} %x_hbm.1, bf16[128,8192]{1,0:T(8,128)(2,1)} %bitcast.10, ...), custom_call_target="tpu_custom_call" | custom-call | tf_op jit(solution)/shard_map/dispatch/pallas_call | solution.py:483
  2.9 17.4 %all_to_all.20.blocks = bf16[8,16,1152]{2,1,0:T(8,128)(2,1)S(1)} all-to-all(bf16[8,16,1152]{2,1,0:T(8,128)(2,1)S(1)} %get-tuple-element.12), channel_id=1, replica_groups=mesh['parts'=2,'store'=8,'tensor'=2] {'store'}, dimensions={0} | all-to-all | bytes 589824 | tf_op jit(solution)/shard_map/all_to_all | solution.py:441
  20.3 0.6 project_query.1
  20.9 0.0 collective-permute-start
  20.9 1.2 %collective-permute-done.other = f32[32,128]{1,0:T(8,128)S(1)} collective-permute-done((f32[32,128]{1,0:T(8,128)S(1)}, f32[32,128]{1,0:T(8,128)S(1)}, u32[]{:S(2)}, u32[]{:S(2)}) %collective-permute-start) | collective-permute-done | bytes 16416 | tf_op jit(solution)/shard_map/ppermute | solution.py:449
  22.2 0.5 expand_query.1
  22.6 11.9 %all_to_all.21.blocks = bf16[8,16,1024]{2,1,0:T(8,128)(2,1)S(1)} all-to-all(bf16[8,16,1024]{2,1,0:T(8,128)(2,1)S(1)} %expand_query.1), channel_id=1, replica_groups=mesh['parts'=2,'store'=8,'tensor'=2] {'store'}, dimensions={0} | all-to-all | bytes 524288 | tf_op jit(solution)/shard_map/all_to_all | solution.py:441
  34.6 0.0 copy-start
  34.6 0.0 copy-start.1
  34.6 8.0 %attend.1 = (bf16[2,16,4096]{2,1,0:T(8,128)(2,1)}, bf16[8,16,1024]{2,1,0:T(8,128)(2,1)S(1)}) custom-call(s32[64]{0:T(128)S(1)} %get-tuple-element.10.meta, bf16[2,16,4096]{2,1,0:T(8,128)(2,1)} %q_hbm.1, bf16[2,16,512]{2,1,0:T(8,128)(2,1)} %kn_hbm.1, bf16[2,16,512]{2,1,0:T(8,128)(2,1)} %vn_hbm.1, bf16[16,512,512]{2,1,0:T(8,128)(2,1)} %k_hbm.1, ...), custom_call_target="tpu_custom_call" | custom-call | tf_op jit(solution)/shard_map/attend/pallas_call | solution.py:530
  42.5 11.5 %all_to_all.22.blocks = bf16[8,16,1024]{2,1,0:T(8,128)(2,1)S(1)} all-to-all(bf16[8,16,1024]{2,1,0:T(8,128)(2,1)S(1)} %get-tuple-element.16), channel_id=1, replica_groups=mesh['parts'=2,'store'=8,'tensor'=2] {'store'}, dimensions={0} | all-to-all | bytes 524288 | tf_op jit(solution)/shard_map/all_to_all | solution.py:441
  54.1 0.0 copy-done
  54.1 0.6 project_output.1.mine
  54.7 0.0 collective-permute-start.1
  54.7 1.2 %collective-permute-done.1.other = f32[32,128]{1,0:T(8,128)S(1)} collective-permute-done((f32[32,128]{1,0:T(8,128)S(1)}, f32[32,128]{1,0:T(8,128)S(1)}, u32[]{:S(2)}, u32[]{:S(2)}) %collective-permute-start.1) | collective-permute-done | bytes 16416 | tf_op jit(solution)/shard_map/ppermute | solution.py:449
  55.9 0.0 copy-done.1
  55.9 0.5 expand_output.1
  56.3 12.6 %all_to_all.23.blocks = bf16[8,16,1024]{2,1,0:T(8,128)(2,1)S(1)} all-to-all(bf16[8,16,1024]{2,1,0:T(8,128)(2,1)S(1)} %expand_output.1), channel_id=1, replica_groups=mesh['parts'=2,'store'=8,'tensor'=2] {'store'}, dimensions={0} | all-to-all | bytes 524288 | tf_op jit(solution)/shard_map/all_to_all | solution.py:441
  69.0 1.5 %collect.1 = bf16[2,16,4096]{2,1,0:T(8,128)(2,1)} custom-call(s32[64]{0:T(128)S(1)} %get-tuple-element.10.meta, bf16[8,16,1024]{2,1,0:T(8,128)(2,1)S(1)} %all_to_all.23.blocks), custom_call_target="tpu_custom_call" | custom-call | tf_op jit(solution)/shard_map/collect/pallas_call | solution.py:562
Async XLA Ops:
  20.9 1.2 %collective-permute-start = (f32[32,128]{1,0:T(8,128)S(1)}, f32[32,128]{1,0:T(8,128)S(1)}, u32[]{:S(2)}, u32[]{:S(2)}) collective-permute-start(f32[32,128]{1,0:T(8,128)S(1)} %get-tuple-element.13.mine), channel_id=1, source_target_pairs={{0,1},{1,0},{2,3},{3,2},{4,5},{5,4},{6,7},{7,6},{8,9},{9,8},{10,11... | collective-permute-start | bytes 49160 | tf_op jit(solution)/shard_map/ppermute | solution.py:449
  34.6 19.5 %copy-start = (bf16[8192,8,16]{0,2,1:T(8,128)(2,1)S(1)}, bf16[8192,8,16]{0,2,1:T(8,128)(2,1)}, u32[]{:S(2)}) copy-start(bf16[8192,8,16]{0,2,1:T(8,128)(2,1)} %param.24) | copy-start | bytes 6291460
  34.6 21.3 %copy-start.1 = (bf16[8,16,4096]{2,1,0:T(8,128)(2,1)S(1)}, bf16[8,16,4096]{2,1,0:T(8,128)(2,1)}, u32[]{:S(2)}) copy-start(bf16[8,16,4096]{2,1,0:T(8,128)(2,1)} %param.25) | copy-start | bytes 3145732
  54.7 1.2 %collective-permute-start.1 = (f32[32,128]{1,0:T(8,128)S(1)}, f32[32,128]{1,0:T(8,128)S(1)}, u32[]{:S(2)}, u32[]{:S(2)}) collective-permute-start(f32[32,128]{1,0:T(8,128)S(1)} %project_output.1.mine), channel_id=1, source_target_pairs={{0,1},{1,0},{2,3},{3,2},{4,5},{5,4},{6,7},{7,6},{8,9},{9,8},{10,11... | collective-permute-start | bytes 49160 | tf_op jit(solution)/shard_map/ppermute | solution.py:449

commit v8 on v7

v8 whole, which is shorter than its diff:
```python
import functools
import math

import jax
import jax.numpy as jnp
from jax import lax
from jax.experimental import pallas as pl
from jax.experimental.pallas import tpu as pltpu
from jax.sharding import PartitionSpec as P

HD = 128
CAP = 2
STEPS = 2
CHUNK = 128
QUAD = 4
BF16 = jnp.bfloat16
F32 = jnp.float32
I32 = jnp.int32
VMEM = pl.BlockSpec(memory_space=pltpu.VMEM)
SMEM = pl.BlockSpec(memory_space=pltpu.SMEM)
HBM = pl.BlockSpec(memory_space=pltpu.HBM)


def iota(shape, dim):
    return lax.broadcasted_iota(I32, shape, dim)


def over(x, n):
    return lax.shift_right_logical(x, jnp.full_like(x, n.bit_length() - 1)) if n & (n - 1) == 0 else x // n


def rest(x, n):
    return x & (n - 1) if n & (n - 1) == 0 else x % n


def one_hot(hits):
    return jnp.where(hits, 1.0, 0.0).astype(BF16)


def stacked(ref, heads, wide):
    return jnp.concatenate(
        [ref[s, :, c * wide : (c + 1) * wide] for c in range(heads) for s in range(STEPS)], axis=0
    )


def gather_matrix(meta, base, owners, heads, rows):
    pairs = heads * STEPS
    shape = (pairs, pairs * rows)
    offset = iota(shape, 1) - iota(shape, 0) * rows
    parts = []
    for i in range(owners):
        row = meta[base + i]
        parts.append(one_hot(offset == jnp.where(row >= 0, row, -rows * pairs)))
    return jnp.concatenate(parts, axis=0)


def scatter_matrix(meta, owners, heads, rows):
    pairs = heads * STEPS
    shape = (rows, CAP * owners * pairs)
    at = iota(shape, 0)
    spot = jnp.zeros(shape, I32)
    for r in range(rows):
        spot = jnp.where(at == r, meta[r] * pairs, spot)
    offset = iota(shape, 1) - spot
    return jnp.concatenate([one_hot(offset == pair) for pair in range(pairs)], axis=0)


def regroup_matrix(owners, heads):
    total = owners * heads * STEPS
    at = iota((total, total), 0)
    head = over(at, owners * STEPS)
    owner = rest(over(at, STEPS), owners)
    return one_hot(
        iota((total, total), 1) == owner * (heads * STEPS) + head * STEPS + rest(at, STEPS)
    )


def ungroup_matrix(owners, heads):
    total = owners * heads * STEPS
    at = iota((total, total), 0)
    owner = over(at, heads * STEPS)
    head = rest(over(at, STEPS), heads)
    return one_hot(
        iota((total, total), 1) == head * (owners * STEPS) + owner * STEPS + rest(at, STEPS)
    )


def exact(matrix, values):
    return jnp.dot(matrix, values, preferred_element_type=F32).astype(BF16)


def dispatch_kernel(
    owners,
    heads,
    adapt,
    rank,
    ids_hbm,
    slot_of_hbm,
    lengths_hbm,
    x_hbm,
    meta,
    first_out,
    second_out,
    slot_at,
    ids,
    slot_of,
    lengths,
    x_ref,
    sems,
):
    pairs = (
        (ids_hbm, ids),
        (slot_of_hbm, slot_of),
        (lengths_hbm, lengths),
        (x_hbm, x_ref),
    )
    copies = [pltpu.make_async_copy(a, b, sems.at[k]) for k, (a, b) in enumerate(pairs)]
    for copy in copies:
        copy.start()
    rows = x_ref.shape[1]
    wide = x_ref.shape[2] // heads
    for copy in copies[:3]:
        copy.wait()
    places = owners * CAP
    row_at = rows
    order = rows + places
    spans = rows + 2 * places
    for p in range(places):
        meta[row_at + p] = -1
        meta[spans + p] = 0
        slot_at[p] = -1
    for r in range(rows):
        slot = slot_of[ids[r]]
        owner = over(slot, adapt)
        place = owner + jnp.where(meta[row_at + owner] >= 0, owners, 0)
        meta[row_at + place] = r
        meta[spans + place] = lengths[r]
        slot_at[place] = rest(slot, adapt)
        meta[r] = place
    for k in range(CAP):
        sizes = [meta[spans + k * owners + i] for i in range(owners)]
        for r in range(owners):
            ahead = jnp.int32(0)
            for q in range(owners):
                if q != r:
                    shorter = sizes[q] <= sizes[r] if q < r else sizes[q] < sizes[r]
                    ahead = ahead + jnp.where(shorter, 1, 0)
            meta[order + k * owners + ahead] = r
    copies[3].wait()
    block = heads * STEPS
    values = stacked(x_ref, heads, wide)
    lane_slot = over(iota((block, adapt * rank), 1), rank)
    for k, out in enumerate((first_out, second_out)):
        base = k * owners
        packed = exact(gather_matrix(meta, row_at + base, owners, heads, rows), values)
        for i in range(owners):
            out[i, :, :wide] = packed[i * block : (i + 1) * block]
            out[i, :, wide:] = one_hot(lane_slot == slot_at[base + i])


def project_kernel(owners, heads, wide, first, a_hbm, blocks, *refs):
    if first:
        part_ref, mask_ref, a_ref, sem = refs
    else:
        mask_in, part_ref, a_ref, sem = refs
    width = heads * wide
    start = pl.multiple_of(lax.axis_index("tensor") * width, width)
    store = pltpu.make_async_copy(a_hbm.at[:, pl.ds(start, width)], a_ref, sem)
    store.start()
    grouped = regroup_matrix(owners, heads)
    items = owners * STEPS
    arrived = jnp.concatenate([blocks[i, :, :wide] for i in range(owners)], axis=0)
    arrived = exact(grouped, arrived)
    if first:
        masks = jnp.concatenate([blocks[i, :, wide:] for i in range(owners)], axis=0)
        mask = jnp.dot(grouped[:items], masks, preferred_element_type=F32)
        mask_ref[...] = mask
    else:
        mask = mask_in[...]
    store.wait()
    total = jnp.zeros(mask.shape, F32)
    for c in range(heads):
        total = total + lax.dot_general(
            arrived[c * items : (c + 1) * items],
            a_ref[:, c * wide : (c + 1) * wide],
            (((1,), (1,)), ((), ())),
            preferred_element_type=F32,
        )
    part_ref[...] = total * mask


def expand_kernel(owners, heads, wide, mine, other, b_hbm, blocks, b_ref, sem):
    store = pltpu.make_async_copy(b_hbm, b_ref, sem)
    store.start()
    low_rank = (mine[...] + other[...]).astype(BF16)
    matrix = ungroup_matrix(owners, heads)
    store.wait()
    pieces = []
    for c in range(heads):
        product = jnp.dot(
            low_rank, b_ref[:, c * wide : (c + 1) * wide], preferred_element_type=F32
        )
        pieces.append((2.0 * product).astype(BF16))
    back = exact(matrix, jnp.concatenate(pieces, axis=0))
    block = heads * STEPS
    for i in range(owners):
        blocks[i] = back[i * block : (i + 1) * block]


def quads(row_of, span_of, rows, sizes, action):
    def body(quad, carry):
        amount = over(span_of(row_of(quad * QUAD + QUAD - 1)) + (CHUNK - 1), CHUNK)
        for size in range(1, sizes + 1):

            @pl.when(amount == size)
            def _():
                action([row_of(quad * QUAD + j) for j in range(QUAD)], size)

        return carry

    lax.fori_loop(0, rows // QUAD, body, 0)


def attend_kernel(
    owners,
    heads,
    chain,
    meta,
    q_hbm,
    kn_hbm,
    vn_hbm,
    k_hbm,
    v_hbm,
    blocks,
    outgoing,
    q_ref,
    kn_ref,
    vn_ref,
    k_ref,
    v_ref,
    mask_ref,
    q_buf,
    o_buf,
    k_sem,
    v_sem,
    sems,
):
    rows = q_hbm.shape[1]
    wide = q_hbm.shape[2] // heads
    groups = wide // HD
    pairs = heads * STEPS
    total = groups * pairs
    width = heads * HD
    fresh_rows = STEPS * rows

    singles = [pltpu.make_async_copy(q_hbm, q_ref, sems.at[0])]
    for k, (source, target) in enumerate(((kn_hbm, kn_ref), (vn_hbm, vn_ref))):
        for t in range(STEPS):
            part = target.at[pl.ds(t * rows, rows)]
            singles.append(pltpu.make_async_copy(source.at[t], part, sems.at[1 + k * STEPS + t]))
    for copy in singles:
        copy.start()

    places = owners * CAP
    own_base = chain * owners

    def slot_at(place):
        return meta[rows + places + own_base + place]

    def span_of(slot):
        return meta[rows + 2 * places + own_base + slot]

    def row_of(slot):
        return jnp.maximum(meta[rows + own_base + slot], 0)

    def copies(slot, size):
        part = pl.ds(0, size * CHUNK)
        row = row_of(slot)
        return (
            pltpu.make_async_copy(k_hbm.at[row, part], k_ref.at[slot, part], k_sem.at[slot]),
            pltpu.make_async_copy(v_hbm.at[row, part], v_ref.at[slot, part], v_sem.at[slot]),
        )

    def begin(slots, size):
        for slot in slots:
            for copy in copies(slot, size):
                copy.start()

    chunks = k_hbm.shape[1] // CHUNK
    quads(slot_at, span_of, owners, chunks, begin)

    head_at = rest(over(iota((total, width), 0), STEPS), heads)
    mask_ref[...] = one_hot(head_at == over(iota((total, width), 1), HD))
    head_own = rest(over(iota((QUAD * total, HD), 0), STEPS), heads)
    blank = jnp.zeros((CHUNK - fresh_rows, width), BF16)
    kn_ref[fresh_rows:, :] = blank
    vn_ref[fresh_rows:, :] = blank

    o_buf[...] = jnp.zeros(o_buf.shape, F32)
    delta = jnp.concatenate([blocks[i] for i in range(owners)], axis=0).astype(F32)
    gather = gather_matrix(meta, rows + own_base, owners, heads, rows)
    for copy in singles:
        copy.wait()
    q_buf[...] = jnp.dot(gather, stacked(q_ref, heads, wide), preferred_element_type=F32) + delta

    factor = math.log2(math.e) / math.sqrt(HD)
    fresh_shape = (total, CHUNK)
    fresh_at = iota(fresh_shape, 1)
    fresh_step = over(fresh_at, rows)
    fresh_row = jnp.where(fresh_step <= rest(iota(fresh_shape, 0), STEPS), rest(fresh_at, rows), rows)
    contract = (((1,), (1,)), ((), ()))

    def attend(slots, size):
        for slot in slots:
            for copy in copies(slot, size):
                copy.wait()
        extent = size * CHUNK
        position = iota((total, extent), 1)
        starts = [pl.multiple_of(slot * pairs, pairs) for slot in slots]
        spreads = []
        for start in starts:
            flat = q_buf[pl.ds(start, pairs), :]
            one = jnp.concatenate(
                [flat[:, j * HD : (j + 1) * HD] for j in range(groups)], axis=0
            ).astype(BF16)
            spreads.append(jnp.concatenate([one] * heads, axis=1) * mask_ref[...])
        cached = [
            lax.dot_general(spread, k_ref[slot, :extent, :], contract, preferred_element_type=F32)
            for slot, spread in zip(slots, spreads)
        ]
        fresh = lax.dot_general(
            jnp.concatenate(spreads, axis=0), kn_ref[...], contract, preferred_element_type=F32
        )
        scores = jnp.concatenate(
            [
                jnp.concatenate(
                    [
                        jnp.where(position < span_of(slot), cached[k], -jnp.inf),
                        jnp.where(fresh_row == row_of(slot), fresh[k * total : (k + 1) * total], -jnp.inf),
                    ],
                    axis=1,
                )
                for k, slot in enumerate(slots)
            ],
            axis=0,
        )
        top = jnp.max(scores, axis=1, keepdims=True)
        weights = jnp.exp2((scores - top) * factor)
        share = 1.0 / jnp.sum(weights, axis=1, keepdims=True)
        weights = weights.astype(BF16)
        mixed = jnp.dot(weights[:, extent:], vn_ref[...], preferred_element_type=F32)
        mixed = mixed + jnp.concatenate(
            [
                jnp.dot(
                    weights[k * total : (k + 1) * total, :extent],
                    v_ref[slot, :extent, :],
                    preferred_element_type=F32,
                )
                for k, slot in enumerate(slots)
            ],
            axis=0,
        )
        own = mixed[:, :HD]
        for c in range(1, heads):
            own = jnp.where(head_own == c, mixed[:, c * HD : (c + 1) * HD], own)
        own = own * share
        for k, start in enumerate(starts):
            one = own[k * total : (k + 1) * total]
            o_buf[pl.ds(start, pairs), :] = jnp.concatenate(
                [one[j * pairs : (j + 1) * pairs] for j in range(groups)], axis=1
            )

    quads(slot_at, span_of, owners, chunks, attend)

    mixed = o_buf[...].astype(BF16)
    for i in range(owners):
        outgoing[i] = mixed[i * pairs : (i + 1) * pairs]


def collect_kernel(owners, heads, meta, first, second, out_hbm, out_ref, sems):
    rows = out_ref.shape[1]
    wide = out_ref.shape[2] // heads
    span = STEPS * rows
    arrived = jnp.concatenate([b[i] for b in (first, second) for i in range(owners)], axis=0)
    spread = scatter_matrix(meta, owners, heads, rows)
    copies = []
    for c in range(heads):
        values = exact(spread[c * span : (c + 1) * span], arrived)
        for s in range(STEPS):
            out_ref[s, :, c * wide : (c + 1) * wide] = values[s * rows : (s + 1) * rows]
        part = (slice(None), slice(None), pl.ds(c * wide, wide))
        copies.append(pltpu.make_async_copy(out_ref.at[part], out_hbm.at[part], sems.at[c]))
        copies[-1].start()
    for copy in copies:
        copy.wait()


def exchange(blocks):
    return lax.all_to_all(blocks, "store", split_axis=0, concat_axis=0, tiled=True)


def in_hbm(array):
    return pltpu.with_memory_space_constraint(array, pltpu.HBM)


def swap_cores(part):
    return lax.ppermute(part, "tensor", [(0, 1), (1, 0)])


def shards(
    x_in,
    q_base,
    k_new,
    v_new,
    cache_k,
    cache_v,
    lengths,
    adapter_ids,
    slot_of,
    a_query,
    b_query,
    a_output,
    b_output,
):
    owners = lax.axis_size("store")
    rows = x_in.shape[1]
    width = x_in.shape[2]
    heads = cache_k.shape[2] // HD
    wide = width // heads
    adapt, rank = a_query.shape[1:]
    lanes = adapt * rank
    block = heads * STEPS
    items = owners * STEPS

    def flat(a_store):
        return in_hbm(jnp.transpose(a_store, (1, 2, 0)).reshape(lanes, a_store.shape[0]))

    shape = jax.ShapeDtypeStruct
    small = pltpu.CompilerParams(vmem_limit_bytes=16 * 1024 * 1024)
    sent = shape((owners, block, wide), BF16)
    marked = shape((owners, block, wide + lanes), BF16)
    meta, *chains = pl.pallas_call(
        functools.partial(dispatch_kernel, owners, heads, adapt, rank),
        out_shape=[shape((rows + 3 * owners * CAP,), I32), marked, marked],
        in_specs=[HBM] * 4,
        out_specs=[SMEM] + [VMEM] * 2,
        scratch_shapes=[
            pltpu.SMEM((owners * CAP,), I32),
            pltpu.SMEM(adapter_ids.shape, I32),
            pltpu.SMEM(slot_of.shape, I32),
            pltpu.SMEM(lengths.shape, I32),
            pltpu.VMEM(x_in.shape, BF16),
            pltpu.SemaphoreType.DMA((4,)),
        ],
        compiler_params=small,
        name="dispatch",
    )(*map(in_hbm, (adapter_ids, slot_of, lengths, x_in)))

    store_scratch = [pltpu.VMEM((lanes, width), BF16), pltpu.SemaphoreType.DMA(())]

    def expand(part, b_store, name):
        return pl.pallas_call(
            functools.partial(expand_kernel, owners, heads, wide),
            out_shape=sent,
            in_specs=[VMEM] * 2 + [HBM],
            out_specs=VMEM,
            scratch_shapes=store_scratch,
            compiler_params=small,
            name=name,
        )(part, swap_cores(part), in_hbm(b_store.reshape(lanes, width)))

    def attend(chain, returned):
        return pl.pallas_call(
            functools.partial(attend_kernel, owners, heads, chain),
            out_shape=sent,
            in_specs=[SMEM] + [HBM] * 5 + [VMEM],
            out_specs=VMEM,
            scratch_shapes=[
                pltpu.VMEM(q_base.shape, BF16),
                pltpu.VMEM((CHUNK, heads * HD), BF16),
                pltpu.VMEM((CHUNK, heads * HD), BF16),
                pltpu.VMEM((owners,) + cache_k.shape[1:], BF16),
                pltpu.VMEM((owners,) + cache_v.shape[1:], BF16),
                pltpu.VMEM((STEPS * wide // HD * heads, heads * HD), BF16),
                pltpu.VMEM((owners * block, wide), F32),
                pltpu.VMEM((owners * block, wide), F32),
                pltpu.SemaphoreType.DMA((owners,)),
                pltpu.SemaphoreType.DMA((owners,)),
                pltpu.SemaphoreType.DMA((1 + 2 * STEPS,)),
            ],
            compiler_params=pltpu.CompilerParams(vmem_limit_bytes=32 * 1024 * 1024),
            name=f"attend_{chain}",
        )(meta, *map(in_hbm, (q_base, k_new, v_new, cache_k, cache_v)), returned)

    def collect(blocks, name):
        return pl.pallas_call(
            functools.partial(collect_kernel, owners, heads),
            out_shape=shape((STEPS, rows, width), BF16),
            in_specs=[SMEM] + [VMEM] * CAP,
            out_specs=HBM,
            scratch_shapes=[
                pltpu.VMEM((STEPS, rows, width), BF16),
                pltpu.SemaphoreType.DMA((heads,)),
            ],
            compiler_params=small,
            name=name,
        )(meta, *blocks)

    attended, finished = [], []
    for chain, blocks in enumerate(chains):
        part, mask = pl.pallas_call(
            functools.partial(project_kernel, owners, heads, wide, True),
            out_shape=[shape((items, lanes), F32)] * 2,
            in_specs=[HBM, VMEM],
            out_specs=[VMEM] * 2,
            scratch_shapes=store_scratch,
            compiler_params=small,
            name=f"project_query_{chain}",
        )(flat(a_query), exchange(blocks))
        returned = exchange(expand(part, b_query, f"expand_query_{chain}"))
        outgoing = attend(chain, returned)
        attended.append(outgoing)
        part = pl.pallas_call(
            functools.partial(project_kernel, owners, heads, wide, False),
            out_shape=shape((items, lanes), F32),
            in_specs=[HBM] + [VMEM] * 2,
            out_specs=VMEM,
            scratch_shapes=store_scratch,
            compiler_params=small,
            name=f"project_output_{chain}",
        )(flat(a_output), exchange(outgoing), mask)
        finished.append(exchange(expand(part, b_output, f"expand_output_{chain}")))
    return (collect(attended, "collect_attended"), collect(finished, "collect_adapters"))


def solution(mesh):
    in_specs = (
        P(None, ("parts", "store"), "tensor"),
        P(None, ("parts", "store"), "tensor"),
        P(None, ("parts", "store"), "tensor"),
        P(None, ("parts", "store"), "tensor"),
        P(("parts", "store"), None, "tensor"),
        P(("parts", "store"), None, "tensor"),
        P(("parts", "store")),
        P(("parts", "store")),
        P("parts"),
        P(None, "store", None),
        P("store", None, "tensor"),
        P(None, "store", None),
        P("store", None, "tensor"),
    )
    out_specs = (P(None, ("parts", "store"), "tensor"), P(None, ("parts", "store"), "tensor"))
    return jax.shard_map(shards, mesh=mesh, in_specs=in_specs, out_specs=out_specs, check_vma=False)
```

time: 71 us -> 98 us (1.38)
  blocking collectives: 53.5 us -> 14.5 us
  starting transfers between devices: 0.01 us -> 27.7 us
  waiting for transfers between devices: 2.4 us -> 23.4 us
  Pallas kernels: 13.8 us -> 31 us
    all_to_all x4 -> x1, blocking collectives: 53.5 us -> 14.5 us  [exchange(): lax.all_to_all(blocks, 'store', split_axis=0, concat_axis=0, tiled=True)]
    all_to_all x0 -> x7, starting transfers between devices: none -> 27.4 us  [exchange(): lax.all_to_all(blocks, 'store', split_axis=0, concat_axis=0, tiled=True)]
    all_to_all x0 -> x7, waiting for transfers between devices: none -> 18.8 us  [exchange(): lax.all_to_all(blocks, 'store', split_axis=0, concat_axis=0, tiled=True)]
    pallas_call x2 -> x4, Pallas kernels: 0.91 us -> 9.14 us  [expand(): pl.pallas_call(functools.partial(expand_kernel, owners, heads, wide), out...]
    pallas_call x2 -> x4, Pallas kernels: 9.45 us -> 13.3 us  [the longest x2 9.93 us: attend(): pl.pallas_call(functools.partial(attend_kernel, owners, heads, chain), ou...]
    pallas_call x1 -> x2, Pallas kernels: 0.6 us -> 3.37 us  [shards(): pl.pallas_call(functools.partial(project_kernel, owners, heads, wide, Tru...]
    pallas_call x1 -> x2, Pallas kernels: 0.6 us -> 3.29 us  [shards(): pl.pallas_call(functools.partial(project_kernel, owners, heads, wide, Fal...]
    ppermute x2 -> x4, waiting for transfers between devices: 2.4 us -> 4.64 us  [swap_cores(): return lax.ppermute(part, 'tensor', [(0, 1), (1, 0)])]
  transfers between devices with their start and end apart: 2 -> 11, of which waited for: 2 -> 11; matrix products, arithmetic and copies ran while one was open for 0% -> 0% of each run, Pallas kernels for 0% -> 28%
where the time goes in v8:
time: 98 us; the launch traced here: 97.4 us
  Pallas kernels  31 us (32%)
  starting transfers between devices  27.7 us (28%)
  waiting for transfers between devices  23.4 us (24%)
  blocking collectives  14.5 us (15%)
    all_to_all x7, starting transfers between devices, exchange(): lax.all_to_all(blocks, 'store', split_axis=0, concat_axis=0, tiled=True)  27.4 us
    all_to_all x7, waiting for transfers between devices, exchange(): lax.all_to_all(blocks, 'store', split_axis=0, concat_axis=0, tiled=True)  18.8 us
    all_to_all x1, blocking collectives, exchange(): lax.all_to_all(blocks, 'store', split_axis=0, concat_axis=0, tiled=True)  14.5 us
    pallas_call x2, Pallas kernels, attend(): pl.pallas_call(functools.partial(attend_kernel, owners, heads, chain), ou...  9.93 us
    pallas_call x4, Pallas kernels, expand(): pl.pallas_call(functools.partial(expand_kernel, owners, heads, wide), out...  9.14 us
    ppermute x4, waiting for transfers between devices, swap_cores(): return lax.ppermute(part, 'tensor', [(0, 1), (1, 0)])  4.64 us
    pallas_call x2, Pallas kernels, collect(): pl.pallas_call(functools.partial(collect_kernel, owners, heads), out_shap...  3.39 us
    pallas_call x2, Pallas kernels, shards(): pl.pallas_call(functools.partial(project_kernel, owners, heads, wide, Tru...  3.37 us
  transfers between devices with their start and end apart: 11, of which 11 were waited for; matrix products, arithmetic and copies ran while one was open for 0% of the time, Pallas kernels for 28%

profile of v8, /device:TPU:0, one launch (start us, length us, event | category | flops | bytes accessed | tf_op | source)
XLA Modules:
  0.0 97.4 jit_solution(15120783730710561168)
XLA Ops:
  0.6 1.9 %dispatch.1 = (s32[64]{0:T(128)S(1)}, bf16[8,8,1152]{2,1,0:T(8,128)(2,1)S(1)}, bf16[8,8,1152]{2,1,0:T(8,128)(2,1)}) custom-call(s32[16]{0:T(128)} %ids_hbm.1, s32[64]{0:T(128)} %slot_of_hbm.1, s32[16]{0:T(128)} %lengths_hbm.1, bf16[2,16,4096]{2,1,0:T(8,128)(2,1)} %x_hbm.1), custom_call_target="tpu_custom_call" | custom-call | tf_op jit(solution)/shard_map/dispatch/pallas_call | solution.py:442
  2.5 14.5 %all_to_all.40.blocks = bf16[8,8,1152]{2,1,0:T(8,128)(2,1)S(1)} all-to-all(bf16[8,8,1152]{2,1,0:T(8,128)(2,1)S(1)} %get-tuple-element.10), channel_id=1, replica_groups=mesh['parts'=2,'store'=8,'tensor'=2] {'store'}, dimensions={0} | all-to-all | bytes 294912 | tf_op jit(solution)/shard_map/all_to_all | solution.py:399
  17.1 3.4 %all-to-all-start.2 = ((bf16[8,8,1152]{2,1,0:T(8,128)(2,1)}), bf16[8,8,1152]{2,1,0:T(8,128)(2,1)S(1)}, u32[]{:S(2)}, u32[]{:S(2)}) async-start(bf16[8,8,1152]{2,1,0:T(8,128)(2,1)} %get-tuple-element.12), calls=%async_computation.2 | async-start | bytes 294912 | tf_op jit(solution)/shard_map/all_to_all | solution.py:399
  20.5 1.7 %project_query_0.1 = (f32[16,128]{1,0:T(8,128)S(1)}, f32[16,128]{1,0:T(8,128)S(1)}) custom-call(bf16[128,8192]{1,0:T(8,128)(2,1)} %bitcast.8, bf16[8,8,1152]{2,1,0:T(8,128)(2,1)S(1)} %all_to_all.40.blocks), custom_call_target="tpu_custom_call" | custom-call | tf_op jit(solution)/shard_map/project_query_0/pallas_call | solution.py:511
  22.2 0.1 collective-permute-start
  22.2 1.2 %collective-permute-done.other = f32[16,128]{1,0:T(8,128)S(1)} collective-permute-done((f32[16,128]{1,0:T(8,128)S(1)}, f32[16,128]{1,0:T(8,128)S(1)}, u32[]{:S(2)}, u32[]{:S(2)}) %collective-permute-start) | collective-permute-done | bytes 8224 | tf_op jit(solution)/shard_map/ppermute | solution.py:407
  23.4 2.3 %expand_query_0.1 = bf16[8,8,1024]{2,1,0:T(8,128)(2,1)} custom-call(f32[16,128]{1,0:T(8,128)S(1)} %get-tuple-element.11.mine, f32[16,128]{1,0:T(8,128)S(1)} %collective-permute-done.other, bf16[128,4096]{1,0:T(8,128)(2,1)} %bitcast.12), custom_call_target="tpu_custom_call" | custom-call | tf_op jit(solution)/shard_map/expand_query_0/pallas_call | solution.py:462
  25.7 2.2 %all-to-all-done.2.blocks = bf16[8,8,1152]{2,1,0:T(8,128)(2,1)S(1)} async-done(((bf16[8,8,1152]{2,1,0:T(8,128)(2,1)}), bf16[8,8,1152]{2,1,0:T(8,128)(2,1)S(1)}, u32[]{:S(2)}, u32[]{:S(2)}) %all-to-all-start.2) | async-done | bytes 147488 | tf_op jit(solution)/shard_map/all_to_all | solution.py:399
  27.9 3.8 %all-to-all-start.1 = ((bf16[8,8,1024]{2,1,0:T(8,128)(2,1)}), bf16[8,8,1024]{2,1,0:T(8,128)(2,1)S(1)}, u32[]{:S(2)}, u32[]{:S(2)}) async-start(bf16[8,8,1024]{2,1,0:T(8,128)(2,1)} %expand_query_0.1), calls=%async_computation.1 | async-start | bytes 262144 | tf_op jit(solution)/shard_map/all_to_all | solution.py:399
  31.6 1.7 %project_query_1.1 = (f32[16,128]{1,0:T(8,128)S(1)}, f32[16,128]{1,0:T(8,128)S(1)}) custom-call(bf16[128,8192]{1,0:T(8,128)(2,1)} %bitcast.9, bf16[8,8,1152]{2,1,0:T(8,128)(2,1)S(1)} %all-to-all-done.2.blocks), custom_call_target="tpu_custom_call" | custom-call | tf_op jit(solution)/shard_map/project_query_1/pallas_call | solution.py:511
  33.3 0.1 collective-permute-start.1
  33.4 1.2 %collective-permute-done.1.other = f32[16,128]{1,0:T(8,128)S(1)} collective-permute-done((f32[16,128]{1,0:T(8,128)S(1)}, f32[16,128]{1,0:T(8,128)S(1)}, u32[]{:S(2)}, u32[]{:S(2)}) %collective-permute-start.1) | collective-permute-done | bytes 8224 | tf_op jit(solution)/shard_map/ppermute | solution.py:407
  34.6 2.3 %expand_query_1.1 = bf16[8,8,1024]{2,1,0:T(8,128)(2,1)} custom-call(f32[16,128]{1,0:T(8,128)S(1)} %get-tuple-element.13.mine, f32[16,128]{1,0:T(8,128)S(1)} %collective-permute-done.1.other, bf16[128,4096]{1,0:T(8,128)(2,1)} %bitcast.13), custom_call_target="tpu_custom_call" | custom-call | tf_op jit(solution)/shard_map/expand_query_1/pallas_call | solution.py:462
  36.9 2.1 %all-to-all-done.1.blocks = bf16[8,8,1024]{2,1,0:T(8,128)(2,1)S(1)} async-done(((bf16[8,8,1024]{2,1,0:T(8,128)(2,1)}), bf16[8,8,1024]{2,1,0:T(8,128)(2,1)S(1)}, u32[]{:S(2)}, u32[]{:S(2)}) %all-to-all-start.1) | async-done | bytes 131104 | tf_op jit(solution)/shard_map/all_to_all | solution.py:399
  39.0 3.9 %all-to-all-start.3 = ((bf16[8,8,1024]{2,1,0:T(8,128)(2,1)}), bf16[8,8,1024]{2,1,0:T(8,128)(2,1)S(1)}, u32[]{:S(2)}, u32[]{:S(2)}) async-start(bf16[8,8,1024]{2,1,0:T(8,128)(2,1)} %expand_query_1.1), calls=%async_computation.3 | async-start | bytes 262144 | tf_op jit(solution)/shard_map/all_to_all | solution.py:399
  42.9 4.4 %attend_0.1.first = bf16[8,8,1024]{2,1,0:T(8,128)(2,1)} custom-call(s32[64]{0:T(128)S(1)} %get-tuple-element.9.meta, bf16[2,16,4096]{2,1,0:T(8,128)(2,1)} %q_hbm.3, bf16[2,16,512]{2,1,0:T(8,128)(2,1)} %kn_hbm.3, bf16[2,16,512]{2,1,0:T(8,128)(2,1)} %vn_hbm.3, bf16[16,512,512]{2,1,0:T(8,128)(2,1)} %k_hbm.3, bf16[16,512,512]{2,1,0:T(8,128)(2,1)} %v_hbm.3, ...), custom_call_target="tpu_custom_call" | custom-call | tf_op jit(solution)/shard_map/attend_0/pallas_call | solution.py:473
  47.3 2.9 %all-to-all-done.3.blocks = bf16[8,8,1024]{2,1,0:T(8,128)(2,1)S(1)} async-done(((bf16[8,8,1024]{2,1,0:T(8,128)(2,1)}), bf16[8,8,1024]{2,1,0:T(8,128)(2,1)S(1)}, u32[]{:S(2)}, u32[]{:S(2)}) %all-to-all-start.3) | async-done | bytes 131104 | tf_op jit(solution)/shard_map/all_to_all | solution.py:399
  50.2 4.2 %all-to-all-start.4 = ((bf16[8,8,1024]{2,1,0:T(8,128)(2,1)}), bf16[8,8,1024]{2,1,0:T(8,128)(2,1)S(1)}, u32[]{:S(2)}, u32[]{:S(2)}) async-start(bf16[8,8,1024]{2,1,0:T(8,128)(2,1)} %attend_0.1.first), calls=%async_computation.4 | async-start | bytes 262144 | tf_op jit(solution)/shard_map/all_to_all | solution.py:399
  54.4 5.5 %attend_1.1.second = bf16[8,8,1024]{2,1,0:T(8,128)(2,1)} custom-call(s32[64]{0:T(128)S(1)} %get-tuple-element.9.meta, bf16[2,16,4096]{2,1,0:T(8,128)(2,1)} %q_hbm.3, bf16[2,16,512]{2,1,0:T(8,128)(2,1)} %kn_hbm.3, bf16[2,16,512]{2,1,0:T(8,128)(2,1)} %vn_hbm.3, bf16[16,512,512]{2,1,0:T(8,128)(2,1)} %k_hbm.3, bf16[16,512,512]{2,1,0:T(8,128)(2,1)} %v_hbm.3, ...), custom_call_target="tpu_custom_call" | custom-call | tf_op jit(solution)/shard_map/attend_1/pallas_call | solution.py:473
  59.9 1.8 %all-to-all-done.4.blocks = bf16[8,8,1024]{2,1,0:T(8,128)(2,1)S(1)} async-done(((bf16[8,8,1024]{2,1,0:T(8,128)(2,1)}), bf16[8,8,1024]{2,1,0:T(8,128)(2,1)S(1)}, u32[]{:S(2)}, u32[]{:S(2)}) %all-to-all-start.4) | async-done | bytes 131104 | tf_op jit(solution)/shard_map/all_to_all | solution.py:399
  61.8 4.4 %all-to-all-start.6 = ((bf16[8,8,1024]{2,1,0:T(8,128)(2,1)}), bf16[8,8,1024]{2,1,0:T(8,128)(2,1)S(1)}, u32[]{:S(2)}, u32[]{:S(2)}) async-start(bf16[8,8,1024]{2,1,0:T(8,128)(2,1)} %attend_1.1.second), calls=%async_computation.6 | async-start | bytes 262144 | tf_op jit(solution)/shard_map/all_to_all | solution.py:399
  66.2 1.6 %project_output_0.1.mine = f32[16,128]{1,0:T(8,128)S(1)} custom-call(bf16[128,8192]{1,0:T(8,128)(2,1)} %bitcast.10, bf16[8,8,1024]{2,1,0:T(8,128)(2,1)S(1)} %all-to-all-done.4.blocks, f32[16,128]{1,0:T(8,128)S(1)} %get-tuple-element.14.refs_0_), custom_call_target="tpu_custom_call" | custom-call | tf_op jit(solution)/shard_map/project_output_0/pallas_call | solution.py:523
  67.9 0.1 collective-permute-start.2
  67.9 1.2 %collective-permute-done.2.other = f32[16,128]{1,0:T(8,128)S(1)} collective-permute-done((f32[16,128]{1,0:T(8,128)S(1)}, f32[16,128]{1,0:T(8,128)S(1)}, u32[]{:S(2)}, u32[]{:S(2)}) %collective-permute-start.2) | collective-permute-done | bytes 8224 | tf_op jit(solution)/shard_map/ppermute | solution.py:407
  69.1 2.3 %expand_output_0.1 = bf16[8,8,1024]{2,1,0:T(8,128)(2,1)} custom-call(f32[16,128]{1,0:T(8,128)S(1)} %project_output_0.1.mine, f32[16,128]{1,0:T(8,128)S(1)} %collective-permute-done.2.other, bf16[128,4096]{1,0:T(8,128)(2,1)} %bitcast.14), custom_call_target="tpu_custom_call" | custom-call | tf_op jit(solution)/shard_map/expand_output_0/pallas_call | solution.py:462
  71.4 2.2 %all-to-all-done.6.blocks = bf16[8,8,1024]{2,1,0:T(8,128)(2,1)S(1)} async-done(((bf16[8,8,1024]{2,1,0:T(8,128)(2,1)}), bf16[8,8,1024]{2,1,0:T(8,128)(2,1)S(1)}, u32[]{:S(2)}, u32[]{:S(2)}) %all-to-all-start.6) | async-done | bytes 131104 | tf_op jit(solution)/shard_map/all_to_all | solution.py:399
  73.6 3.9 %all-to-all-start.5 = ((bf16[8,8,1024]{2,1,0:T(8,128)(2,1)}), bf16[8,8,1024]{2,1,0:T(8,128)(2,1)S(1)}, u32[]{:S(2)}, u32[]{:S(2)}) async-start(bf16[8,8,1024]{2,1,0:T(8,128)(2,1)} %expand_output_0.1), calls=%async_computation.5 | async-start | bytes 262144 | tf_op jit(solution)/shard_map/all_to_all | solution.py:399
  77.4 1.6 %project_output_1.1.mine = f32[16,128]{1,0:T(8,128)S(1)} custom-call(bf16[128,8192]{1,0:T(8,128)(2,1)} %bitcast.11, bf16[8,8,1024]{2,1,0:T(8,128)(2,1)S(1)} %all-to-all-done.6.blocks, f32[16,128]{1,0:T(8,128)S(1)} %get-tuple-element.15.refs_0_), custom_call_target="tpu_custom_call" | custom-call | tf_op jit(solution)/shard_map/project_output_1/pallas_call | solution.py:523
  79.1 0.1 collective-permute-start.3
  79.1 1.2 %collective-permute-done.3.other = f32[16,128]{1,0:T(8,128)S(1)} collective-permute-done((f32[16,128]{1,0:T(8,128)S(1)}, f32[16,128]{1,0:T(8,128)S(1)}, u32[]{:S(2)}, u32[]{:S(2)}) %collective-permute-start.3) | collective-permute-done | bytes 8224 | tf_op jit(solution)/shard_map/ppermute | solution.py:407
  80.3 2.3 %expand_output_1.1 = bf16[8,8,1024]{2,1,0:T(8,128)(2,1)} custom-call(f32[16,128]{1,0:T(8,128)S(1)} %project_output_1.1.mine, f32[16,128]{1,0:T(8,128)S(1)} %collective-permute-done.3.other, bf16[128,4096]{1,0:T(8,128)(2,1)} %bitcast.15), custom_call_target="tpu_custom_call" | custom-call | tf_op jit(solution)/shard_map/expand_output_1/pallas_call | solution.py:462
  82.6 2.1 %all-to-all-done.5.first = bf16[8,8,1024]{2,1,0:T(8,128)(2,1)S(1)} async-done(((bf16[8,8,1024]{2,1,0:T(8,128)(2,1)}), bf16[8,8,1024]{2,1,0:T(8,128)(2,1)S(1)}, u32[]{:S(2)}, u32[]{:S(2)}) %all-to-all-start.5) | async-done | bytes 131104 | tf_op jit(solution)/shard_map/all_to_all | solution.py:399
  84.8 3.9 %all-to-all-start.7 = ((bf16[8,8,1024]{2,1,0:T(8,128)(2,1)}), bf16[8,8,1024]{2,1,0:T(8,128)(2,1)S(1)}, u32[]{:S(2)}, u32[]{:S(2)}) async-start(bf16[8,8,1024]{2,1,0:T(8,128)(2,1)} %expand_output_1.1), calls=%async_computation.7 | async-start | bytes 262144 | tf_op jit(solution)/shard_map/all_to_all | solution.py:399
  88.6 1.9 %collect_attended.1 = bf16[2,16,4096]{2,1,0:T(8,128)(2,1)} custom-call(s32[64]{0:T(128)S(1)} %get-tuple-element.9.meta, bf16[8,8,1024]{2,1,0:T(8,128)(2,1)} %attend_0.1.first, bf16[8,8,1024]{2,1,0:T(8,128)(2,1)} %attend_1.1.second), custom_call_target="tpu_custom_call" | custom-call | tf_op jit(solution)/shard_map/collect_attended/pallas_call | solution.py:496
  90.5 5.4 %all-to-all-done.7.second = bf16[8,8,1024]{2,1,0:T(8,128)(2,1)S(1)} async-done(((bf16[8,8,1024]{2,1,0:T(8,128)(2,1)}), bf16[8,8,1024]{2,1,0:T(8,128)(2,1)S(1)}, u32[]{:S(2)}, u32[]{:S(2)}) %all-to-all-start.7) | async-done | bytes 131104 | tf_op jit(solution)/shard_map/all_to_all | solution.py:399
  96.0 1.5 %collect_adapters.1 = bf16[2,16,4096]{2,1,0:T(8,128)(2,1)} custom-call(s32[64]{0:T(128)S(1)} %get-tuple-element.9.meta, bf16[8,8,1024]{2,1,0:T(8,128)(2,1)S(1)} %all-to-all-done.5.first, bf16[8,8,1024]{2,1,0:T(8,128)(2,1)S(1)} %all-to-all-done.7.second), custom_call_target="tpu_custom_call" | custom-call | tf_op jit(solution)/shard_map/collect_adapters/pallas_call | solution.py:496
Async XLA Ops:
  17.1 10.8 %all-to-all-start.2 = ((bf16[8,8,1152]{2,1,0:T(8,128)(2,1)}), bf16[8,8,1152]{2,1,0:T(8,128)(2,1)S(1)}, u32[]{:S(2)}, u32[]{:S(2)}) async-start(bf16[8,8,1152]{2,1,0:T(8,128)(2,1)} %get-tuple-element.12), calls=%async_computation.2 | async-start | bytes 294912 | tf_op jit(solution)/shard_map/all_to_all | solution.py:399
  22.2 1.2 %collective-permute-start = (f32[16,128]{1,0:T(8,128)S(1)}, f32[16,128]{1,0:T(8,128)S(1)}, u32[]{:S(2)}, u32[]{:S(2)}) collective-permute-start(f32[16,128]{1,0:T(8,128)S(1)} %get-tuple-element.11.mine), channel_id=1, source_target_pairs={{0,1},{1,0},{2,3},{3,2},{4,5},{5,4},{6,7},{7,6},{8,9},{9,8},{10,11... | collective-permute-start | bytes 24584 | tf_op jit(solution)/shard_map/ppermute | solution.py:407
  27.9 11.1 %all-to-all-start.1 = ((bf16[8,8,1024]{2,1,0:T(8,128)(2,1)}), bf16[8,8,1024]{2,1,0:T(8,128)(2,1)S(1)}, u32[]{:S(2)}, u32[]{:S(2)}) async-start(bf16[8,8,1024]{2,1,0:T(8,128)(2,1)} %expand_query_0.1), calls=%async_computation.1 | async-start | bytes 262144 | tf_op jit(solution)/shard_map/all_to_all | solution.py:399
  33.3 1.2 %collective-permute-start.1 = (f32[16,128]{1,0:T(8,128)S(1)}, f32[16,128]{1,0:T(8,128)S(1)}, u32[]{:S(2)}, u32[]{:S(2)}) collective-permute-start(f32[16,128]{1,0:T(8,128)S(1)} %get-tuple-element.13.mine), channel_id=1, source_target_pairs={{0,1},{1,0},{2,3},{3,2},{4,5},{5,4},{6,7},{7,6},{8,9},{9,8},{10,11... | collective-permute-start | bytes 24584 | tf_op jit(solution)/shard_map/ppermute | solution.py:407
  39.0 11.2 %all-to-all-start.3 = ((bf16[8,8,1024]{2,1,0:T(8,128)(2,1)}), bf16[8,8,1024]{2,1,0:T(8,128)(2,1)S(1)}, u32[]{:S(2)}, u32[]{:S(2)}) async-start(bf16[8,8,1024]{2,1,0:T(8,128)(2,1)} %expand_query_1.1), calls=%async_computation.3 | async-start | bytes 262144 | tf_op jit(solution)/shard_map/all_to_all | solution.py:399
  50.2 11.5 %all-to-all-start.4 = ((bf16[8,8,1024]{2,1,0:T(8,128)(2,1)}), bf16[8,8,1024]{2,1,0:T(8,128)(2,1)S(1)}, u32[]{:S(2)}, u32[]{:S(2)}) async-start(bf16[8,8,1024]{2,1,0:T(8,128)(2,1)} %attend_0.1.first), calls=%async_computation.4 | async-start | bytes 262144 | tf_op jit(solution)/shard_map/all_to_all | solution.py:399
  61.8 11.8 %all-to-all-start.6 = ((bf16[8,8,1024]{2,1,0:T(8,128)(2,1)}), bf16[8,8,1024]{2,1,0:T(8,128)(2,1)S(1)}, u32[]{:S(2)}, u32[]{:S(2)}) async-start(bf16[8,8,1024]{2,1,0:T(8,128)(2,1)} %attend_1.1.second), calls=%async_computation.6 | async-start | bytes 262144 | tf_op jit(solution)/shard_map/all_to_all | solution.py:399
  67.9 1.2 %collective-permute-start.2 = (f32[16,128]{1,0:T(8,128)S(1)}, f32[16,128]{1,0:T(8,128)S(1)}, u32[]{:S(2)}, u32[]{:S(2)}) collective-permute-start(f32[16,128]{1,0:T(8,128)S(1)} %project_output_0.1.mine), channel_id=1, source_target_pairs={{0,1},{1,0},{2,3},{3,2},{4,5},{5,4},{6,7},{7,6},{8,9},{9,8},{10,11... | collective-permute-start | bytes 24584 | tf_op jit(solution)/shard_map/ppermute | solution.py:407
  73.6 11.2 %all-to-all-start.5 = ((bf16[8,8,1024]{2,1,0:T(8,128)(2,1)}), bf16[8,8,1024]{2,1,0:T(8,128)(2,1)S(1)}, u32[]{:S(2)}, u32[]{:S(2)}) async-start(bf16[8,8,1024]{2,1,0:T(8,128)(2,1)} %expand_output_0.1), calls=%async_computation.5 | async-start | bytes 262144 | tf_op jit(solution)/shard_map/all_to_all | solution.py:399
  79.1 1.2 %collective-permute-start.3 = (f32[16,128]{1,0:T(8,128)S(1)}, f32[16,128]{1,0:T(8,128)S(1)}, u32[]{:S(2)}, u32[]{:S(2)}) collective-permute-start(f32[16,128]{1,0:T(8,128)S(1)} %project_output_1.1.mine), channel_id=1, source_target_pairs={{0,1},{1,0},{2,3},{3,2},{4,5},{5,4},{6,7},{7,6},{8,9},{9,8},{10,11... | collective-permute-start | bytes 24584 | tf_op jit(solution)/shard_map/ppermute | solution.py:407
  84.8 11.2 %all-to-all-start.7 = ((bf16[8,8,1024]{2,1,0:T(8,128)(2,1)}), bf16[8,8,1024]{2,1,0:T(8,128)(2,1)S(1)}, u32[]{:S(2)}, u32[]{:S(2)}) async-start(bf16[8,8,1024]{2,1,0:T(8,128)(2,1)} %expand_output_1.1), calls=%async_computation.7 | async-start | bytes 262144 | tf_op jit(solution)/shard_map/all_to_all | solution.py:399

commit v9 on v7

--- a/solution.py
+++ b/solution.py
@@ -119,6 +119,10 @@
     return one_hot(
         iota((total, total), 1) == head * (owners * items) + owner * items + rest(at, items)
     )
+
+
+def in_order(arrived, crossed):
+    return [b for k in range(crossed.shape[0]) for b in (arrived[k, 0], crossed[k])]
 
 
 def exact(matrix, values):
@@ -164,6 +168,7 @@
     wide = x_ref.shape[2] // heads
     for copy in copies[:3]:
         copy.wait()
+    parity = rest(lax.axis_index("store"), 2)
     row_at = rows
     order = rows + owners * CAP
     spans = order + rows
@@ -172,7 +177,7 @@
         slot_at[p] = -1
     for r in range(rows):
         slot = slot_of[ids[r]]
-        first = over(slot, adapt) * CAP
+        first = (over(slot, adapt) ^ parity) * CAP
         place = first + jnp.where(meta[row_at + first] >= 0, 1, 0)
         meta[row_at + place] = r
         slot_at[place] = rest(slot, adapt)
@@ -201,7 +206,8 @@
         copy.wait()
 
 
-def project_kernel(owners, heads, wide, first, a_ref, blocks, *refs):
+def project_kernel(owners, heads, wide, first, a_ref, arrived, crossed, *refs):
+    blocks = in_order(arrived, crossed)
     core = lax.axis_index("tensor") if a_ref.shape[1] > heads * wide else 0
     if first:
         part_ref, mask_ref = refs
@@ -209,10 +215,10 @@
         mask_in, part_ref = refs
     grouped = regroup_matrix(owners, heads)
     items = owners * CAP * STEPS
-    arrived = jnp.concatenate([blocks[i, :, :wide] for i in range(owners)], axis=0)
+    arrived = jnp.concatenate([b[:, :wide] for b in blocks], axis=0)
     arrived = exact(grouped, arrived)
     if first:
-        masks = jnp.concatenate([blocks[i, :, wide:] for i in range(owners)], axis=0)
+        masks = jnp.concatenate([b[:, wide:] for b in blocks], axis=0)
         mask = jnp.dot(grouped[:items], masks, preferred_element_type=F32)
         mask_ref[...] = mask
     else:
@@ -265,7 +271,8 @@
     vn_hbm,
     k_hbm,
     v_hbm,
-    blocks,
+    arrived,
+    crossed,
     out_hbm,
     outgoing,
     q_ref,
@@ -326,7 +333,7 @@
 
     delta = jnp.dot(
         unpack_matrix(meta, owners, heads, rows, True),
-        jnp.concatenate([blocks[i] for i in range(owners)], axis=0),
+        jnp.concatenate(in_order(arrived, crossed), axis=0),
         preferred_element_type=F32,
     )
     by_row = by_row_matrix(heads, rows)
@@ -419,11 +426,11 @@
     result.wait()
 
 
-def collect_kernel(owners, heads, meta, blocks, out_hbm, out_ref, sems):
+def collect_kernel(owners, heads, meta, straight, crossed, out_hbm, out_ref, sems):
     rows = out_ref.shape[1]
     wide = out_ref.shape[2] // heads
     span = STEPS * rows
-    arrived = jnp.concatenate([blocks[i] for i in range(owners)], axis=0)
+    arrived = jnp.concatenate(in_order(straight, crossed), axis=0)
     spread = unpack_matrix(meta, owners, heads, rows, False)
     copies = []
     for c in range(heads):
@@ -438,7 +445,14 @@
 
 
 def exchange(blocks):
-    return lax.all_to_all(blocks, "store", split_axis=0, concat_axis=0, tiled=True)
+    owners = blocks.shape[0]
+    paired = blocks.reshape((owners // 2, 2) + blocks.shape[1:])
+    groups = [list(range(parity, owners, 2)) for parity in range(2)]
+    arrived = lax.all_to_all(
+        paired, "store", split_axis=0, concat_axis=0, axis_index_groups=groups, tiled=True
+    )
+    crossed = lax.ppermute(arrived[:, 1], "store", [(s, s ^ 1) for s in range(owners)])
+    return arrived, crossed
 
 
 def in_hbm(array):
@@ -509,11 +523,11 @@
     part, mask = pl.pallas_call(
         functools.partial(project_kernel, owners, heads, wide, True),
         out_shape=[shape((items, lanes), F32)] * 2,
-        in_specs=[VMEM] * 2,
+        in_specs=[VMEM] * 3,
         out_specs=[VMEM] * 2,
         compiler_params=small,
         name="project_query",
-    )(a_near, arrived)
+    )(a_near, *arrived)
 
     def expand(part, b_store, name):
         return pl.pallas_call(
@@ -530,7 +544,7 @@
     attn_out, outgoing = pl.pallas_call(
         functools.partial(attend_kernel, owners, heads),
         out_shape=[shape((STEPS, rows, width), BF16), sent],
-        in_specs=[SMEM] + [HBM] * 5 + [VMEM],
+        in_specs=[SMEM] + [HBM] * 5 + [VMEM] * 2,
         out_specs=[HBM, VMEM],
         scratch_shapes=[
             pltpu.VMEM(q_base.shape, BF16),
@@ -547,22 +561,22 @@
         ],
         compiler_params=pltpu.CompilerParams(vmem_limit_bytes=32 * 1024 * 1024),
         name="attend",
-    )(meta, *map(in_hbm, (q_base, k_new, v_new, cache_k, cache_v)), returned)
+    )(meta, *map(in_hbm, (q_base, k_new, v_new, cache_k, cache_v)), *returned)
 
     arrived = exchange(outgoing)
     part = pl.pallas_call(
         functools.partial(project_kernel, owners, heads, wide, False),
         out_shape=shape((items, lanes), F32),
-        in_specs=[VMEM] * 3,
+        in_specs=[VMEM] * 4,
         out_specs=VMEM,
         compiler_params=small,
         name="project_output",
-    )(flat(a_output), arrived, mask)
+    )(flat(a_output), *arrived, mask)
     returned = exchange(expand(part, b_output.reshape(lanes, width), "expand_output"))
     adapter_out = pl.pallas_call(
         functools.partial(collect_kernel, owners, heads),
         out_shape=shape((STEPS, rows, width), BF16),
-        in_specs=[SMEM, VMEM],
+        in_specs=[SMEM] + [VMEM] * 2,
         out_specs=HBM,
         scratch_shapes=[
             pltpu.VMEM((STEPS, rows, width), BF16),
@@ -570,7 +584,7 @@
         ],
         compiler_params=small,
         name="collect",
-    )(meta, returned)
+    )(meta, *returned)
     return (attn_out, adapter_out)
 
 

time: 71 us -> 86.4 us (1.22)
  waiting for transfers between devices: 2.4 us -> 17.1 us
  starting transfers between devices: 0.01 us -> 5.59 us
  blocking collectives: 53.5 us -> 49.1 us
    ppermute x0 -> x4, waiting for transfers between devices: none -> 14.7 us  [exchange(): lax.ppermute(arrived[:, 1], 'store', [(s, s ^ 1) for s in range(owners)])]
    ppermute x0 -> x4, starting transfers between devices: none -> 5.59 us  [exchange(): lax.ppermute(arrived[:, 1], 'store', [(s, s ^ 1) for s in range(owners)])]
    all_to_all x4, blocking collectives: 53.5 us -> 49.1 us  [exchange(): lax.all_to_all(paired, 'store', split_axis=0, concat_axis=0, axis_index_g...]
  transfers between devices with their start and end apart: 2 -> 6, of which waited for: 2 -> 6; matrix products, arithmetic and copies ran while one was open for 0% -> 0% of each run, Pallas kernels for 0% -> 0%
where the time goes in v9:
time: 86.4 us; the launch traced here: 86.2 us
  blocking collectives  49.1 us (57%)
  waiting for transfers between devices  17.1 us (20%)
  Pallas kernels  13.6 us (16%)
  starting transfers between devices  5.59 us (6%)
    all_to_all x4, blocking collectives, exchange(): lax.all_to_all(paired, 'store', split_axis=0, concat_axis=0, axis_index_g...  49.1 us
    ppermute x4, waiting for transfers between devices, exchange(): lax.ppermute(arrived[:, 1], 'store', [(s, s ^ 1) for s in range(owners)])  14.7 us
    pallas_call x1, Pallas kernels, shards(): pl.pallas_call(functools.partial(attend_kernel, owners, heads), out_shape...  7.73 us
    ppermute x4, starting transfers between devices, exchange(): lax.ppermute(arrived[:, 1], 'store', [(s, s ^ 1) for s in range(owners)])  5.59 us
    ppermute x2, waiting for transfers between devices, swap_cores(): return lax.ppermute(part, 'tensor', [(0, 1), (1, 0)])  2.4 us
    pallas_call x1, Pallas kernels, shards(): pl.pallas_call(functools.partial(dispatch_kernel, owners, heads, adapt, r...  2.28 us
  transfers between devices with their start and end apart: 6, of which 6 were waited for; matrix products, arithmetic and copies ran while one was open for 0% of the time, Pallas kernels for 0%

profile of v9, /device:TPU:0, one launch (start us, length us, event | category | flops | bytes accessed | tf_op | source)
XLA Modules:
  0.0 86.2 jit_solution(7104398359874573187)
XLA Ops:
  0.6 2.3 %dispatch.1 = (s32[64]{0:T(128)S(1)}, bf16[8,16,1152]{2,1,0:T(8,128)(2,1)S(1)}, bf16[128,4096]{1,0:T(8,128)(2,1)S(1)}, bf16[128,4096]{1,0:T(8,128)(2,1)S(1)}) custom-call(s32[16]{0:T(128)} %ids_hbm.1, s32[64]{0:T(128)} %slot_of_hbm.1, s32[16]{0:T(128)} %lengths_hbm.1, bf16[2,16,4096]{2,1,0:T(8,128)(2,1)} %x_hbm.1, bf16[128,8192]{1,0:T(8,128)(2,1)} %bitcast.34, ...), custom_call_target="tpu_custom_call" | custom-call | tf_op jit(solution)/shard_map/dispatch/pallas_call | solution.py:497
  2.9 15.7 %all_to_all.20.arrived = bf16[4,2,16,1152]{3,2,1,0:T(8,128)(2,1)S(1)} all-to-all(bf16[4,2,16,1152]{3,2,1,0:T(8,128)(2,1)S(1)} %bitcast.32), channel_id=1, replica_groups={{0,4,8,12},{2,6,10,14},{1,5,9,13},{3,7,11,15},{16,20,24,28},{18,22,26,3..., dimensions={0} | all-to-all | bytes 589824 | tf_op jit(solution)/shard_map/all_to_all | solution.py:451
  18.6 1.6 %collective-permute-start = (bf16[4,16,1152]{2,1,0:T(8,128)(2,1)S(1)}, bf16[4,16,1152]{2,1,0:T(8,128)(2,1)S(1)}, u32[]{:S(2)}, u32[]{:S(2)}) collective-permute-start(bf16[4,16,1152]{2,1,0:T(8,128)(2,1)S(1)} %slice_bitcast_fusion), channel_id=1, source_target_pairs={{0,2},{2,0},{4,6},{6,4},{8,10},{10,8},{12,14},{14,12},{1,3},{3,1},... | collective-permute-start | bytes 442376 | tf_op jit(solution)/shard_map/ppermute | solution.py:454
  20.2 3.6 %collective-permute-done.crossed = bf16[4,16,1152]{2,1,0:T(8,128)(2,1)S(1)} collective-permute-done((bf16[4,16,1152]{2,1,0:T(8,128)(2,1)S(1)}, bf16[4,16,1152]{2,1,0:T(8,128)(2,1)S(1)}, u32[]{:S(2)}, u32[]{:S(2)}) %collective-permute-start) | collective-permute-done | bytes 147488 | tf_op jit(solution)/shard_map/ppermute | solution.py:454
  23.8 0.6 project_query.1
  24.4 0.0 collective-permute-start.1
  24.4 1.2 %collective-permute-done.1.other = f32[32,128]{1,0:T(8,128)S(1)} collective-permute-done((f32[32,128]{1,0:T(8,128)S(1)}, f32[32,128]{1,0:T(8,128)S(1)}, u32[]{:S(2)}, u32[]{:S(2)}) %collective-permute-start.1) | collective-permute-done | bytes 16416 | tf_op jit(solution)/shard_map/ppermute | solution.py:463
  25.7 0.5 expand_query.1
  26.1 11.9 %all_to_all.21.arrived = bf16[4,2,16,1024]{3,2,1,0:T(8,128)(2,1)S(1)} all-to-all(bf16[4,2,16,1024]{3,2,1,0:T(8,128)(2,1)S(1)} %bitcast.30), channel_id=1, replica_groups={{0,4,8,12},{2,6,10,14},{1,5,9,13},{3,7,11,15},{16,20,24,28},{18,22,26,3..., dimensions={0} | all-to-all | bytes 524288 | tf_op jit(solution)/shard_map/all_to_all | solution.py:451
  38.0 1.6 %collective-permute-start.2 = (bf16[4,16,1024]{2,1,0:T(8,128)(2,1)S(1)}, bf16[4,16,1024]{2,1,0:T(8,128)(2,1)S(1)}, u32[]{:S(2)}, u32[]{:S(2)}) collective-permute-start(bf16[4,16,1024]{2,1,0:T(8,128)(2,1)S(1)} %slice_bitcast_fusion.3), channel_id=1, source_target_pairs={{0,2},{2,0},{4,6},{6,4},{8,10},{10,8},{12,14},{14,12},{1,3},{3,1},... | collective-permute-start | bytes 393224 | tf_op jit(solution)/shard_map/ppermute | solution.py:454
  39.6 3.4 %collective-permute-done.2.crossed = bf16[4,16,1024]{2,1,0:T(8,128)(2,1)S(1)} collective-permute-done((bf16[4,16,1024]{2,1,0:T(8,128)(2,1)S(1)}, bf16[4,16,1024]{2,1,0:T(8,128)(2,1)S(1)}, u32[]{:S(2)}, u32[]{:S(2)}) %collective-permute-start.2) | collective-permute-done | bytes 131104 | tf_op jit(solution)/shard_map/ppermute | solution.py:454
  43.0 0.0 copy-start
  43.0 0.0 copy-start.1
  43.0 7.7 %attend.1 = (bf16[2,16,4096]{2,1,0:T(8,128)(2,1)}, bf16[8,16,1024]{2,1,0:T(8,128)(2,1)S(1)}) custom-call(s32[64]{0:T(128)S(1)} %get-tuple-element.10.meta, bf16[2,16,4096]{2,1,0:T(8,128)(2,1)} %q_hbm.1, bf16[2,16,512]{2,1,0:T(8,128)(2,1)} %kn_hbm.1, bf16[2,16,512]{2,1,0:T(8,128)(2,1)} %vn_hbm.1, bf16[16,512,512]{2,1,0:T(8,128)(2,1)} %k_hbm.1, ...), custom_call_target="tpu_custom_call" | custom-call | tf_op jit(solution)/shard_map/attend/pallas_call | solution.py:544
  50.8 9.7 %all_to_all.22.arrived = bf16[4,2,16,1024]{3,2,1,0:T(8,128)(2,1)S(1)} all-to-all(bf16[4,2,16,1024]{3,2,1,0:T(8,128)(2,1)S(1)} %bitcast.33), channel_id=1, replica_groups={{0,4,8,12},{2,6,10,14},{1,5,9,13},{3,7,11,15},{16,20,24,28},{18,22,26,3..., dimensions={0} | all-to-all | bytes 524288 | tf_op jit(solution)/shard_map/all_to_all | solution.py:451
  60.5 1.2 %collective-permute-start.3 = (bf16[4,16,1024]{2,1,0:T(8,128)(2,1)S(1)}, bf16[4,16,1024]{2,1,0:T(8,128)(2,1)S(1)}, u32[]{:S(2)}, u32[]{:S(2)}) collective-permute-start(bf16[4,16,1024]{2,1,0:T(8,128)(2,1)S(1)} %slice_bitcast_fusion.2), channel_id=1, source_target_pairs={{0,2},{2,0},{4,6},{6,4},{8,10},{10,8},{12,14},{14,12},{1,3},{3,1},... | collective-permute-start | bytes 393224 | tf_op jit(solution)/shard_map/ppermute | solution.py:454
  61.7 3.8 %collective-permute-done.3.crossed = bf16[4,16,1024]{2,1,0:T(8,128)(2,1)S(1)} collective-permute-done((bf16[4,16,1024]{2,1,0:T(8,128)(2,1)S(1)}, bf16[4,16,1024]{2,1,0:T(8,128)(2,1)S(1)}, u32[]{:S(2)}, u32[]{:S(2)}) %collective-permute-start.3) | collective-permute-done | bytes 131104 | tf_op jit(solution)/shard_map/ppermute | solution.py:454
  65.5 0.0 copy-done
  65.5 0.6 project_output.1.mine
  66.1 0.0 collective-permute-start.4
  66.1 1.2 %collective-permute-done.4.other = f32[32,128]{1,0:T(8,128)S(1)} collective-permute-done((f32[32,128]{1,0:T(8,128)S(1)}, f32[32,128]{1,0:T(8,128)S(1)}, u32[]{:S(2)}, u32[]{:S(2)}) %collective-permute-start.4) | collective-permute-done | bytes 16416 | tf_op jit(solution)/shard_map/ppermute | solution.py:463
  67.3 0.0 copy-done.1
  67.3 0.5 expand_output.1
  67.8 11.9 %all_to_all.23.straight = bf16[4,2,16,1024]{3,2,1,0:T(8,128)(2,1)S(1)} all-to-all(bf16[4,2,16,1024]{3,2,1,0:T(8,128)(2,1)S(1)} %bitcast.31), channel_id=1, replica_groups={{0,4,8,12},{2,6,10,14},{1,5,9,13},{3,7,11,15},{16,20,24,28},{18,22,26,3..., dimensions={0} | all-to-all | bytes 524288 | tf_op jit(solution)/shard_map/all_to_all | solution.py:451
  79.7 1.2 %collective-permute-start.5 = (bf16[4,16,1024]{2,1,0:T(8,128)(2,1)S(1)}, bf16[4,16,1024]{2,1,0:T(8,128)(2,1)S(1)}, u32[]{:S(2)}, u32[]{:S(2)}) collective-permute-start(bf16[4,16,1024]{2,1,0:T(8,128)(2,1)S(1)} %slice_bitcast_fusion.1), channel_id=1, source_target_pairs={{0,2},{2,0},{4,6},{6,4},{8,10},{10,8},{12,14},{14,12},{1,3},{3,1},... | collective-permute-start | bytes 393224 | tf_op jit(solution)/shard_map/ppermute | solution.py:454
  80.9 3.8 %collective-permute-done.5.crossed = bf16[4,16,1024]{2,1,0:T(8,128)(2,1)S(1)} collective-permute-done((bf16[4,16,1024]{2,1,0:T(8,128)(2,1)S(1)}, bf16[4,16,1024]{2,1,0:T(8,128)(2,1)S(1)}, u32[]{:S(2)}, u32[]{:S(2)}) %collective-permute-start.5) | collective-permute-done | bytes 131104 | tf_op jit(solution)/shard_map/ppermute | solution.py:454
  84.7 1.5 %collect.1 = bf16[2,16,4096]{2,1,0:T(8,128)(2,1)} custom-call(s32[64]{0:T(128)S(1)} %get-tuple-element.10.meta, bf16[4,2,16,1024]{3,2,1,0:T(8,128)(2,1)S(1)} %all_to_all.23.straight, bf16[4,16,1024]{2,1,0:T(8,128)(2,1)S(1)} %collective-permute-done.5.crossed), custom_call_target="tpu_custom_call" | custom-call | tf_op jit(solution)/shard_map/collect/pallas_call | solution.py:576
  (4 shorter events, 0.0 us)
Async XLA Ops:
  18.6 5.2 %collective-permute-start = (bf16[4,16,1152]{2,1,0:T(8,128)(2,1)S(1)}, bf16[4,16,1152]{2,1,0:T(8,128)(2,1)S(1)}, u32[]{:S(2)}, u32[]{:S(2)}) collective-permute-start(bf16[4,16,1152]{2,1,0:T(8,128)(2,1)S(1)} %slice_bitcast_fusion), channel_id=1, source_target_pairs={{0,2},{2,0},{4,6},{6,4},{8,10},{10,8},{12,14},{14,12},{1,3},{3,1},... | collective-permute-start | bytes 442376 | tf_op jit(solution)/shard_map/ppermute | solution.py:454
  24.4 1.2 %collective-permute-start.1 = (f32[32,128]{1,0:T(8,128)S(1)}, f32[32,128]{1,0:T(8,128)S(1)}, u32[]{:S(2)}, u32[]{:S(2)}) collective-permute-start(f32[32,128]{1,0:T(8,128)S(1)} %get-tuple-element.13.mine), channel_id=1, source_target_pairs={{0,1},{1,0},{2,3},{3,2},{4,5},{5,4},{6,7},{7,6},{8,9},{9,8},{10,11... | collective-permute-start | bytes 49160 | tf_op jit(solution)/shard_map/ppermute | solution.py:463
  38.0 5.0 %collective-permute-start.2 = (bf16[4,16,1024]{2,1,0:T(8,128)(2,1)S(1)}, bf16[4,16,1024]{2,1,0:T(8,128)(2,1)S(1)}, u32[]{:S(2)}, u32[]{:S(2)}) collective-permute-start(bf16[4,16,1024]{2,1,0:T(8,128)(2,1)S(1)} %slice_bitcast_fusion.3), channel_id=1, source_target_pairs={{0,2},{2,0},{4,6},{6,4},{8,10},{10,8},{12,14},{14,12},{1,3},{3,1},... | collective-permute-start | bytes 393224 | tf_op jit(solution)/shard_map/ppermute | solution.py:454
  43.0 22.5 %copy-start = (bf16[8192,8,16]{0,2,1:T(8,128)(2,1)S(1)}, bf16[8192,8,16]{0,2,1:T(8,128)(2,1)}, u32[]{:S(2)}) copy-start(bf16[8192,8,16]{0,2,1:T(8,128)(2,1)} %param.24) | copy-start | bytes 6291460
  43.0 24.3 %copy-start.1 = (bf16[8,16,4096]{2,1,0:T(8,128)(2,1)S(1)}, bf16[8,16,4096]{2,1,0:T(8,128)(2,1)}, u32[]{:S(2)}) copy-start(bf16[8,16,4096]{2,1,0:T(8,128)(2,1)} %param.25) | copy-start | bytes 3145732
  60.5 5.0 %collective-permute-start.3 = (bf16[4,16,1024]{2,1,0:T(8,128)(2,1)S(1)}, bf16[4,16,1024]{2,1,0:T(8,128)(2,1)S(1)}, u32[]{:S(2)}, u32[]{:S(2)}) collective-permute-start(bf16[4,16,1024]{2,1,0:T(8,128)(2,1)S(1)} %slice_bitcast_fusion.2), channel_id=1, source_target_pairs={{0,2},{2,0},{4,6},{6,4},{8,10},{10,8},{12,14},{14,12},{1,3},{3,1},... | collective-permute-start | bytes 393224 | tf_op jit(solution)/shard_map/ppermute | solution.py:454
  66.1 1.2 %collective-permute-start.4 = (f32[32,128]{1,0:T(8,128)S(1)}, f32[32,128]{1,0:T(8,128)S(1)}, u32[]{:S(2)}, u32[]{:S(2)}) collective-permute-start(f32[32,128]{1,0:T(8,128)S(1)} %project_output.1.mine), channel_id=1, source_target_pairs={{0,1},{1,0},{2,3},{3,2},{4,5},{5,4},{6,7},{7,6},{8,9},{9,8},{10,11... | collective-permute-start | bytes 49160 | tf_op jit(solution)/shard_map/ppermute | solution.py:463
  79.7 5.0 %collective-permute-start.5 = (bf16[4,16,1024]{2,1,0:T(8,128)(2,1)S(1)}, bf16[4,16,1024]{2,1,0:T(8,128)(2,1)S(1)}, u32[]{:S(2)}, u32[]{:S(2)}) collective-permute-start(bf16[4,16,1024]{2,1,0:T(8,128)(2,1)S(1)} %slice_bitcast_fusion.1), channel_id=1, source_target_pairs={{0,2},{2,0},{4,6},{6,4},{8,10},{10,8},{12,14},{14,12},{1,3},{3,1},... | collective-permute-start | bytes 393224 | tf_op jit(solution)/shard_map/ppermute | solution.py:454

commit v10 on v7

--- a/solution.py
+++ b/solution.py
@@ -164,6 +164,7 @@
     wide = x_ref.shape[2] // heads
     for copy in copies[:3]:
         copy.wait()
+    me = lax.axis_index("store")
     row_at = rows
     order = rows + owners * CAP
     spans = order + rows
@@ -172,7 +173,7 @@
         slot_at[p] = -1
     for r in range(rows):
         slot = slot_of[ids[r]]
-        first = over(slot, adapt) * CAP
+        first = (over(slot, adapt) ^ me) * CAP
         place = first + jnp.where(meta[row_at + first] >= 0, 1, 0)
         meta[row_at + place] = r
         slot_at[place] = rest(slot, adapt)
@@ -438,7 +439,11 @@
 
 
 def exchange(blocks):
-    return lax.all_to_all(blocks, "store", split_axis=0, concat_axis=0, tiled=True)
+    owners = blocks.shape[0]
+    arrived = [blocks[0]]
+    for i in range(1, owners):
+        arrived.append(lax.ppermute(blocks[i], "store", [(s, s ^ i) for s in range(owners)]))
+    return jnp.stack(arrived)
 
 
 def in_hbm(array):

time: 71 us -> 88.6 us (1.25)
  blocking collectives: 53.5 us -> 0 us
  starting transfers between devices: 0.01 us -> 48.1 us
  waiting for transfers between devices: 2.4 us -> 25.8 us
    all_to_all x4 -> x0, blocking collectives: 53.5 us -> none  [exchange(): lax.all_to_all(blocks, 'store', split_axis=0, concat_axis=0, tiled=True)]
    ppermute x0 -> x28, starting transfers between devices: none -> 48.1 us  [exchange(): lax.ppermute(blocks[i], 'store', [(s, s ^ i) for s in range(owners)])]
    ppermute x0 -> x28, waiting for transfers between devices: none -> 23.4 us  [exchange(): lax.ppermute(blocks[i], 'store', [(s, s ^ i) for s in range(owners)])]
  transfers between devices with their start and end apart: 2 -> 30, of which waited for: 2 -> 10; matrix products, arithmetic and copies ran while one was open for 0% -> 0% of each run, Pallas kernels for 0% -> 0%
where the time goes in v10:
time: 88.6 us; the launch traced here: 88.5 us
  starting transfers between devices  48.1 us (54%)
  waiting for transfers between devices  25.8 us (29%)
  Pallas kernels  13.4 us (15%)
  between operations  0.96 us (1%)
    ppermute x28, starting transfers between devices, exchange(): lax.ppermute(blocks[i], 'store', [(s, s ^ i) for s in range(owners)])  48.1 us
    ppermute x28, waiting for transfers between devices, exchange(): lax.ppermute(blocks[i], 'store', [(s, s ^ i) for s in range(owners)])  23.4 us
    pallas_call x1, Pallas kernels, shards(): pl.pallas_call(functools.partial(attend_kernel, owners, heads), out_shape...  7.5 us
    ppermute x2, waiting for transfers between devices, swap_cores(): return lax.ppermute(part, 'tensor', [(0, 1), (1, 0)])  2.4 us
    pallas_call x1, Pallas kernels, shards(): pl.pallas_call(functools.partial(dispatch_kernel, owners, heads, adapt, r...  2.28 us
  transfers between devices with their start and end apart: 30, of which 10 were waited for; matrix products, arithmetic and copies ran while one was open for 0% of the time, Pallas kernels for 0%

profile of v10, /device:TPU:0, one launch (start us, length us, event | category | flops | bytes accessed | tf_op | source)
XLA Modules:
  0.0 88.5 jit_solution(16878662749551742017)
XLA Ops:
  0.6 2.3 %dispatch.1 = (s32[64]{0:T(128)S(1)}, bf16[8,16,1152]{2,1,0:T(8,128)(2,1)S(1)}, bf16[128,4096]{1,0:T(8,128)(2,1)S(1)}, bf16[128,4096]{1,0:T(8,128)(2,1)S(1)}) custom-call(s32[16]{0:T(128)} %ids_hbm.1, s32[64]{0:T(128)} %slot_of_hbm.1, s32[16]{0:T(128)} %lengths_hbm.1, bf16[2,16,4096]{2,1,0:T(8,128)(2,1)} %x_hbm.1, bf16[128,8192]{1,0:T(8,128)(2,1)} %bitcast.122, ...), custom_call_target="tpu_custom_call" | custom-call | tf_op jit(solution)/shard_map/dispatch/pallas_call | solution.py:488
  3.0 3.0 %collective-permute-start = (bf16[16,1152]{1,0:T(8,128)(2,1)S(1)}, bf16[16,1152]{1,0:T(8,128)(2,1)S(1)}, u32[]{:S(2)}, u32[]{:S(2)}) collective-permute-start(bf16[16,1152]{1,0:T(8,128)(2,1)S(1)} %get-tuple-element.24), channel_id=1, source_target_pairs={{0,2},{2,0},{4,6},{6,4},{8,10},{10,8},{12,14},{14,12},{1,3},{3,1},... | collective-permute-start | bytes 110600 | tf_op jit(solution)/shard_map/ppermute | solution.py:445
  6.0 3.5 %collective-permute-start.6 = (bf16[16,1152]{1,0:T(8,128)(2,1)S(1)}, bf16[16,1152]{1,0:T(8,128)(2,1)S(1)}, u32[]{:S(2)}, u32[]{:S(2)}) collective-permute-start(bf16[16,1152]{1,0:T(8,128)(2,1)S(1)} %get-tuple-element.18), channel_id=1, source_target_pairs={{0,14},{2,12},{4,10},{6,8},{8,6},{10,4},{12,2},{14,0},{1,15},{3,13... | collective-permute-start | bytes 110600 | tf_op jit(solution)/shard_map/ppermute | solution.py:445
  9.5 0.1 collective-permute-start.5
  9.6 1.9 %collective-permute-start.4 = (bf16[16,1152]{1,0:T(8,128)(2,1)S(1)}, bf16[16,1152]{1,0:T(8,128)(2,1)S(1)}, u32[]{:S(2)}, u32[]{:S(2)}) collective-permute-start(bf16[16,1152]{1,0:T(8,128)(2,1)S(1)} %get-tuple-element.20), channel_id=1, source_target_pairs={{0,10},{2,8},{4,14},{6,12},{8,2},{10,0},{12,6},{14,4},{1,11},{3,9}... | collective-permute-start | bytes 110600 | tf_op jit(solution)/shard_map/ppermute | solution.py:445
  11.5 2.1 %collective-permute-start.3 = (bf16[16,1152]{1,0:T(8,128)(2,1)S(1)}, bf16[16,1152]{1,0:T(8,128)(2,1)S(1)}, u32[]{:S(2)}, u32[]{:S(2)}) collective-permute-start(bf16[16,1152]{1,0:T(8,128)(2,1)S(1)} %get-tuple-element.21), channel_id=1, source_target_pairs={{0,8},{2,10},{4,12},{6,14},{8,0},{10,2},{12,4},{14,6},{1,9},{3,11}... | collective-permute-start | bytes 110600 | tf_op jit(solution)/shard_map/ppermute | solution.py:445
  13.6 0.0 collective-permute-done
  13.6 1.2 %collective-permute-start.1 = (bf16[16,1152]{1,0:T(8,128)(2,1)S(1)}, bf16[16,1152]{1,0:T(8,128)(2,1)S(1)}, u32[]{:S(2)}, u32[]{:S(2)}) collective-permute-start(bf16[16,1152]{1,0:T(8,128)(2,1)S(1)} %get-tuple-element.23), channel_id=1, source_target_pairs={{0,4},{2,6},{4,0},{6,2},{8,12},{10,14},{12,8},{14,10},{1,5},{3,7},... | collective-permute-start | bytes 110600 | tf_op jit(solution)/shard_map/ppermute | solution.py:445
  14.9 2.7 %collective-permute-done.1 = bf16[16,1152]{1,0:T(8,128)(2,1)S(1)} collective-permute-done((bf16[16,1152]{1,0:T(8,128)(2,1)S(1)}, bf16[16,1152]{1,0:T(8,128)(2,1)S(1)}, u32[]{:S(2)}, u32[]{:S(2)}) %collective-permute-start.1) | collective-permute-done | bytes 36896 | tf_op jit(solution)/shard_map/ppermute | solution.py:445
  17.6 1.2 %collective-permute-start.2 = (bf16[16,1152]{1,0:T(8,128)(2,1)S(1)}, bf16[16,1152]{1,0:T(8,128)(2,1)S(1)}, u32[]{:S(2)}, u32[]{:S(2)}) collective-permute-start(bf16[16,1152]{1,0:T(8,128)(2,1)S(1)} %get-tuple-element.22), channel_id=1, source_target_pairs={{0,6},{2,4},{4,2},{6,0},{8,14},{10,12},{12,10},{14,8},{1,7},{3,5},... | collective-permute-start | bytes 110600 | tf_op jit(solution)/shard_map/ppermute | solution.py:445
  18.9 3.6 %collective-permute-done.2 = bf16[16,1152]{1,0:T(8,128)(2,1)S(1)} collective-permute-done((bf16[16,1152]{1,0:T(8,128)(2,1)S(1)}, bf16[16,1152]{1,0:T(8,128)(2,1)S(1)}, u32[]{:S(2)}, u32[]{:S(2)}) %collective-permute-start.2) | collective-permute-done | bytes 36896 | tf_op jit(solution)/shard_map/ppermute | solution.py:445
  22.6 0.6 project_query.1
  23.2 1.2 %collective-permute-done.7.other = f32[32,128]{1,0:T(8,128)S(1)} collective-permute-done((f32[32,128]{1,0:T(8,128)S(1)}, f32[32,128]{1,0:T(8,128)S(1)}, u32[]{:S(2)}, u32[]{:S(2)}) %collective-permute-start.7) | collective-permute-done | bytes 16416 | tf_op jit(solution)/shard_map/ppermute | solution.py:454
  24.4 0.4 expand_query.1
  24.9 0.7 collective-permute-start.8
  25.6 4.4 %collective-permute-start.14 = (bf16[16,1024]{1,0:T(8,128)(2,1)S(1)}, bf16[16,1024]{1,0:T(8,128)(2,1)S(1)}, u32[]{:S(2)}, u32[]{:S(2)}) collective-permute-start(bf16[16,1024]{1,0:T(8,128)(2,1)S(1)} %get-tuple-element.42), channel_id=1, source_target_pairs={{0,14},{2,12},{4,10},{6,8},{8,6},{10,4},{12,2},{14,0},{1,15},{3,13... | collective-permute-start | bytes 98312 | tf_op jit(solution)/shard_map/ppermute | solution.py:445
  30.0 0.2 collective-permute-start.13
  30.2 0.7 collective-permute-start.12
  30.9 2.3 %collective-permute-start.11 = (bf16[16,1024]{1,0:T(8,128)(2,1)S(1)}, bf16[16,1024]{1,0:T(8,128)(2,1)S(1)}, u32[]{:S(2)}, u32[]{:S(2)}) collective-permute-start(bf16[16,1024]{1,0:T(8,128)(2,1)S(1)} %get-tuple-element.45), channel_id=1, source_target_pairs={{0,8},{2,10},{4,12},{6,14},{8,0},{10,2},{12,4},{14,6},{1,9},{3,11}... | collective-permute-start | bytes 98312 | tf_op jit(solution)/shard_map/ppermute | solution.py:445
  33.2 1.2 %collective-permute-start.9 = (bf16[16,1024]{1,0:T(8,128)(2,1)S(1)}, bf16[16,1024]{1,0:T(8,128)(2,1)S(1)}, u32[]{:S(2)}, u32[]{:S(2)}) collective-permute-start(bf16[16,1024]{1,0:T(8,128)(2,1)S(1)} %get-tuple-element.47), channel_id=1, source_target_pairs={{0,4},{2,6},{4,0},{6,2},{8,12},{10,14},{12,8},{14,10},{1,5},{3,7},... | collective-permute-start | bytes 98312 | tf_op jit(solution)/shard_map/ppermute | solution.py:445
  34.4 2.7 %collective-permute-done.9 = bf16[16,1024]{1,0:T(8,128)(2,1)S(1)} collective-permute-done((bf16[16,1024]{1,0:T(8,128)(2,1)S(1)}, bf16[16,1024]{1,0:T(8,128)(2,1)S(1)}, u32[]{:S(2)}, u32[]{:S(2)}) %collective-permute-start.9) | collective-permute-done | bytes 32800 | tf_op jit(solution)/shard_map/ppermute | solution.py:445
  37.1 2.1 %collective-permute-start.10 = (bf16[16,1024]{1,0:T(8,128)(2,1)S(1)}, bf16[16,1024]{1,0:T(8,128)(2,1)S(1)}, u32[]{:S(2)}, u32[]{:S(2)}) collective-permute-start(bf16[16,1024]{1,0:T(8,128)(2,1)S(1)} %get-tuple-element.46), channel_id=1, source_target_pairs={{0,6},{2,4},{4,2},{6,0},{8,14},{10,12},{12,10},{14,8},{1,7},{3,5},... | collective-permute-start | bytes 98312 | tf_op jit(solution)/shard_map/ppermute | solution.py:445
  39.2 2.7 %collective-permute-done.10 = bf16[16,1024]{1,0:T(8,128)(2,1)S(1)} collective-permute-done((bf16[16,1024]{1,0:T(8,128)(2,1)S(1)}, bf16[16,1024]{1,0:T(8,128)(2,1)S(1)}, u32[]{:S(2)}, u32[]{:S(2)}) %collective-permute-start.10) | collective-permute-done | bytes 32800 | tf_op jit(solution)/shard_map/ppermute | solution.py:445
  42.0 0.0 copy-start
  42.0 0.0 copy-start.1
  42.1 7.5 %attend.1 = (bf16[2,16,4096]{2,1,0:T(8,128)(2,1)}, bf16[8,16,1024]{2,1,0:T(8,128)(2,1)S(1)}) custom-call(s32[64]{0:T(128)S(1)} %get-tuple-element.10.meta, bf16[2,16,4096]{2,1,0:T(8,128)(2,1)} %q_hbm.1, bf16[2,16,512]{2,1,0:T(8,128)(2,1)} %kn_hbm.1, bf16[2,16,512]{2,1,0:T(8,128)(2,1)} %vn_hbm.1, bf16[16,512,512]{2,1,0:T(8,128)(2,1)} %k_hbm.1, ...), custom_call_target="tpu_custom_call" | custom-call | tf_op jit(solution)/shard_map/attend/pallas_call | solution.py:535
  49.6 1.4 %collective-permute-start.15 = (bf16[16,1024]{1,0:T(8,128)(2,1)S(1)}, bf16[16,1024]{1,0:T(8,128)(2,1)S(1)}, u32[]{:S(2)}, u32[]{:S(2)}) collective-permute-start(bf16[16,1024]{1,0:T(8,128)(2,1)S(1)} %get-tuple-element.40), channel_id=1, source_target_pairs={{0,2},{2,0},{4,6},{6,4},{8,10},{10,8},{12,14},{14,12},{1,3},{3,1},... | collective-permute-start | bytes 98312 | tf_op jit(solution)/shard_map/ppermute | solution.py:445
  51.0 3.5 %collective-permute-start.21 = (bf16[16,1024]{1,0:T(8,128)(2,1)S(1)}, bf16[16,1024]{1,0:T(8,128)(2,1)S(1)}, u32[]{:S(2)}, u32[]{:S(2)}) collective-permute-start(bf16[16,1024]{1,0:T(8,128)(2,1)S(1)} %get-tuple-element.34), channel_id=1, source_target_pairs={{0,14},{2,12},{4,10},{6,8},{8,6},{10,4},{12,2},{14,0},{1,15},{3,13... | collective-permute-start | bytes 98312 | tf_op jit(solution)/shard_map/ppermute | solution.py:445
  54.6 0.4 collective-permute-start.20
  55.0 1.5 %collective-permute-start.19 = (bf16[16,1024]{1,0:T(8,128)(2,1)S(1)}, bf16[16,1024]{1,0:T(8,128)(2,1)S(1)}, u32[]{:S(2)}, u32[]{:S(2)}) collective-permute-start(bf16[16,1024]{1,0:T(8,128)(2,1)S(1)} %get-tuple-element.36), channel_id=1, source_target_pairs={{0,10},{2,8},{4,14},{6,12},{8,2},{10,0},{12,6},{14,4},{1,11},{3,9}... | collective-permute-start | bytes 98312 | tf_op jit(solution)/shard_map/ppermute | solution.py:445
  56.5 2.2 %collective-permute-start.18 = (bf16[16,1024]{1,0:T(8,128)(2,1)S(1)}, bf16[16,1024]{1,0:T(8,128)(2,1)S(1)}, u32[]{:S(2)}, u32[]{:S(2)}) collective-permute-start(bf16[16,1024]{1,0:T(8,128)(2,1)S(1)} %get-tuple-element.37), channel_id=1, source_target_pairs={{0,8},{2,10},{4,12},{6,14},{8,0},{10,2},{12,4},{14,6},{1,9},{3,11}... | collective-permute-start | bytes 98312 | tf_op jit(solution)/shard_map/ppermute | solution.py:445
  58.7 1.3 %collective-permute-start.16 = (bf16[16,1024]{1,0:T(8,128)(2,1)S(1)}, bf16[16,1024]{1,0:T(8,128)(2,1)S(1)}, u32[]{:S(2)}, u32[]{:S(2)}) collective-permute-start(bf16[16,1024]{1,0:T(8,128)(2,1)S(1)} %get-tuple-element.39), channel_id=1, source_target_pairs={{0,4},{2,6},{4,0},{6,2},{8,12},{10,14},{12,8},{14,10},{1,5},{3,7},... | collective-permute-start | bytes 98312 | tf_op jit(solution)/shard_map/ppermute | solution.py:445
  60.0 2.6 %collective-permute-done.16 = bf16[16,1024]{1,0:T(8,128)(2,1)S(1)} collective-permute-done((bf16[16,1024]{1,0:T(8,128)(2,1)S(1)}, bf16[16,1024]{1,0:T(8,128)(2,1)S(1)}, u32[]{:S(2)}, u32[]{:S(2)}) %collective-permute-start.16) | collective-permute-done | bytes 32800 | tf_op jit(solution)/shard_map/ppermute | solution.py:445
  62.6 1.3 %collective-permute-start.17 = (bf16[16,1024]{1,0:T(8,128)(2,1)S(1)}, bf16[16,1024]{1,0:T(8,128)(2,1)S(1)}, u32[]{:S(2)}, u32[]{:S(2)}) collective-permute-start(bf16[16,1024]{1,0:T(8,128)(2,1)S(1)} %get-tuple-element.38), channel_id=1, source_target_pairs={{0,6},{2,4},{4,2},{6,0},{8,14},{10,12},{12,10},{14,8},{1,7},{3,5},... | collective-permute-start | bytes 98312 | tf_op jit(solution)/shard_map/ppermute | solution.py:445
  63.9 3.5 %collective-permute-done.17 = bf16[16,1024]{1,0:T(8,128)(2,1)S(1)} collective-permute-done((bf16[16,1024]{1,0:T(8,128)(2,1)S(1)}, bf16[16,1024]{1,0:T(8,128)(2,1)S(1)}, u32[]{:S(2)}, u32[]{:S(2)}) %collective-permute-start.17) | collective-permute-done | bytes 32800 | tf_op jit(solution)/shard_map/ppermute | solution.py:445
  67.5 0.6 project_output.1.mine
  68.1 1.2 %collective-permute-done.22.other = f32[32,128]{1,0:T(8,128)S(1)} collective-permute-done((f32[32,128]{1,0:T(8,128)S(1)}, f32[32,128]{1,0:T(8,128)S(1)}, u32[]{:S(2)}, u32[]{:S(2)}) %collective-permute-start.22) | collective-permute-done | bytes 16416 | tf_op jit(solution)/shard_map/ppermute | solution.py:454
  69.3 0.5 expand_output.1
  69.8 0.7 collective-permute-start.23
  70.5 4.5 %collective-permute-start.29 = (bf16[16,1024]{1,0:T(8,128)(2,1)S(1)}, bf16[16,1024]{1,0:T(8,128)(2,1)S(1)}, u32[]{:S(2)}, u32[]{:S(2)}) collective-permute-start(bf16[16,1024]{1,0:T(8,128)(2,1)S(1)} %get-tuple-element.26), channel_id=1, source_target_pairs={{0,14},{2,12},{4,10},{6,8},{8,6},{10,4},{12,2},{14,0},{1,15},{3,13... | collective-permute-start | bytes 98312 | tf_op jit(solution)/shard_map/ppermute | solution.py:445
  75.0 0.2 collective-permute-start.28
  75.2 0.6 collective-permute-start.27
  75.8 2.4 %collective-permute-start.26 = (bf16[16,1024]{1,0:T(8,128)(2,1)S(1)}, bf16[16,1024]{1,0:T(8,128)(2,1)S(1)}, u32[]{:S(2)}, u32[]{:S(2)}) collective-permute-start(bf16[16,1024]{1,0:T(8,128)(2,1)S(1)} %get-tuple-element.29), channel_id=1, source_target_pairs={{0,8},{2,10},{4,12},{6,14},{8,0},{10,2},{12,4},{14,6},{1,9},{3,11}... | collective-permute-start | bytes 98312 | tf_op jit(solution)/shard_map/ppermute | solution.py:445
  78.2 1.2 %collective-permute-start.24 = (bf16[16,1024]{1,0:T(8,128)(2,1)S(1)}, bf16[16,1024]{1,0:T(8,128)(2,1)S(1)}, u32[]{:S(2)}, u32[]{:S(2)}) collective-permute-start(bf16[16,1024]{1,0:T(8,128)(2,1)S(1)} %get-tuple-element.31), channel_id=1, source_target_pairs={{0,4},{2,6},{4,0},{6,2},{8,12},{10,14},{12,8},{14,10},{1,5},{3,7},... | collective-permute-start | bytes 98312 | tf_op jit(solution)/shard_map/ppermute | solution.py:445
  79.4 2.7 %collective-permute-done.24 = bf16[16,1024]{1,0:T(8,128)(2,1)S(1)} collective-permute-done((bf16[16,1024]{1,0:T(8,128)(2,1)S(1)}, bf16[16,1024]{1,0:T(8,128)(2,1)S(1)}, u32[]{:S(2)}, u32[]{:S(2)}) %collective-permute-start.24) | collective-permute-done | bytes 32800 | tf_op jit(solution)/shard_map/ppermute | solution.py:445
  82.1 2.1 %collective-permute-start.25 = (bf16[16,1024]{1,0:T(8,128)(2,1)S(1)}, bf16[16,1024]{1,0:T(8,128)(2,1)S(1)}, u32[]{:S(2)}, u32[]{:S(2)}) collective-permute-start(bf16[16,1024]{1,0:T(8,128)(2,1)S(1)} %get-tuple-element.30), channel_id=1, source_target_pairs={{0,6},{2,4},{4,2},{6,0},{8,14},{10,12},{12,10},{14,8},{1,7},{3,5},... | collective-permute-start | bytes 98312 | tf_op jit(solution)/shard_map/ppermute | solution.py:445
  84.2 2.7 %collective-permute-done.25 = bf16[16,1024]{1,0:T(8,128)(2,1)S(1)} collective-permute-done((bf16[16,1024]{1,0:T(8,128)(2,1)S(1)}, bf16[16,1024]{1,0:T(8,128)(2,1)S(1)}, u32[]{:S(2)}, u32[]{:S(2)}) %collective-permute-start.25) | collective-permute-done | bytes 32800 | tf_op jit(solution)/shard_map/ppermute | solution.py:445
  87.0 1.5 %collect.1 = bf16[2,16,4096]{2,1,0:T(8,128)(2,1)} custom-call(s32[64]{0:T(128)S(1)} %get-tuple-element.10.meta, bf16[8,16,1024]{2,1,0:T(8,128)(2,1)S(1)} %constant_dynamic-update-slice_fusion.24.blocks), custom_call_target="tpu_custom_call" | custom-call | tf_op jit(solution)/shard_map/collect/pallas_call | solution.py:567
  (55 shorter events, 0.3 us)
Async XLA Ops:
  3.0 10.7 %collective-permute-start = (bf16[16,1152]{1,0:T(8,128)(2,1)S(1)}, bf16[16,1152]{1,0:T(8,128)(2,1)S(1)}, u32[]{:S(2)}, u32[]{:S(2)}) collective-permute-start(bf16[16,1152]{1,0:T(8,128)(2,1)S(1)} %get-tuple-element.24), channel_id=1, source_target_pairs={{0,2},{2,0},{4,6},{6,4},{8,10},{10,8},{12,14},{14,12},{1,3},{3,1},... | collective-permute-start | bytes 110600 | tf_op jit(solution)/shard_map/ppermute | solution.py:445
  6.0 16.5 %collective-permute-start.6 = (bf16[16,1152]{1,0:T(8,128)(2,1)S(1)}, bf16[16,1152]{1,0:T(8,128)(2,1)S(1)}, u32[]{:S(2)}, u32[]{:S(2)}) collective-permute-start(bf16[16,1152]{1,0:T(8,128)(2,1)S(1)} %get-tuple-element.18), channel_id=1, source_target_pairs={{0,14},{2,12},{4,10},{6,8},{8,6},{10,4},{12,2},{14,0},{1,15},{3,13... | collective-permute-start | bytes 110600 | tf_op jit(solution)/shard_map/ppermute | solution.py:445
  9.5 13.0 %collective-permute-start.5 = (bf16[16,1152]{1,0:T(8,128)(2,1)S(1)}, bf16[16,1152]{1,0:T(8,128)(2,1)S(1)}, u32[]{:S(2)}, u32[]{:S(2)}) collective-permute-start(bf16[16,1152]{1,0:T(8,128)(2,1)S(1)} %get-tuple-element.19), channel_id=1, source_target_pairs={{0,12},{2,14},{4,8},{6,10},{8,4},{10,6},{12,0},{14,2},{1,13},{3,15... | collective-permute-start | bytes 110600 | tf_op jit(solution)/shard_map/ppermute | solution.py:445
  9.6 12.9 %collective-permute-start.4 = (bf16[16,1152]{1,0:T(8,128)(2,1)S(1)}, bf16[16,1152]{1,0:T(8,128)(2,1)S(1)}, u32[]{:S(2)}, u32[]{:S(2)}) collective-permute-start(bf16[16,1152]{1,0:T(8,128)(2,1)S(1)} %get-tuple-element.20), channel_id=1, source_target_pairs={{0,10},{2,8},{4,14},{6,12},{8,2},{10,0},{12,6},{14,4},{1,11},{3,9}... | collective-permute-start | bytes 110600 | tf_op jit(solution)/shard_map/ppermute | solution.py:445
  11.5 11.0 %collective-permute-start.3 = (bf16[16,1152]{1,0:T(8,128)(2,1)S(1)}, bf16[16,1152]{1,0:T(8,128)(2,1)S(1)}, u32[]{:S(2)}, u32[]{:S(2)}) collective-permute-start(bf16[16,1152]{1,0:T(8,128)(2,1)S(1)} %get-tuple-element.21), channel_id=1, source_target_pairs={{0,8},{2,10},{4,12},{6,14},{8,0},{10,2},{12,4},{14,6},{1,9},{3,11}... | collective-permute-start | bytes 110600 | tf_op jit(solution)/shard_map/ppermute | solution.py:445
  13.6 4.0 %collective-permute-start.1 = (bf16[16,1152]{1,0:T(8,128)(2,1)S(1)}, bf16[16,1152]{1,0:T(8,128)(2,1)S(1)}, u32[]{:S(2)}, u32[]{:S(2)}) collective-permute-start(bf16[16,1152]{1,0:T(8,128)(2,1)S(1)} %get-tuple-element.23), channel_id=1, source_target_pairs={{0,4},{2,6},{4,0},{6,2},{8,12},{10,14},{12,8},{14,10},{1,5},{3,7},... | collective-permute-start | bytes 110600 | tf_op jit(solution)/shard_map/ppermute | solution.py:445
  17.6 4.9 %collective-permute-start.2 = (bf16[16,1152]{1,0:T(8,128)(2,1)S(1)}, bf16[16,1152]{1,0:T(8,128)(2,1)S(1)}, u32[]{:S(2)}, u32[]{:S(2)}) collective-permute-start(bf16[16,1152]{1,0:T(8,128)(2,1)S(1)} %get-tuple-element.22), channel_id=1, source_target_pairs={{0,6},{2,4},{4,2},{6,0},{8,14},{10,12},{12,10},{14,8},{1,7},{3,5},... | collective-permute-start | bytes 110600 | tf_op jit(solution)/shard_map/ppermute | solution.py:445
  23.2 1.2 %collective-permute-start.7 = (f32[32,128]{1,0:T(8,128)S(1)}, f32[32,128]{1,0:T(8,128)S(1)}, u32[]{:S(2)}, u32[]{:S(2)}) collective-permute-start(f32[32,128]{1,0:T(8,128)S(1)} %get-tuple-element.13.mine), channel_id=1, source_target_pairs={{0,1},{1,0},{2,3},{3,2},{4,5},{5,4},{6,7},{7,6},{8,9},{9,8},{10,11... | collective-permute-start | bytes 49160 | tf_op jit(solution)/shard_map/ppermute | solution.py:454
  24.9 8.4 %collective-permute-start.8 = (bf16[16,1024]{1,0:T(8,128)(2,1)S(1)}, bf16[16,1024]{1,0:T(8,128)(2,1)S(1)}, u32[]{:S(2)}, u32[]{:S(2)}) collective-permute-start(bf16[16,1024]{1,0:T(8,128)(2,1)S(1)} %get-tuple-element.48), channel_id=1, source_target_pairs={{0,2},{2,0},{4,6},{6,4},{8,10},{10,8},{12,14},{14,12},{1,3},{3,1},... | collective-permute-start | bytes 98312 | tf_op jit(solution)/shard_map/ppermute | solution.py:445
  25.6 16.4 %collective-permute-start.14 = (bf16[16,1024]{1,0:T(8,128)(2,1)S(1)}, bf16[16,1024]{1,0:T(8,128)(2,1)S(1)}, u32[]{:S(2)}, u32[]{:S(2)}) collective-permute-start(bf16[16,1024]{1,0:T(8,128)(2,1)S(1)} %get-tuple-element.42), channel_id=1, source_target_pairs={{0,14},{2,12},{4,10},{6,8},{8,6},{10,4},{12,2},{14,0},{1,15},{3,13... | collective-permute-start | bytes 98312 | tf_op jit(solution)/shard_map/ppermute | solution.py:445
  30.0 12.0 %collective-permute-start.13 = (bf16[16,1024]{1,0:T(8,128)(2,1)S(1)}, bf16[16,1024]{1,0:T(8,128)(2,1)S(1)}, u32[]{:S(2)}, u32[]{:S(2)}) collective-permute-start(bf16[16,1024]{1,0:T(8,128)(2,1)S(1)} %get-tuple-element.43), channel_id=1, source_target_pairs={{0,12},{2,14},{4,8},{6,10},{8,4},{10,6},{12,0},{14,2},{1,13},{3,15... | collective-permute-start | bytes 98312 | tf_op jit(solution)/shard_map/ppermute | solution.py:445
  30.2 11.8 %collective-permute-start.12 = (bf16[16,1024]{1,0:T(8,128)(2,1)S(1)}, bf16[16,1024]{1,0:T(8,128)(2,1)S(1)}, u32[]{:S(2)}, u32[]{:S(2)}) collective-permute-start(bf16[16,1024]{1,0:T(8,128)(2,1)S(1)} %get-tuple-element.44), channel_id=1, source_target_pairs={{0,10},{2,8},{4,14},{6,12},{8,2},{10,0},{12,6},{14,4},{1,11},{3,9}... | collective-permute-start | bytes 98312 | tf_op jit(solution)/shard_map/ppermute | solution.py:445
  30.9 11.1 %collective-permute-start.11 = (bf16[16,1024]{1,0:T(8,128)(2,1)S(1)}, bf16[16,1024]{1,0:T(8,128)(2,1)S(1)}, u32[]{:S(2)}, u32[]{:S(2)}) collective-permute-start(bf16[16,1024]{1,0:T(8,128)(2,1)S(1)} %get-tuple-element.45), channel_id=1, source_target_pairs={{0,8},{2,10},{4,12},{6,14},{8,0},{10,2},{12,4},{14,6},{1,9},{3,11}... | collective-permute-start | bytes 98312 | tf_op jit(solution)/shard_map/ppermute | solution.py:445
  33.2 3.9 %collective-permute-start.9 = (bf16[16,1024]{1,0:T(8,128)(2,1)S(1)}, bf16[16,1024]{1,0:T(8,128)(2,1)S(1)}, u32[]{:S(2)}, u32[]{:S(2)}) collective-permute-start(bf16[16,1024]{1,0:T(8,128)(2,1)S(1)} %get-tuple-element.47), channel_id=1, source_target_pairs={{0,4},{2,6},{4,0},{6,2},{8,12},{10,14},{12,8},{14,10},{1,5},{3,7},... | collective-permute-start | bytes 98312 | tf_op jit(solution)/shard_map/ppermute | solution.py:445
  37.1 4.8 %collective-permute-start.10 = (bf16[16,1024]{1,0:T(8,128)(2,1)S(1)}, bf16[16,1024]{1,0:T(8,128)(2,1)S(1)}, u32[]{:S(2)}, u32[]{:S(2)}) collective-permute-start(bf16[16,1024]{1,0:T(8,128)(2,1)S(1)} %get-tuple-element.46), channel_id=1, source_target_pairs={{0,6},{2,4},{4,2},{6,0},{8,14},{10,12},{12,10},{14,8},{1,7},{3,5},... | collective-permute-start | bytes 98312 | tf_op jit(solution)/shard_map/ppermute | solution.py:445
  42.0 25.5 %copy-start = (bf16[8192,8,16]{0,2,1:T(8,128)(2,1)S(1)}, bf16[8192,8,16]{0,2,1:T(8,128)(2,1)}, u32[]{:S(2)}) copy-start(bf16[8192,8,16]{0,2,1:T(8,128)(2,1)} %param.24) | copy-start | bytes 6291460
  42.0 27.3 %copy-start.1 = (bf16[8,16,4096]{2,1,0:T(8,128)(2,1)S(1)}, bf16[8,16,4096]{2,1,0:T(8,128)(2,1)}, u32[]{:S(2)}) copy-start(bf16[8,16,4096]{2,1,0:T(8,128)(2,1)} %param.25) | copy-start | bytes 3145732
  49.6 9.1 %collective-permute-start.15 = (bf16[16,1024]{1,0:T(8,128)(2,1)S(1)}, bf16[16,1024]{1,0:T(8,128)(2,1)S(1)}, u32[]{:S(2)}, u32[]{:S(2)}) collective-permute-start(bf16[16,1024]{1,0:T(8,128)(2,1)S(1)} %get-tuple-element.40), channel_id=1, source_target_pairs={{0,2},{2,0},{4,6},{6,4},{8,10},{10,8},{12,14},{14,12},{1,3},{3,1},... | collective-permute-start | bytes 98312 | tf_op jit(solution)/shard_map/ppermute | solution.py:445
  51.0 16.4 %collective-permute-start.21 = (bf16[16,1024]{1,0:T(8,128)(2,1)S(1)}, bf16[16,1024]{1,0:T(8,128)(2,1)S(1)}, u32[]{:S(2)}, u32[]{:S(2)}) collective-permute-start(bf16[16,1024]{1,0:T(8,128)(2,1)S(1)} %get-tuple-element.34), channel_id=1, source_target_pairs={{0,14},{2,12},{4,10},{6,8},{8,6},{10,4},{12,2},{14,0},{1,15},{3,13... | collective-permute-start | bytes 98312 | tf_op jit(solution)/shard_map/ppermute | solution.py:445
  54.6 12.9 %collective-permute-start.20 = (bf16[16,1024]{1,0:T(8,128)(2,1)S(1)}, bf16[16,1024]{1,0:T(8,128)(2,1)S(1)}, u32[]{:S(2)}, u32[]{:S(2)}) collective-permute-start(bf16[16,1024]{1,0:T(8,128)(2,1)S(1)} %get-tuple-element.35), channel_id=1, source_target_pairs={{0,12},{2,14},{4,8},{6,10},{8,4},{10,6},{12,0},{14,2},{1,13},{3,15... | collective-permute-start | bytes 98312 | tf_op jit(solution)/shard_map/ppermute | solution.py:445
  55.0 12.5 %collective-permute-start.19 = (bf16[16,1024]{1,0:T(8,128)(2,1)S(1)}, bf16[16,1024]{1,0:T(8,128)(2,1)S(1)}, u32[]{:S(2)}, u32[]{:S(2)}) collective-permute-start(bf16[16,1024]{1,0:T(8,128)(2,1)S(1)} %get-tuple-element.36), channel_id=1, source_target_pairs={{0,10},{2,8},{4,14},{6,12},{8,2},{10,0},{12,6},{14,4},{1,11},{3,9}... | collective-permute-start | bytes 98312 | tf_op jit(solution)/shard_map/ppermute | solution.py:445
  56.5 11.0 %collective-permute-start.18 = (bf16[16,1024]{1,0:T(8,128)(2,1)S(1)}, bf16[16,1024]{1,0:T(8,128)(2,1)S(1)}, u32[]{:S(2)}, u32[]{:S(2)}) collective-permute-start(bf16[16,1024]{1,0:T(8,128)(2,1)S(1)} %get-tuple-element.37), channel_id=1, source_target_pairs={{0,8},{2,10},{4,12},{6,14},{8,0},{10,2},{12,4},{14,6},{1,9},{3,11}... | collective-permute-start | bytes 98312 | tf_op jit(solution)/shard_map/ppermute | solution.py:445
  58.7 3.9 %collective-permute-start.16 = (bf16[16,1024]{1,0:T(8,128)(2,1)S(1)}, bf16[16,1024]{1,0:T(8,128)(2,1)S(1)}, u32[]{:S(2)}, u32[]{:S(2)}) collective-permute-start(bf16[16,1024]{1,0:T(8,128)(2,1)S(1)} %get-tuple-element.39), channel_id=1, source_target_pairs={{0,4},{2,6},{4,0},{6,2},{8,12},{10,14},{12,8},{14,10},{1,5},{3,7},... | collective-permute-start | bytes 98312 | tf_op jit(solution)/shard_map/ppermute | solution.py:445
  62.6 4.8 %collective-permute-start.17 = (bf16[16,1024]{1,0:T(8,128)(2,1)S(1)}, bf16[16,1024]{1,0:T(8,128)(2,1)S(1)}, u32[]{:S(2)}, u32[]{:S(2)}) collective-permute-start(bf16[16,1024]{1,0:T(8,128)(2,1)S(1)} %get-tuple-element.38), channel_id=1, source_target_pairs={{0,6},{2,4},{4,2},{6,0},{8,14},{10,12},{12,10},{14,8},{1,7},{3,5},... | collective-permute-start | bytes 98312 | tf_op jit(solution)/shard_map/ppermute | solution.py:445
  68.1 1.2 %collective-permute-start.22 = (f32[32,128]{1,0:T(8,128)S(1)}, f32[32,128]{1,0:T(8,128)S(1)}, u32[]{:S(2)}, u32[]{:S(2)}) collective-permute-start(f32[32,128]{1,0:T(8,128)S(1)} %project_output.1.mine), channel_id=1, source_target_pairs={{0,1},{1,0},{2,3},{3,2},{4,5},{5,4},{6,7},{7,6},{8,9},{9,8},{10,11... | collective-permute-start | bytes 49160 | tf_op jit(solution)/shard_map/ppermute | solution.py:454
  69.8 8.4 %collective-permute-start.23 = (bf16[16,1024]{1,0:T(8,128)(2,1)S(1)}, bf16[16,1024]{1,0:T(8,128)(2,1)S(1)}, u32[]{:S(2)}, u32[]{:S(2)}) collective-permute-start(bf16[16,1024]{1,0:T(8,128)(2,1)S(1)} %get-tuple-element.32), channel_id=1, source_target_pairs={{0,2},{2,0},{4,6},{6,4},{8,10},{10,8},{12,14},{14,12},{1,3},{3,1},... | collective-permute-start | bytes 98312 | tf_op jit(solution)/shard_map/ppermute | solution.py:445
  70.5 16.4 %collective-permute-start.29 = (bf16[16,1024]{1,0:T(8,128)(2,1)S(1)}, bf16[16,1024]{1,0:T(8,128)(2,1)S(1)}, u32[]{:S(2)}, u32[]{:S(2)}) collective-permute-start(bf16[16,1024]{1,0:T(8,128)(2,1)S(1)} %get-tuple-element.26), channel_id=1, source_target_pairs={{0,14},{2,12},{4,10},{6,8},{8,6},{10,4},{12,2},{14,0},{1,15},{3,13... | collective-permute-start | bytes 98312 | tf_op jit(solution)/shard_map/ppermute | solution.py:445
  75.0 12.0 %collective-permute-start.28 = (bf16[16,1024]{1,0:T(8,128)(2,1)S(1)}, bf16[16,1024]{1,0:T(8,128)(2,1)S(1)}, u32[]{:S(2)}, u32[]{:S(2)}) collective-permute-start(bf16[16,1024]{1,0:T(8,128)(2,1)S(1)} %get-tuple-element.27), channel_id=1, source_target_pairs={{0,12},{2,14},{4,8},{6,10},{8,4},{10,6},{12,0},{14,2},{1,13},{3,15... | collective-permute-start | bytes 98312 | tf_op jit(solution)/shard_map/ppermute | solution.py:445
  75.2 11.8 %collective-permute-start.27 = (bf16[16,1024]{1,0:T(8,128)(2,1)S(1)}, bf16[16,1024]{1,0:T(8,128)(2,1)S(1)}, u32[]{:S(2)}, u32[]{:S(2)}) collective-permute-start(bf16[16,1024]{1,0:T(8,128)(2,1)S(1)} %get-tuple-element.28), channel_id=1, source_target_pairs={{0,10},{2,8},{4,14},{6,12},{8,2},{10,0},{12,6},{14,4},{1,11},{3,9}... | collective-permute-start | bytes 98312 | tf_op jit(solution)/shard_map/ppermute | solution.py:445
  75.8 11.1 %collective-permute-start.26 = (bf16[16,1024]{1,0:T(8,128)(2,1)S(1)}, bf16[16,1024]{1,0:T(8,128)(2,1)S(1)}, u32[]{:S(2)}, u32[]{:S(2)}) collective-permute-start(bf16[16,1024]{1,0:T(8,128)(2,1)S(1)} %get-tuple-element.29), channel_id=1, source_target_pairs={{0,8},{2,10},{4,12},{6,14},{8,0},{10,2},{12,4},{14,6},{1,9},{3,11}... | collective-permute-start | bytes 98312 | tf_op jit(solution)/shard_map/ppermute | solution.py:445
  78.2 3.9 %collective-permute-start.24 = (bf16[16,1024]{1,0:T(8,128)(2,1)S(1)}, bf16[16,1024]{1,0:T(8,128)(2,1)S(1)}, u32[]{:S(2)}, u32[]{:S(2)}) collective-permute-start(bf16[16,1024]{1,0:T(8,128)(2,1)S(1)} %get-tuple-element.31), channel_id=1, source_target_pairs={{0,4},{2,6},{4,0},{6,2},{8,12},{10,14},{12,8},{14,10},{1,5},{3,7},... | collective-permute-start | bytes 98312 | tf_op jit(solution)/shard_map/ppermute | solution.py:445
  82.1 4.8 %collective-permute-start.25 = (bf16[16,1024]{1,0:T(8,128)(2,1)S(1)}, bf16[16,1024]{1,0:T(8,128)(2,1)S(1)}, u32[]{:S(2)}, u32[]{:S(2)}) collective-permute-start(bf16[16,1024]{1,0:T(8,128)(2,1)S(1)} %get-tuple-element.30), channel_id=1, source_target_pairs={{0,6},{2,4},{4,2},{6,0},{8,14},{10,12},{12,10},{14,8},{1,7},{3,5},... | collective-permute-start | bytes 98312 | tf_op jit(solution)/shard_map/ppermute | solution.py:445

commit v11 on v7

--- a/solution.py
+++ b/solution.py
@@ -12,7 +12,6 @@
 CAP = 2
 STEPS = 2
 CHUNK = 128
-QUAD = 4
 BF16 = jnp.bfloat16
 F32 = jnp.float32
 I32 = jnp.int32
@@ -177,15 +176,6 @@
         meta[row_at + place] = r
         slot_at[place] = rest(slot, adapt)
         meta[r] = place
-    sizes = [lengths[r] for r in range(rows)]
-    for r in range(rows):
-        ahead = jnp.int32(0)
-        for q in range(rows):
-            if q != r:
-                shorter = sizes[q] <= sizes[r] if q < r else sizes[q] < sizes[r]
-                ahead = ahead + jnp.where(shorter, 1, 0)
-        meta[order + ahead] = r
-        meta[spans + r] = sizes[r]
     items = CAP * STEPS
     block = heads * items
     copies[3].wait()
@@ -197,6 +187,15 @@
         blocks[i, :, :wide] = packed[i * block : (i + 1) * block]
         slot = jnp.where(first, slot_at[i * CAP], slot_at[i * CAP + 1])
         blocks[i, :, wide:] = one_hot(lane_slot == slot)
+    sizes = [lengths[r] for r in range(rows)]
+    for r in range(rows):
+        ahead = jnp.int32(0)
+        for q in range(rows):
+            if q != r:
+                shorter = sizes[q] <= sizes[r] if q < r else sizes[q] < sizes[r]
+                ahead = ahead + jnp.where(shorter, 1, 0)
+        meta[order + ahead] = r
+        meta[spans + r] = sizes[r]
     for copy in copies[4:]:
         copy.wait()
 
@@ -228,7 +227,8 @@
     part_ref[...] = total * mask
 
 
-def expand_kernel(owners, heads, wide, mine, other, b_ref, blocks):
+def expand_kernel(owners, heads, wide, mine, other, b_ref, *refs):
+    blocks = refs[-1]
     low_rank = (mine[...] + other[...]).astype(BF16)
     pieces = []
     for c in range(heads):
@@ -242,18 +242,18 @@
         blocks[i] = back[i * block : (i + 1) * block]
 
 
-def quads(row_of, span_of, rows, sizes, action):
-    def body(quad, carry):
-        amount = over(span_of(row_of(quad * QUAD + QUAD - 1)) + (CHUNK - 1), CHUNK)
+def in_groups(row_of, span_of, rows, sizes, action):
+    at = 0
+    for count in [rows // 2] + [rows // 4] * 2:
+        group = [row_of(at + j) for j in range(count)]
+        amount = over(span_of(group[-1]) + (CHUNK - 1), CHUNK)
         for size in range(1, sizes + 1):
 
             @pl.when(amount == size)
             def _():
-                action([row_of(quad * QUAD + j) for j in range(QUAD)], size)
-
-        return carry
-
-    lax.fori_loop(0, rows // QUAD, body, 0)
+                action(group, size)
+
+        at += count
 
 
 def attend_kernel(
@@ -266,8 +266,9 @@
     k_hbm,
     v_hbm,
     blocks,
-    out_hbm,
+    mixed_out,
     outgoing,
+    spread_out,
     q_ref,
     kn_ref,
     vn_ref,
@@ -315,25 +316,22 @@
                 copy.start()
 
     chunks = k_hbm.shape[1] // CHUNK
-    quads(row_of, span_of, rows, chunks, begin)
+    in_groups(row_of, span_of, rows, chunks, begin)
 
     head_at = rest(over(iota((total, width), 0), STEPS), heads)
     mask_ref[...] = one_hot(head_at == over(iota((total, width), 1), HD))
-    head_own = rest(over(iota((QUAD * total, HD), 0), STEPS), heads)
+    head_own = rest(over(iota((total, HD), 0), STEPS), heads)
     blank = jnp.zeros((CHUNK - fresh_rows, width), BF16)
     kn_ref[fresh_rows:, :] = blank
     vn_ref[fresh_rows:, :] = blank
 
-    delta = jnp.dot(
-        unpack_matrix(meta, owners, heads, rows, True),
-        jnp.concatenate([blocks[i] for i in range(owners)], axis=0),
-        preferred_element_type=F32,
-    )
-    by_row = by_row_matrix(heads, rows)
+    gather = jnp.concatenate(
+        [by_row_matrix(heads, rows), unpack_matrix(meta, owners, heads, rows, True)], axis=1
+    )
     for copy in singles:
         copy.wait()
-    base = jnp.dot(by_row, stacked(q_ref, heads, wide), preferred_element_type=F32)
-    q_buf[...] = base + delta
+    sources = [stacked(q_ref, heads, wide)] + [blocks[i] for i in range(owners)]
+    q_buf[...] = jnp.dot(gather, jnp.concatenate(sources, axis=0), preferred_element_type=F32)
 
     factor = math.log2(math.e) / math.sqrt(HD)
     fresh_shape = (total, CHUNK)
@@ -356,85 +354,63 @@
                 [flat[:, j * HD : (j + 1) * HD] for j in range(groups)], axis=0
             ).astype(BF16)
             spreads.append(jnp.concatenate([one] * heads, axis=1) * mask_ref[...])
-        cached = [
-            lax.dot_general(spread, k_ref[row, :extent, :], contract, preferred_element_type=F32)
-            for row, spread in zip(rows_in, spreads)
-        ]
-        fresh = lax.dot_general(
-            jnp.concatenate(spreads, axis=0), kn_ref[...], contract, preferred_element_type=F32
-        )
-        scores = jnp.concatenate(
-            [
-                jnp.concatenate(
-                    [
-                        jnp.where(position < span_of(row), cached[k], -jnp.inf),
-                        jnp.where(fresh_row == row, fresh[k * total : (k + 1) * total], -jnp.inf),
-                    ],
-                    axis=1,
-                )
-                for k, row in enumerate(rows_in)
-            ],
-            axis=0,
-        )
-        top = jnp.max(scores, axis=1, keepdims=True)
-        weights = jnp.exp2((scores - top) * factor)
-        share = 1.0 / jnp.sum(weights, axis=1, keepdims=True)
-        weights = weights.astype(BF16)
-        mixed = jnp.dot(weights[:, extent:], vn_ref[...], preferred_element_type=F32)
-        mixed = mixed + jnp.concatenate(
-            [
-                jnp.dot(
-                    weights[k * total : (k + 1) * total, :extent],
-                    v_ref[row, :extent, :],
-                    preferred_element_type=F32,
-                )
-                for k, row in enumerate(rows_in)
-            ],
-            axis=0,
-        )
-        own = mixed[:, :HD]
-        for c in range(1, heads):
-            own = jnp.where(head_own == c, mixed[:, c * HD : (c + 1) * HD], own)
-        own = own * share
-        for k, start in enumerate(starts):
-            one = own[k * total : (k + 1) * total]
+        scores = []
+        for row, spread in zip(rows_in, spreads):
+            keys = jnp.concatenate([k_ref[row, :extent, :], kn_ref[...]], axis=0)
+            score = lax.dot_general(spread, keys, contract, preferred_element_type=F32)
+            cached = jnp.where(position < span_of(row), score[:, :extent], -jnp.inf)
+            fresh = jnp.where(fresh_row == row, score[:, extent:], -jnp.inf)
+            scores.append(jnp.concatenate([cached, fresh], axis=1))
+        tops = [jnp.max(score, axis=1, keepdims=True) for score in scores]
+        weights = [jnp.exp2((score - top) * factor) for score, top in zip(scores, tops)]
+        shares = [1.0 / jnp.sum(weight, axis=1, keepdims=True) for weight in weights]
+        for row, start, weight, share in zip(rows_in, starts, weights, shares):
+            values = jnp.concatenate([v_ref[row, :extent, :], vn_ref[...]], axis=0)
+            mixed = jnp.dot(weight.astype(BF16), values, preferred_element_type=F32)
+            own = mixed[:, :HD]
+            for c in range(1, heads):
+                own = jnp.where(head_own == c, mixed[:, c * HD : (c + 1) * HD], own)
+            own = own * share
             o_buf[pl.ds(start, pairs), :] = jnp.concatenate(
-                [one[j * pairs : (j + 1) * pairs] for j in range(groups)], axis=1
+                [own[j * pairs : (j + 1) * pairs] for j in range(groups)], axis=1
             )
 
-    quads(row_of, span_of, rows, chunks, attend)
+    in_groups(row_of, span_of, rows, chunks, attend)
 
     mixed = o_buf[...].astype(BF16)
-    final = exact(by_pair_matrix(heads, rows), mixed)
-    for c in range(heads):
-        for s in range(STEPS):
-            at = (c * STEPS + s) * rows
-            q_ref[s, :, c * wide : (c + 1) * wide] = final[at : at + rows]
-    result = pltpu.make_async_copy(q_ref, out_hbm, sems.at[0])
-    result.start()
+    mixed_out[...] = mixed
     packed = exact(pack_matrix(meta, owners, heads, rows, True), mixed)
     block = heads * CAP * STEPS
     for i in range(owners):
         outgoing[i] = packed[i * block : (i + 1) * block]
-    result.wait()
-
-
-def collect_kernel(owners, heads, meta, blocks, out_hbm, out_ref, sems):
+    spread_out[...] = unpack_matrix(meta, owners, heads, rows, False)
+
+
+def write_out(matrix, values, heads, out_hbm, out_ref, sems):
     rows = out_ref.shape[1]
     wide = out_ref.shape[2] // heads
     span = STEPS * rows
-    arrived = jnp.concatenate([blocks[i] for i in range(owners)], axis=0)
-    spread = unpack_matrix(meta, owners, heads, rows, False)
     copies = []
     for c in range(heads):
-        values = exact(spread[c * span : (c + 1) * span], arrived)
+        ordered = exact(matrix[c * span : (c + 1) * span], values)
         for s in range(STEPS):
-            out_ref[s, :, c * wide : (c + 1) * wide] = values[s * rows : (s + 1) * rows]
+            out_ref[s, :, c * wide : (c + 1) * wide] = ordered[s * rows : (s + 1) * rows]
         part = (slice(None), slice(None), pl.ds(c * wide, wide))
         copies.append(pltpu.make_async_copy(out_ref.at[part], out_hbm.at[part], sems.at[c]))
         copies[-1].start()
     for copy in copies:
         copy.wait()
+
+
+def finish_kernel(heads, mixed, part, out_hbm, after, out_ref, sems):
+    after[...] = part[: after.shape[0], :]
+    matrix = by_pair_matrix(heads, out_ref.shape[1])
+    write_out(matrix, mixed[...], heads, out_hbm, out_ref, sems)
+
+
+def collect_kernel(owners, heads, spread, blocks, out_hbm, out_ref, sems):
+    arrived = jnp.concatenate([blocks[i] for i in range(owners)], axis=0)
+    write_out(spread, arrived, heads, out_hbm, out_ref, sems)
 
 
 def exchange(blocks):
@@ -515,23 +491,27 @@
         name="project_query",
     )(a_near, arrived)
 
-    def expand(part, b_store, name):
+    def expand(part, other, b_store, name, *after):
         return pl.pallas_call(
             functools.partial(expand_kernel, owners, heads, wide),
             out_shape=sent,
-            in_specs=[VMEM] * 3,
+            in_specs=[VMEM] * (3 + len(after)),
             out_specs=VMEM,
             compiler_params=small,
             name=name,
-        )(part, swap_cores(part), b_store)
-
-    returned = exchange(expand(part, b_near, "expand_query"))
-
-    attn_out, outgoing = pl.pallas_call(
+        )(part, other, b_store, *after)
+
+    returned = exchange(expand(part, swap_cores(part), b_near, "expand_query"))
+
+    mixed, outgoing, spread = pl.pallas_call(
         functools.partial(attend_kernel, owners, heads),
-        out_shape=[shape((STEPS, rows, width), BF16), sent],
+        out_shape=[
+            shape((rows * STEPS * heads, wide), BF16),
+            sent,
+            shape((rows * STEPS * heads, owners * block), BF16),
+        ],
         in_specs=[SMEM] + [HBM] * 5 + [VMEM],
-        out_specs=[HBM, VMEM],
+        out_specs=[VMEM] * 3,
         scratch_shapes=[
             pltpu.VMEM(q_base.shape, BF16),
             pltpu.VMEM((CHUNK, heads * HD), BF16),
@@ -558,19 +538,33 @@
         compiler_params=small,
         name="project_output",
     )(flat(a_output), arrived, mask)
-    returned = exchange(expand(part, b_output.reshape(lanes, width), "expand_output"))
-    adapter_out = pl.pallas_call(
-        functools.partial(collect_kernel, owners, heads),
-        out_shape=shape((STEPS, rows, width), BF16),
-        in_specs=[SMEM, VMEM],
-        out_specs=HBM,
+    ordered = dict(
         scratch_shapes=[
             pltpu.VMEM((STEPS, rows, width), BF16),
             pltpu.SemaphoreType.DMA((heads,)),
         ],
         compiler_params=small,
+    )
+    other = swap_cores(part)
+    attn_out, after = pl.pallas_call(
+        functools.partial(finish_kernel, heads),
+        out_shape=[shape((STEPS, rows, width), BF16), shape((8, lanes), F32)],
+        in_specs=[VMEM] * 2,
+        out_specs=[HBM, VMEM],
+        name="finish",
+        **ordered,
+    )(mixed, part)
+    returned = exchange(
+        expand(part, other, b_output.reshape(lanes, width), "expand_output", after)
+    )
+    adapter_out = pl.pallas_call(
+        functools.partial(collect_kernel, owners, heads),
+        out_shape=shape((STEPS, rows, width), BF16),
+        in_specs=[VMEM] * 2,
+        out_specs=HBM,
         name="collect",
-    )(meta, returned)
+        **ordered,
+    )(spread, returned)
     return (attn_out, adapter_out)
 
 

time: 71 us -> 70.6 us (level)
  waiting for transfers between devices: 2.4 us -> 1.44 us
    ppermute x2, waiting for transfers between devices: 2.4 us -> 1.44 us  [swap_cores(): return lax.ppermute(part, 'tensor', [(0, 1), (1, 0)])]
    pallas_call x0 -> x1, Pallas kernels: none -> 0.95 us  [shards(): pl.pallas_call(functools.partial(finish_kernel, heads), out_shape=[shape(...]
  transfers between devices with their start and end apart: 2 -> 2, of which waited for: 2 -> 2; matrix products, arithmetic and copies ran while one was open for 0% -> 0% of each run, Pallas kernels for 0% -> 1%
where the time goes in v11:
time: 70.6 us; the launch traced here: 70 us
  blocking collectives  54.1 us (77%)
  Pallas kernels  13.8 us (20%)
  waiting for transfers between devices  1.44 us (2%)
    all_to_all x4, blocking collectives, exchange(): lax.all_to_all(blocks, 'store', split_axis=0, concat_axis=0, tiled=True)  54.1 us
    pallas_call x1, Pallas kernels, shards(): pl.pallas_call(functools.partial(attend_kernel, owners, heads), out_shape...  7.51 us
    pallas_call x1, Pallas kernels, shards(): pl.pallas_call(functools.partial(dispatch_kernel, owners, heads, adapt, r...  2.28 us
    ppermute x2, waiting for transfers between devices, swap_cores(): return lax.ppermute(part, 'tensor', [(0, 1), (1, 0)])  1.44 us
  transfers between devices with their start and end apart: 2, of which 2 were waited for; matrix products, arithmetic and copies ran while one was open for 0% of the time, Pallas kernels for 1%

profile of v11, /device:TPU:0, one launch (start us, length us, event | category | flops | bytes accessed | tf_op | source)
XLA Modules:
  0.0 70.0 jit_solution(15753065959136361716)
XLA Ops:
  0.6 2.3 %dispatch.1 = (s32[64]{0:T(128)S(1)}, bf16[8,16,1152]{2,1,0:T(8,128)(2,1)S(1)}, bf16[128,4096]{1,0:T(8,128)(2,1)S(1)}, bf16[128,4096]{1,0:T(8,128)(2,1)S(1)}) custom-call(s32[16]{0:T(128)} %ids_hbm.1, s32[64]{0:T(128)} %slot_of_hbm.1, s32[16]{0:T(128)} %lengths_hbm.1, bf16[2,16,4096]{2,1,0:T(8,128)(2,1)} %x_hbm.1, bf16[128,8192]{1,0:T(8,128)(2,1)} %bitcast.10, ...), custom_call_target="tpu_custom_call" | custom-call | tf_op jit(solution)/shard_map/dispatch/pallas_call | solution.py:459
  2.9 17.4 %all_to_all.20.blocks = bf16[8,16,1152]{2,1,0:T(8,128)(2,1)S(1)} all-to-all(bf16[8,16,1152]{2,1,0:T(8,128)(2,1)S(1)} %get-tuple-element.15), channel_id=1, replica_groups=mesh['parts'=2,'store'=8,'tensor'=2] {'store'}, dimensions={0} | all-to-all | bytes 589824 | tf_op jit(solution)/shard_map/all_to_all | solution.py:417
  20.3 0.6 project_query.1
  20.9 0.0 collective-permute-start
  20.9 1.2 %collective-permute-done.other = f32[32,128]{1,0:T(8,128)S(1)} collective-permute-done((f32[32,128]{1,0:T(8,128)S(1)}, f32[32,128]{1,0:T(8,128)S(1)}, u32[]{:S(2)}, u32[]{:S(2)}) %collective-permute-start) | collective-permute-done | bytes 16416 | tf_op jit(solution)/shard_map/ppermute | solution.py:425
  22.2 0.5 expand_query.1
  22.6 11.9 %all_to_all.21.blocks = bf16[8,16,1024]{2,1,0:T(8,128)(2,1)S(1)} all-to-all(bf16[8,16,1024]{2,1,0:T(8,128)(2,1)S(1)} %expand_query.1), channel_id=1, replica_groups=mesh['parts'=2,'store'=8,'tensor'=2] {'store'}, dimensions={0} | all-to-all | bytes 524288 | tf_op jit(solution)/shard_map/all_to_all | solution.py:417
  34.6 0.0 copy-start
  34.6 0.0 copy-start.1
  34.6 7.5 %attend.1 = (bf16[128,1024]{1,0:T(8,128)(2,1)S(1)}, bf16[8,16,1024]{2,1,0:T(8,128)(2,1)S(1)}, bf16[128,128]{1,0:T(8,128)(2,1)S(1)}) custom-call(s32[64]{0:T(128)S(1)} %get-tuple-element.13.meta, bf16[2,16,4096]{2,1,0:T(8,128)(2,1)} %q_hbm.1, bf16[2,16,512]{2,1,0:T(8,128)(2,1)} %kn_hbm.1, bf16[2,16,512]{2,1,0:T(8,128)(2,1)} %vn_hbm.1, ...), custom_call_target="tpu_custom_call" | custom-call | tf_op jit(solution)/shard_map/attend/pallas_call | solution.py:506
  42.1 12.0 %all_to_all.22.blocks = bf16[8,16,1024]{2,1,0:T(8,128)(2,1)S(1)} all-to-all(bf16[8,16,1024]{2,1,0:T(8,128)(2,1)S(1)} %get-tuple-element.19), channel_id=1, replica_groups=mesh['parts'=2,'store'=8,'tensor'=2] {'store'}, dimensions={0} | all-to-all | bytes 524288 | tf_op jit(solution)/shard_map/all_to_all | solution.py:417
  54.0 0.0 copy-done
  54.0 0.6 project_output.1.part.mine
  54.6 0.0 collective-permute-start.1
  54.7 0.9 %finish.1 = (bf16[2,16,4096]{2,1,0:T(8,128)(2,1)}, f32[8,128]{1,0:T(8,128)S(1)}) custom-call(bf16[128,1024]{1,0:T(8,128)(2,1)S(1)} %get-tuple-element.18.mixed, f32[32,128]{1,0:T(8,128)S(1)} %project_output.1.part.mine), custom_call_target="tpu_custom_call" | custom-call | tf_op jit(solution)/shard_map/finish/pallas_call | solution.py:549
  55.6 0.2 collective-permute-done.1.other
  55.8 0.0 copy-done.1
  55.8 0.5 expand_output.1
  56.3 12.8 %all_to_all.23.blocks = bf16[8,16,1024]{2,1,0:T(8,128)(2,1)S(1)} all-to-all(bf16[8,16,1024]{2,1,0:T(8,128)(2,1)S(1)} %expand_output.1), channel_id=1, replica_groups=mesh['parts'=2,'store'=8,'tensor'=2] {'store'}, dimensions={0} | all-to-all | bytes 524288 | tf_op jit(solution)/shard_map/all_to_all | solution.py:417
  69.1 0.9 %collect.1 = bf16[2,16,4096]{2,1,0:T(8,128)(2,1)} custom-call(bf16[128,128]{1,0:T(8,128)(2,1)S(1)} %get-tuple-element.22.spread, bf16[8,16,1024]{2,1,0:T(8,128)(2,1)S(1)} %all_to_all.23.blocks), custom_call_target="tpu_custom_call" | custom-call | tf_op jit(solution)/shard_map/collect/pallas_call | solution.py:560
Async XLA Ops:
  20.9 1.2 %collective-permute-start = (f32[32,128]{1,0:T(8,128)S(1)}, f32[32,128]{1,0:T(8,128)S(1)}, u32[]{:S(2)}, u32[]{:S(2)}) collective-permute-start(f32[32,128]{1,0:T(8,128)S(1)} %get-tuple-element.16.mine), channel_id=1, source_target_pairs={{0,1},{1,0},{2,3},{3,2},{4,5},{5,4},{6,7},{7,6},{8,9},{9,8},{10,11... | collective-permute-start | bytes 49160 | tf_op jit(solution)/shard_map/ppermute | solution.py:425
  34.6 19.5 %copy-start = (bf16[8192,8,16]{0,2,1:T(8,128)(2,1)S(1)}, bf16[8192,8,16]{0,2,1:T(8,128)(2,1)}, u32[]{:S(2)}) copy-start(bf16[8192,8,16]{0,2,1:T(8,128)(2,1)} %param.24) | copy-start | bytes 6291460
  34.6 21.3 %copy-start.1 = (bf16[8,16,4096]{2,1,0:T(8,128)(2,1)S(1)}, bf16[8,16,4096]{2,1,0:T(8,128)(2,1)}, u32[]{:S(2)}) copy-start(bf16[8,16,4096]{2,1,0:T(8,128)(2,1)} %param.25) | copy-start | bytes 3145732
  54.6 1.2 %collective-permute-start.1 = (f32[32,128]{1,0:T(8,128)S(1)}, f32[32,128]{1,0:T(8,128)S(1)}, u32[]{:S(2)}, u32[]{:S(2)}) collective-permute-start(f32[32,128]{1,0:T(8,128)S(1)} %project_output.1.part.mine), channel_id=1, source_target_pairs={{0,1},{1,0},{2,3},{3,2},{4,5},{5,4},{6,7},{7,6},{8,9},{9,8},{10,11... | collective-permute-start | bytes 49160 | tf_op jit(solution)/shard_map/ppermute | solution.py:425

commit v12 on v11

--- a/solution.py
+++ b/solution.py
@@ -263,8 +263,8 @@
     q_hbm,
     kn_hbm,
     vn_hbm,
-    k_hbm,
-    v_hbm,
+    k_ref,
+    v_ref,
     blocks,
     mixed_out,
     outgoing,
@@ -272,13 +272,9 @@
     q_ref,
     kn_ref,
     vn_ref,
-    k_ref,
-    v_ref,
     mask_ref,
     q_buf,
     o_buf,
-    k_sem,
-    v_sem,
     sems,
 ):
     rows = q_hbm.shape[1]
@@ -303,20 +299,7 @@
     def span_of(row):
         return meta[2 * rows + owners * CAP + row]
 
-    def copies(row, size):
-        part = pl.ds(0, size * CHUNK)
-        return (
-            pltpu.make_async_copy(k_hbm.at[row, part], k_ref.at[row, part], k_sem.at[row]),
-            pltpu.make_async_copy(v_hbm.at[row, part], v_ref.at[row, part], v_sem.at[row]),
-        )
-
-    def begin(rows_in, size):
-        for row in rows_in:
-            for copy in copies(row, size):
-                copy.start()
-
-    chunks = k_hbm.shape[1] // CHUNK
-    in_groups(row_of, span_of, rows, chunks, begin)
+    chunks = k_ref.shape[1] // CHUNK
 
     head_at = rest(over(iota((total, width), 0), STEPS), heads)
     mask_ref[...] = one_hot(head_at == over(iota((total, width), 1), HD))
@@ -341,9 +324,6 @@
     contract = (((1,), (1,)), ((), ()))
 
     def attend(rows_in, size):
-        for row in rows_in:
-            for copy in copies(row, size):
-                copy.wait()
         extent = size * CHUNK
         position = iota((total, extent), 1)
         starts = [pl.multiple_of(row * pairs, pairs) for row in rows_in]
@@ -491,17 +471,17 @@
         name="project_query",
     )(a_near, arrived)
 
-    def expand(part, other, b_store, name, *after):
+    def expand(part, other, b_store, name, caches, *after):
         return pl.pallas_call(
             functools.partial(expand_kernel, owners, heads, wide),
             out_shape=sent,
-            in_specs=[VMEM] * (3 + len(after)),
+            in_specs=[VMEM] * (3 + len(after)) + [HBM] * len(caches),
             out_specs=VMEM,
             compiler_params=small,
             name=name,
-        )(part, other, b_store, *after)
-
-    returned = exchange(expand(part, swap_cores(part), b_near, "expand_query"))
+        )(part, other, b_store, *after, *caches)
+
+    returned = exchange(expand(part, swap_cores(part), b_near, "expand_query", (in_hbm(cache_k), in_hbm(cache_v))))
 
     mixed, outgoing, spread = pl.pallas_call(
         functools.partial(attend_kernel, owners, heads),
@@ -510,24 +490,20 @@
             sent,
             shape((rows * STEPS * heads, owners * block), BF16),
         ],
-        in_specs=[SMEM] + [HBM] * 5 + [VMEM],
+        in_specs=[SMEM] + [HBM] * 3 + [VMEM] * 3,
         out_specs=[VMEM] * 3,
         scratch_shapes=[
             pltpu.VMEM(q_base.shape, BF16),
             pltpu.VMEM((CHUNK, heads * HD), BF16),
             pltpu.VMEM((CHUNK, heads * HD), BF16),
-            pltpu.VMEM(cache_k.shape, BF16),
-            pltpu.VMEM(cache_v.shape, BF16),
             pltpu.VMEM((STEPS * wide // HD * heads, heads * HD), BF16),
             pltpu.VMEM((rows * STEPS * heads, wide), F32),
             pltpu.VMEM((rows * STEPS * heads, wide), F32),
-            pltpu.SemaphoreType.DMA((rows,)),
-            pltpu.SemaphoreType.DMA((rows,)),
             pltpu.SemaphoreType.DMA((1 + 2 * STEPS,)),
         ],
-        compiler_params=pltpu.CompilerParams(vmem_limit_bytes=32 * 1024 * 1024),
+        compiler_params=pltpu.CompilerParams(vmem_limit_bytes=16 * 1024 * 1024),
         name="attend",
-    )(meta, *map(in_hbm, (q_base, k_new, v_new, cache_k, cache_v)), returned)
+    )(meta, *map(in_hbm, (q_base, k_new, v_new)), cache_k, cache_v, returned)
 
     arrived = exchange(outgoing)
     part = pl.pallas_call(
@@ -555,7 +531,7 @@
         **ordered,
     )(mixed, part)
     returned = exchange(
-        expand(part, other, b_output.reshape(lanes, width), "expand_output", after)
+        expand(part, other, b_output.reshape(lanes, width), "expand_output", (), after)
     )
     adapter_out = pl.pallas_call(
         functools.partial(collect_kernel, owners, heads),

time: 70.6 us -> 69.2 us (0.980)
  Pallas kernels: 13.8 us -> 12 us
    pallas_call x1, Pallas kernels: 7.51 us -> 5.56 us  [shards(): pl.pallas_call(functools.partial(attend_kernel, owners, heads), out_shape...]
where the time goes in v12:
time: 69.2 us; the launch traced here: 68.6 us
  blocking collectives  54.4 us (79%)
  Pallas kernels  12 us (17%)
  waiting for transfers between devices  1.44 us (2%)
  between operations  0.75 us (1%)
    all_to_all x4, blocking collectives, exchange(): lax.all_to_all(blocks, 'store', split_axis=0, concat_axis=0, tiled=True)  54.4 us
    pallas_call x1, Pallas kernels, shards(): pl.pallas_call(functools.partial(attend_kernel, owners, heads), out_shape...  5.56 us
    pallas_call x1, Pallas kernels, shards(): pl.pallas_call(functools.partial(dispatch_kernel, owners, heads, adapt, r...  2.42 us
    ppermute x2, waiting for transfers between devices, swap_cores(): return lax.ppermute(part, 'tensor', [(0, 1), (1, 0)])  1.44 us
  transfers between devices with their start and end apart: 2, of which 2 were waited for; matrix products, arithmetic and copies ran while one was open for 0% of the time, Pallas kernels for 1%

profile of v12, /device:TPU:0, one launch (start us, length us, event | category | flops | bytes accessed | tf_op | source)
XLA Modules:
  0.0 68.6 jit_solution(10451692899032317409)
XLA Ops:
  0.6 0.0 slice-start.2
  0.6 2.4 %dispatch.1 = (s32[64]{0:T(128)S(1)}, bf16[8,16,1152]{2,1,0:T(8,128)(2,1)S(1)}, bf16[128,4096]{1,0:T(8,128)(2,1)S(1)}, bf16[128,4096]{1,0:T(8,128)(2,1)S(1)}) custom-call(s32[16]{0:T(128)} %ids_hbm.1, s32[64]{0:T(128)} %slot_of_hbm.1, s32[16]{0:T(128)} %lengths_hbm.1, bf16[2,16,4096]{2,1,0:T(8,128)(2,1)} %x_hbm.1, bf16[128,8192]{1,0:T(8,128)(2,1)} %bitcast.14, ...), custom_call_target="tpu_custom_call" | custom-call | tf_op jit(solution)/shard_map/dispatch/pallas_call | solution.py:439
  3.1 17.4 %all_to_all.20.blocks = bf16[8,16,1152]{2,1,0:T(8,128)(2,1)S(1)} all-to-all(bf16[8,16,1152]{2,1,0:T(8,128)(2,1)S(1)} %get-tuple-element.15), channel_id=1, replica_groups=mesh['parts'=2,'store'=8,'tensor'=2] {'store'}, dimensions={0} | all-to-all | bytes 589824 | tf_op jit(solution)/shard_map/all_to_all | solution.py:397
  20.5 0.0 slice-start
  20.5 0.6 project_query.1
  21.1 0.0 collective-permute-start
  21.1 1.2 %collective-permute-done.other = f32[32,128]{1,0:T(8,128)S(1)} collective-permute-done((f32[32,128]{1,0:T(8,128)S(1)}, f32[32,128]{1,0:T(8,128)S(1)}, u32[]{:S(2)}, u32[]{:S(2)}) %collective-permute-start) | collective-permute-done | bytes 16416 | tf_op jit(solution)/shard_map/ppermute | solution.py:405
  22.3 0.0 slice-start.1
  22.3 0.0 slice-start.3
  22.3 0.5 expand_query.1
  22.8 12.3 %all_to_all.21.blocks = bf16[8,16,1024]{2,1,0:T(8,128)(2,1)S(1)} all-to-all(bf16[8,16,1024]{2,1,0:T(8,128)(2,1)S(1)} %expand_query.1), channel_id=1, replica_groups=mesh['parts'=2,'store'=8,'tensor'=2] {'store'}, dimensions={0} | all-to-all | bytes 524288 | tf_op jit(solution)/shard_map/all_to_all | solution.py:397
  35.1 0.0 slice-done.2
  35.1 0.0 slice-done
  35.1 0.0 slice-done.1
  35.1 0.0 slice-done.3
  35.2 0.0 copy-start
  35.2 0.0 copy-start.1
  35.2 5.6 %attend.1 = (bf16[128,1024]{1,0:T(8,128)(2,1)S(1)}, bf16[8,16,1024]{2,1,0:T(8,128)(2,1)S(1)}, bf16[128,128]{1,0:T(8,128)(2,1)S(1)}) custom-call(s32[64]{0:T(128)S(1)} %get-tuple-element.13.meta, bf16[2,16,4096]{2,1,0:T(8,128)(2,1)} %q_hbm.1, bf16[2,16,512]{2,1,0:T(8,128)(2,1)} %kn_hbm.1, bf16[2,16,512]{2,1,0:T(8,128)(2,1)} %vn_hbm.1, ...), custom_call_target="tpu_custom_call" | custom-call | tf_op jit(solution)/shard_map/attend/pallas_call | solution.py:486
  40.7 11.8 %all_to_all.22.blocks = bf16[8,16,1024]{2,1,0:T(8,128)(2,1)S(1)} all-to-all(bf16[8,16,1024]{2,1,0:T(8,128)(2,1)S(1)} %get-tuple-element.19), channel_id=1, replica_groups=mesh['parts'=2,'store'=8,'tensor'=2] {'store'}, dimensions={0} | all-to-all | bytes 524288 | tf_op jit(solution)/shard_map/all_to_all | solution.py:397
  52.6 0.0 copy-done
  52.6 0.6 project_output.1.part.mine
  53.2 0.0 collective-permute-start.1
  53.2 0.9 %finish.1 = (bf16[2,16,4096]{2,1,0:T(8,128)(2,1)}, f32[8,128]{1,0:T(8,128)S(1)}) custom-call(bf16[128,1024]{1,0:T(8,128)(2,1)S(1)} %get-tuple-element.18.mixed, f32[32,128]{1,0:T(8,128)S(1)} %project_output.1.part.mine), custom_call_target="tpu_custom_call" | custom-call | tf_op jit(solution)/shard_map/finish/pallas_call | solution.py:525
  54.2 0.2 collective-permute-done.1.other
  54.4 0.0 copy-done.1
  54.4 0.5 expand_output.1
  54.9 12.8 %all_to_all.23.blocks = bf16[8,16,1024]{2,1,0:T(8,128)(2,1)S(1)} all-to-all(bf16[8,16,1024]{2,1,0:T(8,128)(2,1)S(1)} %expand_output.1), channel_id=1, replica_groups=mesh['parts'=2,'store'=8,'tensor'=2] {'store'}, dimensions={0} | all-to-all | bytes 524288 | tf_op jit(solution)/shard_map/all_to_all | solution.py:397
  67.6 0.9 %collect.1 = bf16[2,16,4096]{2,1,0:T(8,128)(2,1)} custom-call(bf16[128,128]{1,0:T(8,128)(2,1)S(1)} %get-tuple-element.22.spread, bf16[8,16,1024]{2,1,0:T(8,128)(2,1)S(1)} %all_to_all.23.blocks), custom_call_target="tpu_custom_call" | custom-call | tf_op jit(solution)/shard_map/collect/pallas_call | solution.py:536
  (2 shorter events, 0.0 us)
Async XLA Ops:
  0.6 34.5 %slice-start.2 = ((s8[8388608]{0:T(1024)(128)(4,1)}), s8[4194304]{0:T(1024)(128)(4,1)S(1)}, s32[]{:S(2)}) async-start(s8[8388608]{0:T(1024)(128)(4,1)} %bitcast.10), calls=%async_computation.6 | async-start | bytes 8388608
  20.5 14.6 %slice-start = ((s8[8388608]{0:T(1024)(128)(4,1)}), s8[4194304]{0:T(1024)(128)(4,1)S(1)}, s32[]{:S(2)}) async-start(s8[8388608]{0:T(1024)(128)(4,1)} %bitcast.8), calls=%async_computation.4 | async-start | bytes 8388608
  21.1 1.2 %collective-permute-start = (f32[32,128]{1,0:T(8,128)S(1)}, f32[32,128]{1,0:T(8,128)S(1)}, u32[]{:S(2)}, u32[]{:S(2)}) collective-permute-start(f32[32,128]{1,0:T(8,128)S(1)} %get-tuple-element.16.mine), channel_id=1, source_target_pairs={{0,1},{1,0},{2,3},{3,2},{4,5},{5,4},{6,7},{7,6},{8,9},{9,8},{10,11... | collective-permute-start | bytes 49160 | tf_op jit(solution)/shard_map/ppermute | solution.py:405
  22.3 12.8 %slice-start.1 = ((s8[8388608]{0:T(1024)(128)(4,1)}), s8[4194304]{0:T(1024)(128)(4,1)S(1)}, s32[]{:S(2)}) async-start(s8[8388608]{0:T(1024)(128)(4,1)} %bitcast.8), calls=%async_computation.5 | async-start | bytes 8388608
  22.3 12.8 %slice-start.3 = ((s8[8388608]{0:T(1024)(128)(4,1)}), s8[4194304]{0:T(1024)(128)(4,1)S(1)}, s32[]{:S(2)}) async-start(s8[8388608]{0:T(1024)(128)(4,1)} %bitcast.10), calls=%async_computation.7 | async-start | bytes 8388608
  35.2 17.4 %copy-start = (bf16[8192,8,16]{0,2,1:T(8,128)(2,1)S(1)}, bf16[8192,8,16]{0,2,1:T(8,128)(2,1)}, u32[]{:S(2)}) copy-start(bf16[8192,8,16]{0,2,1:T(8,128)(2,1)} %param.24) | copy-start | bytes 6291460
  35.2 19.2 %copy-start.1 = (bf16[8,16,4096]{2,1,0:T(8,128)(2,1)S(1)}, bf16[8,16,4096]{2,1,0:T(8,128)(2,1)}, u32[]{:S(2)}) copy-start(bf16[8,16,4096]{2,1,0:T(8,128)(2,1)} %param.25) | copy-start | bytes 3145732
  53.2 1.2 %collective-permute-start.1 = (f32[32,128]{1,0:T(8,128)S(1)}, f32[32,128]{1,0:T(8,128)S(1)}, u32[]{:S(2)}, u32[]{:S(2)}) collective-permute-start(f32[32,128]{1,0:T(8,128)S(1)} %project_output.1.part.mine), channel_id=1, source_target_pairs={{0,1},{1,0},{2,3},{3,2},{4,5},{5,4},{6,7},{7,6},{8,9},{9,8},{10,11... | collective-permute-start | bytes 49160 | tf_op jit(solution)/shard_map/ppermute | solution.py:405

commit v13 on v12

--- a/solution.py
+++ b/solution.py
@@ -133,12 +133,10 @@
     slot_of_hbm,
     lengths_hbm,
     x_hbm,
-    a_hbm,
-    b_hbm,
+    k_hbm,
+    v_hbm,
     meta,
     blocks,
-    a_out,
-    b_out,
     slot_at,
     ids,
     slot_of,
@@ -146,15 +144,11 @@
     x_ref,
     sems,
 ):
-    width = x_hbm.shape[2]
-    start = pl.multiple_of(lax.axis_index("tensor") * width, width)
     pairs = (
         (ids_hbm, ids),
         (slot_of_hbm, slot_of),
         (lengths_hbm, lengths),
         (x_hbm, x_ref),
-        (a_hbm.at[:, pl.ds(start, width)], a_out),
-        (b_hbm, b_out),
     )
     copies = [pltpu.make_async_copy(a, b, sems.at[k]) for k, (a, b) in enumerate(pairs)]
     for copy in copies:
@@ -196,8 +190,6 @@
                 ahead = ahead + jnp.where(shorter, 1, 0)
         meta[order + ahead] = r
         meta[spans + r] = sizes[r]
-    for copy in copies[4:]:
-        copy.wait()
 
 
 def project_kernel(owners, heads, wide, first, a_ref, blocks, *refs):
@@ -256,42 +248,46 @@
         at += count
 
 
+def prepare_kernel(
+    owners, heads, meta, q_ref, kn_ref, vn_ref, part, base_out, kn_out, vn_out, mask_out, gather_out, after
+):
+    rows = q_ref.shape[1]
+    wide = q_ref.shape[2] // heads
+    fresh_rows = STEPS * rows
+    base_out[...] = exact(by_row_matrix(heads, rows), stacked(q_ref, heads, wide))
+    blank = jnp.zeros((CHUNK - fresh_rows, heads * HD), BF16)
+    for source, target in ((kn_ref, kn_out), (vn_ref, vn_out)):
+        target[...] = jnp.concatenate([source[t] for t in range(STEPS)] + [blank], axis=0)
+    head_at = rest(over(iota(mask_out.shape, 0), STEPS), heads)
+    mask_out[...] = one_hot(head_at == over(iota(mask_out.shape, 1), HD))
+    gather_out[...] = unpack_matrix(meta, owners, heads, rows, True)
+    after[...] = part[: after.shape[0], :]
+
+
 def attend_kernel(
     owners,
     heads,
+    rows,
     meta,
-    q_hbm,
-    kn_hbm,
-    vn_hbm,
+    base_ref,
+    kn_ref,
+    vn_ref,
+    mask_ref,
+    gather_ref,
     k_ref,
     v_ref,
     blocks,
     mixed_out,
     outgoing,
     spread_out,
-    q_ref,
-    kn_ref,
-    vn_ref,
-    mask_ref,
     q_buf,
     o_buf,
-    sems,
 ):
-    rows = q_hbm.shape[1]
-    wide = q_hbm.shape[2] // heads
+    wide = base_ref.shape[1]
     groups = wide // HD
     pairs = heads * STEPS
     total = groups * pairs
-    width = heads * HD
-    fresh_rows = STEPS * rows
-
-    singles = [pltpu.make_async_copy(q_hbm, q_ref, sems.at[0])]
-    for k, (source, target) in enumerate(((kn_hbm, kn_ref), (vn_hbm, vn_ref))):
-        for t in range(STEPS):
-            part = target.at[pl.ds(t * rows, rows)]
-            singles.append(pltpu.make_async_copy(source.at[t], part, sems.at[1 + k * STEPS + t]))
-    for copy in singles:
-        copy.start()
+    chunks = k_ref.shape[1] // CHUNK
 
     def row_of(place):
         return meta[rows + owners * CAP + place]
@@ -299,23 +295,14 @@
     def span_of(row):
         return meta[2 * rows + owners * CAP + row]
 
-    chunks = k_ref.shape[1] // CHUNK
-
-    head_at = rest(over(iota((total, width), 0), STEPS), heads)
-    mask_ref[...] = one_hot(head_at == over(iota((total, width), 1), HD))
+    delta = jnp.dot(
+        gather_ref[...],
+        jnp.concatenate([blocks[i] for i in range(owners)], axis=0),
+        preferred_element_type=F32,
+    )
+    q_buf[...] = base_ref[...].astype(F32) + delta
+
     head_own = rest(over(iota((total, HD), 0), STEPS), heads)
-    blank = jnp.zeros((CHUNK - fresh_rows, width), BF16)
-    kn_ref[fresh_rows:, :] = blank
-    vn_ref[fresh_rows:, :] = blank
-
-    gather = jnp.concatenate(
-        [by_row_matrix(heads, rows), unpack_matrix(meta, owners, heads, rows, True)], axis=1
-    )
-    for copy in singles:
-        copy.wait()
-    sources = [stacked(q_ref, heads, wide)] + [blocks[i] for i in range(owners)]
-    q_buf[...] = jnp.dot(gather, jnp.concatenate(sources, axis=0), preferred_element_type=F32)
-
     factor = math.log2(math.e) / math.sqrt(HD)
     fresh_shape = (total, CHUNK)
     fresh_at = iota(fresh_shape, 1)
@@ -436,29 +423,27 @@
     small = pltpu.CompilerParams(vmem_limit_bytes=16 * 1024 * 1024)
 
     sent = shape((owners, block, wide), BF16)
-    meta, blocks, a_near, b_near = pl.pallas_call(
+    caches = (in_hbm(cache_k), in_hbm(cache_v))
+    meta, blocks = pl.pallas_call(
         functools.partial(dispatch_kernel, owners, heads, adapt, rank),
         out_shape=[
             shape((3 * rows + owners * CAP,), I32),
             shape((owners, block, wide + lanes), BF16),
-            pltpu.VMEM((lanes, width), BF16),
-            pltpu.VMEM((lanes, width), BF16),
         ],
         in_specs=[HBM] * 6,
-        out_specs=[SMEM] + [VMEM] * 3,
+        out_specs=[SMEM, VMEM],
         scratch_shapes=[
             pltpu.SMEM((owners * CAP,), I32),
             pltpu.SMEM(adapter_ids.shape, I32),
             pltpu.SMEM(slot_of.shape, I32),
             pltpu.SMEM(lengths.shape, I32),
             pltpu.VMEM(x_in.shape, BF16),
-            pltpu.SemaphoreType.DMA((6,)),
+            pltpu.SemaphoreType.DMA((4,)),
         ],
         compiler_params=small,
         name="dispatch",
     )(
-        *map(in_hbm, (adapter_ids, slot_of, lengths, x_in, flat(a_query))),
-        in_hbm(b_query.reshape(lanes, width)),
+        *map(in_hbm, (adapter_ids, slot_of, lengths, x_in)), *caches
     )
 
     arrived = exchange(blocks)
@@ -469,7 +454,7 @@
         out_specs=[VMEM] * 2,
         compiler_params=small,
         name="project_query",
-    )(a_near, arrived)
+    )(flat(a_query), arrived)
 
     def expand(part, other, b_store, name, caches, *after):
         return pl.pallas_call(
@@ -481,29 +466,42 @@
             name=name,
         )(part, other, b_store, *after, *caches)
 
-    returned = exchange(expand(part, swap_cores(part), b_near, "expand_query", (in_hbm(cache_k), in_hbm(cache_v))))
+    other = swap_cores(part)
+    *prepared, after = pl.pallas_call(
+        functools.partial(prepare_kernel, owners, heads),
+        out_shape=[
+            shape((rows * STEPS * heads, wide), BF16),
+            shape((CHUNK, heads * HD), BF16),
+            shape((CHUNK, heads * HD), BF16),
+            shape((STEPS * wide // HD * heads, heads * HD), BF16),
+            shape((rows * STEPS * heads, owners * block), BF16),
+            shape((8, lanes), F32),
+        ],
+        in_specs=[SMEM] + [VMEM] * 4,
+        out_specs=[VMEM] * 6,
+        compiler_params=small,
+        name="prepare",
+    )(meta, q_base, k_new, v_new, part)
+    returned = exchange(
+        expand(part, other, b_query.reshape(lanes, width), "expand_query", caches, after)
+    )
 
     mixed, outgoing, spread = pl.pallas_call(
-        functools.partial(attend_kernel, owners, heads),
+        functools.partial(attend_kernel, owners, heads, rows),
         out_shape=[
             shape((rows * STEPS * heads, wide), BF16),
             sent,
             shape((rows * STEPS * heads, owners * block), BF16),
         ],
-        in_specs=[SMEM] + [HBM] * 3 + [VMEM] * 3,
+        in_specs=[SMEM] + [VMEM] * 8,
         out_specs=[VMEM] * 3,
         scratch_shapes=[
-            pltpu.VMEM(q_base.shape, BF16),
-            pltpu.VMEM((CHUNK, heads * HD), BF16),
-            pltpu.VMEM((CHUNK, heads * HD), BF16),
-            pltpu.VMEM((STEPS * wide // HD * heads, heads * HD), BF16),
             pltpu.VMEM((rows * STEPS * heads, wide), F32),
             pltpu.VMEM((rows * STEPS * heads, wide), F32),
-            pltpu.SemaphoreType.DMA((1 + 2 * STEPS,)),
         ],
-        compiler_params=pltpu.CompilerParams(vmem_limit_bytes=16 * 1024 * 1024),
+        compiler_params=small,
         name="attend",
-    )(meta, *map(in_hbm, (q_base, k_new, v_new)), cache_k, cache_v, returned)
+    )(meta, *prepared, cache_k, cache_v, returned)
 
     arrived = exchange(outgoing)
     part = pl.pallas_call(

time: 69.2 us -> 67.5 us (0.975)
  waiting for transfers between devices: 1.44 us -> 0.62 us
  Pallas kernels: 12 us -> 11.2 us
    ppermute x2, waiting for transfers between devices: 1.44 us -> 0.62 us  [swap_cores(): return lax.ppermute(part, 'tensor', [(0, 1), (1, 0)])]
    pallas_call x1 -> x2, Pallas kernels: 5.56 us -> 5.05 us  [the longest x1 4.28 us: shards(): pl.pallas_call(functools.partial(attend_kernel, owners, heads, rows), out...]
  transfers between devices with their start and end apart: 2 -> 2, of which waited for: 2 -> 2; matrix products, arithmetic and copies ran while one was open for 0% -> 0% of each run, Pallas kernels for 1% -> 3%
where the time goes in v13:
time: 67.5 us; the launch traced here: 67.2 us
  blocking collectives  54.5 us (81%)
  Pallas kernels  11.2 us (17%)
  between operations  0.82 us (1%)
    all_to_all x4, blocking collectives, exchange(): lax.all_to_all(blocks, 'store', split_axis=0, concat_axis=0, tiled=True)  54.5 us
    pallas_call x1, Pallas kernels, shards(): pl.pallas_call(functools.partial(attend_kernel, owners, heads, rows), out...  4.28 us
    pallas_call x1, Pallas kernels, shards(): pl.pallas_call(functools.partial(dispatch_kernel, owners, heads, adapt, r...  2.14 us
  transfers between devices with their start and end apart: 2, of which 2 were waited for; matrix products, arithmetic and copies ran while one was open for 0% of the time, Pallas kernels for 3%

profile of v13, /device:TPU:0, one launch (start us, length us, event | category | flops | bytes accessed | tf_op | source)
XLA Modules:
  0.0 67.2 jit_solution(8461348969602182438)
XLA Ops:
  0.6 0.0 copy-start
  0.6 0.0 copy-start.6
  0.7 0.0 copy-start.5
  0.7 0.0 copy-start.4
  0.7 0.0 copy-start.2
  0.7 0.0 slice-start.2
  0.7 2.1 %dispatch.1 = (s32[64]{0:T(128)S(1)}, bf16[8,16,1152]{2,1,0:T(8,128)(2,1)S(1)}) custom-call(s32[16]{0:T(128)} %ids_hbm.1, s32[64]{0:T(128)} %slot_of_hbm.1, s32[16]{0:T(128)} %lengths_hbm.1, bf16[2,16,4096]{2,1,0:T(8,128)(2,1)} %x_hbm.1, bf16[16,512,512]{2,1,0:T(8,128)(2,1)} %k_ref.1, bf16[16,512,512]{2,1,0:T(8,128)(2,1)} %v_ref.1), custom_call_target="tpu_custom_call" | custom-call | tf_op jit(solution)/shard_map/dispatch/pallas_call | solution.py:427
  2.8 17.5 %all_to_all.20.blocks = bf16[8,16,1152]{2,1,0:T(8,128)(2,1)S(1)} all-to-all(bf16[8,16,1152]{2,1,0:T(8,128)(2,1)S(1)} %get-tuple-element.18), channel_id=1, replica_groups=mesh['parts'=2,'store'=8,'tensor'=2] {'store'}, dimensions={0} | all-to-all | bytes 589824 | tf_op jit(solution)/shard_map/all_to_all | solution.py:384
  20.4 0.0 copy-done
  20.4 0.0 slice-start
  20.4 0.0 slice-start.3
  20.4 0.6 project_query.1
  21.0 0.0 collective-permute-start
  21.0 0.0 copy-done.6
  21.0 0.0 copy-done.5
  21.0 0.0 copy-done.4
  21.0 0.8 %prepare.1 = (bf16[128,1024]{1,0:T(8,128)(2,1)S(1)}, bf16[128,512]{1,0:T(8,128)(2,1)S(1)}, bf16[128,512]{1,0:T(8,128)(2,1)S(1)}, bf16[64,512]{1,0:T(8,128)(2,1)S...) custom-call(s32[64]{0:T(128)S(1)} %get-tuple-element.17.meta, bf16[2,16,4096]{2,1,0:T(8,128)(2,1)S(1)} %copy-done.4, ...), custom_call_target="tpu_custom_call" | custom-call | tf_op jit(solution)/shard_map/prepare/pallas_call | solution.py:470
  21.8 0.4 collective-permute-done.other
  22.2 0.0 copy-done.2
  22.2 0.0 slice-start.1
  22.2 0.5 expand_query.1
  22.7 12.2 %all_to_all.21.blocks = bf16[8,16,1024]{2,1,0:T(8,128)(2,1)S(1)} all-to-all(bf16[8,16,1024]{2,1,0:T(8,128)(2,1)S(1)} %expand_query.1), channel_id=1, replica_groups=mesh['parts'=2,'store'=8,'tensor'=2] {'store'}, dimensions={0} | all-to-all | bytes 524288 | tf_op jit(solution)/shard_map/all_to_all | solution.py:384
  34.9 0.0 slice-done.2
  34.9 0.0 slice-done
  34.9 0.0 slice-done.3
  34.9 0.0 slice-done.1
  34.9 0.0 copy-start.1
  34.9 0.0 copy-start.3
  34.9 4.3 %attend.1 = (bf16[128,1024]{1,0:T(8,128)(2,1)S(1)}, bf16[8,16,1024]{2,1,0:T(8,128)(2,1)S(1)}, bf16[128,128]{1,0:T(8,128)(2,1)S(1)}) custom-call(s32[64]{0:T(128)S(1)} %get-tuple-element.17.meta, bf16[128,1024]{1,0:T(8,128)(2,1)S(1)} %get-tuple-element.20.base_ref, bf16[128,512]{1,0:T(8,128)(2,1)S(1)} %get-tuple-element.21.kn_ref, ...), custom_call_target="tpu_custom_call" | custom-call | tf_op jit(solution)/shard_map/attend/pallas_call | solution.py:489
  39.2 12.0 %all_to_all.22.blocks = bf16[8,16,1024]{2,1,0:T(8,128)(2,1)S(1)} all-to-all(bf16[8,16,1024]{2,1,0:T(8,128)(2,1)S(1)} %get-tuple-element.27), channel_id=1, replica_groups=mesh['parts'=2,'store'=8,'tensor'=2] {'store'}, dimensions={0} | all-to-all | bytes 524288 | tf_op jit(solution)/shard_map/all_to_all | solution.py:384
  51.2 0.0 copy-done.1
  51.2 0.6 project_output.1.part.mine
  51.8 0.0 collective-permute-start.1
  51.8 0.9 %finish.1 = (bf16[2,16,4096]{2,1,0:T(8,128)(2,1)}, f32[8,128]{1,0:T(8,128)S(1)}) custom-call(bf16[128,1024]{1,0:T(8,128)(2,1)S(1)} %get-tuple-element.26.mixed, f32[32,128]{1,0:T(8,128)S(1)} %project_output.1.part.mine), custom_call_target="tpu_custom_call" | custom-call | tf_op jit(solution)/shard_map/finish/pallas_call | solution.py:523
  52.8 0.2 collective-permute-done.1.other
  53.0 0.0 copy-done.3
  53.0 0.5 expand_output.1
  53.5 12.8 %all_to_all.23.blocks = bf16[8,16,1024]{2,1,0:T(8,128)(2,1)S(1)} all-to-all(bf16[8,16,1024]{2,1,0:T(8,128)(2,1)S(1)} %expand_output.1), channel_id=1, replica_groups=mesh['parts'=2,'store'=8,'tensor'=2] {'store'}, dimensions={0} | all-to-all | bytes 524288 | tf_op jit(solution)/shard_map/all_to_all | solution.py:384
  66.2 0.9 %collect.1 = bf16[2,16,4096]{2,1,0:T(8,128)(2,1)} custom-call(bf16[128,128]{1,0:T(8,128)(2,1)S(1)} %get-tuple-element.30.spread, bf16[8,16,1024]{2,1,0:T(8,128)(2,1)S(1)} %all_to_all.23.blocks), custom_call_target="tpu_custom_call" | custom-call | tf_op jit(solution)/shard_map/collect/pallas_call | solution.py:534
  (2 shorter events, 0.0 us)
Async XLA Ops:
  0.6 19.8 %copy-start = (bf16[8192,8,16]{0,2,1:T(8,128)(2,1)S(1)}, bf16[8192,8,16]{0,2,1:T(8,128)(2,1)}, u32[]{:S(2)}) copy-start(bf16[8192,8,16]{0,2,1:T(8,128)(2,1)} %param.22) | copy-start | bytes 6291460
  0.6 20.4 %copy-start.6 = (bf16[2,16,512]{2,1,0:T(8,128)(2,1)S(1)}, bf16[2,16,512]{2,1,0:T(8,128)(2,1)}, u32[]{:S(2)}) copy-start(bf16[2,16,512]{2,1,0:T(8,128)(2,1)} %vn_ref.1) | copy-start | bytes 98308
  0.7 20.4 %copy-start.5 = (bf16[2,16,512]{2,1,0:T(8,128)(2,1)S(1)}, bf16[2,16,512]{2,1,0:T(8,128)(2,1)}, u32[]{:S(2)}) copy-start(bf16[2,16,512]{2,1,0:T(8,128)(2,1)} %kn_ref.1) | copy-start | bytes 98308
  0.7 20.4 %copy-start.4 = (bf16[2,16,4096]{2,1,0:T(8,128)(2,1)S(1)}, bf16[2,16,4096]{2,1,0:T(8,128)(2,1)}, u32[]{:S(2)}) copy-start(bf16[2,16,4096]{2,1,0:T(8,128)(2,1)} %q_ref.1) | copy-start | bytes 786436
  0.7 21.5 %copy-start.2 = (bf16[8,16,4096]{2,1,0:T(8,128)(2,1)S(1)}, bf16[8,16,4096]{2,1,0:T(8,128)(2,1)}, u32[]{:S(2)}) copy-start(bf16[8,16,4096]{2,1,0:T(8,128)(2,1)} %param.23) | copy-start | bytes 3145732
  0.7 34.2 %slice-start.2 = ((s8[8388608]{0:T(1024)(128)(4,1)}), s8[4194304]{0:T(1024)(128)(4,1)S(1)}, s32[]{:S(2)}) async-start(s8[8388608]{0:T(1024)(128)(4,1)} %bitcast.10), calls=%async_computation.6 | async-start | bytes 8388608
  20.4 14.5 %slice-start = ((s8[8388608]{0:T(1024)(128)(4,1)}), s8[4194304]{0:T(1024)(128)(4,1)S(1)}, s32[]{:S(2)}) async-start(s8[8388608]{0:T(1024)(128)(4,1)} %bitcast.8), calls=%async_computation.4 | async-start | bytes 8388608
  20.4 14.5 %slice-start.3 = ((s8[8388608]{0:T(1024)(128)(4,1)}), s8[4194304]{0:T(1024)(128)(4,1)S(1)}, s32[]{:S(2)}) async-start(s8[8388608]{0:T(1024)(128)(4,1)} %bitcast.10), calls=%async_computation.7 | async-start | bytes 8388608
  21.0 1.2 %collective-permute-start = (f32[32,128]{1,0:T(8,128)S(1)}, f32[32,128]{1,0:T(8,128)S(1)}, u32[]{:S(2)}, u32[]{:S(2)}) collective-permute-start(f32[32,128]{1,0:T(8,128)S(1)} %get-tuple-element.19.part.mine), channel_id=1, source_target_pairs={{0,1},{1,0},{2,3},{3,2},{4,5},{5,4},{6,7},{7,6},{8,9},{9,8},{10,11... | collective-permute-start | bytes 49160 | tf_op jit(solution)/shard_map/ppermute | solution.py:392
  22.2 12.7 %slice-start.1 = ((s8[8388608]{0:T(1024)(128)(4,1)}), s8[4194304]{0:T(1024)(128)(4,1)S(1)}, s32[]{:S(2)}) async-start(s8[8388608]{0:T(1024)(128)(4,1)} %bitcast.8), calls=%async_computation.5 | async-start | bytes 8388608
  34.9 16.3 %copy-start.1 = (bf16[8192,8,16]{0,2,1:T(8,128)(2,1)S(1)}, bf16[8192,8,16]{0,2,1:T(8,128)(2,1)}, u32[]{:S(2)}) copy-start(bf16[8192,8,16]{0,2,1:T(8,128)(2,1)} %param.24) | copy-start | bytes 6291460
  34.9 18.1 %copy-start.3 = (bf16[8,16,4096]{2,1,0:T(8,128)(2,1)S(1)}, bf16[8,16,4096]{2,1,0:T(8,128)(2,1)}, u32[]{:S(2)}) copy-start(bf16[8,16,4096]{2,1,0:T(8,128)(2,1)} %param.25) | copy-start | bytes 3145732
  51.8 1.2 %collective-permute-start.1 = (f32[32,128]{1,0:T(8,128)S(1)}, f32[32,128]{1,0:T(8,128)S(1)}, u32[]{:S(2)}, u32[]{:S(2)}) collective-permute-start(f32[32,128]{1,0:T(8,128)S(1)} %project_output.1.part.mine), channel_id=1, source_target_pairs={{0,1},{1,0},{2,3},{3,2},{4,5},{5,4},{6,7},{7,6},{8,9},{9,8},{10,11... | collective-permute-start | bytes 49160 | tf_op jit(solution)/shard_map/ppermute | solution.py:392

commit v14 on v13

--- a/solution.py
+++ b/solution.py
@@ -12,6 +12,7 @@
 CAP = 2
 STEPS = 2
 CHUNK = 128
+LAG = 2
 BF16 = jnp.bfloat16
 F32 = jnp.float32
 I32 = jnp.int32
@@ -158,8 +159,7 @@
     for copy in copies[:3]:
         copy.wait()
     row_at = rows
-    order = rows + owners * CAP
-    spans = order + rows
+    spans = rows + owners * CAP
     for p in range(owners * CAP):
         meta[row_at + p] = -1
         slot_at[p] = -1
@@ -170,6 +170,7 @@
         meta[row_at + place] = r
         slot_at[place] = rest(slot, adapt)
         meta[r] = place
+        meta[spans + r] = lengths[r]
     items = CAP * STEPS
     block = heads * items
     copies[3].wait()
@@ -181,15 +182,6 @@
         blocks[i, :, :wide] = packed[i * block : (i + 1) * block]
         slot = jnp.where(first, slot_at[i * CAP], slot_at[i * CAP + 1])
         blocks[i, :, wide:] = one_hot(lane_slot == slot)
-    sizes = [lengths[r] for r in range(rows)]
-    for r in range(rows):
-        ahead = jnp.int32(0)
-        for q in range(rows):
-            if q != r:
-                shorter = sizes[q] <= sizes[r] if q < r else sizes[q] < sizes[r]
-                ahead = ahead + jnp.where(shorter, 1, 0)
-        meta[order + ahead] = r
-        meta[spans + r] = sizes[r]
 
 
 def project_kernel(owners, heads, wide, first, a_ref, blocks, *refs):
@@ -234,22 +226,41 @@
         blocks[i] = back[i * block : (i + 1) * block]
 
 
-def in_groups(row_of, span_of, rows, sizes, action):
-    at = 0
-    for count in [rows // 2] + [rows // 4] * 2:
-        group = [row_of(at + j) for j in range(count)]
-        amount = over(span_of(group[-1]) + (CHUNK - 1), CHUNK)
-        for size in range(1, sizes + 1):
-
-            @pl.when(amount == size)
-            def _():
-                action(group, size)
-
-        at += count
+def by_shape(amount_of, rows, most, action):
+    half, quarter = rows // 2, rows // 4
+    middle = max(most // 2, 1)
+    low = amount_of(half - 1)
+    high = amount_of(half + quarter - 1)
+    one, two = low <= 1, low <= middle
+    shapes = (
+        (one & (high <= middle), (1, middle, most)),
+        (one & (high > middle), (1, most, most)),
+        (two & (low > 1), (middle, most, most)),
+        (low > middle, (most, most, most)),
+    )
+    for fits, (a, b, c) in shapes:
+
+        @pl.when(fits)
+        def _():
+            action([a] * half + [b] * quarter + [c] * quarter)
 
 
 def prepare_kernel(
-    owners, heads, meta, q_ref, kn_ref, vn_ref, part, base_out, kn_out, vn_out, mask_out, gather_out, after
+    owners,
+    heads,
+    meta,
+    q_ref,
+    kn_ref,
+    vn_ref,
+    part,
+    order,
+    base_out,
+    kn_out,
+    vn_out,
+    mask_out,
+    gather_out,
+    pack_out,
+    after,
 ):
     rows = q_ref.shape[1]
     wide = q_ref.shape[2] // heads
@@ -261,6 +272,15 @@
     head_at = rest(over(iota(mask_out.shape, 0), STEPS), heads)
     mask_out[...] = one_hot(head_at == over(iota(mask_out.shape, 1), HD))
     gather_out[...] = unpack_matrix(meta, owners, heads, rows, True)
+    pack_out[...] = pack_matrix(meta, owners, heads, rows, True)
+    sizes = [meta[rows + owners * CAP + r] for r in range(rows)]
+    for r in range(rows):
+        ahead = jnp.int32(0)
+        for q in range(rows):
+            if q != r:
+                shorter = sizes[q] <= sizes[r] if q < r else sizes[q] < sizes[r]
+                ahead = ahead + jnp.where(shorter, 1, 0)
+        order[ahead] = r
     after[...] = part[: after.shape[0], :]
 
 
@@ -269,17 +289,18 @@
     heads,
     rows,
     meta,
+    order,
     base_ref,
     kn_ref,
     vn_ref,
     mask_ref,
     gather_ref,
+    pack_ref,
     k_ref,
     v_ref,
     blocks,
     mixed_out,
     outgoing,
-    spread_out,
     q_buf,
     o_buf,
 ):
@@ -287,13 +308,9 @@
     groups = wide // HD
     pairs = heads * STEPS
     total = groups * pairs
-    chunks = k_ref.shape[1] // CHUNK
-
-    def row_of(place):
-        return meta[rows + owners * CAP + place]
 
     def span_of(row):
-        return meta[2 * rows + owners * CAP + row]
+        return meta[rows + owners * CAP + row]
 
     delta = jnp.dot(
         gather_ref[...],
@@ -310,47 +327,56 @@
     fresh_row = jnp.where(fresh_step <= rest(iota(fresh_shape, 0), STEPS), rest(fresh_at, rows), rows)
     contract = (((1,), (1,)), ((), ()))
 
-    def attend(rows_in, size):
-        extent = size * CHUNK
-        position = iota((total, extent), 1)
-        starts = [pl.multiple_of(row * pairs, pairs) for row in rows_in]
-        spreads = []
-        for start in starts:
-            flat = q_buf[pl.ds(start, pairs), :]
-            one = jnp.concatenate(
-                [flat[:, j * HD : (j + 1) * HD] for j in range(groups)], axis=0
-            ).astype(BF16)
-            spreads.append(jnp.concatenate([one] * heads, axis=1) * mask_ref[...])
-        scores = []
-        for row, spread in zip(rows_in, spreads):
-            keys = jnp.concatenate([k_ref[row, :extent, :], kn_ref[...]], axis=0)
-            score = lax.dot_general(spread, keys, contract, preferred_element_type=F32)
-            cached = jnp.where(position < span_of(row), score[:, :extent], -jnp.inf)
-            fresh = jnp.where(fresh_row == row, score[:, extent:], -jnp.inf)
-            scores.append(jnp.concatenate([cached, fresh], axis=1))
-        tops = [jnp.max(score, axis=1, keepdims=True) for score in scores]
-        weights = [jnp.exp2((score - top) * factor) for score, top in zip(scores, tops)]
-        shares = [1.0 / jnp.sum(weight, axis=1, keepdims=True) for weight in weights]
-        for row, start, weight, share in zip(rows_in, starts, weights, shares):
-            values = jnp.concatenate([v_ref[row, :extent, :], vn_ref[...]], axis=0)
-            mixed = jnp.dot(weight.astype(BF16), values, preferred_element_type=F32)
-            own = mixed[:, :HD]
-            for c in range(1, heads):
-                own = jnp.where(head_own == c, mixed[:, c * HD : (c + 1) * HD], own)
-            own = own * share
-            o_buf[pl.ds(start, pairs), :] = jnp.concatenate(
-                [own[j * pairs : (j + 1) * pairs] for j in range(groups)], axis=1
-            )
-
-    in_groups(row_of, span_of, rows, chunks, attend)
+    def scores_of(row, extent):
+        flat = q_buf[pl.ds(pl.multiple_of(row * pairs, pairs), pairs), :]
+        one = jnp.concatenate([flat[:, j * HD : (j + 1) * HD] for j in range(groups)], axis=0)
+        spread = jnp.concatenate([one.astype(BF16)] * heads, axis=1) * mask_ref[...]
+        keys = jnp.concatenate([k_ref[row, :extent, :], kn_ref[...]], axis=0)
+        score = lax.dot_general(spread, keys, contract, preferred_element_type=F32)
+        cached = jnp.where(iota((total, extent), 1) < span_of(row), score[:, :extent], -jnp.inf)
+        fresh = jnp.where(fresh_row == row, score[:, extent:], -jnp.inf)
+        return jnp.concatenate([cached, fresh], axis=1)
+
+    def softmax_of(score):
+        top = jnp.max(score, axis=1, keepdims=True)
+        weight = jnp.exp2((score - top) * factor)
+        return weight.astype(BF16), 1.0 / jnp.sum(weight, axis=1, keepdims=True)
+
+    def mix(row, extent, weight, share):
+        values = jnp.concatenate([v_ref[row, :extent, :], vn_ref[...]], axis=0)
+        mixed = jnp.dot(weight, values, preferred_element_type=F32)
+        own = mixed[:, :HD]
+        for c in range(1, heads):
+            own = jnp.where(head_own == c, mixed[:, c * HD : (c + 1) * HD], own)
+        own = own * share
+        o_buf[pl.ds(pl.multiple_of(row * pairs, pairs), pairs), :] = jnp.concatenate(
+            [own[j * pairs : (j + 1) * pairs] for j in range(groups)], axis=1
+        )
+
+    def attend(sizes):
+        ordered = [order[k] for k in range(rows)]
+        extents = [size * CHUNK for size in sizes]
+        scores, weights = {}, {}
+        for t in range(rows + 2 * LAG):
+            if t < rows:
+                scores[t] = scores_of(ordered[t], extents[t])
+            if 0 <= t - LAG < rows:
+                weights[t - LAG] = softmax_of(scores.pop(t - LAG))
+            if 0 <= t - 2 * LAG < rows:
+                done = t - 2 * LAG
+                mix(ordered[done], extents[done], *weights.pop(done))
+
+    def amount_of(place):
+        return over(span_of(order[place]) + (CHUNK - 1), CHUNK)
+
+    by_shape(amount_of, rows, k_ref.shape[1] // CHUNK, attend)
 
     mixed = o_buf[...].astype(BF16)
     mixed_out[...] = mixed
-    packed = exact(pack_matrix(meta, owners, heads, rows, True), mixed)
+    packed = exact(pack_ref[...], mixed)
     block = heads * CAP * STEPS
     for i in range(owners):
         outgoing[i] = packed[i * block : (i + 1) * block]
-    spread_out[...] = unpack_matrix(meta, owners, heads, rows, False)
 
 
 def write_out(matrix, values, heads, out_hbm, out_ref, sems):
@@ -369,9 +395,10 @@
         copy.wait()
 
 
-def finish_kernel(heads, mixed, part, out_hbm, after, out_ref, sems):
+def finish_kernel(heads, mixed, gather_ref, part, out_hbm, after, spread_out, out_ref, sems):
     after[...] = part[: after.shape[0], :]
     matrix = by_pair_matrix(heads, out_ref.shape[1])
+    spread_out[...] = exact(matrix, gather_ref[...])
     write_out(matrix, mixed[...], heads, out_hbm, out_ref, sems)
 
 
@@ -427,7 +454,7 @@
     meta, blocks = pl.pallas_call(
         functools.partial(dispatch_kernel, owners, heads, adapt, rank),
         out_shape=[
-            shape((3 * rows + owners * CAP,), I32),
+            shape((2 * rows + owners * CAP,), I32),
             shape((owners, block, wide + lanes), BF16),
         ],
         in_specs=[HBM] * 6,
@@ -467,18 +494,20 @@
         )(part, other, b_store, *after, *caches)
 
     other = swap_cores(part)
-    *prepared, after = pl.pallas_call(
+    order, *prepared, after = pl.pallas_call(
         functools.partial(prepare_kernel, owners, heads),
         out_shape=[
+            shape((rows,), I32),
             shape((rows * STEPS * heads, wide), BF16),
             shape((CHUNK, heads * HD), BF16),
             shape((CHUNK, heads * HD), BF16),
             shape((STEPS * wide // HD * heads, heads * HD), BF16),
             shape((rows * STEPS * heads, owners * block), BF16),
+            shape((owners * block, rows * STEPS * heads), BF16),
             shape((8, lanes), F32),
         ],
         in_specs=[SMEM] + [VMEM] * 4,
-        out_specs=[VMEM] * 6,
+        out_specs=[SMEM] + [VMEM] * 7,
         compiler_params=small,
         name="prepare",
     )(meta, q_base, k_new, v_new, part)
@@ -486,22 +515,21 @@
         expand(part, other, b_query.reshape(lanes, width), "expand_query", caches, after)
     )
 
-    mixed, outgoing, spread = pl.pallas_call(
+    mixed, outgoing = pl.pallas_call(
         functools.partial(attend_kernel, owners, heads, rows),
         out_shape=[
             shape((rows * STEPS * heads, wide), BF16),
             sent,
-            shape((rows * STEPS * heads, owners * block), BF16),
-        ],
-        in_specs=[SMEM] + [VMEM] * 8,
-        out_specs=[VMEM] * 3,
+        ],
+        in_specs=[SMEM] * 2 + [VMEM] * 9,
+        out_specs=[VMEM] * 2,
         scratch_shapes=[
             pltpu.VMEM((rows * STEPS * heads, wide), F32),
             pltpu.VMEM((rows * STEPS * heads, wide), F32),
         ],
         compiler_params=small,
         name="attend",
-    )(meta, *prepared, cache_k, cache_v, returned)
+    )(meta, order, *prepared, cache_k, cache_v, returned)
 
     arrived = exchange(outgoing)
     part = pl.pallas_call(
@@ -520,14 +548,18 @@
         compiler_params=small,
     )
     other = swap_cores(part)
-    attn_out, after = pl.pallas_call(
+    attn_out, after, spread = pl.pallas_call(
         functools.partial(finish_kernel, heads),
-        out_shape=[shape((STEPS, rows, width), BF16), shape((8, lanes), F32)],
-        in_specs=[VMEM] * 2,
-        out_specs=[HBM, VMEM],
+        out_shape=[
+            shape((STEPS, rows, width), BF16),
+            shape((8, lanes), F32),
+            shape((rows * STEPS * heads, owners * block), BF16),
+        ],
+        in_specs=[VMEM] * 3,
+        out_specs=[HBM, VMEM, VMEM],
         name="finish",
         **ordered,
-    )(mixed, part)
+    )(mixed, prepared[4], part)
     returned = exchange(
         expand(part, other, b_output.reshape(lanes, width), "expand_output", (), after)
     )

time: 67.5 us -> 68.4 us (1.013)
  blocking collectives: 54.5 us -> 55.4 us
    all_to_all x4, blocking collectives: 54.5 us -> 55.4 us  [exchange(): lax.all_to_all(blocks, 'store', split_axis=0, concat_axis=0, tiled=True)]
    pallas_call x1, Pallas kernels: 0.77 us -> 1.55 us  [shards(): pl.pallas_call(functools.partial(prepare_kernel, owners, heads), out_shap...]
  transfers between devices with their start and end apart: 2 -> 2, of which waited for: 2 -> 1; matrix products, arithmetic and copies ran while one was open for 0% -> 0% of each run, Pallas kernels for 3% -> 4%
where the time goes in v14:
time: 68.4 us; the launch traced here: 68.2 us
  blocking collectives  55.4 us (81%)
  Pallas kernels  11.5 us (17%)
  between operations  1.01 us (1%)
    all_to_all x4, blocking collectives, exchange(): lax.all_to_all(blocks, 'store', split_axis=0, concat_axis=0, tiled=True)  55.4 us
    pallas_call x1, Pallas kernels, shards(): pl.pallas_call(functools.partial(attend_kernel, owners, heads, rows), out...  4.2 us
    pallas_call x1, Pallas kernels, shards(): pl.pallas_call(functools.partial(dispatch_kernel, owners, heads, adapt, r...  1.76 us
    pallas_call x1, Pallas kernels, shards(): pl.pallas_call(functools.partial(prepare_kernel, owners, heads), out_shap...  1.55 us
  transfers between devices with their start and end apart: 2, of which 1 were waited for; matrix products, arithmetic and copies ran while one was open for 0% of the time, Pallas kernels for 4%

profile of v14, /device:TPU:0, one launch (start us, length us, event | category | flops | bytes accessed | tf_op | source)
XLA Modules:
  0.0 68.2 jit_solution(15628165312389263013)
XLA Ops:
  0.6 0.0 copy-start
  0.6 0.0 copy-start.6
  0.7 0.0 copy-start.5
  0.7 0.0 copy-start.4
  0.7 0.0 copy-start.2
  0.7 0.0 slice-start.2
  0.7 1.8 %dispatch.1 = (s32[48]{0:T(128)S(1)}, bf16[8,16,1152]{2,1,0:T(8,128)(2,1)S(1)}) custom-call(s32[16]{0:T(128)} %ids_hbm.1, s32[64]{0:T(128)} %slot_of_hbm.1, s32[16]{0:T(128)} %lengths_hbm.1, bf16[2,16,4096]{2,1,0:T(8,128)(2,1)} %x_hbm.1, bf16[16,512,512]{2,1,0:T(8,128)(2,1)} %k_ref.1, bf16[16,512,512]{2,1,0:T(8,128)(2,1)} %v_ref.1), custom_call_target="tpu_custom_call" | custom-call | tf_op jit(solution)/shard_map/dispatch/pallas_call | solution.py:454
  2.5 17.5 %all_to_all.20.blocks = bf16[8,16,1152]{2,1,0:T(8,128)(2,1)S(1)} all-to-all(bf16[8,16,1152]{2,1,0:T(8,128)(2,1)S(1)} %get-tuple-element.20), channel_id=1, replica_groups=mesh['parts'=2,'store'=8,'tensor'=2] {'store'}, dimensions={0} | all-to-all | bytes 589824 | tf_op jit(solution)/shard_map/all_to_all | solution.py:411
  20.0 0.0 copy-done
  20.0 0.0 slice-start
  20.0 0.0 slice-start.3
  20.0 0.6 project_query.1
  20.6 0.0 collective-permute-start
  20.6 0.0 copy-done.6
  20.6 0.0 copy-done.5
  20.7 0.0 copy-done.4
  20.7 1.5 %prepare.1 = (s32[16]{0:T(128)S(1)}, bf16[128,1024]{1,0:T(8,128)(2,1)S(1)}, bf16[128,512]{1,0:T(8,128)(2,1)S(1)}, bf16[128,512]{1,0:T(8,128)(2,1)S(1)}, bf16[64,...) custom-call(s32[48]{0:T(128)S(1)} %get-tuple-element.19.meta, ...), custom_call_target="tpu_custom_call" | custom-call | tf_op jit(solution)/shard_map/prepare/pallas_call | solution.py:497
  22.2 0.0 collective-permute-done.other
  22.2 0.0 copy-done.2
  22.2 0.0 slice-start.1
  22.3 0.5 expand_query.1
  22.7 12.5 %all_to_all.21.blocks = bf16[8,16,1024]{2,1,0:T(8,128)(2,1)S(1)} all-to-all(bf16[8,16,1024]{2,1,0:T(8,128)(2,1)S(1)} %expand_query.1), channel_id=1, replica_groups=mesh['parts'=2,'store'=8,'tensor'=2] {'store'}, dimensions={0} | all-to-all | bytes 524288 | tf_op jit(solution)/shard_map/all_to_all | solution.py:411
  35.2 0.0 slice-done.2
  35.3 0.0 slice-done
  35.3 0.0 slice-done.3
  35.3 0.0 slice-done.1
  35.3 0.0 copy-start.1
  35.3 0.0 copy-start.3
  35.3 4.2 %attend.1 = (bf16[128,1024]{1,0:T(8,128)(2,1)S(1)}, bf16[8,16,1024]{2,1,0:T(8,128)(2,1)S(1)}) custom-call(s32[48]{0:T(128)S(1)} %get-tuple-element.19.meta, s32[16]{0:T(128)S(1)} %get-tuple-element.22.order, bf16[128,1024]{1,0:T(8,128)(2,1)S(1)} %get-tuple-element.23.base_ref, bf16[128,512]{1,0:T(8,128)(2,1)S(1)} %get-tuple-element.24.kn_ref, ...), custom_call_target="tpu_custom_call" | custom-call | tf_op jit(solution)/shard_map/attend/pallas_call | solution.py:518
  39.5 12.5 %all_to_all.22.blocks = bf16[8,16,1024]{2,1,0:T(8,128)(2,1)S(1)} all-to-all(bf16[8,16,1024]{2,1,0:T(8,128)(2,1)S(1)} %get-tuple-element.31), channel_id=1, replica_groups=mesh['parts'=2,'store'=8,'tensor'=2] {'store'}, dimensions={0} | all-to-all | bytes 524288 | tf_op jit(solution)/shard_map/all_to_all | solution.py:411
  52.0 0.0 copy-done.1
  52.0 0.6 project_output.1.part.mine
  52.6 0.0 collective-permute-start.1
  52.6 1.0 %finish.1 = (bf16[2,16,4096]{2,1,0:T(8,128)(2,1)}, f32[8,128]{1,0:T(8,128)S(1)}, bf16[128,128]{1,0:T(8,128)(2,1)S(1)}) custom-call(bf16[128,1024]{1,0:T(8,128)(2,1)S(1)} %get-tuple-element.30.mixed, bf16[128,128]{1,0:T(8,128)(2,1)S(1)} %get-tuple-element.27.gather_ref, f32[32,128]{1,0:T(8,128)S(1)} %project_output.1.part.mine), custom_call_target="tpu_custom_call" | custom-call | tf_op jit(solution)/shard_map/finish/pallas_call | solution.py:551
  53.6 0.2 collective-permute-done.1.other
  53.8 0.0 copy-done.3
  53.8 0.4 expand_output.1
  54.3 12.8 %all_to_all.23.blocks = bf16[8,16,1024]{2,1,0:T(8,128)(2,1)S(1)} all-to-all(bf16[8,16,1024]{2,1,0:T(8,128)(2,1)S(1)} %expand_output.1), channel_id=1, replica_groups=mesh['parts'=2,'store'=8,'tensor'=2] {'store'}, dimensions={0} | all-to-all | bytes 524288 | tf_op jit(solution)/shard_map/all_to_all | solution.py:411
  67.1 0.9 %collect.1 = bf16[2,16,4096]{2,1,0:T(8,128)(2,1)} custom-call(bf16[128,128]{1,0:T(8,128)(2,1)S(1)} %get-tuple-element.34.spread, bf16[8,16,1024]{2,1,0:T(8,128)(2,1)S(1)} %all_to_all.23.blocks), custom_call_target="tpu_custom_call" | custom-call | tf_op jit(solution)/shard_map/collect/pallas_call | solution.py:566
  (2 shorter events, 0.0 us)
Async XLA Ops:
  0.6 19.4 %copy-start = (bf16[8192,8,16]{0,2,1:T(8,128)(2,1)S(1)}, bf16[8192,8,16]{0,2,1:T(8,128)(2,1)}, u32[]{:S(2)}) copy-start(bf16[8192,8,16]{0,2,1:T(8,128)(2,1)} %param.22) | copy-start | bytes 6291460
  0.6 20.0 %copy-start.6 = (bf16[2,16,512]{2,1,0:T(8,128)(2,1)S(1)}, bf16[2,16,512]{2,1,0:T(8,128)(2,1)}, u32[]{:S(2)}) copy-start(bf16[2,16,512]{2,1,0:T(8,128)(2,1)} %vn_ref.1) | copy-start | bytes 98308
  0.7 20.0 %copy-start.5 = (bf16[2,16,512]{2,1,0:T(8,128)(2,1)S(1)}, bf16[2,16,512]{2,1,0:T(8,128)(2,1)}, u32[]{:S(2)}) copy-start(bf16[2,16,512]{2,1,0:T(8,128)(2,1)} %kn_ref.1) | copy-start | bytes 98308
  0.7 20.0 %copy-start.4 = (bf16[2,16,4096]{2,1,0:T(8,128)(2,1)S(1)}, bf16[2,16,4096]{2,1,0:T(8,128)(2,1)}, u32[]{:S(2)}) copy-start(bf16[2,16,4096]{2,1,0:T(8,128)(2,1)} %q_ref.1) | copy-start | bytes 786436
  0.7 21.6 %copy-start.2 = (bf16[8,16,4096]{2,1,0:T(8,128)(2,1)S(1)}, bf16[8,16,4096]{2,1,0:T(8,128)(2,1)}, u32[]{:S(2)}) copy-start(bf16[8,16,4096]{2,1,0:T(8,128)(2,1)} %param.23) | copy-start | bytes 3145732
  0.7 34.6 %slice-start.2 = ((s8[8388608]{0:T(1024)(128)(4,1)}), s8[4194304]{0:T(1024)(128)(4,1)S(1)}, s32[]{:S(2)}) async-start(s8[8388608]{0:T(1024)(128)(4,1)} %bitcast.10), calls=%async_computation.6 | async-start | bytes 8388608
  20.0 15.2 %slice-start = ((s8[8388608]{0:T(1024)(128)(4,1)}), s8[4194304]{0:T(1024)(128)(4,1)S(1)}, s32[]{:S(2)}) async-start(s8[8388608]{0:T(1024)(128)(4,1)} %bitcast.8), calls=%async_computation.4 | async-start | bytes 8388608
  20.0 15.2 %slice-start.3 = ((s8[8388608]{0:T(1024)(128)(4,1)}), s8[4194304]{0:T(1024)(128)(4,1)S(1)}, s32[]{:S(2)}) async-start(s8[8388608]{0:T(1024)(128)(4,1)} %bitcast.10), calls=%async_computation.7 | async-start | bytes 8388608
  20.6 1.6 %collective-permute-start = (f32[32,128]{1,0:T(8,128)S(1)}, f32[32,128]{1,0:T(8,128)S(1)}, u32[]{:S(2)}, u32[]{:S(2)}) collective-permute-start(f32[32,128]{1,0:T(8,128)S(1)} %get-tuple-element.21.part.mine), channel_id=1, source_target_pairs={{0,1},{1,0},{2,3},{3,2},{4,5},{5,4},{6,7},{7,6},{8,9},{9,8},{10,11... | collective-permute-start | bytes 49160 | tf_op jit(solution)/shard_map/ppermute | solution.py:419
  22.2 13.0 %slice-start.1 = ((s8[8388608]{0:T(1024)(128)(4,1)}), s8[4194304]{0:T(1024)(128)(4,1)S(1)}, s32[]{:S(2)}) async-start(s8[8388608]{0:T(1024)(128)(4,1)} %bitcast.8), calls=%async_computation.5 | async-start | bytes 8388608
  35.3 16.7 %copy-start.1 = (bf16[8192,8,16]{0,2,1:T(8,128)(2,1)S(1)}, bf16[8192,8,16]{0,2,1:T(8,128)(2,1)}, u32[]{:S(2)}) copy-start(bf16[8192,8,16]{0,2,1:T(8,128)(2,1)} %param.24) | copy-start | bytes 6291460
  35.3 18.5 %copy-start.3 = (bf16[8,16,4096]{2,1,0:T(8,128)(2,1)S(1)}, bf16[8,16,4096]{2,1,0:T(8,128)(2,1)}, u32[]{:S(2)}) copy-start(bf16[8,16,4096]{2,1,0:T(8,128)(2,1)} %param.25) | copy-start | bytes 3145732
  52.6 1.2 %collective-permute-start.1 = (f32[32,128]{1,0:T(8,128)S(1)}, f32[32,128]{1,0:T(8,128)S(1)}, u32[]{:S(2)}, u32[]{:S(2)}) collective-permute-start(f32[32,128]{1,0:T(8,128)S(1)} %project_output.1.part.mine), channel_id=1, source_target_pairs={{0,1},{1,0},{2,3},{3,2},{4,5},{5,4},{6,7},{7,6},{8,9},{9,8},{10,11... | collective-permute-start | bytes 49160 | tf_op jit(solution)/shard_map/ppermute | solution.py:419

commit v15 on v14

--- a/solution.py
+++ b/solution.py
@@ -11,7 +11,6 @@
 HD = 128
 CAP = 2
 STEPS = 2
-CHUNK = 128
 LAG = 2
 BF16 = jnp.bfloat16
 F32 = jnp.float32
@@ -226,23 +225,20 @@
         blocks[i] = back[i * block : (i + 1) * block]
 
 
-def by_shape(amount_of, rows, most, action):
+def by_shape(span_at, rows, most, action):
     half, quarter = rows // 2, rows // 4
-    middle = max(most // 2, 1)
-    low = amount_of(half - 1)
-    high = amount_of(half + quarter - 1)
-    one, two = low <= 1, low <= middle
-    shapes = (
-        (one & (high <= middle), (1, middle, most)),
-        (one & (high > middle), (1, most, most)),
-        (two & (low > 1), (middle, most, most)),
-        (low > middle, (most, most, most)),
-    )
-    for fits, (a, b, c) in shapes:
-
-        @pl.when(fits)
-        def _():
-            action([a] * half + [b] * quarter + [c] * quarter)
+    lower = ((most // 8, most // 4), (most // 4, most // 4), (most // 4, most // 2), (most, most))
+    upper = ((most // 4, most), (most // 2, most), (most * 3 // 4, most), (most, most))
+    for at, shapes in ((0, lower), (half, upper)):
+        first, last = span_at(at + quarter - 1), span_at(at + half - 1)
+        open_yet = True
+        for a, b in shapes:
+            fits = (first <= a) & (last <= b) & open_yet
+            open_yet = open_yet & ~((first <= a) & (last <= b))
+
+            @pl.when(fits)
+            def _():
+                action(at, [a] * quarter + [b] * quarter)
 
 
 def prepare_kernel(
@@ -264,23 +260,22 @@
 ):
     rows = q_ref.shape[1]
     wide = q_ref.shape[2] // heads
-    fresh_rows = STEPS * rows
     base_out[...] = exact(by_row_matrix(heads, rows), stacked(q_ref, heads, wide))
-    blank = jnp.zeros((CHUNK - fresh_rows, heads * HD), BF16)
     for source, target in ((kn_ref, kn_out), (vn_ref, vn_out)):
-        target[...] = jnp.concatenate([source[t] for t in range(STEPS)] + [blank], axis=0)
+        target[...] = jnp.concatenate([source[t] for t in range(STEPS)], axis=0)
     head_at = rest(over(iota(mask_out.shape, 0), STEPS), heads)
     mask_out[...] = one_hot(head_at == over(iota(mask_out.shape, 1), HD))
     gather_out[...] = unpack_matrix(meta, owners, heads, rows, True)
     pack_out[...] = pack_matrix(meta, owners, heads, rows, True)
     sizes = [meta[rows + owners * CAP + r] for r in range(rows)]
+    ahead = [jnp.int32(0)] * rows
     for r in range(rows):
-        ahead = jnp.int32(0)
-        for q in range(rows):
-            if q != r:
-                shorter = sizes[q] <= sizes[r] if q < r else sizes[q] < sizes[r]
-                ahead = ahead + jnp.where(shorter, 1, 0)
-        order[ahead] = r
+        for q in range(r):
+            shorter = jnp.where(sizes[q] <= sizes[r], 1, 0)
+            ahead[r] = ahead[r] + shorter
+            ahead[q] = ahead[q] + (1 - shorter)
+    for r in range(rows):
+        order[ahead[r]] = r
     after[...] = part[: after.shape[0], :]
 
 
@@ -321,7 +316,7 @@
 
     head_own = rest(over(iota((total, HD), 0), STEPS), heads)
     factor = math.log2(math.e) / math.sqrt(HD)
-    fresh_shape = (total, CHUNK)
+    fresh_shape = (total, STEPS * rows)
     fresh_at = iota(fresh_shape, 1)
     fresh_step = over(fresh_at, rows)
     fresh_row = jnp.where(fresh_step <= rest(iota(fresh_shape, 0), STEPS), rest(fresh_at, rows), rows)
@@ -353,23 +348,20 @@
             [own[j * pairs : (j + 1) * pairs] for j in range(groups)], axis=1
         )
 
-    def attend(sizes):
-        ordered = [order[k] for k in range(rows)]
-        extents = [size * CHUNK for size in sizes]
+    def attend(at, extents):
+        count = len(extents)
+        ordered = [order[at + k] for k in range(count)]
         scores, weights = {}, {}
-        for t in range(rows + 2 * LAG):
-            if t < rows:
+        for t in range(count + 2 * LAG):
+            if t < count:
                 scores[t] = scores_of(ordered[t], extents[t])
-            if 0 <= t - LAG < rows:
+            if 0 <= t - LAG < count:
                 weights[t - LAG] = softmax_of(scores.pop(t - LAG))
-            if 0 <= t - 2 * LAG < rows:
+            if 0 <= t - 2 * LAG < count:
                 done = t - 2 * LAG
                 mix(ordered[done], extents[done], *weights.pop(done))
 
-    def amount_of(place):
-        return over(span_of(order[place]) + (CHUNK - 1), CHUNK)
-
-    by_shape(amount_of, rows, k_ref.shape[1] // CHUNK, attend)
+    by_shape(lambda place: span_of(order[place]), rows, k_ref.shape[1], attend)
 
     mixed = o_buf[...].astype(BF16)
     mixed_out[...] = mixed
@@ -499,8 +491,8 @@
         out_shape=[
             shape((rows,), I32),
             shape((rows * STEPS * heads, wide), BF16),
-            shape((CHUNK, heads * HD), BF16),
-            shape((CHUNK, heads * HD), BF16),
+            shape((STEPS * rows, heads * HD), BF16),
+            shape((STEPS * rows, heads * HD), BF16),
             shape((STEPS * wide // HD * heads, heads * HD), BF16),
             shape((rows * STEPS * heads, owners * block), BF16),
             shape((owners * block, rows * STEPS * heads), BF16),

time: 68.4 us -> 68.1 us (level)
  no operation moved by 1% of the time
where the time goes in v15:
time: 68.1 us; the launch traced here: 67.9 us
  blocking collectives  55.6 us (82%)
  Pallas kernels  11.1 us (16%)
  between operations  0.84 us (1%)
    all_to_all x4, blocking collectives, exchange(): lax.all_to_all(blocks, 'store', split_axis=0, concat_axis=0, tiled=True)  55.6 us
    pallas_call x1, Pallas kernels, shards(): pl.pallas_call(functools.partial(attend_kernel, owners, heads, rows), out...  3.83 us
    pallas_call x1, Pallas kernels, shards(): pl.pallas_call(functools.partial(dispatch_kernel, owners, heads, adapt, r...  1.76 us
    pallas_call x1, Pallas kernels, shards(): pl.pallas_call(functools.partial(prepare_kernel, owners, heads), out_shap...  1.5 us
  transfers between devices with their start and end apart: 2, of which 1 were waited for; matrix products, arithmetic and copies ran while one was open for 0% of the time, Pallas kernels for 4%

profile of v15, /device:TPU:0, one launch (start us, length us, event | category | flops | bytes accessed | tf_op | source)
XLA Modules:
  0.0 67.9 jit_solution(1257526599896383035)
XLA Ops:
  0.6 0.0 copy-start
  0.6 0.0 copy-start.6
  0.7 0.0 copy-start.5
  0.7 0.0 copy-start.4
  0.7 0.0 copy-start.2
  0.7 0.0 slice-start.2
  0.7 1.8 %dispatch.1 = (s32[48]{0:T(128)S(1)}, bf16[8,16,1152]{2,1,0:T(8,128)(2,1)S(1)}) custom-call(s32[16]{0:T(128)} %ids_hbm.1, s32[64]{0:T(128)} %slot_of_hbm.1, s32[16]{0:T(128)} %lengths_hbm.1, bf16[2,16,4096]{2,1,0:T(8,128)(2,1)} %x_hbm.1, bf16[16,512,512]{2,1,0:T(8,128)(2,1)} %k_ref.1, bf16[16,512,512]{2,1,0:T(8,128)(2,1)} %v_ref.1), custom_call_target="tpu_custom_call" | custom-call | tf_op jit(solution)/shard_map/dispatch/pallas_call | solution.py:446
  2.5 17.5 %all_to_all.20.blocks = bf16[8,16,1152]{2,1,0:T(8,128)(2,1)S(1)} all-to-all(bf16[8,16,1152]{2,1,0:T(8,128)(2,1)S(1)} %get-tuple-element.20), channel_id=1, replica_groups=mesh['parts'=2,'store'=8,'tensor'=2] {'store'}, dimensions={0} | all-to-all | bytes 589824 | tf_op jit(solution)/shard_map/all_to_all | solution.py:403
  20.0 0.0 copy-done
  20.0 0.0 slice-start
  20.0 0.0 slice-start.3
  20.0 0.6 project_query.1
  20.6 0.0 collective-permute-start
  20.6 0.0 copy-done.6
  20.6 0.0 copy-done.5
  20.7 0.0 copy-done.4
  20.7 1.5 %prepare.1 = (s32[16]{0:T(128)S(1)}, bf16[128,1024]{1,0:T(8,128)(2,1)S(1)}, bf16[32,512]{1,0:T(8,128)(2,1)S(1)}, bf16[32,512]{1,0:T(8,128)(2,1)S(1)}, bf16[64,51...) custom-call(s32[48]{0:T(128)S(1)} %get-tuple-element.19.meta, ...), custom_call_target="tpu_custom_call" | custom-call | tf_op jit(solution)/shard_map/prepare/pallas_call | solution.py:489
  22.2 0.0 collective-permute-done.other
  22.2 0.0 copy-done.2
  22.2 0.0 slice-start.1
  22.2 0.5 expand_query.1
  22.7 12.5 %all_to_all.21.blocks = bf16[8,16,1024]{2,1,0:T(8,128)(2,1)S(1)} all-to-all(bf16[8,16,1024]{2,1,0:T(8,128)(2,1)S(1)} %expand_query.1), channel_id=1, replica_groups=mesh['parts'=2,'store'=8,'tensor'=2] {'store'}, dimensions={0} | all-to-all | bytes 524288 | tf_op jit(solution)/shard_map/all_to_all | solution.py:403
  35.2 0.0 slice-done.2
  35.2 0.0 slice-done
  35.2 0.0 slice-done.3
  35.2 0.0 slice-done.1
  35.2 0.0 copy-start.1
  35.3 0.0 copy-start.3
  35.3 3.8 %attend.1 = (bf16[128,1024]{1,0:T(8,128)(2,1)S(1)}, bf16[8,16,1024]{2,1,0:T(8,128)(2,1)S(1)}) custom-call(s32[48]{0:T(128)S(1)} %get-tuple-element.19.meta, s32[16]{0:T(128)S(1)} %get-tuple-element.22.order, bf16[128,1024]{1,0:T(8,128)(2,1)S(1)} %get-tuple-element.23.base_ref, bf16[32,512]{1,0:T(8,128)(2,1)S(1)} %get-tuple-element.24.kn_ref, ...), custom_call_target="tpu_custom_call" | custom-call | tf_op jit(solution)/shard_map/attend/pallas_call | solution.py:510
  39.1 12.8 %all_to_all.22.blocks = bf16[8,16,1024]{2,1,0:T(8,128)(2,1)S(1)} all-to-all(bf16[8,16,1024]{2,1,0:T(8,128)(2,1)S(1)} %get-tuple-element.31), channel_id=1, replica_groups=mesh['parts'=2,'store'=8,'tensor'=2] {'store'}, dimensions={0} | all-to-all | bytes 524288 | tf_op jit(solution)/shard_map/all_to_all | solution.py:403
  51.9 0.0 copy-done.1
  51.9 0.6 project_output.1.part.mine
  52.5 0.0 collective-permute-start.1
  52.5 1.0 %finish.1 = (bf16[2,16,4096]{2,1,0:T(8,128)(2,1)}, f32[8,128]{1,0:T(8,128)S(1)}, bf16[128,128]{1,0:T(8,128)(2,1)S(1)}) custom-call(bf16[128,1024]{1,0:T(8,128)(2,1)S(1)} %get-tuple-element.30.mixed, bf16[128,128]{1,0:T(8,128)(2,1)S(1)} %get-tuple-element.27.gather_ref, f32[32,128]{1,0:T(8,128)S(1)} %project_output.1.part.mine), custom_call_target="tpu_custom_call" | custom-call | tf_op jit(solution)/shard_map/finish/pallas_call | solution.py:543
  53.5 0.2 collective-permute-done.1.other
  53.7 0.0 copy-done.3
  53.7 0.5 expand_output.1
  54.2 12.8 %all_to_all.23.blocks = bf16[8,16,1024]{2,1,0:T(8,128)(2,1)S(1)} all-to-all(bf16[8,16,1024]{2,1,0:T(8,128)(2,1)S(1)} %expand_output.1), channel_id=1, replica_groups=mesh['parts'=2,'store'=8,'tensor'=2] {'store'}, dimensions={0} | all-to-all | bytes 524288 | tf_op jit(solution)/shard_map/all_to_all | solution.py:403
  66.9 0.9 %collect.1 = bf16[2,16,4096]{2,1,0:T(8,128)(2,1)} custom-call(bf16[128,128]{1,0:T(8,128)(2,1)S(1)} %get-tuple-element.34.spread, bf16[8,16,1024]{2,1,0:T(8,128)(2,1)S(1)} %all_to_all.23.blocks), custom_call_target="tpu_custom_call" | custom-call | tf_op jit(solution)/shard_map/collect/pallas_call | solution.py:558
  (2 shorter events, 0.0 us)
Async XLA Ops:
  0.6 19.4 %copy-start = (bf16[8192,8,16]{0,2,1:T(8,128)(2,1)S(1)}, bf16[8192,8,16]{0,2,1:T(8,128)(2,1)}, u32[]{:S(2)}) copy-start(bf16[8192,8,16]{0,2,1:T(8,128)(2,1)} %param.22) | copy-start | bytes 6291460
  0.6 20.0 %copy-start.6 = (bf16[2,16,512]{2,1,0:T(8,128)(2,1)S(1)}, bf16[2,16,512]{2,1,0:T(8,128)(2,1)}, u32[]{:S(2)}) copy-start(bf16[2,16,512]{2,1,0:T(8,128)(2,1)} %vn_ref.1) | copy-start | bytes 98308
  0.7 20.0 %copy-start.5 = (bf16[2,16,512]{2,1,0:T(8,128)(2,1)S(1)}, bf16[2,16,512]{2,1,0:T(8,128)(2,1)}, u32[]{:S(2)}) copy-start(bf16[2,16,512]{2,1,0:T(8,128)(2,1)} %kn_ref.1) | copy-start | bytes 98308
  0.7 20.0 %copy-start.4 = (bf16[2,16,4096]{2,1,0:T(8,128)(2,1)S(1)}, bf16[2,16,4096]{2,1,0:T(8,128)(2,1)}, u32[]{:S(2)}) copy-start(bf16[2,16,4096]{2,1,0:T(8,128)(2,1)} %q_ref.1) | copy-start | bytes 786436
  0.7 21.5 %copy-start.2 = (bf16[8,16,4096]{2,1,0:T(8,128)(2,1)S(1)}, bf16[8,16,4096]{2,1,0:T(8,128)(2,1)}, u32[]{:S(2)}) copy-start(bf16[8,16,4096]{2,1,0:T(8,128)(2,1)} %param.23) | copy-start | bytes 3145732
  0.7 34.5 %slice-start.2 = ((s8[8388608]{0:T(1024)(128)(4,1)}), s8[4194304]{0:T(1024)(128)(4,1)S(1)}, s32[]{:S(2)}) async-start(s8[8388608]{0:T(1024)(128)(4,1)} %bitcast.10), calls=%async_computation.6 | async-start | bytes 8388608
  20.0 15.2 %slice-start = ((s8[8388608]{0:T(1024)(128)(4,1)}), s8[4194304]{0:T(1024)(128)(4,1)S(1)}, s32[]{:S(2)}) async-start(s8[8388608]{0:T(1024)(128)(4,1)} %bitcast.8), calls=%async_computation.4 | async-start | bytes 8388608
  20.0 15.2 %slice-start.3 = ((s8[8388608]{0:T(1024)(128)(4,1)}), s8[4194304]{0:T(1024)(128)(4,1)S(1)}, s32[]{:S(2)}) async-start(s8[8388608]{0:T(1024)(128)(4,1)} %bitcast.10), calls=%async_computation.7 | async-start | bytes 8388608
  20.6 1.6 %collective-permute-start = (f32[32,128]{1,0:T(8,128)S(1)}, f32[32,128]{1,0:T(8,128)S(1)}, u32[]{:S(2)}, u32[]{:S(2)}) collective-permute-start(f32[32,128]{1,0:T(8,128)S(1)} %get-tuple-element.21.part.mine), channel_id=1, source_target_pairs={{0,1},{1,0},{2,3},{3,2},{4,5},{5,4},{6,7},{7,6},{8,9},{9,8},{10,11... | collective-permute-start | bytes 49160 | tf_op jit(solution)/shard_map/ppermute | solution.py:411
  22.2 13.0 %slice-start.1 = ((s8[8388608]{0:T(1024)(128)(4,1)}), s8[4194304]{0:T(1024)(128)(4,1)S(1)}, s32[]{:S(2)}) async-start(s8[8388608]{0:T(1024)(128)(4,1)} %bitcast.8), calls=%async_computation.5 | async-start | bytes 8388608
  35.2 16.7 %copy-start.1 = (bf16[8192,8,16]{0,2,1:T(8,128)(2,1)S(1)}, bf16[8192,8,16]{0,2,1:T(8,128)(2,1)}, u32[]{:S(2)}) copy-start(bf16[8192,8,16]{0,2,1:T(8,128)(2,1)} %param.24) | copy-start | bytes 6291460
  35.3 18.4 %copy-start.3 = (bf16[8,16,4096]{2,1,0:T(8,128)(2,1)S(1)}, bf16[8,16,4096]{2,1,0:T(8,128)(2,1)}, u32[]{:S(2)}) copy-start(bf16[8,16,4096]{2,1,0:T(8,128)(2,1)} %param.25) | copy-start | bytes 3145732
  52.5 1.2 %collective-permute-start.1 = (f32[32,128]{1,0:T(8,128)S(1)}, f32[32,128]{1,0:T(8,128)S(1)}, u32[]{:S(2)}, u32[]{:S(2)}) collective-permute-start(f32[32,128]{1,0:T(8,128)S(1)} %project_output.1.part.mine), channel_id=1, source_target_pairs={{0,1},{1,0},{2,3},{3,2},{4,5},{5,4},{6,7},{7,6},{8,9},{9,8},{10,11... | collective-permute-start | bytes 49160 | tf_op jit(solution)/shard_map/ppermute | solution.py:411

commit v16 on v15

--- a/solution.py
+++ b/solution.py
@@ -164,7 +164,9 @@
         slot_at[p] = -1
     for r in range(rows):
         slot = slot_of[ids[r]]
-        first = over(slot, adapt) * CAP
+        owner = over(slot, adapt)
+        half = over(owner, 2)
+        first = jnp.where(rest(owner, 2) == 0, half, owners - 1 - half) * CAP
         place = first + jnp.where(meta[row_at + first] >= 0, 1, 0)
         meta[row_at + place] = r
         slot_at[place] = rest(slot, adapt)
@@ -400,7 +402,11 @@
 
 
 def exchange(blocks):
-    return lax.all_to_all(blocks, "store", split_axis=0, concat_axis=0, tiled=True)
+    owners = blocks.shape[0]
+    cycle = list(range(0, owners, 2)) + list(range(owners - 1, 0, -2))
+    return lax.all_to_all(
+        blocks, "store", split_axis=0, concat_axis=0, axis_index_groups=[cycle], tiled=True
+    )
 
 
 def in_hbm(array):

time: 68.1 us -> 67 us (0.984)
  blocking collectives: 55.6 us -> 54.4 us
    all_to_all x4, blocking collectives: 55.6 us -> 54.4 us  [exchange(): lax.all_to_all(blocks, 'store', split_axis=0, concat_axis=0, axis_index_g...]
where the time goes in v16:
time: 67 us; the launch traced here: 66.4 us
  blocking collectives  54.4 us (81%)
  Pallas kernels  10.9 us (16%)
  between operations  0.84 us (1%)
    all_to_all x4, blocking collectives, exchange(): lax.all_to_all(blocks, 'store', split_axis=0, concat_axis=0, axis_index_g...  54.4 us
    pallas_call x1, Pallas kernels, shards(): pl.pallas_call(functools.partial(attend_kernel, owners, heads, rows), out...  3.6 us
    pallas_call x1, Pallas kernels, shards(): pl.pallas_call(functools.partial(dispatch_kernel, owners, heads, adapt, r...  1.76 us
    pallas_call x1, Pallas kernels, shards(): pl.pallas_call(functools.partial(prepare_kernel, owners, heads), out_shap...  1.5 us
  transfers between devices with their start and end apart: 2, of which 1 were waited for; matrix products, arithmetic and copies ran while one was open for 0% of the time, Pallas kernels for 4%

profile of v16, /device:TPU:0, one launch (start us, length us, event | category | flops | bytes accessed | tf_op | source)
XLA Modules:
  0.0 66.4 jit_solution(16207623150599339827)
XLA Ops:
  0.6 0.0 copy-start
  0.6 0.0 copy-start.6
  0.7 0.0 copy-start.5
  0.7 0.0 copy-start.4
  0.7 0.0 copy-start.2
  0.7 0.0 slice-start.2
  0.7 1.8 %dispatch.1 = (s32[48]{0:T(128)S(1)}, bf16[8,16,1152]{2,1,0:T(8,128)(2,1)S(1)}) custom-call(s32[16]{0:T(128)} %ids_hbm.1, s32[64]{0:T(128)} %slot_of_hbm.1, s32[16]{0:T(128)} %lengths_hbm.1, bf16[2,16,4096]{2,1,0:T(8,128)(2,1)} %x_hbm.1, bf16[16,512,512]{2,1,0:T(8,128)(2,1)} %k_ref.1, bf16[16,512,512]{2,1,0:T(8,128)(2,1)} %v_ref.1), custom_call_target="tpu_custom_call" | custom-call | tf_op jit(solution)/shard_map/dispatch/pallas_call | solution.py:452
  2.5 17.5 %all_to_all.20.blocks = bf16[8,16,1152]{2,1,0:T(8,128)(2,1)S(1)} all-to-all(bf16[8,16,1152]{2,1,0:T(8,128)(2,1)S(1)} %get-tuple-element.20), channel_id=1, replica_groups={{0,4,8,12,14,10,6,2},{1,5,9,13,15,11,7,3},{16,20,24,28,30,26,22,18},{17..., dimensions={0} | all-to-all | bytes 589824 | tf_op jit(solution)/shard_map/all_to_all | solution.py:407
  20.0 0.0 copy-done
  20.0 0.0 slice-start
  20.0 0.0 slice-start.3
  20.0 0.6 project_query.1
  20.6 0.0 collective-permute-start
  20.6 0.0 copy-done.6
  20.6 0.0 copy-done.5
  20.7 0.0 copy-done.4
  20.7 1.5 %prepare.1 = (s32[16]{0:T(128)S(1)}, bf16[128,1024]{1,0:T(8,128)(2,1)S(1)}, bf16[32,512]{1,0:T(8,128)(2,1)S(1)}, bf16[32,512]{1,0:T(8,128)(2,1)S(1)}, bf16[64,51...) custom-call(s32[48]{0:T(128)S(1)} %get-tuple-element.19.meta, ...), custom_call_target="tpu_custom_call" | custom-call | tf_op jit(solution)/shard_map/prepare/pallas_call | solution.py:495
  22.2 0.0 collective-permute-done.other
  22.2 0.0 copy-done.2
  22.2 0.0 slice-start.1
  22.2 0.5 expand_query.1
  22.7 12.9 %all_to_all.21.blocks = bf16[8,16,1024]{2,1,0:T(8,128)(2,1)S(1)} all-to-all(bf16[8,16,1024]{2,1,0:T(8,128)(2,1)S(1)} %expand_query.1), channel_id=1, replica_groups={{0,4,8,12,14,10,6,2},{1,5,9,13,15,11,7,3},{16,20,24,28,30,26,22,18},{17..., dimensions={0} | all-to-all | bytes 524288 | tf_op jit(solution)/shard_map/all_to_all | solution.py:407
  35.6 0.0 slice-done.2
  35.6 0.0 slice-done
  35.6 0.0 slice-done.3
  35.6 0.0 slice-done.1
  35.6 0.0 copy-start.1
  35.6 0.0 copy-start.3
  35.6 3.6 %attend.1 = (bf16[128,1024]{1,0:T(8,128)(2,1)S(1)}, bf16[8,16,1024]{2,1,0:T(8,128)(2,1)S(1)}) custom-call(s32[48]{0:T(128)S(1)} %get-tuple-element.19.meta, s32[16]{0:T(128)S(1)} %get-tuple-element.22.order, bf16[128,1024]{1,0:T(8,128)(2,1)S(1)} %get-tuple-element.23.base_ref, bf16[32,512]{1,0:T(8,128)(2,1)S(1)} %get-tuple-element.24.kn_ref, ...), custom_call_target="tpu_custom_call" | custom-call | tf_op jit(solution)/shard_map/attend/pallas_call | solution.py:516
  39.3 11.5 %all_to_all.22.blocks = bf16[8,16,1024]{2,1,0:T(8,128)(2,1)S(1)} all-to-all(bf16[8,16,1024]{2,1,0:T(8,128)(2,1)S(1)} %get-tuple-element.31), channel_id=1, replica_groups={{0,4,8,12,14,10,6,2},{1,5,9,13,15,11,7,3},{16,20,24,28,30,26,22,18},{17..., dimensions={0} | all-to-all | bytes 524288 | tf_op jit(solution)/shard_map/all_to_all | solution.py:407
  50.8 0.0 copy-done.1
  50.8 0.6 project_output.1.part.mine
  51.3 0.0 collective-permute-start.1
  51.4 1.0 %finish.1 = (bf16[2,16,4096]{2,1,0:T(8,128)(2,1)}, f32[8,128]{1,0:T(8,128)S(1)}, bf16[128,128]{1,0:T(8,128)(2,1)S(1)}) custom-call(bf16[128,1024]{1,0:T(8,128)(2,1)S(1)} %get-tuple-element.30.mixed, bf16[128,128]{1,0:T(8,128)(2,1)S(1)} %get-tuple-element.27.gather_ref, f32[32,128]{1,0:T(8,128)S(1)} %project_output.1.part.mine), custom_call_target="tpu_custom_call" | custom-call | tf_op jit(solution)/shard_map/finish/pallas_call | solution.py:549
  52.3 0.2 collective-permute-done.1.other
  52.6 0.0 copy-done.3
  52.6 0.5 expand_output.1
  53.0 12.5 %all_to_all.23.blocks = bf16[8,16,1024]{2,1,0:T(8,128)(2,1)S(1)} all-to-all(bf16[8,16,1024]{2,1,0:T(8,128)(2,1)S(1)} %expand_output.1), channel_id=1, replica_groups={{0,4,8,12,14,10,6,2},{1,5,9,13,15,11,7,3},{16,20,24,28,30,26,22,18},{17..., dimensions={0} | all-to-all | bytes 524288 | tf_op jit(solution)/shard_map/all_to_all | solution.py:407
  65.5 0.9 %collect.1 = bf16[2,16,4096]{2,1,0:T(8,128)(2,1)} custom-call(bf16[128,128]{1,0:T(8,128)(2,1)S(1)} %get-tuple-element.34.spread, bf16[8,16,1024]{2,1,0:T(8,128)(2,1)S(1)} %all_to_all.23.blocks), custom_call_target="tpu_custom_call" | custom-call | tf_op jit(solution)/shard_map/collect/pallas_call | solution.py:564
  (2 shorter events, 0.0 us)
Async XLA Ops:
  0.6 19.4 %copy-start = (bf16[8192,8,16]{0,2,1:T(8,128)(2,1)S(1)}, bf16[8192,8,16]{0,2,1:T(8,128)(2,1)}, u32[]{:S(2)}) copy-start(bf16[8192,8,16]{0,2,1:T(8,128)(2,1)} %param.22) | copy-start | bytes 6291460
  0.6 20.0 %copy-start.6 = (bf16[2,16,512]{2,1,0:T(8,128)(2,1)S(1)}, bf16[2,16,512]{2,1,0:T(8,128)(2,1)}, u32[]{:S(2)}) copy-start(bf16[2,16,512]{2,1,0:T(8,128)(2,1)} %vn_ref.1) | copy-start | bytes 98308
  0.7 20.0 %copy-start.5 = (bf16[2,16,512]{2,1,0:T(8,128)(2,1)S(1)}, bf16[2,16,512]{2,1,0:T(8,128)(2,1)}, u32[]{:S(2)}) copy-start(bf16[2,16,512]{2,1,0:T(8,128)(2,1)} %kn_ref.1) | copy-start | bytes 98308
  0.7 20.0 %copy-start.4 = (bf16[2,16,4096]{2,1,0:T(8,128)(2,1)S(1)}, bf16[2,16,4096]{2,1,0:T(8,128)(2,1)}, u32[]{:S(2)}) copy-start(bf16[2,16,4096]{2,1,0:T(8,128)(2,1)} %q_ref.1) | copy-start | bytes 786436
  0.7 21.5 %copy-start.2 = (bf16[8,16,4096]{2,1,0:T(8,128)(2,1)S(1)}, bf16[8,16,4096]{2,1,0:T(8,128)(2,1)}, u32[]{:S(2)}) copy-start(bf16[8,16,4096]{2,1,0:T(8,128)(2,1)} %param.23) | copy-start | bytes 3145732
  0.7 34.9 %slice-start.2 = ((s8[8388608]{0:T(1024)(128)(4,1)}), s8[4194304]{0:T(1024)(128)(4,1)S(1)}, s32[]{:S(2)}) async-start(s8[8388608]{0:T(1024)(128)(4,1)} %bitcast.10), calls=%async_computation.6 | async-start | bytes 8388608
  20.0 15.6 %slice-start = ((s8[8388608]{0:T(1024)(128)(4,1)}), s8[4194304]{0:T(1024)(128)(4,1)S(1)}, s32[]{:S(2)}) async-start(s8[8388608]{0:T(1024)(128)(4,1)} %bitcast.8), calls=%async_computation.4 | async-start | bytes 8388608
  20.0 15.6 %slice-start.3 = ((s8[8388608]{0:T(1024)(128)(4,1)}), s8[4194304]{0:T(1024)(128)(4,1)S(1)}, s32[]{:S(2)}) async-start(s8[8388608]{0:T(1024)(128)(4,1)} %bitcast.10), calls=%async_computation.7 | async-start | bytes 8388608
  20.6 1.6 %collective-permute-start = (f32[32,128]{1,0:T(8,128)S(1)}, f32[32,128]{1,0:T(8,128)S(1)}, u32[]{:S(2)}, u32[]{:S(2)}) collective-permute-start(f32[32,128]{1,0:T(8,128)S(1)} %get-tuple-element.21.part.mine), channel_id=1, source_target_pairs={{0,1},{1,0},{2,3},{3,2},{4,5},{5,4},{6,7},{7,6},{8,9},{9,8},{10,11... | collective-permute-start | bytes 49160 | tf_op jit(solution)/shard_map/ppermute | solution.py:417
  22.2 13.4 %slice-start.1 = ((s8[8388608]{0:T(1024)(128)(4,1)}), s8[4194304]{0:T(1024)(128)(4,1)S(1)}, s32[]{:S(2)}) async-start(s8[8388608]{0:T(1024)(128)(4,1)} %bitcast.8), calls=%async_computation.5 | async-start | bytes 8388608
  35.6 15.1 %copy-start.1 = (bf16[8192,8,16]{0,2,1:T(8,128)(2,1)S(1)}, bf16[8192,8,16]{0,2,1:T(8,128)(2,1)}, u32[]{:S(2)}) copy-start(bf16[8192,8,16]{0,2,1:T(8,128)(2,1)} %param.24) | copy-start | bytes 6291460
  35.6 16.9 %copy-start.3 = (bf16[8,16,4096]{2,1,0:T(8,128)(2,1)S(1)}, bf16[8,16,4096]{2,1,0:T(8,128)(2,1)}, u32[]{:S(2)}) copy-start(bf16[8,16,4096]{2,1,0:T(8,128)(2,1)} %param.25) | copy-start | bytes 3145732
  51.3 1.2 %collective-permute-start.1 = (f32[32,128]{1,0:T(8,128)S(1)}, f32[32,128]{1,0:T(8,128)S(1)}, u32[]{:S(2)}, u32[]{:S(2)}) collective-permute-start(f32[32,128]{1,0:T(8,128)S(1)} %project_output.1.part.mine), channel_id=1, source_target_pairs={{0,1},{1,0},{2,3},{3,2},{4,5},{5,4},{6,7},{7,6},{8,9},{9,8},{10,11... | collective-permute-start | bytes 49160 | tf_op jit(solution)/shard_map/ppermute | solution.py:417

commit v17 on v16

--- a/solution.py
+++ b/solution.py
@@ -12,6 +12,7 @@
 CAP = 2
 STEPS = 2
 LAG = 2
+SPLIT = 2
 BF16 = jnp.bfloat16
 F32 = jnp.float32
 I32 = jnp.int32
@@ -135,6 +136,8 @@
     x_hbm,
     k_hbm,
     v_hbm,
+    k_again,
+    v_again,
     meta,
     blocks,
     slot_at,
@@ -450,12 +453,12 @@
     sent = shape((owners, block, wide), BF16)
     caches = (in_hbm(cache_k), in_hbm(cache_v))
     meta, blocks = pl.pallas_call(
-        functools.partial(dispatch_kernel, owners, heads, adapt, rank),
+        functools.partial(dispatch_kernel, owners, SPLIT, adapt, rank),
         out_shape=[
             shape((2 * rows + owners * CAP,), I32),
-            shape((owners, block, wide + lanes), BF16),
-        ],
-        in_specs=[HBM] * 6,
+            shape((owners, SPLIT * CAP * STEPS, width // SPLIT + lanes), BF16),
+        ],
+        in_specs=[HBM] * 8,
         out_specs=[SMEM, VMEM],
         scratch_shapes=[
             pltpu.SMEM((owners * CAP,), I32),
@@ -468,12 +471,12 @@
         compiler_params=small,
         name="dispatch",
     )(
-        *map(in_hbm, (adapter_ids, slot_of, lengths, x_in)), *caches
+        *map(in_hbm, (adapter_ids, slot_of, lengths, x_in)), *caches, *caches
     )
 
     arrived = exchange(blocks)
     part, mask = pl.pallas_call(
-        functools.partial(project_kernel, owners, heads, wide, True),
+        functools.partial(project_kernel, owners, SPLIT, width // SPLIT, True),
         out_shape=[shape((items, lanes), F32)] * 2,
         in_specs=[VMEM] * 2,
         out_specs=[VMEM] * 2,
@@ -510,7 +513,7 @@
         name="prepare",
     )(meta, q_base, k_new, v_new, part)
     returned = exchange(
-        expand(part, other, b_query.reshape(lanes, width), "expand_query", caches, after)
+        expand(part, other, b_query.reshape(lanes, width), "expand_query", (), after)
     )
 
     mixed, outgoing = pl.pallas_call(

time: 67 us -> 66.1 us (0.987)
  no operation moved by 1% of the time
where the time goes in v17:
time: 66.1 us; the launch traced here: 66 us
  blocking collectives  53.8 us (81%)
  Pallas kernels  11 us (17%)
  between operations  0.82 us (1%)
    all_to_all x4, blocking collectives, exchange(): lax.all_to_all(blocks, 'store', split_axis=0, concat_axis=0, axis_index_g...  53.8 us
    pallas_call x1, Pallas kernels, shards(): pl.pallas_call(functools.partial(attend_kernel, owners, heads, rows), out...  3.83 us
    pallas_call x1, Pallas kernels, shards(): pl.pallas_call(functools.partial(dispatch_kernel, owners, SPLIT, adapt, r...  1.75 us
    pallas_call x1, Pallas kernels, shards(): pl.pallas_call(functools.partial(prepare_kernel, owners, heads), out_shap...  1.51 us
  transfers between devices with their start and end apart: 2, of which 1 were waited for; matrix products, arithmetic and copies ran while one was open for 0% of the time, Pallas kernels for 4%

profile of v17, /device:TPU:0, one launch (start us, length us, event | category | flops | bytes accessed | tf_op | source)
XLA Modules:
  0.0 66.0 jit_solution(2237824998328940852)
XLA Ops:
  0.6 0.0 copy-start.2
  0.6 0.0 copy-start.8
  0.7 0.0 copy-start.7
  0.7 0.0 copy-start.6
  0.7 0.0 copy-start.4
  0.7 0.0 copy-start
  0.7 0.0 copy-start.1
  0.7 1.7 %dispatch.1 = (s32[48]{0:T(128)S(1)}, bf16[8,8,2176]{2,1,0:T(8,128)(2,1)S(1)}) custom-call(s32[16]{0:T(128)} %ids_hbm.1, s32[64]{0:T(128)} %slot_of_hbm.1, s32[16]{0:T(128)} %lengths_hbm.1, bf16[2,16,4096]{2,1,0:T(8,128)(2,1)} %x_hbm.1, bf16[16,512,512]{2,1,0:T(8,128)(2,1)} %k_ref.1, bf16[16,512,512]{2,1,0:T(8,128)(2,1)} %v_ref.1, ...), custom_call_target="tpu_custom_call" | custom-call | tf_op jit(solution)/shard_map/dispatch/pallas_call | solution.py:455
  2.5 17.4 %all_to_all.20.blocks = bf16[8,8,2176]{2,1,0:T(8,128)(2,1)S(1)} all-to-all(bf16[8,8,2176]{2,1,0:T(8,128)(2,1)S(1)} %get-tuple-element.20), channel_id=1, replica_groups={{0,4,8,12,14,10,6,2},{1,5,9,13,15,11,7,3},{16,20,24,28,30,26,22,18},{17..., dimensions={0} | all-to-all | bytes 557056 | tf_op jit(solution)/shard_map/all_to_all | solution.py:410
  19.9 0.0 copy-done.2
  19.9 0.5 project_query.1
  20.4 0.0 collective-permute-start
  20.4 0.0 copy-done.8
  20.5 0.0 copy-done.7
  20.5 0.0 copy-done.6
  20.5 1.5 %prepare.1 = (s32[16]{0:T(128)S(1)}, bf16[128,1024]{1,0:T(8,128)(2,1)S(1)}, bf16[32,512]{1,0:T(8,128)(2,1)S(1)}, bf16[32,512]{1,0:T(8,128)(2,1)S(1)}, bf16[64,51...) custom-call(s32[48]{0:T(128)S(1)} %get-tuple-element.19.meta, ...), custom_call_target="tpu_custom_call" | custom-call | tf_op jit(solution)/shard_map/prepare/pallas_call | solution.py:498
  22.0 0.0 collective-permute-done.other
  22.0 0.0 copy-done.4
  22.0 0.5 expand_query.1
  22.5 12.6 %all_to_all.21.blocks = bf16[8,16,1024]{2,1,0:T(8,128)(2,1)S(1)} all-to-all(bf16[8,16,1024]{2,1,0:T(8,128)(2,1)S(1)} %expand_query.1), channel_id=1, replica_groups={{0,4,8,12,14,10,6,2},{1,5,9,13,15,11,7,3},{16,20,24,28,30,26,22,18},{17..., dimensions={0} | all-to-all | bytes 524288 | tf_op jit(solution)/shard_map/all_to_all | solution.py:410
  35.1 0.0 copy-done
  35.1 0.0 copy-done.1
  35.1 0.0 copy-start.3
  35.1 0.0 copy-start.5
  35.1 3.8 %attend.1 = (bf16[128,1024]{1,0:T(8,128)(2,1)S(1)}, bf16[8,16,1024]{2,1,0:T(8,128)(2,1)S(1)}) custom-call(s32[48]{0:T(128)S(1)} %get-tuple-element.19.meta, s32[16]{0:T(128)S(1)} %get-tuple-element.22.order, bf16[128,1024]{1,0:T(8,128)(2,1)S(1)} %get-tuple-element.23.base_ref, bf16[32,512]{1,0:T(8,128)(2,1)S(1)} %get-tuple-element.24.kn_ref, ...), custom_call_target="tpu_custom_call" | custom-call | tf_op jit(solution)/shard_map/attend/pallas_call | solution.py:519
  39.0 11.3 %all_to_all.22.blocks = bf16[8,16,1024]{2,1,0:T(8,128)(2,1)S(1)} all-to-all(bf16[8,16,1024]{2,1,0:T(8,128)(2,1)S(1)} %get-tuple-element.31), channel_id=1, replica_groups={{0,4,8,12,14,10,6,2},{1,5,9,13,15,11,7,3},{16,20,24,28,30,26,22,18},{17..., dimensions={0} | all-to-all | bytes 524288 | tf_op jit(solution)/shard_map/all_to_all | solution.py:410
  50.3 0.0 copy-done.3
  50.3 0.6 project_output.1.part.mine
  50.9 0.0 collective-permute-start.1
  50.9 1.0 %finish.1 = (bf16[2,16,4096]{2,1,0:T(8,128)(2,1)}, f32[8,128]{1,0:T(8,128)S(1)}, bf16[128,128]{1,0:T(8,128)(2,1)S(1)}) custom-call(bf16[128,1024]{1,0:T(8,128)(2,1)S(1)} %get-tuple-element.30.mixed, bf16[128,128]{1,0:T(8,128)(2,1)S(1)} %get-tuple-element.27.gather_ref, f32[32,128]{1,0:T(8,128)S(1)} %project_output.1.part.mine), custom_call_target="tpu_custom_call" | custom-call | tf_op jit(solution)/shard_map/finish/pallas_call | solution.py:552
  51.9 0.2 collective-permute-done.1.other
  52.1 0.0 copy-done.5
  52.1 0.4 expand_output.1
  52.5 12.5 %all_to_all.23.blocks = bf16[8,16,1024]{2,1,0:T(8,128)(2,1)S(1)} all-to-all(bf16[8,16,1024]{2,1,0:T(8,128)(2,1)S(1)} %expand_output.1), channel_id=1, replica_groups={{0,4,8,12,14,10,6,2},{1,5,9,13,15,11,7,3},{16,20,24,28,30,26,22,18},{17..., dimensions={0} | all-to-all | bytes 524288 | tf_op jit(solution)/shard_map/all_to_all | solution.py:410
  65.0 0.9 %collect.1 = bf16[2,16,4096]{2,1,0:T(8,128)(2,1)} custom-call(bf16[128,128]{1,0:T(8,128)(2,1)S(1)} %get-tuple-element.34.spread, bf16[8,16,1024]{2,1,0:T(8,128)(2,1)S(1)} %all_to_all.23.blocks), custom_call_target="tpu_custom_call" | custom-call | tf_op jit(solution)/shard_map/collect/pallas_call | solution.py:567
Async XLA Ops:
  0.6 19.2 %copy-start.2 = (bf16[8192,8,16]{0,2,1:T(8,128)(2,1)S(1)}, bf16[8192,8,16]{0,2,1:T(8,128)(2,1)}, u32[]{:S(2)}) copy-start(bf16[8192,8,16]{0,2,1:T(8,128)(2,1)} %param.22) | copy-start | bytes 6291460
  0.6 19.8 %copy-start.8 = (bf16[2,16,512]{2,1,0:T(8,128)(2,1)S(1)}, bf16[2,16,512]{2,1,0:T(8,128)(2,1)}, u32[]{:S(2)}) copy-start(bf16[2,16,512]{2,1,0:T(8,128)(2,1)} %vn_ref.1) | copy-start | bytes 98308
  0.7 19.8 %copy-start.7 = (bf16[2,16,512]{2,1,0:T(8,128)(2,1)S(1)}, bf16[2,16,512]{2,1,0:T(8,128)(2,1)}, u32[]{:S(2)}) copy-start(bf16[2,16,512]{2,1,0:T(8,128)(2,1)} %kn_ref.1) | copy-start | bytes 98308
  0.7 19.8 %copy-start.6 = (bf16[2,16,4096]{2,1,0:T(8,128)(2,1)S(1)}, bf16[2,16,4096]{2,1,0:T(8,128)(2,1)}, u32[]{:S(2)}) copy-start(bf16[2,16,4096]{2,1,0:T(8,128)(2,1)} %q_ref.1) | copy-start | bytes 786436
  0.7 21.3 %copy-start.4 = (bf16[8,16,4096]{2,1,0:T(8,128)(2,1)S(1)}, bf16[8,16,4096]{2,1,0:T(8,128)(2,1)}, u32[]{:S(2)}) copy-start(bf16[8,16,4096]{2,1,0:T(8,128)(2,1)} %param.23) | copy-start | bytes 3145732
  0.7 34.4 %copy-start = (bf16[16,512,512]{2,1,0:T(8,128)(2,1)S(1)}, bf16[16,512,512]{2,1,0:T(8,128)(2,1)}, u32[]{:S(2)}) copy-start(bf16[16,512,512]{2,1,0:T(8,128)(2,1)} %k_ref.1) | copy-start | bytes 25165828
  0.7 34.4 %copy-start.1 = (bf16[16,512,512]{2,1,0:T(8,128)(2,1)S(1)}, bf16[16,512,512]{2,1,0:T(8,128)(2,1)}, u32[]{:S(2)}) copy-start(bf16[16,512,512]{2,1,0:T(8,128)(2,1)} %v_ref.1) | copy-start | bytes 25165828
  20.4 1.6 %collective-permute-start = (f32[32,128]{1,0:T(8,128)S(1)}, f32[32,128]{1,0:T(8,128)S(1)}, u32[]{:S(2)}, u32[]{:S(2)}) collective-permute-start(f32[32,128]{1,0:T(8,128)S(1)} %get-tuple-element.21.part.mine), channel_id=1, source_target_pairs={{0,1},{1,0},{2,3},{3,2},{4,5},{5,4},{6,7},{7,6},{8,9},{9,8},{10,11... | collective-permute-start | bytes 49160 | tf_op jit(solution)/shard_map/ppermute | solution.py:420
  35.1 15.2 %copy-start.3 = (bf16[8192,8,16]{0,2,1:T(8,128)(2,1)S(1)}, bf16[8192,8,16]{0,2,1:T(8,128)(2,1)}, u32[]{:S(2)}) copy-start(bf16[8192,8,16]{0,2,1:T(8,128)(2,1)} %param.24) | copy-start | bytes 6291460
  35.1 17.0 %copy-start.5 = (bf16[8,16,4096]{2,1,0:T(8,128)(2,1)S(1)}, bf16[8,16,4096]{2,1,0:T(8,128)(2,1)}, u32[]{:S(2)}) copy-start(bf16[8,16,4096]{2,1,0:T(8,128)(2,1)} %param.25) | copy-start | bytes 3145732
  50.9 1.2 %collective-permute-start.1 = (f32[32,128]{1,0:T(8,128)S(1)}, f32[32,128]{1,0:T(8,128)S(1)}, u32[]{:S(2)}, u32[]{:S(2)}) collective-permute-start(f32[32,128]{1,0:T(8,128)S(1)} %project_output.1.part.mine), channel_id=1, source_target_pairs={{0,1},{1,0},{2,3},{3,2},{4,5},{5,4},{6,7},{7,6},{8,9},{9,8},{10,11... | collective-permute-start | bytes 49160 | tf_op jit(solution)/shard_map/ppermute | solution.py:420

commit v18 on v17

--- a/solution.py
+++ b/solution.py
@@ -99,22 +99,26 @@
     return one_hot(iota(shape, 1) == rest(at, rows) * pairs + over(at, rows))
 
 
-def regroup_matrix(owners, heads):
+def turned(place, owners, core):
+    return place + rest(core, 2) * (owners - 1 - 2 * place)
+
+
+def regroup_matrix(owners, heads, core):
     items = CAP * STEPS
     total = owners * heads * items
     at = iota((total, total), 0)
     head = over(at, owners * items)
-    owner = rest(over(at, items), owners)
+    owner = turned(rest(over(at, items), owners), owners, core)
     return one_hot(
         iota((total, total), 1) == owner * (heads * items) + head * items + rest(at, items)
     )
 
 
-def ungroup_matrix(owners, heads):
+def ungroup_matrix(owners, heads, core):
     items = CAP * STEPS
     total = owners * heads * items
     at = iota((total, total), 0)
-    owner = over(at, heads * items)
+    owner = turned(over(at, heads * items), owners, core)
     head = rest(over(at, items), heads)
     return one_hot(
         iota((total, total), 1) == head * (owners * items) + owner * items + rest(at, items)
@@ -160,6 +164,7 @@
     wide = x_ref.shape[2] // heads
     for copy in copies[:3]:
         copy.wait()
+    core = lax.axis_index("tensor")
     row_at = rows
     spans = rows + owners * CAP
     for p in range(owners * CAP):
@@ -169,7 +174,7 @@
         slot = slot_of[ids[r]]
         owner = over(slot, adapt)
         half = over(owner, 2)
-        first = jnp.where(rest(owner, 2) == 0, half, owners - 1 - half) * CAP
+        first = turned(jnp.where(rest(owner, 2) == 0, half, owners - 1 - half), owners, core) * CAP
         place = first + jnp.where(meta[row_at + first] >= 0, 1, 0)
         meta[row_at + place] = r
         slot_at[place] = rest(slot, adapt)
@@ -189,12 +194,12 @@
 
 
 def project_kernel(owners, heads, wide, first, a_ref, blocks, *refs):
-    core = lax.axis_index("tensor") if a_ref.shape[1] > heads * wide else 0
+    core = lax.axis_index("tensor")
     if first:
         part_ref, mask_ref = refs
     else:
         mask_in, part_ref = refs
-    grouped = regroup_matrix(owners, heads)
+    grouped = regroup_matrix(owners, heads, core)
     items = owners * CAP * STEPS
     arrived = jnp.concatenate([blocks[i, :, :wide] for i in range(owners)], axis=0)
     arrived = exact(grouped, arrived)
@@ -224,7 +229,7 @@
             low_rank, b_ref[:, c * wide : (c + 1) * wide], preferred_element_type=F32
         )
         pieces.append((2.0 * product).astype(BF16))
-    back = exact(ungroup_matrix(owners, heads), jnp.concatenate(pieces, axis=0))
+    back = exact(ungroup_matrix(owners, heads, lax.axis_index("tensor")), jnp.concatenate(pieces, axis=0))
     block = heads * CAP * STEPS
     for i in range(owners):
         blocks[i] = back[i * block : (i + 1) * block]
@@ -406,9 +411,19 @@
 
 def exchange(blocks):
     owners = blocks.shape[0]
+    cores = lax.axis_size("tensor")
     cycle = list(range(0, owners, 2)) + list(range(owners - 1, 0, -2))
+    groups = [
+        [s * cores + core for s in (cycle if core % 2 == 0 else cycle[::-1])]
+        for core in range(cores)
+    ]
     return lax.all_to_all(
-        blocks, "store", split_axis=0, concat_axis=0, axis_index_groups=[cycle], tiled=True
+        blocks,
+        ("store", "tensor"),
+        split_axis=0,
+        concat_axis=0,
+        axis_index_groups=groups,
+        tiled=True,
     )
 
 

time: 66.1 us -> 65.9 us (level)
  blocking collectives: 53.8 us -> 52.9 us
    all_to_all x4, blocking collectives: 53.8 us -> 52.9 us  [exchange(): lax.all_to_all(blocks, ('store', 'tensor'), split_axis=0, concat_axis=0,...]
where the time goes in v18:
time: 65.9 us; the launch traced here: 65.3 us
  blocking collectives  52.9 us (80%)
  Pallas kernels  11.3 us (17%)
  between operations  0.82 us (1%)
    all_to_all x4, blocking collectives, exchange(): lax.all_to_all(blocks, ('store', 'tensor'), split_axis=0, concat_axis=0,...  52.9 us
    pallas_call x1, Pallas kernels, shards(): pl.pallas_call(functools.partial(attend_kernel, owners, heads, rows), out...  4.12 us
    pallas_call x1, Pallas kernels, shards(): pl.pallas_call(functools.partial(dispatch_kernel, owners, SPLIT, adapt, r...  1.75 us
    pallas_call x1, Pallas kernels, shards(): pl.pallas_call(functools.partial(prepare_kernel, owners, heads), out_shap...  1.51 us
  transfers between devices with their start and end apart: 2, of which 1 were waited for; matrix products, arithmetic and copies ran while one was open for 0% of the time, Pallas kernels for 4%

profile of v18, /device:TPU:0, one launch (start us, length us, event | category | flops | bytes accessed | tf_op | source)
XLA Modules:
  0.0 65.3 jit_solution(9727506592930415228)
XLA Ops:
  0.6 0.0 copy-start.2
  0.6 0.0 copy-start.8
  0.7 0.0 copy-start.7
  0.7 0.0 copy-start.6
  0.7 0.0 copy-start.4
  0.7 0.0 copy-start
  0.7 0.0 copy-start.1
  0.7 1.7 %dispatch.1 = (s32[48]{0:T(128)S(1)}, bf16[8,8,2176]{2,1,0:T(8,128)(2,1)S(1)}) custom-call(s32[16]{0:T(128)} %ids_hbm.1, s32[64]{0:T(128)} %slot_of_hbm.1, s32[16]{0:T(128)} %lengths_hbm.1, bf16[2,16,4096]{2,1,0:T(8,128)(2,1)} %x_hbm.1, bf16[16,512,512]{2,1,0:T(8,128)(2,1)} %k_ref.1, bf16[16,512,512]{2,1,0:T(8,128)(2,1)} %v_ref.1, ...), custom_call_target="tpu_custom_call" | custom-call | tf_op jit(solution)/shard_map/dispatch/pallas_call | solution.py:470
  2.5 16.6 %all_to_all.20.blocks = bf16[8,8,2176]{2,1,0:T(8,128)(2,1)S(1)} all-to-all(bf16[8,8,2176]{2,1,0:T(8,128)(2,1)S(1)} %get-tuple-element.20), channel_id=1, replica_groups={{0,4,8,12,14,10,6,2},{3,7,11,15,13,9,5,1},{16,20,24,28,30,26,22,18},{19..., dimensions={0} | all-to-all | bytes 557056 | tf_op jit(solution)/shard_map/all_to_all | solution.py:420
  19.1 0.0 copy-done.2
  19.1 0.6 project_query.1
  19.6 0.0 collective-permute-start
  19.7 0.0 copy-done.8
  19.7 0.0 copy-done.7
  19.7 0.0 copy-done.6
  19.7 1.5 %prepare.1 = (s32[16]{0:T(128)S(1)}, bf16[128,1024]{1,0:T(8,128)(2,1)S(1)}, bf16[32,512]{1,0:T(8,128)(2,1)S(1)}, bf16[32,512]{1,0:T(8,128)(2,1)S(1)}, bf16[64,51...) custom-call(s32[48]{0:T(128)S(1)} %get-tuple-element.19.meta, ...), custom_call_target="tpu_custom_call" | custom-call | tf_op jit(solution)/shard_map/prepare/pallas_call | solution.py:513
  21.2 0.0 collective-permute-done.other
  21.2 0.0 copy-done.4
  21.2 0.5 expand_query.1
  21.7 12.6 %all_to_all.21.blocks = bf16[8,16,1024]{2,1,0:T(8,128)(2,1)S(1)} all-to-all(bf16[8,16,1024]{2,1,0:T(8,128)(2,1)S(1)} %expand_query.1), channel_id=1, replica_groups={{0,4,8,12,14,10,6,2},{3,7,11,15,13,9,5,1},{16,20,24,28,30,26,22,18},{19..., dimensions={0} | all-to-all | bytes 524288 | tf_op jit(solution)/shard_map/all_to_all | solution.py:420
  34.3 0.0 copy-done
  34.3 0.0 copy-done.1
  34.3 0.0 copy-start.3
  34.3 0.0 copy-start.5
  34.3 4.1 %attend.1 = (bf16[128,1024]{1,0:T(8,128)(2,1)S(1)}, bf16[8,16,1024]{2,1,0:T(8,128)(2,1)S(1)}) custom-call(s32[48]{0:T(128)S(1)} %get-tuple-element.19.meta, s32[16]{0:T(128)S(1)} %get-tuple-element.22.order, bf16[128,1024]{1,0:T(8,128)(2,1)S(1)} %get-tuple-element.23.base_ref, bf16[32,512]{1,0:T(8,128)(2,1)S(1)} %get-tuple-element.24.kn_ref, ...), custom_call_target="tpu_custom_call" | custom-call | tf_op jit(solution)/shard_map/attend/pallas_call | solution.py:534
  38.4 11.3 %all_to_all.22.blocks = bf16[8,16,1024]{2,1,0:T(8,128)(2,1)S(1)} all-to-all(bf16[8,16,1024]{2,1,0:T(8,128)(2,1)S(1)} %get-tuple-element.31), channel_id=1, replica_groups={{0,4,8,12,14,10,6,2},{3,7,11,15,13,9,5,1},{16,20,24,28,30,26,22,18},{19..., dimensions={0} | all-to-all | bytes 524288 | tf_op jit(solution)/shard_map/all_to_all | solution.py:420
  49.7 0.0 copy-done.3
  49.7 0.6 project_output.1.part.mine
  50.3 0.0 collective-permute-start.1
  50.3 1.0 %finish.1 = (bf16[2,16,4096]{2,1,0:T(8,128)(2,1)}, f32[8,128]{1,0:T(8,128)S(1)}, bf16[128,128]{1,0:T(8,128)(2,1)S(1)}) custom-call(bf16[128,1024]{1,0:T(8,128)(2,1)S(1)} %get-tuple-element.30.mixed, bf16[128,128]{1,0:T(8,128)(2,1)S(1)} %get-tuple-element.27.gather_ref, f32[32,128]{1,0:T(8,128)S(1)} %project_output.1.part.mine), custom_call_target="tpu_custom_call" | custom-call | tf_op jit(solution)/shard_map/finish/pallas_call | solution.py:567
  51.3 0.2 collective-permute-done.1.other
  51.5 0.0 copy-done.5
  51.5 0.4 expand_output.1
  52.0 12.4 %all_to_all.23.blocks = bf16[8,16,1024]{2,1,0:T(8,128)(2,1)S(1)} all-to-all(bf16[8,16,1024]{2,1,0:T(8,128)(2,1)S(1)} %expand_output.1), channel_id=1, replica_groups={{0,4,8,12,14,10,6,2},{3,7,11,15,13,9,5,1},{16,20,24,28,30,26,22,18},{19..., dimensions={0} | all-to-all | bytes 524288 | tf_op jit(solution)/shard_map/all_to_all | solution.py:420
  64.4 0.9 %collect.1 = bf16[2,16,4096]{2,1,0:T(8,128)(2,1)} custom-call(bf16[128,128]{1,0:T(8,128)(2,1)S(1)} %get-tuple-element.34.spread, bf16[8,16,1024]{2,1,0:T(8,128)(2,1)S(1)} %all_to_all.23.blocks), custom_call_target="tpu_custom_call" | custom-call | tf_op jit(solution)/shard_map/collect/pallas_call | solution.py:582
Async XLA Ops:
  0.6 18.4 %copy-start.2 = (bf16[8192,8,16]{0,2,1:T(8,128)(2,1)S(1)}, bf16[8192,8,16]{0,2,1:T(8,128)(2,1)}, u32[]{:S(2)}) copy-start(bf16[8192,8,16]{0,2,1:T(8,128)(2,1)} %param.22) | copy-start | bytes 6291460
  0.6 19.0 %copy-start.8 = (bf16[2,16,512]{2,1,0:T(8,128)(2,1)S(1)}, bf16[2,16,512]{2,1,0:T(8,128)(2,1)}, u32[]{:S(2)}) copy-start(bf16[2,16,512]{2,1,0:T(8,128)(2,1)} %vn_ref.1) | copy-start | bytes 98308
  0.7 19.0 %copy-start.7 = (bf16[2,16,512]{2,1,0:T(8,128)(2,1)S(1)}, bf16[2,16,512]{2,1,0:T(8,128)(2,1)}, u32[]{:S(2)}) copy-start(bf16[2,16,512]{2,1,0:T(8,128)(2,1)} %kn_ref.1) | copy-start | bytes 98308
  0.7 19.0 %copy-start.6 = (bf16[2,16,4096]{2,1,0:T(8,128)(2,1)S(1)}, bf16[2,16,4096]{2,1,0:T(8,128)(2,1)}, u32[]{:S(2)}) copy-start(bf16[2,16,4096]{2,1,0:T(8,128)(2,1)} %q_ref.1) | copy-start | bytes 786436
  0.7 20.6 %copy-start.4 = (bf16[8,16,4096]{2,1,0:T(8,128)(2,1)S(1)}, bf16[8,16,4096]{2,1,0:T(8,128)(2,1)}, u32[]{:S(2)}) copy-start(bf16[8,16,4096]{2,1,0:T(8,128)(2,1)} %param.23) | copy-start | bytes 3145732
  0.7 33.6 %copy-start = (bf16[16,512,512]{2,1,0:T(8,128)(2,1)S(1)}, bf16[16,512,512]{2,1,0:T(8,128)(2,1)}, u32[]{:S(2)}) copy-start(bf16[16,512,512]{2,1,0:T(8,128)(2,1)} %k_ref.1) | copy-start | bytes 25165828
  0.7 33.6 %copy-start.1 = (bf16[16,512,512]{2,1,0:T(8,128)(2,1)S(1)}, bf16[16,512,512]{2,1,0:T(8,128)(2,1)}, u32[]{:S(2)}) copy-start(bf16[16,512,512]{2,1,0:T(8,128)(2,1)} %v_ref.1) | copy-start | bytes 25165828
  19.6 1.6 %collective-permute-start = (f32[32,128]{1,0:T(8,128)S(1)}, f32[32,128]{1,0:T(8,128)S(1)}, u32[]{:S(2)}, u32[]{:S(2)}) collective-permute-start(f32[32,128]{1,0:T(8,128)S(1)} %get-tuple-element.21.part.mine), channel_id=1, source_target_pairs={{0,1},{1,0},{2,3},{3,2},{4,5},{5,4},{6,7},{7,6},{8,9},{9,8},{10,11... | collective-permute-start | bytes 49160 | tf_op jit(solution)/shard_map/ppermute | solution.py:435
  34.3 15.5 %copy-start.3 = (bf16[8192,8,16]{0,2,1:T(8,128)(2,1)S(1)}, bf16[8192,8,16]{0,2,1:T(8,128)(2,1)}, u32[]{:S(2)}) copy-start(bf16[8192,8,16]{0,2,1:T(8,128)(2,1)} %param.24) | copy-start | bytes 6291460
  34.3 17.3 %copy-start.5 = (bf16[8,16,4096]{2,1,0:T(8,128)(2,1)S(1)}, bf16[8,16,4096]{2,1,0:T(8,128)(2,1)}, u32[]{:S(2)}) copy-start(bf16[8,16,4096]{2,1,0:T(8,128)(2,1)} %param.25) | copy-start | bytes 3145732
  50.3 1.2 %collective-permute-start.1 = (f32[32,128]{1,0:T(8,128)S(1)}, f32[32,128]{1,0:T(8,128)S(1)}, u32[]{:S(2)}, u32[]{:S(2)}) collective-permute-start(f32[32,128]{1,0:T(8,128)S(1)} %project_output.1.part.mine), channel_id=1, source_target_pairs={{0,1},{1,0},{2,3},{3,2},{4,5},{5,4},{6,7},{7,6},{8,9},{9,8},{10,11... | collective-permute-start | bytes 49160 | tf_op jit(solution)/shard_map/ppermute | solution.py:435

commit v19 on v18

--- a/solution.py
+++ b/solution.py
@@ -97,6 +97,10 @@
     shape = (pairs * rows, pairs * rows)
     at = iota(shape, 0)
     return one_hot(iota(shape, 1) == rest(at, rows) * pairs + over(at, rows))
+
+
+def stride_of(owners):
+    return 3 if owners % 3 else 1
 
 
 def turned(place, owners, core):
@@ -174,7 +178,9 @@
         slot = slot_of[ids[r]]
         owner = over(slot, adapt)
         half = over(owner, 2)
-        first = turned(jnp.where(rest(owner, 2) == 0, half, owners - 1 - half), owners, core) * CAP
+        along = jnp.where(rest(owner, 2) == 0, half, owners - 1 - half)
+        along = rest(along * pow(stride_of(owners), -1, owners), owners)
+        first = turned(along, owners, core) * CAP
         place = first + jnp.where(meta[row_at + first] >= 0, 1, 0)
         meta[row_at + place] = r
         slot_at[place] = rest(slot, adapt)
@@ -286,6 +292,7 @@
             ahead[q] = ahead[q] + (1 - shorter)
     for r in range(rows):
         order[ahead[r]] = r
+        order[rows + r] = sizes[r]
     after[...] = part[: after.shape[0], :]
 
 
@@ -293,7 +300,6 @@
     owners,
     heads,
     rows,
-    meta,
     order,
     base_ref,
     kn_ref,
@@ -315,7 +321,7 @@
     total = groups * pairs
 
     def span_of(row):
-        return meta[rows + owners * CAP + row]
+        return order[rows + row]
 
     delta = jnp.dot(
         gather_ref[...],
@@ -413,6 +419,7 @@
     owners = blocks.shape[0]
     cores = lax.axis_size("tensor")
     cycle = list(range(0, owners, 2)) + list(range(owners - 1, 0, -2))
+    cycle = [cycle[i * stride_of(owners) % owners] for i in range(owners)]
     groups = [
         [s * cores + core for s in (cycle if core % 2 == 0 else cycle[::-1])]
         for core in range(cores)
@@ -513,7 +520,7 @@
     order, *prepared, after = pl.pallas_call(
         functools.partial(prepare_kernel, owners, heads),
         out_shape=[
-            shape((rows,), I32),
+            shape((2 * rows,), I32),
             shape((rows * STEPS * heads, wide), BF16),
             shape((STEPS * rows, heads * HD), BF16),
             shape((STEPS * rows, heads * HD), BF16),
@@ -537,7 +544,7 @@
             shape((rows * STEPS * heads, wide), BF16),
             sent,
         ],
-        in_specs=[SMEM] * 2 + [VMEM] * 9,
+        in_specs=[SMEM] + [VMEM] * 9,
         out_specs=[VMEM] * 2,
         scratch_shapes=[
             pltpu.VMEM((rows * STEPS * heads, wide), F32),
@@ -545,7 +552,7 @@
         ],
         compiler_params=small,
         name="attend",
-    )(meta, order, *prepared, cache_k, cache_v, returned)
+    )(order, *prepared, cache_k, cache_v, returned)
 
     arrived = exchange(outgoing)
     part = pl.pallas_call(

time: 65.9 us -> 64.7 us (0.982)
  no operation moved by 1% of the time
where the time goes in v19:
time: 64.7 us; the launch traced here: 64.5 us
  blocking collectives  52.6 us (81%)
  Pallas kernels  10.8 us (17%)
  between operations  0.82 us (1%)
    all_to_all x4, blocking collectives, exchange(): lax.all_to_all(blocks, ('store', 'tensor'), split_axis=0, concat_axis=0,...  52.6 us
    pallas_call x1, Pallas kernels, shards(): pl.pallas_call(functools.partial(attend_kernel, owners, heads, rows), out...  3.61 us
    pallas_call x1, Pallas kernels, shards(): pl.pallas_call(functools.partial(dispatch_kernel, owners, SPLIT, adapt, r...  1.75 us
    pallas_call x1, Pallas kernels, shards(): pl.pallas_call(functools.partial(prepare_kernel, owners, heads), out_shap...  1.51 us
  transfers between devices with their start and end apart: 2, of which 1 were waited for; matrix products, arithmetic and copies ran while one was open for 0% of the time, Pallas kernels for 4%

profile of v19, /device:TPU:0, one launch (start us, length us, event | category | flops | bytes accessed | tf_op | source)
XLA Modules:
  0.0 64.5 jit_solution(8904756119117053372)
XLA Ops:
  0.6 0.0 copy-start.2
  0.6 0.0 copy-start.8
  0.7 0.0 copy-start.7
  0.7 0.0 copy-start.6
  0.7 0.0 copy-start.4
  0.7 0.0 copy-start
  0.7 0.0 copy-start.1
  0.7 1.7 %dispatch.1 = (s32[48]{0:T(128)S(1)}, bf16[8,8,2176]{2,1,0:T(8,128)(2,1)S(1)}) custom-call(s32[16]{0:T(128)} %ids_hbm.1, s32[64]{0:T(128)} %slot_of_hbm.1, s32[16]{0:T(128)} %lengths_hbm.1, bf16[2,16,4096]{2,1,0:T(8,128)(2,1)} %x_hbm.1, bf16[16,512,512]{2,1,0:T(8,128)(2,1)} %k_ref.1, bf16[16,512,512]{2,1,0:T(8,128)(2,1)} %v_ref.1, ...), custom_call_target="tpu_custom_call" | custom-call | tf_op jit(solution)/shard_map/dispatch/pallas_call | solution.py:477
  2.5 16.0 %all_to_all.20.blocks = bf16[8,8,2176]{2,1,0:T(8,128)(2,1)S(1)} all-to-all(bf16[8,8,2176]{2,1,0:T(8,128)(2,1)S(1)} %get-tuple-element.20), channel_id=1, replica_groups={{0,12,6,4,14,2,8,10},{11,9,3,15,5,7,13,1},{16,28,22,20,30,18,24,26},{27..., dimensions={0} | all-to-all | bytes 557056 | tf_op jit(solution)/shard_map/all_to_all | solution.py:427
  18.5 0.0 copy-done.2
  18.5 0.6 project_query.1
  19.1 0.0 collective-permute-start
  19.1 0.0 copy-done.8
  19.1 0.0 copy-done.7
  19.1 0.0 copy-done.6
  19.1 1.5 %prepare.1 = (s32[32]{0:T(128)S(1)}, bf16[128,1024]{1,0:T(8,128)(2,1)S(1)}, bf16[32,512]{1,0:T(8,128)(2,1)S(1)}, bf16[32,512]{1,0:T(8,128)(2,1)S(1)}, bf16[64,51...) custom-call(s32[48]{0:T(128)S(1)} %get-tuple-element.19.meta, ...), custom_call_target="tpu_custom_call" | custom-call | tf_op jit(solution)/shard_map/prepare/pallas_call | solution.py:520
  20.7 0.0 collective-permute-done.other
  20.7 0.0 copy-done.4
  20.7 0.5 expand_query.1
  21.1 11.9 %all_to_all.21.blocks = bf16[8,16,1024]{2,1,0:T(8,128)(2,1)S(1)} all-to-all(bf16[8,16,1024]{2,1,0:T(8,128)(2,1)S(1)} %expand_query.1), channel_id=1, replica_groups={{0,12,6,4,14,2,8,10},{11,9,3,15,5,7,13,1},{16,28,22,20,30,18,24,26},{27..., dimensions={0} | all-to-all | bytes 524288 | tf_op jit(solution)/shard_map/all_to_all | solution.py:427
  33.0 0.0 copy-done
  33.0 0.0 copy-done.1
  33.0 0.0 copy-start.3
  33.0 0.0 copy-start.5
  33.1 3.6 %attend.1 = (bf16[128,1024]{1,0:T(8,128)(2,1)S(1)}, bf16[8,16,1024]{2,1,0:T(8,128)(2,1)S(1)}) custom-call(s32[32]{0:T(128)S(1)} %get-tuple-element.22.order, bf16[128,1024]{1,0:T(8,128)(2,1)S(1)} %get-tuple-element.23.base_ref, bf16[32,512]{1,0:T(8,128)(2,1)S(1)} %get-tuple-element.24.kn_ref, bf16[32,512]{1,0:T(8,128)(2,1)S(1)} %get-tuple-element.25.vn_ref, ...), custom_call_target="tpu_custom_call" | custom-call | tf_op jit(solution)/shard_map/attend/pallas_call | solution.py:541
  36.7 12.9 %all_to_all.22.blocks = bf16[8,16,1024]{2,1,0:T(8,128)(2,1)S(1)} all-to-all(bf16[8,16,1024]{2,1,0:T(8,128)(2,1)S(1)} %get-tuple-element.31), channel_id=1, replica_groups={{0,12,6,4,14,2,8,10},{11,9,3,15,5,7,13,1},{16,28,22,20,30,18,24,26},{27..., dimensions={0} | all-to-all | bytes 524288 | tf_op jit(solution)/shard_map/all_to_all | solution.py:427
  49.6 0.0 copy-done.3
  49.6 0.6 project_output.1.part.mine
  50.2 0.0 collective-permute-start.1
  50.2 1.0 %finish.1 = (bf16[2,16,4096]{2,1,0:T(8,128)(2,1)}, f32[8,128]{1,0:T(8,128)S(1)}, bf16[128,128]{1,0:T(8,128)(2,1)S(1)}) custom-call(bf16[128,1024]{1,0:T(8,128)(2,1)S(1)} %get-tuple-element.30.mixed, bf16[128,128]{1,0:T(8,128)(2,1)S(1)} %get-tuple-element.27.gather_ref, f32[32,128]{1,0:T(8,128)S(1)} %project_output.1.part.mine), custom_call_target="tpu_custom_call" | custom-call | tf_op jit(solution)/shard_map/finish/pallas_call | solution.py:574
  51.2 0.2 collective-permute-done.1.other
  51.4 0.0 copy-done.5
  51.4 0.5 expand_output.1
  51.8 11.7 %all_to_all.23.blocks = bf16[8,16,1024]{2,1,0:T(8,128)(2,1)S(1)} all-to-all(bf16[8,16,1024]{2,1,0:T(8,128)(2,1)S(1)} %expand_output.1), channel_id=1, replica_groups={{0,12,6,4,14,2,8,10},{11,9,3,15,5,7,13,1},{16,28,22,20,30,18,24,26},{27..., dimensions={0} | all-to-all | bytes 524288 | tf_op jit(solution)/shard_map/all_to_all | solution.py:427
  63.6 0.9 %collect.1 = bf16[2,16,4096]{2,1,0:T(8,128)(2,1)} custom-call(bf16[128,128]{1,0:T(8,128)(2,1)S(1)} %get-tuple-element.34.spread, bf16[8,16,1024]{2,1,0:T(8,128)(2,1)S(1)} %all_to_all.23.blocks), custom_call_target="tpu_custom_call" | custom-call | tf_op jit(solution)/shard_map/collect/pallas_call | solution.py:589
Async XLA Ops:
  0.6 17.9 %copy-start.2 = (bf16[8192,8,16]{0,2,1:T(8,128)(2,1)S(1)}, bf16[8192,8,16]{0,2,1:T(8,128)(2,1)}, u32[]{:S(2)}) copy-start(bf16[8192,8,16]{0,2,1:T(8,128)(2,1)} %param.22) | copy-start | bytes 6291460
  0.6 18.5 %copy-start.8 = (bf16[2,16,512]{2,1,0:T(8,128)(2,1)S(1)}, bf16[2,16,512]{2,1,0:T(8,128)(2,1)}, u32[]{:S(2)}) copy-start(bf16[2,16,512]{2,1,0:T(8,128)(2,1)} %vn_ref.1) | copy-start | bytes 98308
  0.7 18.5 %copy-start.7 = (bf16[2,16,512]{2,1,0:T(8,128)(2,1)S(1)}, bf16[2,16,512]{2,1,0:T(8,128)(2,1)}, u32[]{:S(2)}) copy-start(bf16[2,16,512]{2,1,0:T(8,128)(2,1)} %kn_ref.1) | copy-start | bytes 98308
  0.7 18.5 %copy-start.6 = (bf16[2,16,4096]{2,1,0:T(8,128)(2,1)S(1)}, bf16[2,16,4096]{2,1,0:T(8,128)(2,1)}, u32[]{:S(2)}) copy-start(bf16[2,16,4096]{2,1,0:T(8,128)(2,1)} %q_ref.1) | copy-start | bytes 786436
  0.7 20.0 %copy-start.4 = (bf16[8,16,4096]{2,1,0:T(8,128)(2,1)S(1)}, bf16[8,16,4096]{2,1,0:T(8,128)(2,1)}, u32[]{:S(2)}) copy-start(bf16[8,16,4096]{2,1,0:T(8,128)(2,1)} %param.23) | copy-start | bytes 3145732
  0.7 32.4 %copy-start = (bf16[16,512,512]{2,1,0:T(8,128)(2,1)S(1)}, bf16[16,512,512]{2,1,0:T(8,128)(2,1)}, u32[]{:S(2)}) copy-start(bf16[16,512,512]{2,1,0:T(8,128)(2,1)} %k_ref.1) | copy-start | bytes 25165828
  0.7 32.4 %copy-start.1 = (bf16[16,512,512]{2,1,0:T(8,128)(2,1)S(1)}, bf16[16,512,512]{2,1,0:T(8,128)(2,1)}, u32[]{:S(2)}) copy-start(bf16[16,512,512]{2,1,0:T(8,128)(2,1)} %v_ref.1) | copy-start | bytes 25165828
  19.1 1.6 %collective-permute-start = (f32[32,128]{1,0:T(8,128)S(1)}, f32[32,128]{1,0:T(8,128)S(1)}, u32[]{:S(2)}, u32[]{:S(2)}) collective-permute-start(f32[32,128]{1,0:T(8,128)S(1)} %get-tuple-element.21.part.mine), channel_id=1, source_target_pairs={{0,1},{1,0},{2,3},{3,2},{4,5},{5,4},{6,7},{7,6},{8,9},{9,8},{10,11... | collective-permute-start | bytes 49160 | tf_op jit(solution)/shard_map/ppermute | solution.py:442
  33.0 16.5 %copy-start.3 = (bf16[8192,8,16]{0,2,1:T(8,128)(2,1)S(1)}, bf16[8192,8,16]{0,2,1:T(8,128)(2,1)}, u32[]{:S(2)}) copy-start(bf16[8192,8,16]{0,2,1:T(8,128)(2,1)} %param.24) | copy-start | bytes 6291460
  33.0 18.3 %copy-start.5 = (bf16[8,16,4096]{2,1,0:T(8,128)(2,1)S(1)}, bf16[8,16,4096]{2,1,0:T(8,128)(2,1)}, u32[]{:S(2)}) copy-start(bf16[8,16,4096]{2,1,0:T(8,128)(2,1)} %param.25) | copy-start | bytes 3145732
  50.2 1.2 %collective-permute-start.1 = (f32[32,128]{1,0:T(8,128)S(1)}, f32[32,128]{1,0:T(8,128)S(1)}, u32[]{:S(2)}, u32[]{:S(2)}) collective-permute-start(f32[32,128]{1,0:T(8,128)S(1)} %project_output.1.part.mine), channel_id=1, source_target_pairs={{0,1},{1,0},{2,3},{3,2},{4,5},{5,4},{6,7},{7,6},{8,9},{9,8},{10,11... | collective-permute-start | bytes 49160 | tf_op jit(solution)/shard_map/ppermute | solution.py:442

commit v20 on v19

--- a/solution.py
+++ b/solution.py
@@ -170,7 +170,8 @@
         copy.wait()
     core = lax.axis_index("tensor")
     row_at = rows
-    spans = rows + owners * CAP
+    order = rows + owners * CAP
+    spans = order + rows
     for p in range(owners * CAP):
         meta[row_at + p] = -1
         slot_at[p] = -1
@@ -185,7 +186,16 @@
         meta[row_at + place] = r
         slot_at[place] = rest(slot, adapt)
         meta[r] = place
-        meta[spans + r] = lengths[r]
+    sizes = [lengths[r] for r in range(rows)]
+    ahead = [jnp.int32(0)] * rows
+    for r in range(rows):
+        for q in range(r):
+            shorter = jnp.where(sizes[q] <= sizes[r], 1, 0)
+            ahead[r] = ahead[r] + shorter
+            ahead[q] = ahead[q] + (1 - shorter)
+    for r in range(rows):
+        meta[order + ahead[r]] = r
+        meta[spans + r] = sizes[r]
     items = CAP * STEPS
     block = heads * items
     copies[3].wait()
@@ -265,7 +275,6 @@
     kn_ref,
     vn_ref,
     part,
-    order,
     base_out,
     kn_out,
     vn_out,
@@ -283,16 +292,6 @@
     mask_out[...] = one_hot(head_at == over(iota(mask_out.shape, 1), HD))
     gather_out[...] = unpack_matrix(meta, owners, heads, rows, True)
     pack_out[...] = pack_matrix(meta, owners, heads, rows, True)
-    sizes = [meta[rows + owners * CAP + r] for r in range(rows)]
-    ahead = [jnp.int32(0)] * rows
-    for r in range(rows):
-        for q in range(r):
-            shorter = jnp.where(sizes[q] <= sizes[r], 1, 0)
-            ahead[r] = ahead[r] + shorter
-            ahead[q] = ahead[q] + (1 - shorter)
-    for r in range(rows):
-        order[ahead[r]] = r
-        order[rows + r] = sizes[r]
     after[...] = part[: after.shape[0], :]
 
 
@@ -300,7 +299,7 @@
     owners,
     heads,
     rows,
-    order,
+    meta,
     base_ref,
     kn_ref,
     vn_ref,
@@ -321,7 +320,10 @@
     total = groups * pairs
 
     def span_of(row):
-        return order[rows + row]
+        return meta[2 * rows + owners * CAP + row]
+
+    def row_at(place):
+        return meta[rows + owners * CAP + place]
 
     delta = jnp.dot(
         gather_ref[...],
@@ -366,7 +368,7 @@
 
     def attend(at, extents):
         count = len(extents)
-        ordered = [order[at + k] for k in range(count)]
+        ordered = [row_at(at + k) for k in range(count)]
         scores, weights = {}, {}
         for t in range(count + 2 * LAG):
             if t < count:
@@ -377,7 +379,7 @@
                 done = t - 2 * LAG
                 mix(ordered[done], extents[done], *weights.pop(done))
 
-    by_shape(lambda place: span_of(order[place]), rows, k_ref.shape[1], attend)
+    by_shape(lambda place: span_of(row_at(place)), rows, k_ref.shape[1], attend)
 
     mixed = o_buf[...].astype(BF16)
     mixed_out[...] = mixed
@@ -477,7 +479,7 @@
     meta, blocks = pl.pallas_call(
         functools.partial(dispatch_kernel, owners, SPLIT, adapt, rank),
         out_shape=[
-            shape((2 * rows + owners * CAP,), I32),
+            shape((3 * rows + owners * CAP,), I32),
             shape((owners, SPLIT * CAP * STEPS, width // SPLIT + lanes), BF16),
         ],
         in_specs=[HBM] * 8,
@@ -517,10 +519,9 @@
         )(part, other, b_store, *after, *caches)
 
     other = swap_cores(part)
-    order, *prepared, after = pl.pallas_call(
+    *prepared, after = pl.pallas_call(
         functools.partial(prepare_kernel, owners, heads),
         out_shape=[
-            shape((2 * rows,), I32),
             shape((rows * STEPS * heads, wide), BF16),
             shape((STEPS * rows, heads * HD), BF16),
             shape((STEPS * rows, heads * HD), BF16),
@@ -530,7 +531,7 @@
             shape((8, lanes), F32),
         ],
         in_specs=[SMEM] + [VMEM] * 4,
-        out_specs=[SMEM] + [VMEM] * 7,
+        out_specs=[VMEM] * 7,
         compiler_params=small,
         name="prepare",
     )(meta, q_base, k_new, v_new, part)
@@ -552,7 +553,7 @@
         ],
         compiler_params=small,
         name="attend",
-    )(order, *prepared, cache_k, cache_v, returned)
+    )(meta, *prepared, cache_k, cache_v, returned)
 
     arrived = exchange(outgoing)
     part = pl.pallas_call(

time: 64.7 us -> 63.8 us (0.986)
  blocking collectives: 52.6 us -> 51.7 us
    all_to_all x4, blocking collectives: 52.6 us -> 51.7 us  [exchange(): lax.all_to_all(blocks, ('store', 'tensor'), split_axis=0, concat_axis=0,...]
    pallas_call x1, Pallas kernels: 1.51 us -> 0.78 us  [shards(): pl.pallas_call(functools.partial(prepare_kernel, owners, heads), out_shap...]
  transfers between devices with their start and end apart: 2 -> 2, of which waited for: 1 -> 2; matrix products, arithmetic and copies ran while one was open for 0% -> 0% of each run, Pallas kernels for 4% -> 3%
where the time goes in v20:
time: 63.8 us; the launch traced here: 63.6 us
  blocking collectives  51.7 us (81%)
  Pallas kernels  10.5 us (16%)
  between operations  0.81 us (1%)
    all_to_all x4, blocking collectives, exchange(): lax.all_to_all(blocks, ('store', 'tensor'), split_axis=0, concat_axis=0,...  51.7 us
    pallas_call x1, Pallas kernels, shards(): pl.pallas_call(functools.partial(attend_kernel, owners, heads, rows), out...  3.84 us
    pallas_call x1, Pallas kernels, shards(): pl.pallas_call(functools.partial(dispatch_kernel, owners, SPLIT, adapt, r...  1.9 us
  transfers between devices with their start and end apart: 2, of which 2 were waited for; matrix products, arithmetic and copies ran while one was open for 0% of the time, Pallas kernels for 3%

profile of v20, /device:TPU:0, one launch (start us, length us, event | category | flops | bytes accessed | tf_op | source)
XLA Modules:
  0.0 63.6 jit_solution(8670993205507203382)
XLA Ops:
  0.6 0.0 copy-start.2
  0.6 0.0 copy-start.8
  0.7 0.0 copy-start.7
  0.7 0.0 copy-start.6
  0.7 0.0 copy-start.4
  0.7 0.0 copy-start
  0.7 0.0 copy-start.1
  0.7 1.9 %dispatch.1 = (s32[64]{0:T(128)S(1)}, bf16[8,8,2176]{2,1,0:T(8,128)(2,1)S(1)}) custom-call(s32[16]{0:T(128)} %ids_hbm.1, s32[64]{0:T(128)} %slot_of_hbm.1, s32[16]{0:T(128)} %lengths_hbm.1, bf16[2,16,4096]{2,1,0:T(8,128)(2,1)} %x_hbm.1, bf16[16,512,512]{2,1,0:T(8,128)(2,1)} %k_ref.1, bf16[16,512,512]{2,1,0:T(8,128)(2,1)} %v_ref.1, ...), custom_call_target="tpu_custom_call" | custom-call | tf_op jit(solution)/shard_map/dispatch/pallas_call | solution.py:479
  2.6 16.0 %all_to_all.20.blocks = bf16[8,8,2176]{2,1,0:T(8,128)(2,1)S(1)} all-to-all(bf16[8,8,2176]{2,1,0:T(8,128)(2,1)S(1)} %get-tuple-element.19), channel_id=1, replica_groups={{0,12,6,4,14,2,8,10},{11,9,3,15,5,7,13,1},{16,28,22,20,30,18,24,26},{27..., dimensions={0} | all-to-all | bytes 557056 | tf_op jit(solution)/shard_map/all_to_all | solution.py:429
  18.7 0.0 copy-done.2
  18.7 0.6 project_query.1
  19.2 0.0 collective-permute-start
  19.3 0.0 copy-done.8
  19.3 0.0 copy-done.7
  19.3 0.0 copy-done.6
  19.3 0.8 %prepare.1 = (bf16[128,1024]{1,0:T(8,128)(2,1)S(1)}, bf16[32,512]{1,0:T(8,128)(2,1)S(1)}, bf16[32,512]{1,0:T(8,128)(2,1)S(1)}, bf16[64,512]{1,0:T(8,128)(2,1)S(1...) custom-call(s32[64]{0:T(128)S(1)} %get-tuple-element.18.meta, ...), custom_call_target="tpu_custom_call" | custom-call | tf_op jit(solution)/shard_map/prepare/pallas_call | solution.py:522
  20.1 0.4 collective-permute-done.other
  20.4 0.0 copy-done.4
  20.4 0.5 expand_query.1
  20.9 11.9 %all_to_all.21.blocks = bf16[8,16,1024]{2,1,0:T(8,128)(2,1)S(1)} all-to-all(bf16[8,16,1024]{2,1,0:T(8,128)(2,1)S(1)} %expand_query.1), channel_id=1, replica_groups={{0,12,6,4,14,2,8,10},{11,9,3,15,5,7,13,1},{16,28,22,20,30,18,24,26},{27..., dimensions={0} | all-to-all | bytes 524288 | tf_op jit(solution)/shard_map/all_to_all | solution.py:429
  32.8 0.0 copy-done
  32.8 0.0 copy-done.1
  32.8 0.0 copy-start.3
  32.8 0.0 copy-start.5
  32.8 3.8 %attend.1 = (bf16[128,1024]{1,0:T(8,128)(2,1)S(1)}, bf16[8,16,1024]{2,1,0:T(8,128)(2,1)S(1)}) custom-call(s32[64]{0:T(128)S(1)} %get-tuple-element.18.meta, bf16[128,1024]{1,0:T(8,128)(2,1)S(1)} %get-tuple-element.21.base_ref, bf16[32,512]{1,0:T(8,128)(2,1)S(1)} %get-tuple-element.22.kn_ref, bf16[32,512]{1,0:T(8,128)(2,1)S(1)} %get-tuple-element.23.vn_ref, ...), custom_call_target="tpu_custom_call" | custom-call | tf_op jit(solution)/shard_map/attend/pallas_call | solution.py:542
  36.7 12.4 %all_to_all.22.blocks = bf16[8,16,1024]{2,1,0:T(8,128)(2,1)S(1)} all-to-all(bf16[8,16,1024]{2,1,0:T(8,128)(2,1)S(1)} %get-tuple-element.29), channel_id=1, replica_groups={{0,12,6,4,14,2,8,10},{11,9,3,15,5,7,13,1},{16,28,22,20,30,18,24,26},{27..., dimensions={0} | all-to-all | bytes 524288 | tf_op jit(solution)/shard_map/all_to_all | solution.py:429
  49.1 0.0 copy-done.3
  49.1 0.6 project_output.1.part.mine
  49.7 0.0 collective-permute-start.1
  49.7 1.0 %finish.1 = (bf16[2,16,4096]{2,1,0:T(8,128)(2,1)}, f32[8,128]{1,0:T(8,128)S(1)}, bf16[128,128]{1,0:T(8,128)(2,1)S(1)}) custom-call(bf16[128,1024]{1,0:T(8,128)(2,1)S(1)} %get-tuple-element.28.mixed, bf16[128,128]{1,0:T(8,128)(2,1)S(1)} %get-tuple-element.25.gather_ref, f32[32,128]{1,0:T(8,128)S(1)} %project_output.1.part.mine), custom_call_target="tpu_custom_call" | custom-call | tf_op jit(solution)/shard_map/finish/pallas_call | solution.py:575
  50.7 0.2 collective-permute-done.1.other
  50.9 0.0 copy-done.5
  50.9 0.4 expand_output.1
  51.3 11.4 %all_to_all.23.blocks = bf16[8,16,1024]{2,1,0:T(8,128)(2,1)S(1)} all-to-all(bf16[8,16,1024]{2,1,0:T(8,128)(2,1)S(1)} %expand_output.1), channel_id=1, replica_groups={{0,12,6,4,14,2,8,10},{11,9,3,15,5,7,13,1},{16,28,22,20,30,18,24,26},{27..., dimensions={0} | all-to-all | bytes 524288 | tf_op jit(solution)/shard_map/all_to_all | solution.py:429
  62.7 0.9 %collect.1 = bf16[2,16,4096]{2,1,0:T(8,128)(2,1)} custom-call(bf16[128,128]{1,0:T(8,128)(2,1)S(1)} %get-tuple-element.32.spread, bf16[8,16,1024]{2,1,0:T(8,128)(2,1)S(1)} %all_to_all.23.blocks), custom_call_target="tpu_custom_call" | custom-call | tf_op jit(solution)/shard_map/collect/pallas_call | solution.py:590
Async XLA Ops:
  0.6 18.0 %copy-start.2 = (bf16[8192,8,16]{0,2,1:T(8,128)(2,1)S(1)}, bf16[8192,8,16]{0,2,1:T(8,128)(2,1)}, u32[]{:S(2)}) copy-start(bf16[8192,8,16]{0,2,1:T(8,128)(2,1)} %param.22) | copy-start | bytes 6291460
  0.6 18.6 %copy-start.8 = (bf16[2,16,512]{2,1,0:T(8,128)(2,1)S(1)}, bf16[2,16,512]{2,1,0:T(8,128)(2,1)}, u32[]{:S(2)}) copy-start(bf16[2,16,512]{2,1,0:T(8,128)(2,1)} %vn_ref.1) | copy-start | bytes 98308
  0.7 18.6 %copy-start.7 = (bf16[2,16,512]{2,1,0:T(8,128)(2,1)S(1)}, bf16[2,16,512]{2,1,0:T(8,128)(2,1)}, u32[]{:S(2)}) copy-start(bf16[2,16,512]{2,1,0:T(8,128)(2,1)} %kn_ref.1) | copy-start | bytes 98308
  0.7 18.6 %copy-start.6 = (bf16[2,16,4096]{2,1,0:T(8,128)(2,1)S(1)}, bf16[2,16,4096]{2,1,0:T(8,128)(2,1)}, u32[]{:S(2)}) copy-start(bf16[2,16,4096]{2,1,0:T(8,128)(2,1)} %q_ref.1) | copy-start | bytes 786436
  0.7 19.8 %copy-start.4 = (bf16[8,16,4096]{2,1,0:T(8,128)(2,1)S(1)}, bf16[8,16,4096]{2,1,0:T(8,128)(2,1)}, u32[]{:S(2)}) copy-start(bf16[8,16,4096]{2,1,0:T(8,128)(2,1)} %param.23) | copy-start | bytes 3145732
  0.7 32.1 %copy-start = (bf16[16,512,512]{2,1,0:T(8,128)(2,1)S(1)}, bf16[16,512,512]{2,1,0:T(8,128)(2,1)}, u32[]{:S(2)}) copy-start(bf16[16,512,512]{2,1,0:T(8,128)(2,1)} %k_ref.1) | copy-start | bytes 25165828
  0.7 32.1 %copy-start.1 = (bf16[16,512,512]{2,1,0:T(8,128)(2,1)S(1)}, bf16[16,512,512]{2,1,0:T(8,128)(2,1)}, u32[]{:S(2)}) copy-start(bf16[16,512,512]{2,1,0:T(8,128)(2,1)} %v_ref.1) | copy-start | bytes 25165828
  19.2 1.2 %collective-permute-start = (f32[32,128]{1,0:T(8,128)S(1)}, f32[32,128]{1,0:T(8,128)S(1)}, u32[]{:S(2)}, u32[]{:S(2)}) collective-permute-start(f32[32,128]{1,0:T(8,128)S(1)} %get-tuple-element.20.part.mine), channel_id=1, source_target_pairs={{0,1},{1,0},{2,3},{3,2},{4,5},{5,4},{6,7},{7,6},{8,9},{9,8},{10,11... | collective-permute-start | bytes 49160 | tf_op jit(solution)/shard_map/ppermute | solution.py:444
  32.8 16.2 %copy-start.3 = (bf16[8192,8,16]{0,2,1:T(8,128)(2,1)S(1)}, bf16[8192,8,16]{0,2,1:T(8,128)(2,1)}, u32[]{:S(2)}) copy-start(bf16[8192,8,16]{0,2,1:T(8,128)(2,1)} %param.24) | copy-start | bytes 6291460
  32.8 18.1 %copy-start.5 = (bf16[8,16,4096]{2,1,0:T(8,128)(2,1)S(1)}, bf16[8,16,4096]{2,1,0:T(8,128)(2,1)}, u32[]{:S(2)}) copy-start(bf16[8,16,4096]{2,1,0:T(8,128)(2,1)} %param.25) | copy-start | bytes 3145732
  49.7 1.2 %collective-permute-start.1 = (f32[32,128]{1,0:T(8,128)S(1)}, f32[32,128]{1,0:T(8,128)S(1)}, u32[]{:S(2)}, u32[]{:S(2)}) collective-permute-start(f32[32,128]{1,0:T(8,128)S(1)} %project_output.1.part.mine), channel_id=1, source_target_pairs={{0,1},{1,0},{2,3},{3,2},{4,5},{5,4},{6,7},{7,6},{8,9},{9,8},{10,11... | collective-permute-start | bytes 49160 | tf_op jit(solution)/shard_map/ppermute | solution.py:444

commit v21 on v20

--- a/solution.py
+++ b/solution.py
@@ -103,8 +103,14 @@
     return 3 if owners % 3 else 1
 
 
-def turned(place, owners, core):
-    return place + rest(core, 2) * (owners - 1 - 2 * place)
+def to_block(place, owners, core):
+    other = owners - 1 - rest(place * stride_of(owners), owners)
+    return place + rest(core, 2) * (other - place)
+
+
+def to_place(block, owners, core):
+    other = rest((owners - 1 - block) * pow(stride_of(owners), -1, owners), owners)
+    return block + rest(core, 2) * (other - block)
 
 
 def regroup_matrix(owners, heads, core):
@@ -112,7 +118,7 @@
     total = owners * heads * items
     at = iota((total, total), 0)
     head = over(at, owners * items)
-    owner = turned(rest(over(at, items), owners), owners, core)
+    owner = to_block(rest(over(at, items), owners), owners, core)
     return one_hot(
         iota((total, total), 1) == owner * (heads * items) + head * items + rest(at, items)
     )
@@ -122,7 +128,7 @@
     items = CAP * STEPS
     total = owners * heads * items
     at = iota((total, total), 0)
-    owner = turned(over(at, heads * items), owners, core)
+    owner = to_place(over(at, heads * items), owners, core)
     head = rest(over(at, items), heads)
     return one_hot(
         iota((total, total), 1) == head * (owners * items) + owner * items + rest(at, items)
@@ -181,7 +187,7 @@
         half = over(owner, 2)
         along = jnp.where(rest(owner, 2) == 0, half, owners - 1 - half)
         along = rest(along * pow(stride_of(owners), -1, owners), owners)
-        first = turned(along, owners, core) * CAP
+        first = to_block(along, owners, core) * CAP
         place = first + jnp.where(meta[row_at + first] >= 0, 1, 0)
         meta[row_at + place] = r
         slot_at[place] = rest(slot, adapt)
@@ -421,9 +427,9 @@
     owners = blocks.shape[0]
     cores = lax.axis_size("tensor")
     cycle = list(range(0, owners, 2)) + list(range(owners - 1, 0, -2))
-    cycle = [cycle[i * stride_of(owners) % owners] for i in range(owners)]
+    strided = [cycle[i * stride_of(owners) % owners] for i in range(owners)]
     groups = [
-        [s * cores + core for s in (cycle if core % 2 == 0 else cycle[::-1])]
+        [s * cores + core for s in (strided if core % 2 == 0 else cycle[::-1])]
         for core in range(cores)
     ]
     return lax.all_to_all(

time: 63.8 us -> 64.9 us (1.017)
  blocking collectives: 51.7 us -> 52.9 us
    all_to_all x4, blocking collectives: 51.7 us -> 52.9 us  [exchange(): lax.all_to_all(blocks, ('store', 'tensor'), split_axis=0, concat_axis=0,...]
where the time goes in v21:
time: 64.9 us; the launch traced here: 64.6 us
  blocking collectives  52.9 us (82%)
  Pallas kernels  10.3 us (16%)
  between operations  0.81 us (1%)
    all_to_all x4, blocking collectives, exchange(): lax.all_to_all(blocks, ('store', 'tensor'), split_axis=0, concat_axis=0,...  52.9 us
    pallas_call x1, Pallas kernels, shards(): pl.pallas_call(functools.partial(attend_kernel, owners, heads, rows), out...  3.61 us
    pallas_call x1, Pallas kernels, shards(): pl.pallas_call(functools.partial(dispatch_kernel, owners, SPLIT, adapt, r...  1.9 us
  transfers between devices with their start and end apart: 2, of which 2 were waited for; matrix products, arithmetic and copies ran while one was open for 0% of the time, Pallas kernels for 3%

profile of v21, /device:TPU:0, one launch (start us, length us, event | category | flops | bytes accessed | tf_op | source)
XLA Modules:
  0.0 64.6 jit_solution(8599238131036720698)
XLA Ops:
  0.6 0.0 copy-start.2
  0.6 0.0 copy-start.8
  0.7 0.0 copy-start.7
  0.7 0.0 copy-start.6
  0.7 0.0 copy-start.4
  0.7 0.0 copy-start
  0.7 0.0 copy-start.1
  0.7 1.9 %dispatch.1 = (s32[64]{0:T(128)S(1)}, bf16[8,8,2176]{2,1,0:T(8,128)(2,1)S(1)}) custom-call(s32[16]{0:T(128)} %ids_hbm.1, s32[64]{0:T(128)} %slot_of_hbm.1, s32[16]{0:T(128)} %lengths_hbm.1, bf16[2,16,4096]{2,1,0:T(8,128)(2,1)} %x_hbm.1, bf16[16,512,512]{2,1,0:T(8,128)(2,1)} %k_ref.1, bf16[16,512,512]{2,1,0:T(8,128)(2,1)} %v_ref.1, ...), custom_call_target="tpu_custom_call" | custom-call | tf_op jit(solution)/shard_map/dispatch/pallas_call | solution.py:485
  2.6 16.6 %all_to_all.20.blocks = bf16[8,8,2176]{2,1,0:T(8,128)(2,1)S(1)} all-to-all(bf16[8,8,2176]{2,1,0:T(8,128)(2,1)S(1)} %get-tuple-element.19), channel_id=1, replica_groups={{0,12,6,4,14,2,8,10},{3,7,11,15,13,9,5,1},{16,28,22,20,30,18,24,26},{19..., dimensions={0} | all-to-all | bytes 557056 | tf_op jit(solution)/shard_map/all_to_all | solution.py:435
  19.3 0.0 copy-done.2
  19.3 0.6 project_query.1
  19.8 0.0 collective-permute-start
  19.9 0.0 copy-done.8
  19.9 0.0 copy-done.7
  19.9 0.0 copy-done.6
  19.9 0.8 %prepare.1 = (bf16[128,1024]{1,0:T(8,128)(2,1)S(1)}, bf16[32,512]{1,0:T(8,128)(2,1)S(1)}, bf16[32,512]{1,0:T(8,128)(2,1)S(1)}, bf16[64,512]{1,0:T(8,128)(2,1)S(1...) custom-call(s32[64]{0:T(128)S(1)} %get-tuple-element.18.meta, ...), custom_call_target="tpu_custom_call" | custom-call | tf_op jit(solution)/shard_map/prepare/pallas_call | solution.py:528
  20.7 0.4 collective-permute-done.other
  21.1 0.0 copy-done.4
  21.1 0.5 expand_query.1
  21.5 12.3 %all_to_all.21.blocks = bf16[8,16,1024]{2,1,0:T(8,128)(2,1)S(1)} all-to-all(bf16[8,16,1024]{2,1,0:T(8,128)(2,1)S(1)} %expand_query.1), channel_id=1, replica_groups={{0,12,6,4,14,2,8,10},{3,7,11,15,13,9,5,1},{16,28,22,20,30,18,24,26},{19..., dimensions={0} | all-to-all | bytes 524288 | tf_op jit(solution)/shard_map/all_to_all | solution.py:435
  33.8 0.0 copy-done
  33.8 0.0 copy-done.1
  33.8 0.0 copy-start.3
  33.8 0.0 copy-start.5
  33.8 3.6 %attend.1 = (bf16[128,1024]{1,0:T(8,128)(2,1)S(1)}, bf16[8,16,1024]{2,1,0:T(8,128)(2,1)S(1)}) custom-call(s32[64]{0:T(128)S(1)} %get-tuple-element.18.meta, bf16[128,1024]{1,0:T(8,128)(2,1)S(1)} %get-tuple-element.21.base_ref, bf16[32,512]{1,0:T(8,128)(2,1)S(1)} %get-tuple-element.22.kn_ref, bf16[32,512]{1,0:T(8,128)(2,1)S(1)} %get-tuple-element.23.vn_ref, ...), custom_call_target="tpu_custom_call" | custom-call | tf_op jit(solution)/shard_map/attend/pallas_call | solution.py:548
  37.4 12.0 %all_to_all.22.blocks = bf16[8,16,1024]{2,1,0:T(8,128)(2,1)S(1)} all-to-all(bf16[8,16,1024]{2,1,0:T(8,128)(2,1)S(1)} %get-tuple-element.29), channel_id=1, replica_groups={{0,12,6,4,14,2,8,10},{3,7,11,15,13,9,5,1},{16,28,22,20,30,18,24,26},{19..., dimensions={0} | all-to-all | bytes 524288 | tf_op jit(solution)/shard_map/all_to_all | solution.py:435
  49.4 0.0 copy-done.3
  49.4 0.6 project_output.1.part.mine
  50.0 0.0 collective-permute-start.1
  50.1 1.0 %finish.1 = (bf16[2,16,4096]{2,1,0:T(8,128)(2,1)}, f32[8,128]{1,0:T(8,128)S(1)}, bf16[128,128]{1,0:T(8,128)(2,1)S(1)}) custom-call(bf16[128,1024]{1,0:T(8,128)(2,1)S(1)} %get-tuple-element.28.mixed, bf16[128,128]{1,0:T(8,128)(2,1)S(1)} %get-tuple-element.25.gather_ref, f32[32,128]{1,0:T(8,128)S(1)} %project_output.1.part.mine), custom_call_target="tpu_custom_call" | custom-call | tf_op jit(solution)/shard_map/finish/pallas_call | solution.py:581
  51.0 0.2 collective-permute-done.1.other
  51.2 0.0 copy-done.5
  51.3 0.5 expand_output.1
  51.7 12.0 %all_to_all.23.blocks = bf16[8,16,1024]{2,1,0:T(8,128)(2,1)S(1)} all-to-all(bf16[8,16,1024]{2,1,0:T(8,128)(2,1)S(1)} %expand_output.1), channel_id=1, replica_groups={{0,12,6,4,14,2,8,10},{3,7,11,15,13,9,5,1},{16,28,22,20,30,18,24,26},{19..., dimensions={0} | all-to-all | bytes 524288 | tf_op jit(solution)/shard_map/all_to_all | solution.py:435
  63.7 0.9 %collect.1 = bf16[2,16,4096]{2,1,0:T(8,128)(2,1)} custom-call(bf16[128,128]{1,0:T(8,128)(2,1)S(1)} %get-tuple-element.32.spread, bf16[8,16,1024]{2,1,0:T(8,128)(2,1)S(1)} %all_to_all.23.blocks), custom_call_target="tpu_custom_call" | custom-call | tf_op jit(solution)/shard_map/collect/pallas_call | solution.py:596
Async XLA Ops:
  0.6 18.6 %copy-start.2 = (bf16[8192,8,16]{0,2,1:T(8,128)(2,1)S(1)}, bf16[8192,8,16]{0,2,1:T(8,128)(2,1)}, u32[]{:S(2)}) copy-start(bf16[8192,8,16]{0,2,1:T(8,128)(2,1)} %param.22) | copy-start | bytes 6291460
  0.6 19.2 %copy-start.8 = (bf16[2,16,512]{2,1,0:T(8,128)(2,1)S(1)}, bf16[2,16,512]{2,1,0:T(8,128)(2,1)}, u32[]{:S(2)}) copy-start(bf16[2,16,512]{2,1,0:T(8,128)(2,1)} %vn_ref.1) | copy-start | bytes 98308
  0.7 19.2 %copy-start.7 = (bf16[2,16,512]{2,1,0:T(8,128)(2,1)S(1)}, bf16[2,16,512]{2,1,0:T(8,128)(2,1)}, u32[]{:S(2)}) copy-start(bf16[2,16,512]{2,1,0:T(8,128)(2,1)} %kn_ref.1) | copy-start | bytes 98308
  0.7 19.2 %copy-start.6 = (bf16[2,16,4096]{2,1,0:T(8,128)(2,1)S(1)}, bf16[2,16,4096]{2,1,0:T(8,128)(2,1)}, u32[]{:S(2)}) copy-start(bf16[2,16,4096]{2,1,0:T(8,128)(2,1)} %q_ref.1) | copy-start | bytes 786436
  0.7 20.4 %copy-start.4 = (bf16[8,16,4096]{2,1,0:T(8,128)(2,1)S(1)}, bf16[8,16,4096]{2,1,0:T(8,128)(2,1)}, u32[]{:S(2)}) copy-start(bf16[8,16,4096]{2,1,0:T(8,128)(2,1)} %param.23) | copy-start | bytes 3145732
  0.7 33.1 %copy-start = (bf16[16,512,512]{2,1,0:T(8,128)(2,1)S(1)}, bf16[16,512,512]{2,1,0:T(8,128)(2,1)}, u32[]{:S(2)}) copy-start(bf16[16,512,512]{2,1,0:T(8,128)(2,1)} %k_ref.1) | copy-start | bytes 25165828
  0.7 33.1 %copy-start.1 = (bf16[16,512,512]{2,1,0:T(8,128)(2,1)S(1)}, bf16[16,512,512]{2,1,0:T(8,128)(2,1)}, u32[]{:S(2)}) copy-start(bf16[16,512,512]{2,1,0:T(8,128)(2,1)} %v_ref.1) | copy-start | bytes 25165828
  19.8 1.2 %collective-permute-start = (f32[32,128]{1,0:T(8,128)S(1)}, f32[32,128]{1,0:T(8,128)S(1)}, u32[]{:S(2)}, u32[]{:S(2)}) collective-permute-start(f32[32,128]{1,0:T(8,128)S(1)} %get-tuple-element.20.part.mine), channel_id=1, source_target_pairs={{0,1},{1,0},{2,3},{3,2},{4,5},{5,4},{6,7},{7,6},{8,9},{9,8},{10,11... | collective-permute-start | bytes 49160 | tf_op jit(solution)/shard_map/ppermute | solution.py:450
  33.8 15.7 %copy-start.3 = (bf16[8192,8,16]{0,2,1:T(8,128)(2,1)S(1)}, bf16[8192,8,16]{0,2,1:T(8,128)(2,1)}, u32[]{:S(2)}) copy-start(bf16[8192,8,16]{0,2,1:T(8,128)(2,1)} %param.24) | copy-start | bytes 6291460
  33.8 17.5 %copy-start.5 = (bf16[8,16,4096]{2,1,0:T(8,128)(2,1)S(1)}, bf16[8,16,4096]{2,1,0:T(8,128)(2,1)}, u32[]{:S(2)}) copy-start(bf16[8,16,4096]{2,1,0:T(8,128)(2,1)} %param.25) | copy-start | bytes 3145732
  50.0 1.2 %collective-permute-start.1 = (f32[32,128]{1,0:T(8,128)S(1)}, f32[32,128]{1,0:T(8,128)S(1)}, u32[]{:S(2)}, u32[]{:S(2)}) collective-permute-start(f32[32,128]{1,0:T(8,128)S(1)} %project_output.1.part.mine), channel_id=1, source_target_pairs={{0,1},{1,0},{2,3},{3,2},{4,5},{5,4},{6,7},{7,6},{8,9},{9,8},{10,11... | collective-permute-start | bytes 49160 | tf_op jit(solution)/shard_map/ppermute | solution.py:450

commit v22 on v20

--- a/solution.py
+++ b/solution.py
@@ -12,7 +12,7 @@
 CAP = 2
 STEPS = 2
 LAG = 2
-SPLIT = 2
+SPLIT = 4
 BF16 = jnp.bfloat16
 F32 = jnp.float32
 I32 = jnp.int32

time: 63.8 us -> 64.2 us (level)
  no operation moved by 1% of the time
where the time goes in v22:
time: 64.2 us; the launch traced here: 63.8 us
  blocking collectives  52.1 us (81%)
  Pallas kernels  10.3 us (16%)
  between operations  0.79 us (1%)
    all_to_all x4, blocking collectives, exchange(): lax.all_to_all(blocks, ('store', 'tensor'), split_axis=0, concat_axis=0,...  52.1 us
    pallas_call x1, Pallas kernels, shards(): pl.pallas_call(functools.partial(attend_kernel, owners, heads, rows), out...  3.62 us
    pallas_call x1, Pallas kernels, shards(): pl.pallas_call(functools.partial(dispatch_kernel, owners, SPLIT, adapt, r...  1.9 us
  transfers between devices with their start and end apart: 2, of which 2 were waited for; matrix products, arithmetic and copies ran while one was open for 0% of the time, Pallas kernels for 3%

profile of v22, /device:TPU:0, one launch (start us, length us, event | category | flops | bytes accessed | tf_op | source)
XLA Modules:
  0.0 63.8 jit_solution(12023755434404278453)
XLA Ops:
  0.6 0.0 copy-start.2
  0.6 0.0 copy-start.8
  0.7 0.0 copy-start.7
  0.7 0.0 copy-start.6
  0.7 0.0 copy-start.4
  0.7 0.0 copy-start
  0.7 0.0 copy-start.1
  0.7 1.9 %dispatch.1 = (s32[64]{0:T(128)S(1)}, bf16[8,16,1152]{2,1,0:T(8,128)(2,1)S(1)}) custom-call(s32[16]{0:T(128)} %ids_hbm.1, s32[64]{0:T(128)} %slot_of_hbm.1, s32[16]{0:T(128)} %lengths_hbm.1, bf16[2,16,4096]{2,1,0:T(8,128)(2,1)} %x_hbm.1, bf16[16,512,512]{2,1,0:T(8,128)(2,1)} %k_ref.1, bf16[16,512,512]{2,1,0:T(8,128)(2,1)} %v_ref.1, ...), custom_call_target="tpu_custom_call" | custom-call | tf_op jit(solution)/shard_map/dispatch/pallas_call | solution.py:479
  2.6 16.2 %all_to_all.20.blocks = bf16[8,16,1152]{2,1,0:T(8,128)(2,1)S(1)} all-to-all(bf16[8,16,1152]{2,1,0:T(8,128)(2,1)S(1)} %get-tuple-element.19), channel_id=1, replica_groups={{0,12,6,4,14,2,8,10},{11,9,3,15,5,7,13,1},{16,28,22,20,30,18,24,26},{27..., dimensions={0} | all-to-all | bytes 589824 | tf_op jit(solution)/shard_map/all_to_all | solution.py:429
  18.8 0.0 copy-done.2
  18.8 0.6 project_query.1
  19.4 0.0 collective-permute-start
  19.4 0.0 copy-done.8
  19.4 0.0 copy-done.7
  19.4 0.0 copy-done.6
  19.5 0.8 %prepare.1 = (bf16[128,1024]{1,0:T(8,128)(2,1)S(1)}, bf16[32,512]{1,0:T(8,128)(2,1)S(1)}, bf16[32,512]{1,0:T(8,128)(2,1)S(1)}, bf16[64,512]{1,0:T(8,128)(2,1)S(1...) custom-call(s32[64]{0:T(128)S(1)} %get-tuple-element.18.meta, ...), custom_call_target="tpu_custom_call" | custom-call | tf_op jit(solution)/shard_map/prepare/pallas_call | solution.py:522
  20.2 0.4 collective-permute-done.other
  20.6 0.0 copy-done.4
  20.6 0.5 expand_query.1
  21.1 12.1 %all_to_all.21.blocks = bf16[8,16,1024]{2,1,0:T(8,128)(2,1)S(1)} all-to-all(bf16[8,16,1024]{2,1,0:T(8,128)(2,1)S(1)} %expand_query.1), channel_id=1, replica_groups={{0,12,6,4,14,2,8,10},{11,9,3,15,5,7,13,1},{16,28,22,20,30,18,24,26},{27..., dimensions={0} | all-to-all | bytes 524288 | tf_op jit(solution)/shard_map/all_to_all | solution.py:429
  33.1 0.0 copy-done
  33.2 0.0 copy-done.1
  33.2 0.0 copy-start.3
  33.2 0.0 copy-start.5
  33.2 3.6 %attend.1 = (bf16[128,1024]{1,0:T(8,128)(2,1)S(1)}, bf16[8,16,1024]{2,1,0:T(8,128)(2,1)S(1)}) custom-call(s32[64]{0:T(128)S(1)} %get-tuple-element.18.meta, bf16[128,1024]{1,0:T(8,128)(2,1)S(1)} %get-tuple-element.21.base_ref, bf16[32,512]{1,0:T(8,128)(2,1)S(1)} %get-tuple-element.22.kn_ref, bf16[32,512]{1,0:T(8,128)(2,1)S(1)} %get-tuple-element.23.vn_ref, ...), custom_call_target="tpu_custom_call" | custom-call | tf_op jit(solution)/shard_map/attend/pallas_call | solution.py:542
  36.8 12.5 %all_to_all.22.blocks = bf16[8,16,1024]{2,1,0:T(8,128)(2,1)S(1)} all-to-all(bf16[8,16,1024]{2,1,0:T(8,128)(2,1)S(1)} %get-tuple-element.29), channel_id=1, replica_groups={{0,12,6,4,14,2,8,10},{11,9,3,15,5,7,13,1},{16,28,22,20,30,18,24,26},{27..., dimensions={0} | all-to-all | bytes 524288 | tf_op jit(solution)/shard_map/all_to_all | solution.py:429
  49.2 0.0 copy-done.3
  49.2 0.6 project_output.1.part.mine
  49.8 0.0 collective-permute-start.1
  49.9 1.0 %finish.1 = (bf16[2,16,4096]{2,1,0:T(8,128)(2,1)}, f32[8,128]{1,0:T(8,128)S(1)}, bf16[128,128]{1,0:T(8,128)(2,1)S(1)}) custom-call(bf16[128,1024]{1,0:T(8,128)(2,1)S(1)} %get-tuple-element.28.mixed, bf16[128,128]{1,0:T(8,128)(2,1)S(1)} %get-tuple-element.25.gather_ref, f32[32,128]{1,0:T(8,128)S(1)} %project_output.1.part.mine), custom_call_target="tpu_custom_call" | custom-call | tf_op jit(solution)/shard_map/finish/pallas_call | solution.py:575
  50.8 0.2 collective-permute-done.1.other
  51.0 0.0 copy-done.5
  51.1 0.4 expand_output.1
  51.5 11.4 %all_to_all.23.blocks = bf16[8,16,1024]{2,1,0:T(8,128)(2,1)S(1)} all-to-all(bf16[8,16,1024]{2,1,0:T(8,128)(2,1)S(1)} %expand_output.1), channel_id=1, replica_groups={{0,12,6,4,14,2,8,10},{11,9,3,15,5,7,13,1},{16,28,22,20,30,18,24,26},{27..., dimensions={0} | all-to-all | bytes 524288 | tf_op jit(solution)/shard_map/all_to_all | solution.py:429
  62.9 0.9 %collect.1 = bf16[2,16,4096]{2,1,0:T(8,128)(2,1)} custom-call(bf16[128,128]{1,0:T(8,128)(2,1)S(1)} %get-tuple-element.32.spread, bf16[8,16,1024]{2,1,0:T(8,128)(2,1)S(1)} %all_to_all.23.blocks), custom_call_target="tpu_custom_call" | custom-call | tf_op jit(solution)/shard_map/collect/pallas_call | solution.py:590
Async XLA Ops:
  0.6 18.2 %copy-start.2 = (bf16[8192,8,16]{0,2,1:T(8,128)(2,1)S(1)}, bf16[8192,8,16]{0,2,1:T(8,128)(2,1)}, u32[]{:S(2)}) copy-start(bf16[8192,8,16]{0,2,1:T(8,128)(2,1)} %param.22) | copy-start | bytes 6291460
  0.6 18.8 %copy-start.8 = (bf16[2,16,512]{2,1,0:T(8,128)(2,1)S(1)}, bf16[2,16,512]{2,1,0:T(8,128)(2,1)}, u32[]{:S(2)}) copy-start(bf16[2,16,512]{2,1,0:T(8,128)(2,1)} %vn_ref.1) | copy-start | bytes 98308
  0.7 18.8 %copy-start.7 = (bf16[2,16,512]{2,1,0:T(8,128)(2,1)S(1)}, bf16[2,16,512]{2,1,0:T(8,128)(2,1)}, u32[]{:S(2)}) copy-start(bf16[2,16,512]{2,1,0:T(8,128)(2,1)} %kn_ref.1) | copy-start | bytes 98308
  0.7 18.8 %copy-start.6 = (bf16[2,16,4096]{2,1,0:T(8,128)(2,1)S(1)}, bf16[2,16,4096]{2,1,0:T(8,128)(2,1)}, u32[]{:S(2)}) copy-start(bf16[2,16,4096]{2,1,0:T(8,128)(2,1)} %q_ref.1) | copy-start | bytes 786436
  0.7 19.9 %copy-start.4 = (bf16[8,16,4096]{2,1,0:T(8,128)(2,1)S(1)}, bf16[8,16,4096]{2,1,0:T(8,128)(2,1)}, u32[]{:S(2)}) copy-start(bf16[8,16,4096]{2,1,0:T(8,128)(2,1)} %param.23) | copy-start | bytes 3145732
  0.7 32.5 %copy-start = (bf16[16,512,512]{2,1,0:T(8,128)(2,1)S(1)}, bf16[16,512,512]{2,1,0:T(8,128)(2,1)}, u32[]{:S(2)}) copy-start(bf16[16,512,512]{2,1,0:T(8,128)(2,1)} %k_ref.1) | copy-start | bytes 25165828
  0.7 32.5 %copy-start.1 = (bf16[16,512,512]{2,1,0:T(8,128)(2,1)S(1)}, bf16[16,512,512]{2,1,0:T(8,128)(2,1)}, u32[]{:S(2)}) copy-start(bf16[16,512,512]{2,1,0:T(8,128)(2,1)} %v_ref.1) | copy-start | bytes 25165828
  19.4 1.2 %collective-permute-start = (f32[32,128]{1,0:T(8,128)S(1)}, f32[32,128]{1,0:T(8,128)S(1)}, u32[]{:S(2)}, u32[]{:S(2)}) collective-permute-start(f32[32,128]{1,0:T(8,128)S(1)} %get-tuple-element.20.part.mine), channel_id=1, source_target_pairs={{0,1},{1,0},{2,3},{3,2},{4,5},{5,4},{6,7},{7,6},{8,9},{9,8},{10,11... | collective-permute-start | bytes 49160 | tf_op jit(solution)/shard_map/ppermute | solution.py:444
  33.2 16.1 %copy-start.3 = (bf16[8192,8,16]{0,2,1:T(8,128)(2,1)S(1)}, bf16[8192,8,16]{0,2,1:T(8,128)(2,1)}, u32[]{:S(2)}) copy-start(bf16[8192,8,16]{0,2,1:T(8,128)(2,1)} %param.24) | copy-start | bytes 6291460
  33.2 17.9 %copy-start.5 = (bf16[8,16,4096]{2,1,0:T(8,128)(2,1)S(1)}, bf16[8,16,4096]{2,1,0:T(8,128)(2,1)}, u32[]{:S(2)}) copy-start(bf16[8,16,4096]{2,1,0:T(8,128)(2,1)} %param.25) | copy-start | bytes 3145732
  49.8 1.2 %collective-permute-start.1 = (f32[32,128]{1,0:T(8,128)S(1)}, f32[32,128]{1,0:T(8,128)S(1)}, u32[]{:S(2)}, u32[]{:S(2)}) collective-permute-start(f32[32,128]{1,0:T(8,128)S(1)} %project_output.1.part.mine), channel_id=1, source_target_pairs={{0,1},{1,0},{2,3},{3,2},{4,5},{5,4},{6,7},{7,6},{8,9},{9,8},{10,11... | collective-permute-start | bytes 49160 | tf_op jit(solution)/shard_map/ppermute | solution.py:444
